TPU v7x, 32 devices: a whole 2x2x4 slice. The times are simulated.
32 devices in a mesh: dp: 4 (over y, x), fsdp: 8 (over z, core).
Axes of the slice: x: 2, y: 2, z: 4, core: 2. Of those that a mesh axis runs over, the one named last changes fastest.
Arguments:
- tokens: bfloat16 [4, 8192, 512], P('dp', 'fsdp'), may hold values from -6 to 6
- offsets: int32 [4, 5], P('dp'), may hold values from 0 to 8192, as said below
- padding: int32 [4, 8192], P('dp', 'fsdp'), may hold values from 0 to 1, as said below
- feature_bank: float32 [64, 256], replicated, may hold values from -5 to 5
- ln1_gain: bfloat16 [512], P(('dp', 'fsdp')), may hold values from 0.5 to 1.5
- ln1_bias: bfloat16 [512], P(('dp', 'fsdp')), may hold values from -3 to 3
- w_qkv: bfloat16 [512, 1536], P(('dp', 'fsdp')), may hold values from -0.25 to 0.25
- w_out: bfloat16 [512, 512], P(('dp', 'fsdp')), may hold values from -6 to 6
- ln2_gain: bfloat16 [512], P(('dp', 'fsdp')), may hold values from 0.5 to 1.5
- ln2_bias: bfloat16 [512], P(('dp', 'fsdp')), may hold values from -3 to 3
- w_up: bfloat16 [512, 2048], P(('dp', 'fsdp')), may hold values from -0.25 to 0.25
- b_up: bfloat16 [2048], P(('dp', 'fsdp')), may hold values from -3 to 3
- w_down: bfloat16 [2048, 512], P(('dp', 'fsdp')), may hold values from -0.125 to 0.125
- b_down: bfloat16 [512], P(('dp', 'fsdp')), may hold values from -3 to 3
- cotangent: bfloat16 [4, 8192, 512], P('dp', 'fsdp'), may hold values from -6 to 6
Outputs:
- mixed: bfloat16 [4, 8192, 512], P('dp', 'fsdp')
- grad_tokens: float32 [4, 8192, 512], P('dp', 'fsdp')
- grad_ln1_gain: float32 [512], P(('dp', 'fsdp'))
- grad_ln1_bias: float32 [512], P(('dp', 'fsdp'))
- grad_w_qkv: float32 [512, 1536], P(('dp', 'fsdp'))
- grad_w_out: float32 [512, 512], P(('dp', 'fsdp'))
- grad_ln2_gain: float32 [512], P(('dp', 'fsdp'))
- grad_ln2_bias: float32 [512], P(('dp', 'fsdp'))
- grad_w_up: float32 [512, 2048], P(('dp', 'fsdp'))
- grad_b_up: float32 [2048], P(('dp', 'fsdp'))
- grad_w_down: float32 [2048, 512], P(('dp', 'fsdp'))
- grad_b_down: float32 [512], P(('dp', 'fsdp'))
Inputs may be any that keep to these rules, and one draw needn't show every extreme that they name: Each row's offsets rise from 0 to 8192; cell c of the row holds slots offsets[c] to offsets[c+1] - 1, at least one slot. `padding`: the first slot of every cell is 1.
All inputs are finite; a program needn't handle non-finite values.
Results may differ from a plain program's by a relative error of at most 0.035.
Values may be sent and summed in bfloat16 or wider, within the bound.
No kernel may reach another device: no remote copies, remote signals or barrier semaphores. Data moves between devices by JAX's collectives and lax.ppermute only.
A program may use at most 192 MiB of HBM per device.

v0:
```python
import jax
import jax.numpy as jnp
from jax import lax
from jax.sharding import PartitionSpec as P

HEADS = 8
FEATS = 256
HEAD = 64


def layer_norm(values, gain, shift):
    center = values - jnp.mean(values, -1, keepdims=True)
    spread = jnp.mean(center * center, -1, keepdims=True)
    return center * lax.rsqrt(spread + 1e-05) * gain + shift


def feature_map(projected, omega):
    scaled = projected.reshape(projected.shape[0], HEADS, HEAD) * HEAD ** (-0.25)
    lifted = jnp.einsum("nhe,em->nhm", scaled, omega, precision=lax.Precision.HIGHEST)
    return jnp.exp(lifted - 0.5 * jnp.sum(scaled * scaled, -1, keepdims=True)) * FEATS ** (-0.5)


def inner_rows(left, right):
    return lax.dot_general(
        left, right, (((0,), (0,)), ((), ())), preferred_element_type=jnp.float32
    )


def outer_cols(left, right):
    return lax.dot_general(
        left, right, (((1,), (1,)), ((), ())), preferred_element_type=jnp.float32
    )


def local(
    tokens,
    offsets,
    padding,
    feature_bank,
    ln1_gain,
    ln1_bias,
    w_qkv,
    w_out,
    ln2_gain,
    ln2_bias,
    w_up,
    b_up,
    w_down,
    b_down,
    cotangent,
):
    shards = (ln1_gain, ln1_bias, w_qkv, w_out, ln2_gain, ln2_bias, w_up, b_up, w_down, b_down)
    gathered = (
        lax.all_gather(shards[0], ("dp", "fsdp"), axis=0, tiled=True),
        lax.all_gather(shards[1], ("dp", "fsdp"), axis=0, tiled=True),
        lax.all_gather(shards[2], ("dp", "fsdp"), axis=0, tiled=True),
        lax.all_gather(shards[3], ("dp", "fsdp"), axis=0, tiled=True),
        lax.all_gather(shards[4], ("dp", "fsdp"), axis=0, tiled=True),
        lax.all_gather(shards[5], ("dp", "fsdp"), axis=0, tiled=True),
        lax.all_gather(shards[6], ("dp", "fsdp"), axis=0, tiled=True),
        lax.all_gather(shards[7], ("dp", "fsdp"), axis=0, tiled=True),
        lax.all_gather(shards[8], ("dp", "fsdp"), axis=0, tiled=True),
        lax.all_gather(shards[9], ("dp", "fsdp"), axis=0, tiled=True),
    )
    (
        gain_one,
        shift_one,
        qkv_full,
        out_full,
        gain_two,
        shift_two,
        up_full,
        up_bias,
        down_full,
        down_bias,
    ) = gathered
    length = tokens.shape[1]
    width = tokens.shape[2]
    inputs_f = tokens[0].astype(jnp.float32)
    place = lax.axis_index("fsdp") * length + jnp.arange(length, dtype=jnp.int32)
    bounds = offsets[0]
    member = ((place[:, None] >= bounds[None, :-1]) & (place[:, None] < bounds[None, 1:])).astype(
        jnp.float32
    )
    member_low = member.astype(jnp.bfloat16)
    keep = padding[0].astype(jnp.float32)[:, None, None]
    normed = layer_norm(
        inputs_f, gain_one.astype(jnp.float32), shift_one.astype(jnp.float32)
    ).astype(jnp.bfloat16)
    project = jnp.dot(normed, qkv_full, preferred_element_type=jnp.float32)
    query = project[:, :width]
    key_part = project[:, width : 2 * width]
    value_part = project[:, 2 * width :]
    q_feat = feature_map(query, feature_bank).astype(jnp.bfloat16)
    k_feat = (keep * feature_map(key_part, feature_bank)).astype(jnp.bfloat16)
    values = value_part.reshape(length, HEADS, HEAD).astype(jnp.bfloat16)
    value_cells = values[:, :, None, :] * member_low[:, None, :, None]
    state_part = jnp.einsum(
        "nhm,nhce->chme", k_feat, value_cells, preferred_element_type=jnp.float32
    )
    total_part = jnp.einsum("nc,nhm->chm", member_low, k_feat, preferred_element_type=jnp.float32)
    state_sum, total_sum = (
        lax.psum(state_part.astype(jnp.bfloat16), "fsdp").astype(jnp.float32),
        lax.psum(total_part.astype(jnp.bfloat16), "fsdp").astype(jnp.float32),
    )
    state_low = state_sum.astype(jnp.bfloat16)
    total_low = total_sum.astype(jnp.bfloat16)
    numer_all = jnp.einsum("nhm,chme->nhce", q_feat, state_low, preferred_element_type=jnp.float32)
    numer = jnp.sum(numer_all * member[:, None, :, None], 2)
    denom_all = jnp.einsum("nhm,chm->nhc", q_feat, total_low, preferred_element_type=jnp.float32)
    denom = jnp.sum(denom_all * member[:, None, :], 2)
    attend = (keep * numer / denom[:, :, None]).reshape(length, width).astype(jnp.bfloat16)
    middle = inputs_f + jnp.dot(attend, out_full, preferred_element_type=jnp.float32)
    normed_two = layer_norm(
        middle, gain_two.astype(jnp.float32), shift_two.astype(jnp.float32)
    ).astype(jnp.bfloat16)
    hidden = jnp.dot(normed_two, up_full, preferred_element_type=jnp.float32) + up_bias.astype(
        jnp.float32
    )
    active = jax.nn.gelu(hidden).astype(jnp.bfloat16)
    mixed = middle + (
        jnp.dot(active, down_full, preferred_element_type=jnp.float32)
        + down_bias.astype(jnp.float32)
    )
    gathered = (
        lax.all_gather(shards[0], ("dp", "fsdp"), axis=0, tiled=True),
        lax.all_gather(shards[1], ("dp", "fsdp"), axis=0, tiled=True),
        lax.all_gather(shards[2], ("dp", "fsdp"), axis=0, tiled=True),
        lax.all_gather(shards[3], ("dp", "fsdp"), axis=0, tiled=True),
        lax.all_gather(shards[4], ("dp", "fsdp"), axis=0, tiled=True),
        lax.all_gather(shards[5], ("dp", "fsdp"), axis=0, tiled=True),
        lax.all_gather(shards[6], ("dp", "fsdp"), axis=0, tiled=True),
        lax.all_gather(shards[7], ("dp", "fsdp"), axis=0, tiled=True),
        lax.all_gather(shards[8], ("dp", "fsdp"), axis=0, tiled=True),
        lax.all_gather(shards[9], ("dp", "fsdp"), axis=0, tiled=True),
    )
    (
        gain_one,
        shift_one,
        qkv_full,
        out_full,
        gain_two,
        shift_two,
        up_full,
        up_bias,
        down_full,
        down_bias,
    ) = gathered
    grad_out_low = cotangent[0]
    grad_out = grad_out_low.astype(jnp.float32)
    grad_down_bias = jnp.sum(grad_out, 0)
    grad_down = inner_rows(active, grad_out_low)
    _, gelu_back = jax.vjp(jax.nn.gelu, hidden)
    grad_hidden = gelu_back(outer_cols(grad_out_low, down_full))[0].astype(jnp.bfloat16)
    grad_up_bias = jnp.sum(grad_hidden, 0, dtype=jnp.float32)
    grad_up = inner_rows(normed_two, grad_hidden)
    _, norm_two_back = jax.vjp(
        layer_norm, middle, gain_two.astype(jnp.float32), shift_two.astype(jnp.float32)
    )
    grad_mid_norm, grad_gain_two, grad_shift_two = norm_two_back(outer_cols(grad_hidden, up_full))
    grad_middle = grad_out + grad_mid_norm
    grad_mid_low = grad_middle.astype(jnp.bfloat16)
    grad_outproj = inner_rows(attend, grad_mid_low)
    grad_attend = outer_cols(grad_mid_low, out_full).astype(jnp.bfloat16).astype(jnp.float32)
    grad_attend = grad_attend.reshape(length, HEADS, HEAD)
    grad_numer = (keep * grad_attend / denom[:, :, None]).astype(jnp.bfloat16)
    grad_denom = (-jnp.sum(keep * grad_attend * numer, -1) / (denom * denom)).astype(jnp.bfloat16)
    numer_cells = grad_numer[:, :, None, :] * member_low[:, None, :, None]
    denom_cells = grad_denom[:, :, None] * member_low[:, None, :]
    grad_q_feat = jnp.einsum(
        "nhce,chme->nhm", numer_cells, state_low, preferred_element_type=jnp.float32
    ) + jnp.einsum("nhc,chm->nhm", denom_cells, total_low, preferred_element_type=jnp.float32)
    state_grad_part = jnp.einsum(
        "nhm,nhce->chme", q_feat, numer_cells, preferred_element_type=jnp.float32
    )
    total_grad_part = jnp.einsum(
        "nhm,nhc->chm", q_feat, denom_cells, preferred_element_type=jnp.float32
    )
    state_grad, total_grad = (
        lax.psum(state_grad_part.astype(jnp.bfloat16), "fsdp").astype(jnp.float32),
        lax.psum(total_grad_part.astype(jnp.bfloat16), "fsdp").astype(jnp.float32),
    )
    state_grad_low = state_grad.astype(jnp.bfloat16)
    total_grad_low = total_grad.astype(jnp.bfloat16)
    grad_k_feat = jnp.einsum(
        "nhce,chme->nhm", value_cells, state_grad_low, preferred_element_type=jnp.float32
    ) + jnp.einsum("nc,chm->nhm", member_low, total_grad_low, preferred_element_type=jnp.float32)
    values_all = jnp.einsum(
        "nhm,chme->nhce", k_feat, state_grad_low, preferred_element_type=jnp.float32
    )
    grad_values = jnp.sum(values_all * member[:, None, :, None], 2).reshape(length, width)
    _, query_back = jax.vjp(lambda projected: feature_map(projected, feature_bank), query)
    _, key_back = jax.vjp(lambda projected: feature_map(projected, feature_bank), key_part)
    grad_query = query_back(grad_q_feat)[0]
    grad_key = key_back(keep * grad_k_feat)[0]
    grad_project = jnp.concatenate([grad_query, grad_key, grad_values], 1).astype(jnp.bfloat16)
    grad_qkv = inner_rows(normed, grad_project)
    _, norm_one_back = jax.vjp(
        layer_norm, inputs_f, gain_one.astype(jnp.float32), shift_one.astype(jnp.float32)
    )
    grad_in_norm, grad_gain_one, grad_shift_one = norm_one_back(outer_cols(grad_project, qkv_full))
    grad_tokens = grad_middle + grad_in_norm
    reduced = (
        lax.psum_scatter(grad_gain_one, ("dp", "fsdp"), scatter_dimension=0, tiled=True),
        lax.psum_scatter(grad_shift_one, ("dp", "fsdp"), scatter_dimension=0, tiled=True),
        lax.psum_scatter(grad_qkv, ("dp", "fsdp"), scatter_dimension=0, tiled=True),
        lax.psum_scatter(grad_outproj, ("dp", "fsdp"), scatter_dimension=0, tiled=True),
        lax.psum_scatter(grad_gain_two, ("dp", "fsdp"), scatter_dimension=0, tiled=True),
        lax.psum_scatter(grad_shift_two, ("dp", "fsdp"), scatter_dimension=0, tiled=True),
        lax.psum_scatter(grad_up, ("dp", "fsdp"), scatter_dimension=0, tiled=True),
        lax.psum_scatter(grad_up_bias, ("dp", "fsdp"), scatter_dimension=0, tiled=True),
        lax.psum_scatter(grad_down, ("dp", "fsdp"), scatter_dimension=0, tiled=True),
        lax.psum_scatter(grad_down_bias, ("dp", "fsdp"), scatter_dimension=0, tiled=True),
    )
    return (
        mixed.astype(jnp.bfloat16)[None],
        grad_tokens[None],
        reduced[0],
        reduced[1],
        reduced[2],
        reduced[3],
        reduced[4],
        reduced[5],
        reduced[6],
        reduced[7],
        reduced[8],
        reduced[9],
    )


def solution(mesh):
    return jax.shard_map(
        local,
        mesh=mesh,
        in_specs=(
            P("dp", "fsdp", None),
            P("dp", None),
            P("dp", "fsdp"),
            P(),
            P(("dp", "fsdp")),
            P(("dp", "fsdp")),
            P(("dp", "fsdp"), None),
            P(("dp", "fsdp"), None),
            P(("dp", "fsdp")),
            P(("dp", "fsdp")),
            P(("dp", "fsdp"), None),
            P(("dp", "fsdp")),
            P(("dp", "fsdp"), None),
            P(("dp", "fsdp")),
            P("dp", "fsdp", None),
        ),
        out_specs=(
            P("dp", "fsdp", None),
            P("dp", "fsdp", None),
            P(("dp", "fsdp")),
            P(("dp", "fsdp")),
            P(("dp", "fsdp"), None),
            P(("dp", "fsdp"), None),
            P(("dp", "fsdp")),
            P(("dp", "fsdp")),
            P(("dp", "fsdp"), None),
            P(("dp", "fsdp")),
            P(("dp", "fsdp"), None),
            P(("dp", "fsdp")),
        ),
        check_vma=False,
    )
```

profile of v0, /device:TPU:0, one launch (start us, length us, event | category | flops | bytes accessed | tf_op | source)
XLA Modules:
  0.0 895.5 jit_solution(7559815844898302324)
XLA Ops:
  11.8 42.2 %all-reduce.13 = (bf16[512]{0:T(512)(128)(2,1)S(1)}, bf16[512]{0:T(512)(128)(2,1)S(1)}, bf16[512]{0:T(512)(128)(2,1)S(1)}, bf16[512]{0:T(512)(128)(2,1)S(1)}, bf...) all-reduce(bf16[512]{0:T(512)(128)(2,1)S(1)} %dynamic-update-slice., ...), channel_id=1, replica_groups=mesh['dp'=4,'fsdp'=8] {'dp','fsdp'}, use_global_device_ids=true, to_apply=%add.1 | all-reduce | flops 4608 | bytes 18432
  55.2 13.9 %all-gather.4.cloned.1.call-done = bf16[512,1536]{1,0:T(8,128)(2,1)} async-done(((bf16[16,1536]{1,0:T(8,128)(2,1)}), bf16[512,1536]{1,0:T(8,128)(2,1)}) %all-gather.4.cloned.1.call-update) | async-done | bytes 1572880 | tf_op jit(solution)/shard_map/all_gather | solution.py:56
  69.1 3.4 fusion.114
  72.6 3.6 slice_add_fusion
  81.8 11.1 %multiply_convert_fusion.2 = (bf16[1024,8,256]{0,2,1:T(8,128)(2,1)S(1)}, f32[1024,8,256]{0,2,1:T(8,128)}) fusion(f32[1024]{0:T(1024)S(1)} %broadcast_multiply_fusion.2, f32[1024,8]{0,1:T(8,128)S(1)} %broadcast_multiply_fusion.1, f32[1024,8,64]{0,2,1:T(8,128)S(1)} %bitcast.196, f32[64,256]{1,0:T(8,128)S(1)} %copy-done), kind=kOutput, calls=%fused_computation.24 | convolution fusion | flops 1616904192 | bytes 14782464 | tf_op jit(solution)/shard_map/nhe,em->nhm/dot_general | solution.py:19
  99.9 45.1 %all_gather.39 = bf16[512,512]{1,0:T(8,128)(2,1)} all-gather(bf16[16,512]{1,0:T(8,128)(2,1)S(1)} %copy-done.28), channel_id=1, replica_groups=mesh['dp'=4,'fsdp'=8] {'dp','fsdp'}, dimensions={0}, use_global_device_ids=true | all-gather | bytes 540672 | tf_op jit(solution)/shard_map/all_gather | solution.py:57
  152.7 3.4 convolution_convert_fusion.2
  156.1 26.1 %psum.29 = bf16[4,8,256]{2,0,1:T(4,128)(2,1)S(1)} all-reduce(bf16[4,8,256]{2,0,1:T(4,128)(2,1)S(1)} %convolution_convert_fusion.2), channel_id=1, replica_groups=mesh['dp'=4,'fsdp'=8] {'fsdp'}, use_global_device_ids=true, to_apply=%region_6.0 | all-reduce | flops 8192 | bytes 32768 | tf_op jit(solution)/shard_map/psum | solution.py:104
  182.5 11.1 %multiply_convert_fusion.1 = (bf16[1024,8,256]{0,2,1:T(8,128)(2,1)S(1)}, f32[1024,8,256]{0,2,1:T(8,128)}) fusion(f32[1024,8]{0,1:T(8,128)S(1)} %broadcast_multiply_fusion, f32[1024,8,64]{0,2,1:T(8,128)S(1)} %bitcast.195, f32[64,256]{1,0:T(8,128)S(1)} %copy-done), kind=kOutput, calls=%fused_computation.22 | convolution fusion | flops 1616904192 | bytes 14778368 | tf_op jit(solution)/shard_map/nhe,em->nhm/dot_general | solution.py:19
  196.3 4.0 fusion.12
  203.0 11.9 %all-gather.6.cloned.1.call-done = bf16[512,2048]{1,0:T(8,128)(2,1)} async-done(((bf16[16,2048]{1,0:T(8,128)(2,1)}), bf16[512,2048]{1,0:T(8,128)(2,1)}) %all-gather.6.cloned.1.call-update) | async-done | bytes 2097168 | tf_op jit(solution)/shard_map/all_gather | solution.py:60
  214.9 7.3 fusion.117
  222.2 50.9 %all-gather.8.cloned.1.call-done = bf16[2048,512]{1,0:T(8,128)(2,1)} async-done(((bf16[64,512]{1,0:T(8,128)(2,1)}), bf16[2048,512]{1,0:T(8,128)(2,1)}) %all-gather.8.cloned.1.call-update) | async-done | bytes 2097168 | tf_op jit(solution)/shard_map/all_gather | solution.py:62
  273.1 10.7 %convert_reduce_fusion = (f32[2048]{0:T(1024)S(1)}, bf16[1024,2048]{1,0:T(8,128)(2,1)S(1)}) fusion(f32[1024,2048]{1,0:T(8,128)} %fusion.117, f32[2048]{0:T(1024)S(1)} %convert_element_type.172, bf16[2048,512]{1,0:T(8,128)(2,1)} %all-gather.8.cloned.1.call-done, bf16[1,1024,512]{2,1,0:T(8,128)(2,1)} %param.29), kind=kOutput, calls=%fused_computation.20 | convolution fusion | flops 2195716096 | bytes 15745024 | tf_op jit(solution)/shard_map/dot_general | solution.py:30
  283.8 3.7 fusion.123
  302.2 3.4 fusion.87
  305.6 28.9 %psum.31 = bf16[4,8,256]{2,0,1:T(4,128)(2,1)S(1)} all-reduce(bf16[4,8,256]{2,0,1:T(4,128)(2,1)S(1)} %fusion.87), channel_id=1, replica_groups=mesh['dp'=4,'fsdp'=8] {'fsdp'}, use_global_device_ids=true, to_apply=%region_15.0 | all-reduce | flops 8192 | bytes 32768 | tf_op jit(solution)/shard_map/psum | solution.py:181
  337.4 7.0 fusion.121
  346.2 10.6 %fusion.52 = bf16[1024,8,64]{0,2,1:T(8,128)(2,1)} fusion(f32[1024,8,64]{0,2,1:T(8,128)} %bitcast.198, f32[1024,8,256]{0,2,1:T(8,128)} %get-tuple-element.87, f32[1024,8]{0,1:T(8,128)S(1)} %negate_multiply_fusion.1, f32[64,256]{1,0:T(8,128)S(1)} %copy-done), kind=kOutput, calls=%fused_computation.74 | convolution fusion | flops 1612709888 | bytes 11632640 | tf_op jit(solution)/shard_map/transpose(jvp(nhe,em->nhm))/dot_general | solution.py:19
  356.8 3.4 all-reduce.19.cloned.1.call-done
  363.1 5.4 fusion.120
  370.1 5.8 fusion.50
  377.0 3.6 fusion.83
  380.7 6.6 fusion.116
  387.6 9.8 %fusion.88 = f32[2048,512]{1,0:T(8,128)} fusion(bf16[1,1024,512]{2,1,0:T(8,128)(2,1)} %param.29, f32[1024,2048]{1,0:T(8,128)} %fusion.117, f32[2048]{0:T(1024)S(1)} %convert_element_type.172), kind=kOutput, calls=%fused_computation.110 | convolution fusion | flops 2168455168 | bytes 13639680 | tf_op jit(solution)/shard_map/dot_general | solution.py:24
  397.4 8.7 fusion.81
  408.8 4.9 fusion.122
  423.5 39.5 %all-reduce.12 = (f32[512]{0:T(512)S(1)}, f32[512]{0:T(512)S(1)}, f32[512]{0:T(512)S(1)}, f32[512]{0:T(512)S(1)}, f32[2048]{0:T(1024)S(1)}, /*index=5*/f32[512]{0:T(512)S(1)}) all-reduce(f32[512]{0:T(512)S(1)} %get-tuple-element.50, f32[512]{0:T(512)S(1)} %get-tuple-element.88, ...), channel_id=2, replica_groups=mesh['dp'=4,'fsdp'=8] {'dp','fsdp'}, use_global_device_ids=true, to_apply=%region_21.0.clone | all-reduce | flops 4608 | bytes 36864
  466.5 30.2 %reduce-scatter.7.cloned.1.call-done = f32[16,512]{1,0:T(8,128)} async-done(((f32[512,512]{1,0:T(8,128)}), f32[16,512]{1,0:T(8,128)}) %reduce-scatter.7.cloned.1.call-update) | async-done | bytes 32784 | tf_op jit(solution)/shard_map/reduce_scatter | solution.py:207
  496.7 104.7 %reduce-scatter.5.cloned.1.call-done = f32[16,1536]{1,0:T(8,128)} async-done(((f32[512,1536]{1,0:T(8,128)}), f32[16,1536]{1,0:T(8,128)}) %reduce-scatter.5.cloned.1.call-update) | async-done | bytes 98320 | tf_op jit(solution)/shard_map/reduce_scatter | solution.py:206
  601.5 144.7 %reduce-scatter.9.cloned.1.call-done = f32[16,2048]{1,0:T(8,128)} async-done(((f32[512,2048]{1,0:T(8,128)}), f32[16,2048]{1,0:T(8,128)}) %reduce-scatter.9.cloned.1.call-update) | async-done | bytes 131088 | tf_op jit(solution)/shard_map/reduce_scatter | solution.py:210
  746.1 142.3 %reduce-scatter.11.cloned.1.call-done = f32[64,512]{1,0:T(8,128)} async-done(((f32[2048,512]{1,0:T(8,128)}), f32[64,512]{1,0:T(8,128)}) %reduce-scatter.11.cloned.1.call-update) | async-done | bytes 131088 | tf_op jit(solution)/shard_map/reduce_scatter | solution.py:212
  (175 shorter events, 72.5 us)
Async XLA Ops:
  7.2 74.6 %copy-start = (f32[64,256]{1,0:T(8,128)S(1)}, f32[64,256]{1,0:T(8,128)}, u32[]{:S(2)}) copy-start(f32[64,256]{1,0:T(8,128)} %param.18) | copy-start | bytes 196612
  7.2 3.1 copy-start.32
  7.2 3.3 copy-start.33
  7.2 3.6 copy-start.34
  7.2 3.8 copy-start.35
  7.2 4.0 copy-start.36
  7.2 4.3 copy-start.37
  7.3 61.9 %all-gather.4.cloned.1.call-start = ((), (), s32[]{:S(2)}) async-start(), calls=%async_computation.4 | async-start | bytes 1622016 | tf_op jit(solution)/shard_map/all_gather | solution.py:56
  8.0 188.3 %all-reduce.17.cloned.1.call-start = ((), (), s32[]{:S(2)}) async-start(), calls=%async_computation.5 | async-start | bytes 2097152 | tf_op jit(solution)/shard_map/psum | solution.py:103
  8.7 45.8 %copy-start.29 = (s32[1,5]{1,0:T(1,128)S(1)}, s32[1,5]{1,0:T(1,128)}, u32[]{:S(2)}) copy-start(s32[1,5]{1,0:T(1,128)} %param.16) | copy-start | bytes 64
  81.8 13.1 %copy-start.21 = (bf16[1024,512]{0,1:T(8,128)(2,1)S(1)}, bf16[1024,512]{0,1:T(8,128)(2,1)}, u32[]{:S(2)}) copy-start(bf16[1024,512]{0,1:T(8,128)(2,1)} %copy.72) | copy-start | bytes 3145732
  94.9 3.7 copy-start.20
  97.2 2.8 copy-start.28
  97.2 117.7 %all-gather.6.cloned.1.call-start = ((), (), s32[]{:S(2)}) async-start(), calls=%async_computation.6 | async-start | bytes 2162688 | tf_op jit(solution)/shard_map/all_gather | solution.py:60
  97.9 175.1 %all-gather.8.cloned.1.call-start = ((), (), s32[]{:S(2)}) async-start(), calls=%async_computation.7 | async-start | bytes 2162688 | tf_op jit(solution)/shard_map/all_gather | solution.py:62
  98.5 261.7 %all-reduce.19.cloned.1.call-start = ((), (), s32[]{:S(2)}) async-start(), calls=%async_computation.8 | async-start | bytes 2097152 | tf_op jit(solution)/shard_map/psum | solution.py:180
  273.1 10.7 %copy-start.30 = (bf16[512,2048]{1,0:T(8,128)(2,1)S(1)}, bf16[512,2048]{1,0:T(8,128)(2,1)}, u32[]{:S(2)}) copy-start(bf16[512,2048]{1,0:T(8,128)(2,1)} %all-gather.6.cloned.1.call-done) | copy-start | bytes 6291460
  283.8 3.7 copy-start.39
  290.4 2.4 copy-start.5
  297.3 2.6 copy-start.2
  302.2 194.6 %reduce-scatter.7.cloned.1.call-start = ((), (), s32[]{:S(2)}) async-start(), calls=%async_computation.10 | async-start | bytes 1081344 | tf_op jit(solution)/shard_map/reduce_scatter | solution.py:207
  337.4 7.0 copy-start.14
  337.4 7.0 copy-start.18
  346.1 255.3 %reduce-scatter.5.cloned.1.call-start = ((), (), s32[]{:S(2)}) async-start(), calls=%async_computation.9 | async-start | bytes 3244032 | tf_op jit(solution)/shard_map/reduce_scatter | solution.py:206
  363.0 5.5 copy-start.7
  363.1 5.5 copy-start.31
  369.9 6.1 copy-start.38
  370.1 6.8 copy-start.22
  380.6 365.5 %reduce-scatter.9.cloned.1.call-start = ((), (), s32[]{:S(2)}) async-start(), calls=%async_computation.11 | async-start | bytes 4325376 | tf_op jit(solution)/shard_map/reduce_scatter | solution.py:210
  387.3 501.2 %reduce-scatter.11.cloned.1.call-start = ((), (), s32[]{:S(2)}) async-start(), calls=%async_computation.12 | async-start | bytes 4325376 | tf_op jit(solution)/shard_map/reduce_scatter | solution.py:212
  406.1 2.7 copy-start.23
  406.1 2.7 copy-start.25
  (17 other events, 23.8 us)
Sparse Core Ops, SparseCore 0:
  11.1 57.9 all-gather.3
  97.3 58.9 all-reduce.16
  159.3 55.5 all-gather.5
  217.7 55.3 all-gather.7
  302.3 57.8 all-reduce.18
  362.9 133.8 reduce-scatter.6
  503.6 97.8 reduce-scatter.4
  604.4 141.6 reduce-scatter.8
  749.1 139.3 reduce-scatter.10
where the time goes:
time: 905 us; the launch traced here: 896 us
  waiting for transfers between devices  504 us (56%)
  blocking collectives  182 us (20%)
  matrix products  136 us (15%)
  local copies, waits for them, and re-layouts  44.5 us (5%)
  between operations  14.9 us (2%)
  other arithmetic  13.6 us (2%)
    reduce_scatter x1, waiting for transfers between devices, local(): lax.psum_scatter(grad_up, ('dp', 'fsdp'), scatter_dimension=0, tiled=True)  145 us
    reduce_scatter x1, waiting for transfers between devices, local(): lax.psum_scatter(grad_down, ('dp', 'fsdp'), scatter_dimension=0, tiled=True)  142 us
    reduce_scatter x1, waiting for transfers between devices, local(): lax.psum_scatter(grad_qkv, ('dp', 'fsdp'), scatter_dimension=0, tiled=True)  105 us
    unnamed x2, blocking collectives  81.8 us
    all_gather x1, waiting for transfers between devices, local(): lax.all_gather(shards[8], ('dp', 'fsdp'), axis=0, tiled=True)  50.9 us
    all_gather x1, blocking collectives, local(): lax.all_gather(shards[3], ('dp', 'fsdp'), axis=0, tiled=True)  45.1 us
    dot_general x4, matrix products, feature_map(): jnp.einsum('nhe,em->nhm', scaled, omega, precision=lax.Precision.HIGHEST)  38.7 us
    reduce_scatter x1, waiting for transfers between devices, local(): lax.psum_scatter(grad_outproj, ('dp', 'fsdp'), scatter_dimension=0, tiled...  30.2 us
  transfers between devices with their start and end apart: 9, of which 8 were waited for; matrix products, arithmetic and copies ran while one was open for 15% of the time, Pallas kernels for 0%

commit v1 on v0

v1 whole, which is shorter than its diff:
```python
import functools
import math

import jax
import jax.numpy as jnp
from jax import lax
from jax.experimental import pallas as pl
from jax.experimental.pallas import tpu as pltpu
from jax.sharding import PartitionSpec as P

HEADS = 8
FEATS = 256
HEAD = 64
PAIRS = HEADS // 2
SCALE = HEAD ** (-0.25)
LOGF = 0.5 * math.log(FEATS)
BLK = 256
KVROWS = 272
BF = jnp.bfloat16
F32 = jnp.float32
VMEM_LIMIT = 56 * 1024 * 1024


def dot(a, b):
    return jnp.dot(a, b, preferred_element_type=F32)


def dot_nt(a, b):
    return lax.dot_general(a, b, (((1,), (1,)), ((), ())), preferred_element_type=F32)


def dot_tn(a, b):
    return lax.dot_general(a, b, (((0,), (0,)), ((), ())), preferred_element_type=F32)


def norm_stats(x):
    width = x.shape[-1]
    c = x - jnp.sum(x, -1, keepdims=True) * (1.0 / width)
    r = lax.rsqrt(jnp.sum(c * c, -1, keepdims=True) * (1.0 / width) + 1e-05)
    return c * r, r


def lane_low(n):
    return lax.broadcasted_iota(jnp.int32, (n, 128), 1) < HEAD


def phi_pair(u, rhs_main, rhs_rest):
    low = lane_low(u.shape[0])
    s = u * SCALE
    hi = s.astype(BF)
    lo = (s - hi.astype(F32)).astype(BF)
    both = jnp.concatenate([hi, lo], 1)
    s2 = s * s
    feats = []
    for odd in (0, 1):
        lifted = dot(both, rhs_main[odd]) + dot(hi, rhs_rest[odd])
        half = jnp.sum(jnp.where(low, 0.0, s2) if odd else jnp.where(low, s2, 0.0), -1, keepdims=True)
        feats.append(jnp.exp(lifted - (0.5 * half + LOGF)))
    return s, feats


def cell_range(sc, blk, cells):
    first = sc[cells + 1] + blk * BLK
    last = first + BLK - 1
    lo = jnp.int32(0)
    hi = jnp.int32(0)
    for c in range(1, cells):
        lo += (sc[c] <= first).astype(jnp.int32)
        hi += (sc[c] <= last).astype(jnp.int32)
    return lo, hi, first


def cell_mask(sc, c, first, cols):
    place = lax.broadcasted_iota(jnp.int32, (BLK, cols), 0) + first
    return (place >= sc[c]) & (place < sc[c + 1])


def store_sums(acc, keep_ref, send_ref, core, cells, summed):
    rows = lax.broadcasted_iota(jnp.int32, (16, FEATS), 0)
    for slot, out in ((0, keep_ref), (1, send_ref)):
        base = (core ^ slot) * PAIRS
        for c in range(cells):
            tail = jnp.zeros((16, FEATS), F32)
            for i in range(PAIRS):
                part = acc[c, base + i]
                body, rest = (part[HEAD:], part[:HEAD]) if i % 2 else (part[:HEAD], part[HEAD:])
                out[c, i * HEAD : (i + 1) * HEAD, :] = body.astype(BF)
                line = jnp.sum(rest, 0, keepdims=True) if summed else rest[0:1]
                tail = jnp.where(rows == i, line, tail)
            out[c, PAIRS * HEAD :, :] = tail.astype(BF)


def load_sums(own_ref, other_ref, full, core, cells, single):
    rows = lax.broadcasted_iota(jnp.int32, (HEAD, FEATS), 0)
    for slot, src in ((0, own_ref), (1, other_ref)):
        base = (core ^ slot) * PAIRS
        for c in range(cells):
            tail = src[c, PAIRS * HEAD :, :].astype(F32)
            for i in range(PAIRS):
                body = src[c, i * HEAD : (i + 1) * HEAD, :]
                line = jnp.broadcast_to(tail[i : i + 1], (HEAD, FEATS))
                if single:
                    line = jnp.where(rows == 0, line, 0.0)
                line = line.astype(BF)
                if i % 2:
                    full[c, base + i, :HEAD, :] = line
                    full[c, base + i, HEAD:, :] = body
                else:
                    full[c, base + i, :HEAD, :] = body
                    full[c, base + i, HEAD:, :] = line


def key_kernel(
    cells, sc, x, keep, gain, shift, wk, wv, rm, rr, a1_o, sk_o, pk_o, vr_o, kept, sent, acc
):
    blk = pl.program_id(0)

    @pl.when(blk == 0)
    def _():
        acc[...] = jnp.zeros_like(acc)

    z, _ = norm_stats(x[...].astype(F32))
    a1 = (z * gain[...] + shift[...]).astype(BF)
    a1_o[...] = a1
    keys = dot(a1, wk[...])
    vr_o[...] = dot(a1, wv[...]).astype(BF)
    for p in range(PAIRS):
        s, feats = phi_pair(keys[:, 128 * p : 128 * p + 128], rm, rr)
        sk_o[:, 128 * p : 128 * p + 128] = s.astype(BF)
        for odd in (0, 1):
            h = 2 * p + odd
            pk_o[:, FEATS * h : FEATS * (h + 1)] = (keep[...] * feats[odd]).astype(BF)
    lo, hi, first = cell_range(sc, blk, cells)
    low = lane_low(BLK)

    def one(c, carry):
        mask = cell_mask(sc, c, first, 128)
        for p in range(PAIRS):
            v = vr_o[:, 128 * p : 128 * p + 128].astype(F32)
            for odd in (0, 1):
                h = 2 * p + odd
                aug = jnp.where(low, 1.0, v) if odd else jnp.where(low, v, 1.0)
                aug = jnp.where(mask, aug, 0.0).astype(BF)
                acc[c, h] += dot_tn(aug, pk_o[:, FEATS * h : FEATS * (h + 1)])
        return carry

    lax.fori_loop(lo, hi + 1, one, 0)

    @pl.when(blk == pl.num_programs(0) - 1)
    def _():
        store_sums(acc, kept, sent, sc[cells + 2], cells, False)


def rows_spec(cols):
    return pl.BlockSpec((BLK, cols), lambda i: (i, 0))


def whole_spec(shape):
    return pl.BlockSpec(shape, lambda i: (0,) * len(shape))


SMEM = pl.BlockSpec(memory_space=pltpu.SMEM)


def params():
    return pltpu.CompilerParams(vmem_limit_bytes=VMEM_LIMIT, dimension_semantics=("arbitrary",))


def sums_shape(cells):
    return (cells, KVROWS, FEATS)


def run_keys(sc, x, keep, gain, shift, wk, wv, rm, rr, cells):
    n, d = x.shape
    return pl.pallas_call(
        functools.partial(key_kernel, cells),
        grid=(n // BLK,),
        in_specs=[
            SMEM, rows_spec(d), rows_spec(1), whole_spec((1, d)), whole_spec((1, d)),
            whole_spec(wk.shape), whole_spec(wv.shape), whole_spec(rm.shape), whole_spec(rr.shape),
        ],
        out_specs=[
            rows_spec(d), rows_spec(d), rows_spec(HEADS * FEATS), rows_spec(d),
            whole_spec(sums_shape(cells)), whole_spec(sums_shape(cells)),
        ],
        out_shape=[
            jax.ShapeDtypeStruct((n, d), BF),
            jax.ShapeDtypeStruct((n, d), BF),
            jax.ShapeDtypeStruct((n, HEADS * FEATS), BF),
            jax.ShapeDtypeStruct((n, d), BF),
            jax.ShapeDtypeStruct(sums_shape(cells), BF),
            jax.ShapeDtypeStruct(sums_shape(cells), BF),
        ],
        scratch_shapes=[pltpu.VMEM((cells, HEADS, 128, FEATS), F32)],
        compiler_params=params(),
        cost_estimate=pl.CostEstimate(flops=8 * 10**9, bytes_accessed=10 * 10**6, transcendentals=2 * 10**6),
        name="keys",
    )(sc, x, keep, gain, shift, wk, wv, rm, rr)


def query_kernel(a1, wq, rm, rr, sq_o, pq_o):
    q = dot(a1[...], wq[...])
    for p in range(PAIRS):
        s, feats = phi_pair(q[:, 128 * p : 128 * p + 128], rm, rr)
        sq_o[:, 128 * p : 128 * p + 128] = s.astype(BF)
        for odd in (0, 1):
            h = 2 * p + odd
            pq_o[:, FEATS * h : FEATS * (h + 1)] = feats[odd].astype(BF)


def run_queries(a1, wq, rm, rr):
    n, d = a1.shape
    return pl.pallas_call(
        query_kernel,
        grid=(n // BLK,),
        in_specs=[rows_spec(d), whole_spec(wq.shape), whole_spec(rm.shape), whole_spec(rr.shape)],
        out_specs=[rows_spec(d), rows_spec(HEADS * FEATS)],
        out_shape=[
            jax.ShapeDtypeStruct((n, d), BF),
            jax.ShapeDtypeStruct((n, HEADS * FEATS), BF),
        ],
        compiler_params=params(),
        cost_estimate=pl.CostEstimate(flops=5 * 10**9, bytes_accessed=7 * 10**6, transcendentals=2 * 10**6),
        name="queries",
    )(a1, wq, rm, rr)


def spread_kernel(cells, sc, kept, got, out):
    for z in range(out.shape[0]):
        c = sc[8 + z]
        out[z] = (kept[c].astype(F32) + got[c].astype(F32)).astype(BF)


def run_spread(sc, kept, got, chips, cells):
    vm = pl.BlockSpec(memory_space=pltpu.VMEM)
    return pl.pallas_call(
        functools.partial(spread_kernel, cells),
        in_specs=[SMEM, vm, vm],
        out_specs=vm,
        out_shape=jax.ShapeDtypeStruct((chips, KVROWS, FEATS), BF),
        compiler_params=pltpu.CompilerParams(vmem_limit_bytes=VMEM_LIMIT),
        cost_estimate=pl.CostEstimate(flops=10**6, bytes_accessed=2 * 10**6, transcendentals=0),
        name="spread",
    )(sc, kept, got)


def collect_kernel(cells, chips, sc, kept, got, far, out):
    me = sc[16]
    before = jnp.zeros((KVROWS, FEATS), F32)
    after = jnp.zeros((KVROWS, FEATS), F32)
    for z in range(chips):
        part = far[z].astype(F32)
        before += jnp.where(z < me, part, 0.0)
        after += jnp.where(z > me, part, 0.0)
    for c in range(cells):
        total = kept[c].astype(F32) + got[c].astype(F32)
        total += jnp.where(sc[17] == c, before, 0.0) + jnp.where(sc[18] == c, after, 0.0)
        out[c] = total.astype(BF)


def run_collect(sc, kept, got, far, cells):
    vm = pl.BlockSpec(memory_space=pltpu.VMEM)
    return pl.pallas_call(
        functools.partial(collect_kernel, cells, far.shape[0]),
        in_specs=[SMEM, vm, vm, vm],
        out_specs=vm,
        out_shape=jax.ShapeDtypeStruct(kept.shape, BF),
        compiler_params=pltpu.CompilerParams(vmem_limit_bytes=VMEM_LIMIT),
        cost_estimate=pl.CostEstimate(flops=10**6, bytes_accessed=2 * 10**6, transcendentals=0),
        name="collect",
    )(sc, kept, got, far)


def middle_kernel(
    cells, sc, x, dy_r, keep_r, pq, own, other, w_out, gain, shift, w_up, b_up, w_down, b_down,
    mixed_o, gr_o, dpre_o, a2_o, ar_o, do_o, dx_o, grads_o, vec_o, vup_o, kept, sent,
    full, acc, num_s, den_s,
):
    blk = pl.program_id(0)

    @pl.when(blk == 0)
    def _():
        acc[...] = jnp.zeros_like(acc)
        vec_o[...] = jnp.zeros_like(vec_o)
        vup_o[...] = jnp.zeros_like(vup_o)
        load_sums(own, other, full, sc[cells + 2], cells, False)

    lo, hi, first = cell_range(sc, blk, cells)
    low = lane_low(BLK)

    def attend(c, carry):
        mask = cell_mask(sc, c, first, 128)
        for p in range(PAIRS):
            h = 2 * p
            lanes = slice(128 * p, 128 * p + 128)
            r0 = dot_nt(pq[:, FEATS * h : FEATS * (h + 1)], full[c, h])
            r1 = dot_nt(pq[:, FEATS * (h + 1) : FEATS * (h + 2)], full[c, h + 1])
            num = jnp.where(low, r0, r1)
            den = pltpu.roll(jnp.where(low, r1, r0), HEAD, 1)
            num_s[:, lanes] = jnp.where(mask, num, num_s[:, lanes])
            den_s[:, lanes] = jnp.where(mask, den, den_s[:, lanes])
        return carry

    lax.fori_loop(lo, hi + 1, attend, 0)
    keep = keep_r[...]
    inv = 1.0 / den_s[...]
    ar = (keep * num_s[...] * inv).astype(BF)
    ar_o[...] = ar
    x2 = x[...].astype(F32) + dot(ar, w_out[...])
    z2, r2 = norm_stats(x2)
    g2 = gain[...]
    a2 = (z2 * g2 + shift[...]).astype(BF)
    a2_o[...] = a2
    dy = dy_r[...]
    mixed = x2 + b_down[...]
    da2 = jnp.zeros_like(x2)
    width = x2.shape[1]
    k0 = math.sqrt(2.0 / math.pi)
    for j in range(w_up.shape[1] // width):
        cols = slice(j * width, (j + 1) * width)
        pre = dot(a2, w_up[:, cols]) + b_up[:, cols]
        sq = pre * pre
        t = jnp.tanh(k0 * pre * (1.0 + 0.044715 * sq))
        half = 0.5 * (1.0 + t)
        slope = half + 0.5 * pre * (1.0 - t * t) * (k0 + (3.0 * 0.044715 * k0) * sq)
        gr = (pre * half).astype(BF)
        gr_o[:, cols] = gr
        mixed += dot(gr, w_down[cols, :])
        dpre = (dot_nt(dy, w_down[cols, :]) * slope).astype(BF)
        dpre_o[:, cols] = dpre
        da2 += dot_nt(dpre, w_up[:, cols])
        vup_o[:, cols] += jnp.sum(dpre.astype(F32), 0, keepdims=True)
    mixed_o[...] = mixed.astype(BF)
    dyf = dy.astype(F32)
    dz = da2 * g2
    m1 = jnp.sum(dz, -1, keepdims=True) * (1.0 / width)
    m2 = jnp.sum(dz * z2, -1, keepdims=True) * (1.0 / width)
    dx2 = dyf + r2 * (dz - m1 - z2 * m2)
    dx_o[...] = dx2
    vec_o[0:1, :] += jnp.sum(da2 * z2, 0, keepdims=True)
    vec_o[1:2, :] += jnp.sum(da2, 0, keepdims=True)
    vec_o[2:3, :] += jnp.sum(dyf, 0, keepdims=True)
    do = dx2.astype(BF)
    do_o[...] = do
    dattn = keep * dot_nt(do, w_out[...]).astype(BF).astype(F32)
    dnum = dattn * inv
    dden = -dnum * num_s[...] * inv
    for p in range(PAIRS):
        lanes = slice(128 * p, 128 * p + 128)
        mine = dnum[:, lanes]
        swap = pltpu.roll(dden[:, lanes], HEAD, 1)
        h = 2 * p
        grads_o[:, 128 * h : 128 * h + 128] = jnp.where(low, mine, swap).astype(BF)
        grads_o[:, 128 * h + 128 : 128 * h + 256] = jnp.where(low, swap, mine).astype(BF)

    def gather(c, carry):
        mask = cell_mask(sc, c, first, 128)
        for h in range(HEADS):
            part = grads_o[:, 128 * h : 128 * h + 128]
            part = jnp.where(mask, part.astype(F32), 0.0).astype(BF)
            acc[c, h] += dot_tn(part, pq[:, FEATS * h : FEATS * (h + 1)])
        return carry

    lax.fori_loop(lo, hi + 1, gather, 0)

    @pl.when(blk == pl.num_programs(0) - 1)
    def _():
        store_sums(acc, kept, sent, sc[cells + 2], cells, True)


def run_middle(sc, x, dy, keep, pq, own, other, w_out, gain, shift, w_up, b_up, w_down, b_down, cells):
    n, d = x.shape
    ff = w_up.shape[1]
    wide = HEADS * 128
    return pl.pallas_call(
        functools.partial(middle_kernel, cells),
        grid=(n // BLK,),
        in_specs=[
            SMEM, rows_spec(d), rows_spec(d), rows_spec(1), rows_spec(HEADS * FEATS),
            whole_spec(own.shape), whole_spec(other.shape), whole_spec((d, d)), whole_spec((1, d)), whole_spec((1, d)),
            whole_spec((d, ff)), whole_spec((1, ff)), whole_spec((ff, d)), whole_spec((1, d)),
        ],
        out_specs=[
            rows_spec(d), rows_spec(ff), rows_spec(ff), rows_spec(d), rows_spec(d), rows_spec(d),
            rows_spec(d), rows_spec(wide), whole_spec((8, d)), whole_spec((1, ff)),
            whole_spec(sums_shape(cells)), whole_spec(sums_shape(cells)),
        ],
        out_shape=[
            jax.ShapeDtypeStruct((n, d), BF),
            jax.ShapeDtypeStruct((n, ff), BF),
            jax.ShapeDtypeStruct((n, ff), BF),
            jax.ShapeDtypeStruct((n, d), BF),
            jax.ShapeDtypeStruct((n, d), BF),
            jax.ShapeDtypeStruct((n, d), BF),
            jax.ShapeDtypeStruct((n, d), F32),
            jax.ShapeDtypeStruct((n, wide), BF),
            jax.ShapeDtypeStruct((8, d), F32),
            jax.ShapeDtypeStruct((1, ff), F32),
            jax.ShapeDtypeStruct(sums_shape(cells), BF),
            jax.ShapeDtypeStruct(sums_shape(cells), BF),
        ],
        scratch_shapes=[
            pltpu.VMEM((cells, HEADS, 128, FEATS), BF),
            pltpu.VMEM((cells, HEADS, 128, FEATS), F32),
            pltpu.VMEM((BLK, d), F32),
            pltpu.VMEM((BLK, d), F32),
        ],
        compiler_params=params(),
        cost_estimate=pl.CostEstimate(flops=14 * 10**9, bytes_accessed=30 * 10**6, transcendentals=2 * 10**6),
        name="middle",
    )(sc, x, dy, keep, pq, own, other, w_out, gain, shift, w_up, b_up, w_down, b_down)


def phi_back(s, feats, rhs, low):
    r0 = dot(feats[0].astype(BF), rhs[0])
    r1 = dot(feats[1].astype(BF), rhs[1])
    total = pltpu.roll(jnp.where(low, r1, r0), HEAD, 1)
    return (jnp.where(low, r0, r1) - s * total) * SCALE


def query_back_kernel(cells, sc, grads, pq, sq, own, other, rhs, dq_o, full, g_s):
    blk = pl.program_id(0)

    @pl.when(blk == 0)
    def _():
        load_sums(own, other, full, sc[cells + 2], cells, False)

    lo, hi, first = cell_range(sc, blk, cells)
    low = lane_low(BLK)

    def one(c, carry):
        mask = cell_mask(sc, c, first, FEATS)
        for h in range(HEADS):
            cols = slice(FEATS * h, FEATS * (h + 1))
            g = dot(grads[:, 128 * h : 128 * h + 128], full[c, h])
            g_s[:, cols] = jnp.where(mask, g, g_s[:, cols])
        return carry

    lax.fori_loop(lo, hi + 1, one, 0)
    for p in range(PAIRS):
        lanes = slice(128 * p, 128 * p + 128)
        feats = []
        for odd in (0, 1):
            cols = slice(FEATS * (2 * p + odd), FEATS * (2 * p + odd + 1))
            feats.append(g_s[:, cols] * pq[:, cols].astype(F32))
        dq_o[:, lanes] = phi_back(sq[:, lanes].astype(F32), feats, rhs, low).astype(BF)


def run_query_back(sc, grads, pq, sq, own, other, rhs, cells):
    n, d = sq.shape
    return pl.pallas_call(
        functools.partial(query_back_kernel, cells),
        grid=(n // BLK,),
        in_specs=[
            SMEM, rows_spec(HEADS * 128), rows_spec(HEADS * FEATS), rows_spec(d),
            whole_spec(own.shape), whole_spec(other.shape), whole_spec(rhs.shape),
        ],
        out_specs=rows_spec(d),
        out_shape=jax.ShapeDtypeStruct((n, d), BF),
        scratch_shapes=[
            pltpu.VMEM((cells, HEADS, 128, FEATS), BF),
            pltpu.VMEM((BLK, HEADS * FEATS), F32),
        ],
        compiler_params=params(),
        cost_estimate=pl.CostEstimate(flops=3 * 10**9, bytes_accessed=8 * 10**6, transcendentals=0),
        name="query_back",
    )(sc, grads, pq, sq, own, other, rhs)


def key_back_kernel(
    cells, sc, x, a1, gain, pk, vr, sk, dq, dx, own, other, rhs, wq, wk, wv, gt_o, dk_o, dv_o, vec_o, full, g_s, v_s
):
    blk = pl.program_id(0)

    @pl.when(blk == 0)
    def _():
        vec_o[...] = jnp.zeros_like(vec_o)
        load_sums(own, other, full, sc[cells + 2], cells, True)

    lo, hi, first = cell_range(sc, blk, cells)
    low = lane_low(BLK)

    def one(c, carry):
        mask = cell_mask(sc, c, first, FEATS)
        narrow = cell_mask(sc, c, first, 128)
        for p in range(PAIRS):
            lanes = slice(128 * p, 128 * p + 128)
            v = vr[:, lanes].astype(F32)
            outs = []
            for odd in (0, 1):
                h = 2 * p + odd
                cols = slice(FEATS * h, FEATS * (h + 1))
                aug = (jnp.where(low, 1.0, v) if odd else jnp.where(low, v, 1.0)).astype(BF)
                g = dot(aug, full[c, h])
                g_s[:, cols] = jnp.where(mask, g, g_s[:, cols])
                outs.append(dot_nt(pk[:, cols], full[c, h]))
            v_s[:, lanes] = jnp.where(narrow, jnp.where(low, outs[0], outs[1]), v_s[:, lanes])
        return carry

    lax.fori_loop(lo, hi + 1, one, 0)
    for p in range(PAIRS):
        lanes = slice(128 * p, 128 * p + 128)
        feats = []
        for odd in (0, 1):
            cols = slice(FEATS * (2 * p + odd), FEATS * (2 * p + odd + 1))
            feats.append(g_s[:, cols] * pk[:, cols].astype(F32))
        dk_o[:, lanes] = phi_back(sk[:, lanes].astype(F32), feats, rhs, low).astype(BF)
    dv = v_s[...].astype(BF)
    dv_o[...] = dv
    da1 = dot_nt(dq[...], wq[...]) + dot_nt(dk_o[...], wk[...]) + dot_nt(dv, wv[...])
    z, r = norm_stats(x[...].astype(F32))
    width = z.shape[1]
    dz = da1 * gain[...]
    m1 = jnp.sum(dz, -1, keepdims=True) * (1.0 / width)
    m2 = jnp.sum(dz * z, -1, keepdims=True) * (1.0 / width)
    gt_o[...] = dx[...] + r * (dz - m1 - z * m2)
    vec_o[0:1, :] += jnp.sum(da1 * z, 0, keepdims=True)
    vec_o[1:2, :] += jnp.sum(da1, 0, keepdims=True)


def run_key_back(sc, x, a1, gain, pk, vr, sk, dq, dx, own, other, rhs, wq, wk, wv, cells):
    n, d = x.shape
    return pl.pallas_call(
        functools.partial(key_back_kernel, cells),
        grid=(n // BLK,),
        in_specs=[
            SMEM, rows_spec(d), rows_spec(d), whole_spec((1, d)), rows_spec(HEADS * FEATS), rows_spec(d),
            rows_spec(d), rows_spec(d), rows_spec(d), whole_spec(own.shape), whole_spec(other.shape),
            whole_spec(rhs.shape), whole_spec(wq.shape), whole_spec(wk.shape), whole_spec(wv.shape),
        ],
        out_specs=[rows_spec(d), rows_spec(d), rows_spec(d), whole_spec((8, d))],
        out_shape=[
            jax.ShapeDtypeStruct((n, d), F32),
            jax.ShapeDtypeStruct((n, d), BF),
            jax.ShapeDtypeStruct((n, d), BF),
            jax.ShapeDtypeStruct((8, d), F32),
        ],
        scratch_shapes=[
            pltpu.VMEM((cells, HEADS, 128, FEATS), BF),
            pltpu.VMEM((BLK, HEADS * FEATS), F32),
            pltpu.VMEM((BLK, d), F32),
        ],
        compiler_params=params(),
        cost_estimate=pl.CostEstimate(flops=5 * 10**9, bytes_accessed=12 * 10**6, transcendentals=0),
        name="key_back",
    )(sc, x, a1, gain, pk, vr, sk, dq, dx, own, other, rhs, wq, wk, wv)


AXES = ("dp", "fsdp")


def pair_axis(x, size, flip, axis):
    return lax.ppermute(x, axis, [(i, i ^ flip) for i in range(size)])


def same_core_groups(dp, fsdp):
    return [[d * fsdp + 2 * z + c for d in range(dp) for z in range(fsdp // 2)] for c in range(2)]


def chip_groups(fsdp):
    return [[2 * z + c for z in range(fsdp // 2)] for c in range(2)]


def local(dp, fsdp, tokens, offsets, padding, feature_bank, ln1_gain, ln1_bias, w_qkv, w_out, ln2_gain, ln2_bias,
          w_up, b_up, w_down, b_down, cotangent):
    ndev = dp * fsdp
    x = tokens[0]
    dy = cotangent[0]
    n, d = x.shape
    ff = w_up.shape[1]
    cells = offsets.shape[1] - 1
    chips = fsdp // 2
    rows = d // ndev
    wide = ff // d
    frow = ff // ndev
    spot = lax.axis_index("fsdp")
    core = spot % 2
    zpos = spot // 2
    bounds = offsets[0]

    starts = jnp.arange(chips, dtype=jnp.int32) * (2 * n)
    inner = bounds[1:cells]
    first_cell = jnp.sum((inner[None, :] <= starts[:, None]).astype(jnp.int32), 1)
    last_cell = jnp.sum((inner[None, :] <= starts[:, None] + (2 * n - 1)).astype(jnp.int32), 1)
    asked = jnp.where(jnp.arange(chips) > zpos, first_cell, last_cell)
    one = lambda v: jnp.reshape(v, (1,)).astype(jnp.int32)
    own_first = jnp.sum((inner <= zpos * (2 * n)).astype(jnp.int32))
    own_last = jnp.sum((inner <= zpos * (2 * n) + (2 * n - 1)).astype(jnp.int32))

    whi = feature_bank.astype(BF)
    wlo = (feature_bank - whi.astype(F32)).astype(BF)
    none = jnp.zeros_like(whi)
    rm = jnp.stack([jnp.concatenate([whi, none, whi, none], 0), jnp.concatenate([none, whi, none, whi], 0)])
    rr = jnp.stack([jnp.concatenate([wlo, none], 0), jnp.concatenate([none, wlo], 0)])
    ones = jnp.ones((FEATS, HEAD), BF)
    rback = jnp.stack([jnp.concatenate([whi.T, ones], 1), jnp.concatenate([ones, whi.T], 1)])
    keep = padding[0].astype(F32)[:, None]

    vecs = jnp.concatenate(
        [v.reshape(rows, -1) for v in (ln1_gain, ln1_bias, ln2_gain, ln2_bias, b_down, b_up)]
        + [jnp.zeros((rows, 128 - 5 - wide), BF)], 1
    )
    paired = dp == 4 and fsdp == 8
    lead = jnp.concatenate([w_qkv[:, d:], vecs], 1)
    rest = (w_qkv[:, :d], w_out, w_up)
    if paired:
        mine = lax.all_to_all(
            jnp.broadcast_to(lead[None], (ndev // 2,) + lead.shape), AXES, 0, 0,
            axis_index_groups=same_core_groups(dp, fsdp), tiled=True,
        )
        theirs = pair_axis(mine, fsdp, 1, "fsdp")
        lead_all = jnp.stack(
            [jnp.where(core == 0, mine, theirs), jnp.where(core == 0, theirs, mine)], 1
        ).reshape(d, -1)
    else:
        lead_all = lax.all_gather(lead, AXES, axis=0, tiled=True)
    body = jnp.concatenate(
        [w_qkv[:, :d], w_out] + [w_up[:, j * d : (j + 1) * d] for j in range(wide)] + [w_down], 0
    )
    body_all = lax.all_gather(body, AXES, axis=0, tiled=True).reshape(ndev, -1, d)
    take = lambda lo, size: body_all[:, lo : lo + size].reshape(ndev * size, d)
    wq = take(0, rows)
    wo = take(rows, rows)
    wup = jnp.concatenate([take((2 + j) * rows, rows) for j in range(wide)], 1)
    wdn = take((2 + wide) * rows, frow)
    wk, wv = lead_all[:, :d], lead_all[:, d : 2 * d]
    vt = lead_all[:, 2 * d :].astype(F32)
    line = lambda i: vt[:, i].reshape(1, d)
    up_bias = vt[:, 5 : 5 + wide].reshape(1, ff)

    sc = jnp.concatenate([bounds, one(spot * n), one(core if paired else jnp.int32(0)), jnp.zeros((1,), jnp.int32)])
    if paired:
        sc = jnp.concatenate([sc, jnp.pad(asked, (0, 8 - chips)), one(zpos), one(own_first), one(own_last)])
    sc = sc.astype(jnp.int32)

    def exchange(kept, sent):
        if not paired:
            total = lax.psum(jnp.stack([kept, sent]), "fsdp")
            return total[0], total[1]
        got = pair_axis(sent, fsdp, 1, "fsdp")
        out = run_spread(sc, kept, got, chips, cells)
        far = lax.all_to_all(out, "fsdp", 0, 0, axis_index_groups=chip_groups(fsdp), tiled=True)
        done = run_collect(sc, kept, got, far, cells)
        return done, pair_axis(done, fsdp, 1, "fsdp")

    a1, sk, pk, vr, kept, sent = run_keys(sc, x, keep, line(0), line(1), wk, wv, rm, rr, cells)
    own, other = exchange(kept, sent)
    sq, pq = run_queries(a1, wq, rm, rr)
    mixed, gr, dpre, a2, ar, do, dx2, grads, vec2, vup, kept, sent = run_middle(
        sc, x, dy, keep, pq, own, other, wo, line(2), line(3), wup, up_bias, wdn, line(4), cells
    )
    d_own, d_other = exchange(kept, sent)
    dq = run_query_back(sc, grads, pq, sq, own, other, rback, cells)

    def blocks(g, size):
        return g.astype(BF).reshape(ndev, size, d)

    gup = dot_tn(a2, dpre)
    gbody = jnp.concatenate(
        [blocks(dot_tn(a1, dq), rows), blocks(dot_tn(ar, do), rows)]
        + [blocks(gup[:, j * d : (j + 1) * d], rows) for j in range(wide)]
        + [blocks(dot_tn(gr, dy), frow)], 1
    )

    def scatter(g, split):
        if not paired:
            return lax.psum_scatter(g.astype(F32), AXES, scatter_dimension=0, tiled=True)[0]
        g = g.reshape((ndev // 2, 2) + g.shape[1:])
        pick = lambda c: lax.dynamic_index_in_dim(g, c, 1, keepdims=False)
        got = pair_axis(pick(1 - core), fsdp, 1, "fsdp")
        half = (pick(core).astype(F32) + got.astype(F32)).astype(BF)
        if split:
            part = lax.all_to_all(half, "dp", 0, 0, tiled=True).reshape((dp, chips) + g.shape[2:])
            half = jnp.sum(part.astype(F32), 0).astype(BF)
            part = lax.all_to_all(half, "fsdp", 0, 0, axis_index_groups=chip_groups(fsdp), tiled=True)
        else:
            part = lax.all_to_all(half, AXES, 0, 0, axis_index_groups=same_core_groups(dp, fsdp), tiled=True)
        return jnp.sum(part.astype(F32), 0)

    gbody = scatter(gbody, True)
    gt, dk, dv, vec1 = run_key_back(
        sc, x, a1, line(0), pk, vr, sk, dq, dx2, d_own, d_other, rback, wq, wk, wv, cells
    )
    vgrads = jnp.concatenate(
        [vec1[0:2].T, vec2[0:3].T, vup.reshape(d, wide), jnp.zeros((d, 128 - 5 - wide), F32)], 1
    )
    glead = jnp.concatenate([dot_tn(a1, dk), dot_tn(a1, dv), vgrads], 1).astype(BF)
    glead = scatter(glead.reshape(ndev, rows, -1), False)
    gvec = glead[:, 2 * d :]
    flat = lambda i: gvec[:, i]
    return (
        mixed[None],
        gt[None],
        flat(0),
        flat(1),
        jnp.concatenate([gbody[:rows], glead[:, : 2 * d]], 1),
        gbody[rows : 2 * rows],
        flat(2),
        flat(3),
        jnp.concatenate([gbody[(2 + j) * rows : (3 + j) * rows] for j in range(wide)], 1),
        gvec[:, 5 : 5 + wide].reshape(-1),
        gbody[(2 + wide) * rows :],
        flat(4),
    )


def solution(mesh):
    both = P(("dp", "fsdp"))
    mat = P(("dp", "fsdp"), None)
    act = P("dp", "fsdp", None)
    return jax.shard_map(
        functools.partial(local, mesh.shape["dp"], mesh.shape["fsdp"]),
        mesh=mesh,
        in_specs=(act, P("dp", None), P("dp", "fsdp"), P(), both, both, mat, mat, both, both, mat, both, mat, both, act),
        out_specs=(act, act, both, both, mat, mat, both, both, mat, both, mat, both),
        check_vma=False,
    )
```

time: 905 us -> 307 us (0.34)
  waiting for transfers between devices: 504 us -> 94.9 us
  blocking collectives: 182 us -> 21.5 us
  matrix products: 136 us -> 14.1 us
  Pallas kernels: 0 us -> 74.7 us
  starting transfers between devices: 0.61 us -> 25 us
    reduce_scatter x4 -> x0, waiting for transfers between devices: 422 us -> none  [the longest x1 145 us: local(): lax.psum_scatter(grad_up, ('dp', 'fsdp'), scatter_dimension=0, tiled=True)]
    dot_general x27 -> x6, matrix products: 136 us -> 14.1 us  [dot_tn(): lax.dot_general(a, b, (((0,), (0,)), ((), ())), preferred_element_type=F32)]
    all_to_all x0 -> x5, waiting for transfers between devices: none -> 85 us  [the longest x1 18.6 us: exchange(): lax.all_to_all(out, 'fsdp', 0, 0, axis_index_groups=chip_groups(fsdp), ti...]
    unnamed x2 -> x0, blocking collectives: 81.8 us -> none
    all_gather x3 -> x1, waiting for transfers between devices: 76.7 us -> 0.01 us  [local(): lax.all_gather(body, AXES, axis=0, tiled=True).reshape(ndev, -1, d)]
    pallas_call x0 -> x9, Pallas kernels: none -> 74.7 us  [the longest x1 28.8 us: run_middle(): pl.pallas_call(functools.partial(middle_kernel, cells), grid=(n // BLK,),...]
    psum x2 -> x0, blocking collectives: 55 us -> none  [the longest x1 28.9 us: local(): lax.psum(total_grad_part.astype(jnp.bfloat16), 'fsdp').astype(jnp.float32)]
    all_gather x1 -> x0, blocking collectives: 45.1 us -> none  [local(): lax.all_gather(shards[3], ('dp', 'fsdp'), axis=0, tiled=True)]
  transfers between devices with their start and end apart: 9 -> 13, of which waited for: 8 -> 9; matrix products, arithmetic and copies ran while one was open for 15% -> 14% of each run, Pallas kernels for 0% -> 13%
where the time goes in v1:
time: 307 us; the launch traced here: 305 us
  waiting for transfers between devices  94.9 us (31%)
  Pallas kernels  74.7 us (24%)
  local copies, waits for them, and re-layouts  47.4 us (15%)
  starting transfers between devices  25 us (8%)
  blocking collectives  21.5 us (7%)
  between operations  14.6 us (5%)
  matrix products  14.1 us (5%)
  other arithmetic  12.8 us (4%)
    pallas_call x1, Pallas kernels, run_middle(): pl.pallas_call(functools.partial(middle_kernel, cells), grid=(n // BLK,),...  28.8 us
    all_to_all x1, blocking collectives, exchange(): lax.all_to_all(out, 'fsdp', 0, 0, axis_index_groups=chip_groups(fsdp), ti...  21.5 us
    all_to_all x1, waiting for transfers between devices, exchange(): lax.all_to_all(out, 'fsdp', 0, 0, axis_index_groups=chip_groups(fsdp), ti...  18.6 us
    all_to_all x1, waiting for transfers between devices, local(): lax.all_to_all(jnp.broadcast_to(lead[None], (ndev // 2,) + lead.shape), A...  17.9 us
    all_to_all x1, waiting for transfers between devices, scatter(): lax.all_to_all(half, AXES, 0, 0, axis_index_groups=same_core_groups(dp, f...  16.9 us
    all_to_all x1, waiting for transfers between devices, scatter(): lax.all_to_all(half, 'dp', 0, 0, tiled=True)  16.3 us
    all_to_all x1, waiting for transfers between devices, scatter(): lax.all_to_all(half, 'fsdp', 0, 0, axis_index_groups=chip_groups(fsdp), t...  15.3 us
    dot_general x6, matrix products, dot_tn(): lax.dot_general(a, b, (((0,), (0,)), ((), ())), preferred_element_type=F32)  14.1 us
  transfers between devices with their start and end apart: 13, of which 9 were waited for; matrix products, arithmetic and copies ran while one was open for 14% of the time, Pallas kernels for 13%

profile of v1, /device:TPU:0, one launch (start us, length us, event | category | flops | bytes accessed | tf_op | source)
XLA Modules:
  0.0 304.9 jit_solution(3735338480694313203)
XLA Ops:
  19.3 8.3 %all-to-all-start = ((bf16[16,16,1152]{2,1,0:T(8,128)(2,1)}), bf16[16,16,1152]{2,1,0:T(8,128)(2,1)S(1)}, u32[]{:S(2)}, u32[]{:S(2)}) async-start(bf16[16,16,1152]{2,1,0:T(8,128)(2,1)} %broadcast_in_dim.13), calls=%async_computation | async-start | bytes 1179648 | tf_op jit(solution)/shard_map/all_to_all | solution.py:607
  29.8 17.9 %all-to-all-done = bf16[16,16,1152]{2,1,0:T(8,128)(2,1)S(1)} async-done(((bf16[16,16,1152]{2,1,0:T(8,128)(2,1)}), bf16[16,16,1152]{2,1,0:T(8,128)(2,1)S(1)}, u32[]{:S(2)}, u32[]{:S(2)}) %all-to-all-start) | async-done | bytes 589856 | tf_op jit(solution)/shard_map/all_to_all | solution.py:607
  55.7 10.6 %keys.1 = (bf16[1024,512]{1,0:T(8,128)(2,1)}, bf16[1024,512]{1,0:T(8,128)(2,1)}, bf16[1024,2048]{1,0:T(8,128)(2,1)}, bf16[1024,512]{1,0:T(8,128)(2,1)}, bf16[4,2...) custom-call(s32[19]{0:T(128)} %concatenate.69.sc, bf16[1024,512]{1,0:T(8,128)(2,1)} %bitcast.135, ...), custom_call_target="tpu_custom_call" | custom-call | flops 8000000000 | bytes 10000000 | tf_op jit(solution)/shard_map/keys/pallas_call | solution.py:175
  69.5 2.2 spread.2
  71.7 3.7 %all-to-all-start.1 = ((bf16[4,272,256]{2,1,0:T(8,128)(2,1)}), bf16[4,272,256]{2,1,0:T(8,128)(2,1)S(1)}, u32[]{:S(2)}, u32[]{:S(2)}) async-start(bf16[4,272,256]{2,1,0:T(8,128)(2,1)} %spread.2), calls=%async_computation.1 | async-start | bytes 1114112 | tf_op jit(solution)/shard_map/all_to_all | solution.py:642
  77.0 18.6 %all-to-all-done.1.far = bf16[4,272,256]{2,1,0:T(8,128)(2,1)S(1)} async-done(((bf16[4,272,256]{2,1,0:T(8,128)(2,1)}), bf16[4,272,256]{2,1,0:T(8,128)(2,1)S(1)}, u32[]{:S(2)}, u32[]{:S(2)}) %all-to-all-start.1) | async-done | bytes 557088 | tf_op jit(solution)/shard_map/all_to_all | solution.py:642
  96.5 2.6 collect.2.own
  99.1 3.4 %fusion.7 = (bf16[32,16,512]{2,1,0:T(8,128)(2,1)S(1)}, bf16[32,16,512]{2,1,0:T(8,128)(2,1)S(1)}, bf16[32,16,512]{2,1,0:T(8,128)(2,1)S(1)}, bf16[32,16,512]{2,1,0...) fusion(bf16[32,160,512]{2,1,0:T(8,128)(2,1)} %bitcast.98), kind=kLoop, calls=%fused_computation.72 | loop fusion | bytes 6291456 | tf_op jit(solution)/shard_map/slice | solution.py:621
  104.2 3.2 %slice.201 = bf16[32,64,512]{2,1,0:T(8,128)(2,1)} slice(bf16[32,160,512]{2,1,0:T(8,128)(2,1)} %bitcast.99), slice={[0:32], [96:160], [0:512]} | slice | bytes 4194304 | tf_op jit(solution)/shard_map/slice | solution.py:621
  107.3 6.5 %queries.1 = (bf16[1024,512]{1,0:T(8,128)(2,1)}, bf16[1024,2048]{1,0:T(8,128)(2,1)}) custom-call(bf16[1024,512]{1,0:T(8,128)(2,1)} %get-tuple-element.36.a1, bf16[512,512]{1,0:T(8,128)(2,1)} %bitcast.113, bf16[2,256,256]{2,1,0:T(8,128)(2,1)} %copy.66.rm, bf16[2,128,256]{2,1,0:T(8,128)(2,1)} %copy.67.rr), custom_call_target="tpu_custom_call" | custom-call | flops 5000000000 | bytes 7000000 | tf_op jit(solution)/shard_map/queries/pallas_call | solution.py:213
  114.7 28.8 %middle.1 = (bf16[1024,512]{1,0:T(8,128)(2,1)}, bf16[1024,2048]{1,0:T(8,128)(2,1)}, bf16[1024,2048]{1,0:T(8,128)(2,1)}, bf16[1024,512]{1,0:T(8,128)(2,1)}, bf16[...) custom-call(s32[19]{0:T(128)} %concatenate.69.sc, ...), custom_call_target="tpu_custom_call" | custom-call | flops 14000000000 | bytes 30000000 | tf_op jit(solution)/shard_map/middle/pallas_call | solution.py:375
  143.5 4.9 %convolution_convert_fusion.1 = bf16[512,2048]{1,0:T(8,128)(2,1)S(1)} fusion(bf16[1024,512]{1,0:T(8,128)(2,1)} %get-tuple-element.57, bf16[1024,2048]{1,0:T(8,128)(2,1)} %get-tuple-element.58), kind=kOutput, calls=%fused_computation.3 | convolution fusion | flops 2148532224 | bytes 7340032 | tf_op jit(solution)/shard_map/dot_general | solution.py:33
  148.6 7.6 %query_back.1.dq = bf16[1024,512]{1,0:T(8,128)(2,1)} custom-call(s32[19]{0:T(128)} %concatenate.69.sc, bf16[1024,1024]{1,0:T(8,128)(2,1)} %get-tuple-element.44.grads, bf16[1024,2048]{1,0:T(8,128)(2,1)} %get-tuple-element.37.pq, bf16[1024,512]{1,0:T(8,128)(2,1)} %get-tuple-element.45.sq, bf16[4,272,256]{2,1,0:T(8,128)(2,1)} %collect.2.own, ...), custom_call_target="tpu_custom_call" | custom-call | flops 3000000000 | bytes 8000000 | tf_op jit(solution)/shard_map/query_back/pallas_call | solution.py:451
  156.2 2.1 convolution_convert_fusion.3
  159.0 2.4 convolution_convert_fusion
  162.7 2.3 copy-done
  167.2 5.2 %collective-permute-done.3.got = bf16[4,272,256]{2,1,0:T(8,128)(2,1)S(1)} collective-permute-done((bf16[4,272,256]{2,1,0:T(8,128)(2,1)S(1)}, bf16[4,272,256]{2,1,0:T(8,128)(2,1)S(1)}, u32[]{:S(2)}, u32[]{:S(2)}) %collective-permute-start.3) | collective-permute-done | bytes 557088 | tf_op jit(solution)/shard_map/ppermute | solution.py:553
  173.2 2.2 spread.3
  175.4 21.5 %all_to_all.30.far = bf16[4,272,256]{2,1,0:T(8,128)(2,1)} all-to-all(bf16[4,272,256]{2,1,0:T(8,128)(2,1)} %spread.3), channel_id=1, replica_groups={{0,2,4,6},{1,3,5,7},{8,10,12,14},{9,11,13,15},{16,18,20,22},{17,19,21,2..., dimensions={0} | all-to-all | bytes 1114112 | tf_op jit(solution)/shard_map/all_to_all | solution.py:642
  196.9 2.7 collect.3.own
  202.5 11.5 %key_back.1 = (f32[1024,512]{1,0:T(8,128)}, bf16[1024,512]{1,0:T(8,128)(2,1)}, bf16[1024,512]{1,0:T(8,128)(2,1)}, f32[8,512]{1,0:T(8,128)}) custom-call(s32[19]{0:T(128)} %concatenate.69.sc, bf16[1024,512]{1,0:T(8,128)(2,1)} %bitcast.137, bf16[1024,512]{1,0:T(8,128)(2,1)} %get-tuple-element.36.a1, f32[1,512]{1,0:T(1,128)} %bitcast.123, ...), custom_call_target="tpu_custom_call" | custom-call | flops 5000000000 | bytes 12000000 | tf_op jit(solution)/shard_map/key_back/pallas_call | solution.py:523
  214.0 4.1 %fusion = bf16[16,160,512]{2,1,0:T(8,128)(2,1)} fusion(bf16[16,160,512]{2,1,0:T(8,128)(2,1)} %collective-permute-done.6, bf16[16,2,160,512]{3,2,1,0:T(8,128)(2,1)S(1)} %bitcast.97, s32[]{:T(128)S(6)} %select_n.43), kind=kLoop, calls=%fused_computation.1 | loop fusion | flops 5242880 | bytes 7864324 | tf_op jit(solution)/shard_map/convert_element_type | solution.py:671
  218.1 4.8 %all-to-all-start.4 = ((bf16[16,160,512]{2,1,0:T(8,128)(2,1)}), bf16[16,160,512]{2,1,0:T(8,128)(2,1)S(1)}, u32[]{:S(2)}, u32[]{:S(2)}) async-start(bf16[16,160,512]{2,1,0:T(8,128)(2,1)} %fusion), calls=%async_computation.4 | async-start | bytes 5242880 | tf_op jit(solution)/shard_map/all_to_all | solution.py:673
  223.8 2.4 convolution_convert_fusion.4
  228.5 3.2 %concatenate.84 = bf16[16,2,16,1152]{3,2,1,0:T(8,128)(2,1)} concatenate(bf16[16,2,16,512]{3,2,1,0:T(8,128)(2,1)} %bitcast.119, bf16[16,2,16,512]{3,2,1,0:T(8,128)(2,1)S(1)} %bitcast.118, bf16[16,2,16,2]{3,2,1,0:T(8,128)(2,1)S(1)} %bitcast.121, bf16[16,2,16,3]{3,2,1,0:T(8,128)(2,1)S(1)} %bitcast.120, bf16[16,2,16,4]{3,2,1,0:T(8,128)(2,1)S(1)} %concatenate.83, ...), dimensions={3} | concatenate | bytes 2359296 | tf_op jit(solution)/shard_map/concatenate | solution.py:687
  232.8 2.0 collective-permute-done.5
  234.8 2.0 fusion.1
  236.9 16.3 %all-to-all-done.4 = bf16[16,160,512]{2,1,0:T(8,128)(2,1)S(1)} async-done(((bf16[16,160,512]{2,1,0:T(8,128)(2,1)}), bf16[16,160,512]{2,1,0:T(8,128)(2,1)S(1)}, u32[]{:S(2)}, u32[]{:S(2)}) %all-to-all-start.4) | async-done | bytes 2621472 | tf_op jit(solution)/shard_map/all_to_all | solution.py:673
  253.1 3.6 %all-to-all-start.3 = ((bf16[16,16,1152]{2,1,0:T(8,128)(2,1)}), bf16[16,16,1152]{2,1,0:T(8,128)(2,1)S(1)}, u32[]{:S(2)}, u32[]{:S(2)}) async-start(bf16[16,16,1152]{2,1,0:T(8,128)(2,1)} %fusion.1), calls=%async_computation.3 | async-start | bytes 1179648 | tf_op jit(solution)/shard_map/all_to_all | solution.py:677
  258.2 16.9 %all-to-all-done.3 = bf16[16,16,1152]{2,1,0:T(8,128)(2,1)S(1)} async-done(((bf16[16,16,1152]{2,1,0:T(8,128)(2,1)}), bf16[16,16,1152]{2,1,0:T(8,128)(2,1)S(1)}, u32[]{:S(2)}, u32[]{:S(2)}) %all-to-all-start.3) | async-done | bytes 589856 | tf_op jit(solution)/shard_map/all_to_all | solution.py:677
  275.0 3.5 %all-to-all-start.5 = ((bf16[4,160,512]{2,1,0:T(8,128)(2,1)}), bf16[4,160,512]{2,1,0:T(8,128)(2,1)S(1)}, u32[]{:S(2)}, u32[]{:S(2)}) async-start(bf16[4,160,512]{2,1,0:T(8,128)(2,1)} %reduce_sum.71), calls=%async_computation.5 | async-start | bytes 1310720 | tf_op jit(solution)/shard_map/all_to_all | solution.py:675
  280.1 15.3 %all-to-all-done.5 = bf16[4,160,512]{2,1,0:T(8,128)(2,1)S(1)} async-done(((bf16[4,160,512]{2,1,0:T(8,128)(2,1)}), bf16[4,160,512]{2,1,0:T(8,128)(2,1)S(1)}, u32[]{:S(2)}, u32[]{:S(2)}) %all-to-all-start.5) | async-done | bytes 655392 | tf_op jit(solution)/shard_map/all_to_all | solution.py:675
  (130 shorter events, 48.2 us)
Async XLA Ops:
  7.2 43.3 %copy-start.7 = (s32[1,5]{1,0:T(1,128)S(1)}, s32[1,5]{1,0:T(1,128)}, u32[]{:S(2)}) copy-start(s32[1,5]{1,0:T(1,128)} %param.16) | copy-start | bytes 64
  7.2 42.2 %copy-start.6 = (s32[1,1024]{1,0:T(1,128)S(1)}, s32[1,1024]{1,0:T(1,128)}, u32[]{:S(2)}) copy-start(s32[1,1024]{1,0:T(1,128)} %param.17) | copy-start | bytes 12292
  7.2 91.9 %all-gather.2.cloned.1.call-start = ((), (), s32[]{:S(2)}) async-start(), calls=%async_computation.6 | async-start | bytes 5406720 | tf_op jit(solution)/shard_map/all_gather | solution.py:620
  19.3 28.3 %all-to-all-start = ((bf16[16,16,1152]{2,1,0:T(8,128)(2,1)}), bf16[16,16,1152]{2,1,0:T(8,128)(2,1)S(1)}, u32[]{:S(2)}, u32[]{:S(2)}) async-start(bf16[16,16,1152]{2,1,0:T(8,128)(2,1)} %broadcast_in_dim.13), calls=%async_computation | async-start | bytes 1179648 | tf_op jit(solution)/shard_map/all_to_all | solution.py:607
  47.6 5.5 %collective-permute-start = (bf16[16,16,1152]{2,1,0:T(8,128)(2,1)S(1)}, bf16[16,16,1152]{2,1,0:T(8,128)(2,1)S(1)}, u32[]{:S(2)}, u32[]{:S(2)}) collective-permute-start(bf16[16,16,1152]{2,1,0:T(8,128)(2,1)S(1)} %all-to-all-done), channel_id=1, source_target_pairs={{0,1},{1,0},{2,3},{3,2},{4,5},{5,4},{6,7},{7,6},{8,9},{9,8},{10,11... | collective-permute-start | bytes 1769480 | tf_op jit(solution)/shard_map/ppermute | solution.py:553
  66.3 2.4 collective-permute-start.1
  68.7 0.8 copy-start.1
  71.7 24.0 %all-to-all-start.1 = ((bf16[4,272,256]{2,1,0:T(8,128)(2,1)}), bf16[4,272,256]{2,1,0:T(8,128)(2,1)S(1)}, u32[]{:S(2)}, u32[]{:S(2)}) async-start(bf16[4,272,256]{2,1,0:T(8,128)(2,1)} %spread.2), calls=%async_computation.1 | async-start | bytes 1114112 | tf_op jit(solution)/shard_map/all_to_all | solution.py:642
  95.7 0.8 copy-start.3
  99.1 14.7 %collective-permute-start.2 = (bf16[4,272,256]{2,1,0:T(8,128)(2,1)}, bf16[4,272,256]{2,1,0:T(8,128)(2,1)S(1)}, u32[]{:S(2)}, u32[]{:S(2)}) collective-permute-start(bf16[4,272,256]{2,1,0:T(8,128)(2,1)} %collect.2.own), channel_id=1, source_target_pairs={{0,1},{1,0},{2,3},{3,2},{4,5},{5,4},{6,7},{7,6},{8,9},{9,8},{10,11... | collective-permute-start | bytes 1671176 | tf_op jit(solution)/shard_map/ppermute | solution.py:553
  113.9 0.8 copy-start.10
  148.6 7.6 %copy-start.12 = (bf16[1024,512]{1,0:T(8,128)(2,1)S(1)}, bf16[1024,512]{1,0:T(8,128)(2,1)}, u32[]{:S(2)}) copy-start(bf16[1024,512]{1,0:T(8,128)(2,1)} %get-tuple-element.36.a1) | copy-start | bytes 3145732
  156.2 2.2 copy-start.8
  156.2 2.8 copy-start.17
  159.0 2.4 copy-start.14
  159.0 2.4 copy-start.15
  162.4 4.8 %copy-start.9 = (bf16[4,272,256]{2,1,0:T(8,128)(2,1)S(1)}, bf16[4,272,256]{2,1,0:T(8,128)(2,1)}, u32[]{:S(2)}) copy-start(bf16[4,272,256]{2,1,0:T(8,128)(2,1)} %get-tuple-element.48) | copy-start | bytes 1671172
  162.7 2.3 copy-start
  165.0 35.5 %copy-start.5 = (f32[1,2048]{1,0:T(1,128)S(1)}, f32[1,2048]{1,0:T(1,128)}, u32[]{:S(2)}) copy-start(f32[1,2048]{1,0:T(1,128)} %get-tuple-element.54) | copy-start | bytes 24580
  166.7 47.3 %collective-permute-start.6 = (bf16[16,160,512]{2,1,0:T(8,128)(2,1)}, bf16[16,160,512]{2,1,0:T(8,128)(2,1)}, u32[]{:S(2)}, u32[]{:S(2)}) collective-permute-start(bf16[16,160,512]{2,1,0:T(8,128)(2,1)} %dynamic-slice_bitcast_fusion), channel_id=1, source_target_pairs={{0,1},{1,0},{2,3},{3,2},{4,5},{5,4},{6,7},{7,6},{8,9},{9,8},{10,11... | collective-permute-start | bytes 7864328 | tf_op jit(solution)/shard_map/ppermute | solution.py:553
  167.2 5.2 %collective-permute-start.3 = (bf16[4,272,256]{2,1,0:T(8,128)(2,1)S(1)}, bf16[4,272,256]{2,1,0:T(8,128)(2,1)S(1)}, u32[]{:S(2)}, u32[]{:S(2)}) collective-permute-start(bf16[4,272,256]{2,1,0:T(8,128)(2,1)S(1)} %copy-done.9), channel_id=1, source_target_pairs={{0,1},{1,0},{2,3},{3,2},{4,5},{5,4},{6,7},{7,6},{8,9},{9,8},{10,11... | collective-permute-start | bytes 1671176 | tf_op jit(solution)/shard_map/ppermute | solution.py:553
  172.4 0.8 copy-start.2
  199.5 2.2 collective-permute-start.4
  200.3 13.8 %slice-start = ((s8[5242880]{0:T(1024)(128)(4,1)}), s8[1048576]{0:T(1024)(128)(4,1)S(1)}, s32[]{:S(2)}) async-start(s8[5242880]{0:T(1024)(128)(4,1)} %bitcast.96), calls=%async_computation.7 | async-start | bytes 2097152
  201.7 0.8 copy-start.11
  202.5 11.5 %slice-start.1 = ((s8[5242880]{0:T(1024)(128)(4,1)}), s8[4194304]{0:T(1024)(128)(4,1)S(1)}, s32[]{:S(2)}) async-start(s8[5242880]{0:T(1024)(128)(4,1)} %bitcast.96), calls=%async_computation.8 | async-start | bytes 8388608
  218.1 35.0 %all-to-all-start.4 = ((bf16[16,160,512]{2,1,0:T(8,128)(2,1)}), bf16[16,160,512]{2,1,0:T(8,128)(2,1)S(1)}, u32[]{:S(2)}, u32[]{:S(2)}) async-start(bf16[16,160,512]{2,1,0:T(8,128)(2,1)} %fusion), calls=%async_computation.4 | async-start | bytes 5242880 | tf_op jit(solution)/shard_map/all_to_all | solution.py:673
  223.8 2.4 copy-start.13
  223.8 2.4 copy-start.16
  232.8 2.1 collective-permute-start.5
  253.1 21.9 %all-to-all-start.3 = ((bf16[16,16,1152]{2,1,0:T(8,128)(2,1)}), bf16[16,16,1152]{2,1,0:T(8,128)(2,1)S(1)}, u32[]{:S(2)}, u32[]{:S(2)}) async-start(bf16[16,16,1152]{2,1,0:T(8,128)(2,1)} %fusion.1), calls=%async_computation.3 | async-start | bytes 1179648 | tf_op jit(solution)/shard_map/all_to_all | solution.py:677
  275.0 20.4 %all-to-all-start.5 = ((bf16[4,160,512]{2,1,0:T(8,128)(2,1)}), bf16[4,160,512]{2,1,0:T(8,128)(2,1)S(1)}, u32[]{:S(2)}, u32[]{:S(2)}) async-start(bf16[4,160,512]{2,1,0:T(8,128)(2,1)} %reduce_sum.71), calls=%async_computation.5 | async-start | bytes 1310720 | tf_op jit(solution)/shard_map/all_to_all | solution.py:675
  (1 other events, 0.7 us)
Sparse Core Ops, SparseCore 0:
  13.2 77.9 all-gather.1

commit v2 on v1

v2 whole, which is shorter than its diff:
```python
import functools
import math

import jax
import jax.numpy as jnp
from jax import lax
from jax.experimental import pallas as pl
from jax.experimental.pallas import tpu as pltpu
from jax.sharding import PartitionSpec as P

HEADS = 8
FEATS = 256
HEAD = 64
PAIRS = HEADS // 2
SCALE = HEAD ** (-0.25)
LOGF = 0.5 * math.log(FEATS)
BLK = 256
KVROWS = 272
BF = jnp.bfloat16
F32 = jnp.float32
VMEM_LIMIT = 56 * 1024 * 1024


def dot(a, b):
    return jnp.dot(a, b, preferred_element_type=F32)


def dot_nt(a, b):
    return lax.dot_general(a, b, (((1,), (1,)), ((), ())), preferred_element_type=F32)


def dot_tn(a, b):
    return lax.dot_general(a, b, (((0,), (0,)), ((), ())), preferred_element_type=F32)


def norm_stats(x):
    width = x.shape[-1]
    c = x - jnp.sum(x, -1, keepdims=True) * (1.0 / width)
    r = lax.rsqrt(jnp.sum(c * c, -1, keepdims=True) * (1.0 / width) + 1e-05)
    return c * r, r


def lane_low(n):
    return lax.broadcasted_iota(jnp.int32, (n, 128), 1) < HEAD


def phi_pair(u, rhs_main, rhs_rest):
    low = lane_low(u.shape[0])
    s = u * SCALE
    hi = s.astype(BF)
    lo = (s - hi.astype(F32)).astype(BF)
    both = jnp.concatenate([hi, lo], 1)
    s2 = s * s
    feats = []
    for odd in (0, 1):
        lifted = dot(both, rhs_main[odd]) + dot(hi, rhs_rest[odd])
        half = jnp.sum(jnp.where(low, 0.0, s2) if odd else jnp.where(low, s2, 0.0), -1, keepdims=True)
        feats.append(jnp.exp(lifted - (0.5 * half + LOGF)))
    return s, feats


def cell_range(bounds, blk, cells):
    first = lax.axis_index("fsdp") * (pl.num_programs(0) * BLK) + blk * BLK
    return cell_at(bounds, first, cells), cell_at(bounds, first + BLK - 1, cells), first


def cell_at(bounds, slot, cells):
    cell = jnp.int32(0)
    for c in range(1, cells):
        cell += (bounds[0, c] <= slot).astype(jnp.int32)
    return cell


def cell_mask(bounds, c, first, cols):
    place = lax.broadcasted_iota(jnp.int32, (BLK, cols), 0) + first
    return (place >= bounds[0, c]) & (place < bounds[0, c + 1])


def store_sums(acc, out, cells, summed):
    rows = lax.broadcasted_iota(jnp.int32, (16, FEATS), 0)
    for half in (0, 1):
        for c in range(cells):
            tail = jnp.zeros((16, FEATS), F32)
            for i in range(PAIRS):
                part = acc[c, half * PAIRS + i]
                body, rest = (part[HEAD:], part[:HEAD]) if i % 2 else (part[:HEAD], part[HEAD:])
                out[half, c, i * HEAD : (i + 1) * HEAD, :] = body.astype(BF)
                line = jnp.sum(rest, 0, keepdims=True) if summed else rest[0:1]
                tail = jnp.where(rows == i, line, tail)
            out[half, c, PAIRS * HEAD :, :] = tail.astype(BF)


def load_sums(bounds, sums, full, slots, cells, single):
    rows = lax.broadcasted_iota(jnp.int32, (HEAD, FEATS), 0)
    spot = lax.axis_index("fsdp")
    if len(sums) > 1:
        own, got, far_own, far_other = sums
        core = spot % 2
        start = (spot // 2) * (2 * slots)
        first, last = cell_at(bounds, start, cells), cell_at(bounds, start + 2 * slots - 1, cells)
    for slot in (0, 1):
        if len(sums) > 1:
            half = core ^ slot
            far = far_other if slot else far_own
            before = jnp.zeros(far.shape[1:], F32)
            after = jnp.zeros(far.shape[1:], F32)
            for z in range(far.shape[0]):
                part = far[z].astype(F32)
                before += jnp.where(z < spot // 2, part, 0.0)
                after += jnp.where(z > spot // 2, part, 0.0)
        else:
            half = slot
        for c in range(cells):
            if len(sums) > 1:
                total = own[half, c].astype(F32) + got[half, c].astype(F32)
                total += jnp.where(first == c, before, 0.0) + jnp.where(last == c, after, 0.0)
            else:
                total = sums[0][half, c].astype(F32)
            for i in range(PAIRS):
                body = total[i * HEAD : (i + 1) * HEAD].astype(BF)
                line = jnp.broadcast_to(total[PAIRS * HEAD + i : PAIRS * HEAD + i + 1], (HEAD, FEATS))
                if single:
                    line = jnp.where(rows == 0, line, 0.0)
                line = line.astype(BF)
                h = half * PAIRS + i
                full[c, h, :HEAD, :] = line if i % 2 else body
                full[c, h, HEAD:, :] = body if i % 2 else line


def feature_parts(bank, main, rest):
    w = bank[...]
    hi = w.astype(BF)
    lo = (w - hi.astype(F32)).astype(BF)
    none = jnp.zeros_like(hi)
    main[0] = jnp.concatenate([hi, none, hi, none], 0)
    main[1] = jnp.concatenate([none, hi, none, hi], 0)
    rest[0] = jnp.concatenate([lo, none], 0)
    rest[1] = jnp.concatenate([none, lo], 0)


def back_parts(bank, rhs):
    hi = bank[...].astype(BF)
    ones = jnp.ones_like(hi)
    rhs[0] = jnp.concatenate([hi, ones], 0)
    rhs[1] = jnp.concatenate([ones, hi], 0)


FEATURE_SCRATCH = [pltpu.VMEM((2, 4 * HEAD, FEATS), BF), pltpu.VMEM((2, 2 * HEAD, FEATS), BF)]


def copies(pieces, places, target, sems):
    spot = lax.axis_index("fsdp")
    core = spot % 2
    chip = lax.axis_index("dp") * (target.shape[0] // lax.axis_size("dp")) + spot // 2
    made = []
    for i, (masks, lo, hi) in enumerate(places):
        for side in (0, 1):
            src = pieces[i + side * len(places)]
            for k, mask in enumerate(masks):
                dst = target.at[chip ^ mask, core ^ side, lo:hi]
                made.append(pltpu.make_async_copy(src.at[k], dst, sems.at[len(made)]))
    return made


def both_cores(value):
    mine = lax.axis_index("fsdp") % 2 == 0
    a, b = value[:, 0], value[:, 1]
    return jnp.where(mine, a, b), jnp.where(mine, b, a)


def columns(ref, lo, hi):
    value = ref[..., lo:hi]
    return value.reshape(-1, value.shape[-1])


def key_kernel(cells, places, bounds, x, keep, bank, *refs):
    count = 2 * len(places) if places else 1
    pieces, (a1_o, sk_o, pk_o, vr_o, sums_o, vec_o), refs = refs[:count], refs[count : count + 6], refs[count + 6 :]
    if places:
        w, acc, rm, rr, sems = refs
    else:
        w = pieces[0]
        acc, rm, rr = refs
    blk = pl.program_id(0)
    d = x.shape[1]

    @pl.when(blk == 0)
    def _():
        if places:
            made = copies(pieces, places, w, sems)
            for copy in made:
                copy.start()
        acc[...] = jnp.zeros_like(acc)
        feature_parts(bank, rm, rr)
        if places:
            for copy in made:
                copy.wait()
        vec_o[...] = columns(w, 3 * d, 3 * d + 128).astype(F32).T[:16]

    z, _ = norm_stats(x[...].astype(F32))
    a1 = (z * vec_o[0:1] + vec_o[1:2]).astype(BF)
    a1_o[...] = a1
    keys = dot(a1, columns(w, d, 2 * d))
    vr_o[...] = dot(a1, columns(w, 2 * d, 3 * d)).astype(BF)
    for p in range(PAIRS):
        s, feats = phi_pair(keys[:, 128 * p : 128 * p + 128], rm, rr)
        sk_o[:, 128 * p : 128 * p + 128] = s.astype(BF)
        for odd in (0, 1):
            h = 2 * p + odd
            pk_o[:, FEATS * h : FEATS * (h + 1)] = (keep[...] * feats[odd]).astype(BF)
    lo, hi, first = cell_range(bounds, blk, cells)
    low = lane_low(BLK)

    def one(c, carry):
        mask = cell_mask(bounds, c, first, 128)
        for p in range(PAIRS):
            v = vr_o[:, 128 * p : 128 * p + 128].astype(F32)
            for odd in (0, 1):
                h = 2 * p + odd
                aug = jnp.where(low, 1.0, v) if odd else jnp.where(low, v, 1.0)
                aug = jnp.where(mask, aug, 0.0).astype(BF)
                acc[c, h] += dot_tn(aug, pk_o[:, FEATS * h : FEATS * (h + 1)])
        return carry

    lax.fori_loop(lo, hi + 1, one, 0)

    @pl.when(blk == pl.num_programs(0) - 1)
    def _():
        store_sums(acc, sums_o, cells, False)


def rows_spec(cols):
    return pl.BlockSpec((BLK, cols), lambda i: (i, 0))


def whole_spec(shape):
    return pl.BlockSpec(shape, lambda i: (0,) * len(shape))


def whole_specs(arrays):
    return [whole_spec(v.shape) for v in arrays]


SMEM = pl.BlockSpec(memory_space=pltpu.SMEM)
ANY = pl.BlockSpec(memory_space=pl.ANY)
VM = pl.BlockSpec(memory_space=pltpu.VMEM)


def params():
    return pltpu.CompilerParams(vmem_limit_bytes=VMEM_LIMIT, dimension_semantics=("arbitrary",))


def cost(gflop, mb):
    return pl.CostEstimate(flops=int(gflop * 1e3), bytes_accessed=int(mb * 1e3), transcendentals=0)


def sums_shape(cells):
    return (2, cells, KVROWS, FEATS)


def shape(*dims, kind=BF):
    return jax.ShapeDtypeStruct(dims, kind)


def run_keys(bounds, x, keep, bank, pieces, places, cells):
    n, d = x.shape
    out_specs = [
        rows_spec(d), rows_spec(d), rows_spec(HEADS * FEATS), rows_spec(d), whole_spec(sums_shape(cells)), whole_spec((16, d)),
    ]
    out_shape = [
        shape(n, d), shape(n, d), shape(n, HEADS * FEATS), shape(n, d), shape(*sums_shape(cells)), shape(16, d, kind=F32),
    ]
    scratch = [pltpu.VMEM((cells, HEADS, 128, FEATS), F32)] + FEATURE_SCRATCH
    if places:
        piece = pieces[0].shape
        w = (d // (2 * piece[1]), 2) + piece[1:]
        out_specs.append(whole_spec(w))
        out_shape.append(shape(*w))
        scratch.append(pltpu.SemaphoreType.DMA((d // piece[1],)))
    return pl.pallas_call(
        functools.partial(key_kernel, cells, places),
        grid=(n // BLK,),
        in_specs=[SMEM, rows_spec(d), rows_spec(1), whole_spec(bank.shape)]
        + ([ANY] * len(pieces) if places else whole_specs(pieces)),
        out_specs=out_specs,
        out_shape=out_shape,
        scratch_shapes=scratch,
        compiler_params=params(),
        cost_estimate=cost(8, 10),
        name="keys",
    )(bounds, x, keep, bank, *pieces)


def shuffle(j, rows, wide, d):
    a = lax.broadcasted_iota(jnp.int32, (d, d // wide), 0)
    b = lax.broadcasted_iota(jnp.int32, (d, d // wide), 1)
    hit = (a // (rows * wide) == b // rows) & (a % (rows * wide) == rows * j + b % rows)
    return jnp.where(hit, 1.0, 0.0).astype(BF)


def pad_rows(lines, count):
    return jnp.concatenate(lines + [jnp.zeros((count - len(lines), lines[0].shape[1]), lines[0].dtype)], 0)


def in_order(table, rows, wide):
    d = table.shape[1]
    part = d // wide
    total = jnp.zeros((8, d), F32)
    for j in range(wide):
        lines = pad_rows([table[5 + j : 6 + j, part * k : part * (k + 1)] for k in range(wide)], 8)
        total += dot_nt(lines.astype(BF), shuffle(j, rows, wide, d))
    return total


def by_owner(lines, rows, wide):
    d = lines.shape[1]
    out = []
    for j in range(wide):
        got = dot(lines.astype(BF), shuffle(j, rows, wide, d))
        out.append(jnp.concatenate([got[k : k + 1] for k in range(wide)], 1))
    return out


def query_kernel(rows, wide, a1, wq, bank, vec, sq_o, pq_o, up_o, rm, rr):
    @pl.when(pl.program_id(0) == 0)
    def _():
        feature_parts(bank, rm, rr)
        up_o[...] = in_order(vec[...], rows, wide)

    q = dot(a1[...], wq[...])
    for p in range(PAIRS):
        s, feats = phi_pair(q[:, 128 * p : 128 * p + 128], rm, rr)
        sq_o[:, 128 * p : 128 * p + 128] = s.astype(BF)
        for odd in (0, 1):
            h = 2 * p + odd
            pq_o[:, FEATS * h : FEATS * (h + 1)] = feats[odd].astype(BF)


def run_queries(a1, w, bank, vec, rows, wide):
    n, d = a1.shape
    return pl.pallas_call(
        functools.partial(query_kernel, rows, wide),
        grid=(n // BLK,),
        in_specs=[rows_spec(d), whole_spec((d, d)), whole_spec(bank.shape), whole_spec(vec.shape)],
        out_specs=[rows_spec(d), rows_spec(HEADS * FEATS), whole_spec((8, d))],
        out_shape=[shape(n, d), shape(n, HEADS * FEATS), shape(8, d, kind=F32)],
        scratch_shapes=FEATURE_SCRATCH,
        compiler_params=params(),
        cost_estimate=cost(5, 7),
        name="queries",
    )(a1, w, bank, vec)


def spread_kernel(cells, slots, bounds, own, got, out):
    spot = lax.axis_index("fsdp")
    core = spot % 2
    for z in range(out.shape[0]):
        c = cell_at(bounds, z * (2 * slots) + jnp.where(z > spot // 2, 0, 2 * slots - 1), cells)
        out[z] = (own[core, c].astype(F32) + got[core, c].astype(F32)).astype(BF)


def run_spread(bounds, own, got, chips, slots, cells):
    return pl.pallas_call(
        functools.partial(spread_kernel, cells, slots),
        in_specs=[SMEM, VM, VM],
        out_specs=VM,
        out_shape=shape(chips, KVROWS, FEATS),
        compiler_params=pltpu.CompilerParams(vmem_limit_bytes=VMEM_LIMIT),
        cost_estimate=cost(0.001, 2),
        name="spread",
    )(bounds, own, got)


def middle_kernel(cells, slots, nsums, places, bounds, x, dy_r, keep_r, pq, vec, b_up, *refs):
    sums, refs = refs[:nsums], refs[nsums:]
    count = 2 * len(places) if places else 3
    pieces, refs = refs[:count], refs[count:]
    mixed_o, gr_o, dpre_o, a2_o, ar_o, do_o, dx_o, grads_o, vec_o, vup_o, sums_o, full = refs[:12]
    acc, num_s, den_s = refs[12:15]
    blk = pl.program_id(0)
    width = x.shape[1]
    wide = gr_o.shape[1] // width
    if places:
        w, sems = refs[15:]
        rows = width // (2 * w.shape[0])
        base = rows * (1 + wide)
        w_out = lambda: w[:, :, 0:rows, :].reshape(width, width)
        w_up = lambda j: w[:, :, rows * (1 + j) : rows * (2 + j), :].reshape(width, width)
        w_down = lambda j: w[j * (w.shape[0] // wide) : (j + 1) * (w.shape[0] // wide), :, base:, :].reshape(width, width)
    else:
        w_out = lambda: pieces[0][...]
        w_up = lambda j: pieces[1][:, j * width : (j + 1) * width]
        w_down = lambda j: pieces[2][j * width : (j + 1) * width, :]

    @pl.when(blk == 0)
    def _():
        if places:
            for copy in copies(pieces, places, w, sems):
                copy.start()
        acc[...] = jnp.zeros_like(acc)
        vec_o[...] = jnp.zeros_like(vec_o)
        vup_o[...] = jnp.zeros_like(vup_o)
        load_sums(bounds, sums, full, slots, cells, False)

    lo, hi, first = cell_range(bounds, blk, cells)
    low = lane_low(BLK)

    def attend(c, carry):
        mask = cell_mask(bounds, c, first, 128)
        for p in range(PAIRS):
            h = 2 * p
            lanes = slice(128 * p, 128 * p + 128)
            r0 = dot_nt(pq[:, FEATS * h : FEATS * (h + 1)], full[c, h])
            r1 = dot_nt(pq[:, FEATS * (h + 1) : FEATS * (h + 2)], full[c, h + 1])
            num = jnp.where(low, r0, r1)
            den = pltpu.roll(jnp.where(low, r1, r0), HEAD, 1)
            num_s[:, lanes] = jnp.where(mask, num, num_s[:, lanes])
            den_s[:, lanes] = jnp.where(mask, den, den_s[:, lanes])
        return carry

    lax.fori_loop(lo, hi + 1, attend, 0)
    if places:
        @pl.when(blk == 0)
        def _():
            for copy in copies(pieces, places, w, sems):
                copy.wait()

    keep = keep_r[...]
    inv = 1.0 / den_s[...]
    ar = (keep * num_s[...] * inv).astype(BF)
    ar_o[...] = ar
    x2 = x[...].astype(F32) + dot(ar, w_out())
    z2, r2 = norm_stats(x2)
    g2 = vec[2:3]
    a2 = (z2 * g2 + vec[3:4]).astype(BF)
    a2_o[...] = a2
    dy = dy_r[...]
    mixed = x2 + vec[4:5]
    da2 = jnp.zeros_like(x2)
    k0 = math.sqrt(2.0 / math.pi)
    k1 = 0.044715 * k0
    for j in range(wide):
        cols = slice(j * width, (j + 1) * width)
        pre = dot(a2, w_up(j)) + b_up[j : j + 1]
        sq = pre * pre
        t = jnp.tanh(pre * (k0 + k1 * sq))
        half = 0.5 + 0.5 * t
        act = pre * half
        slope = half + act * (1.0 - t) * (k0 + (3.0 * k1) * sq)
        gr = act.astype(BF)
        gr_o[:, cols] = gr
        mixed += dot(gr, w_down(j))
        dpre = (dot_nt(dy, w_down(j)) * slope).astype(BF)
        dpre_o[:, cols] = dpre
        da2 += dot_nt(dpre, w_up(j))
        vup_o[j : j + 1] += jnp.sum(dpre.astype(F32), 0, keepdims=True)
    mixed_o[...] = mixed.astype(BF)
    dyf = dy.astype(F32)
    dz = da2 * g2
    m1 = jnp.sum(dz, -1, keepdims=True) * (1.0 / width)
    m2 = jnp.sum(dz * z2, -1, keepdims=True) * (1.0 / width)
    dx2 = dyf + r2 * (dz - m1 - z2 * m2)
    dx_o[...] = dx2
    vec_o[2:3, :] += jnp.sum(da2 * z2, 0, keepdims=True)
    vec_o[3:4, :] += jnp.sum(da2, 0, keepdims=True)
    vec_o[4:5, :] += jnp.sum(dyf, 0, keepdims=True)
    do = dx2.astype(BF)
    do_o[...] = do
    dattn = keep * dot_nt(do, w_out()).astype(BF).astype(F32)
    dnum = dattn * inv
    dden = -dnum * num_s[...] * inv
    for p in range(PAIRS):
        lanes = slice(128 * p, 128 * p + 128)
        mine = dnum[:, lanes]
        swap = pltpu.roll(dden[:, lanes], HEAD, 1)
        h = 2 * p
        grads_o[:, 128 * h : 128 * h + 128] = jnp.where(low, mine, swap).astype(BF)
        grads_o[:, 128 * h + 128 : 128 * h + 256] = jnp.where(low, swap, mine).astype(BF)

    def gather(c, carry):
        mask = cell_mask(bounds, c, first, 128)
        for h in range(HEADS):
            part = grads_o[:, 128 * h : 128 * h + 128]
            part = jnp.where(mask, part.astype(F32), 0.0).astype(BF)
            acc[c, h] += dot_tn(part, pq[:, FEATS * h : FEATS * (h + 1)])
        return carry

    lax.fori_loop(lo, hi + 1, gather, 0)

    @pl.when(blk == pl.num_programs(0) - 1)
    def _():
        store_sums(acc, sums_o, cells, True)


def run_middle(bounds, x, dy, keep, pq, vec, b_up, sums, pieces, places, ff, cells):
    n, d = x.shape
    wide = HEADS * 128
    full = (cells, HEADS, 128, FEATS)
    scratch = [pltpu.VMEM(full, F32), pltpu.VMEM((BLK, d), F32), pltpu.VMEM((BLK, d), F32)]
    if places:
        rows = max(hi for _, _, hi in places)
        chips = 1 + max(m for masks, _, _ in places for m in masks)
        number = 2 * sum(len(masks) for masks, _, _ in places)
        scratch += [pltpu.VMEM((chips, 2, rows, d), BF), pltpu.SemaphoreType.DMA((number,))]
    return pl.pallas_call(
        functools.partial(middle_kernel, cells, n, len(sums), places),
        grid=(n // BLK,),
        in_specs=[
            SMEM, rows_spec(d), rows_spec(d), rows_spec(1), rows_spec(HEADS * FEATS), whole_spec(vec.shape), whole_spec(b_up.shape),
        ]
        + whole_specs(sums)
        + ([ANY] * len(pieces) if places else whole_specs(pieces)),
        out_specs=[
            rows_spec(d), rows_spec(ff), rows_spec(ff), rows_spec(d), rows_spec(d), rows_spec(d),
            rows_spec(d), rows_spec(wide), whole_spec((16, d)), whole_spec((8, d)),
            whole_spec(sums_shape(cells)), whole_spec(full),
        ],
        out_shape=[
            shape(n, d), shape(n, ff), shape(n, ff), shape(n, d), shape(n, d), shape(n, d),
            shape(n, d, kind=F32), shape(n, wide), shape(16, d, kind=F32), shape(8, d, kind=F32),
            shape(*sums_shape(cells)), shape(*full),
        ],
        scratch_shapes=scratch,
        compiler_params=params(),
        cost_estimate=cost(14, 30),
        name="middle",
    )(bounds, x, dy, keep, pq, vec, b_up, *sums, *pieces)


def phi_back(s, feats, rhs, low):
    r0 = dot_nt(feats[0].astype(BF), rhs[0])
    r1 = dot_nt(feats[1].astype(BF), rhs[1])
    total = pltpu.roll(jnp.where(low, r1, r0), HEAD, 1)
    return (jnp.where(low, r0, r1) - s * total) * SCALE


def query_back_kernel(cells, bounds, grads, pq, sq, full, bank, a1, dq_o, gq_o, g_s, acc, rhs):
    blk = pl.program_id(0)

    @pl.when(blk == 0)
    def _():
        back_parts(bank, rhs)
        acc[...] = jnp.zeros_like(acc)

    lo, hi, first = cell_range(bounds, blk, cells)
    low = lane_low(BLK)

    def one(c, carry):
        mask = cell_mask(bounds, c, first, FEATS)
        for h in range(HEADS):
            cols = slice(FEATS * h, FEATS * (h + 1))
            g = dot(grads[:, 128 * h : 128 * h + 128], full[c, h])
            g_s[:, cols] = jnp.where(mask, g, g_s[:, cols])
        return carry

    lax.fori_loop(lo, hi + 1, one, 0)
    for p in range(PAIRS):
        lanes = slice(128 * p, 128 * p + 128)
        feats = []
        for odd in (0, 1):
            cols = slice(FEATS * (2 * p + odd), FEATS * (2 * p + odd + 1))
            feats.append(g_s[:, cols] * pq[:, cols].astype(F32))
        dq_o[:, lanes] = phi_back(sq[:, lanes].astype(F32), feats, rhs, low).astype(BF)
    acc[...] += dot_tn(a1[...], dq_o[...])

    @pl.when(blk == pl.num_programs(0) - 1)
    def _():
        gq_o[...] = acc[...].astype(BF)


def run_query_back(bounds, grads, pq, sq, full, bank, a1, cells):
    n, d = sq.shape
    return pl.pallas_call(
        functools.partial(query_back_kernel, cells),
        grid=(n // BLK,),
        in_specs=[
            SMEM, rows_spec(HEADS * 128), rows_spec(HEADS * FEATS), rows_spec(d),
            whole_spec(full.shape), whole_spec(bank.shape), rows_spec(d),
        ],
        out_specs=[rows_spec(d), whole_spec((d, d))],
        out_shape=[shape(n, d), shape(d, d)],
        scratch_shapes=[
            pltpu.VMEM((BLK, HEADS * FEATS), F32), pltpu.VMEM((d, d), F32), pltpu.VMEM((2, 128, FEATS), BF),
        ],
        compiler_params=params(),
        cost_estimate=cost(3, 8),
        name="query_back",
    )(bounds, grads, pq, sq, full, bank, a1)


def weight_kernel(rows, a2, dpre, gr, dy, ar, do, keep_o, send_o):
    j = pl.program_id(0)
    d = a2.shape[1]

    def put(value, block, lo, size):
        count = d // (2 * size)
        kept, sent = both_cores(value.reshape(count, 2, size, d))
        at = (pl.ds(block * count, count), pl.ds(lo, size))
        keep_o[at] = kept.astype(BF)
        send_o[at] = sent.astype(BF)

    @pl.when(j == 0)
    def _():
        put(dot_tn(ar[...], do[...]), 0, 0, rows)

    put(dot_tn(a2[...], dpre[...]), 0, pl.multiple_of(rows * (1 + j), rows), rows)
    wide = (keep_o.shape[1] // rows - 1) // 2
    put(dot_tn(gr[...], dy[...]), j, rows * (1 + wide), rows * wide)


def run_weights(a2, dpre, gr, dy, ar, do, rows):
    n, d = a2.shape
    wide = dpre.shape[1] // d
    out = (d // (2 * rows), rows * (1 + 2 * wide), d)
    cols = pl.BlockSpec((n, d), lambda j: (0, j))
    whole = whole_spec((n, d))
    return pl.pallas_call(
        functools.partial(weight_kernel, rows),
        grid=(wide,),
        in_specs=[whole, cols, cols, whole, whole, whole],
        out_specs=[whole_spec(out), whole_spec(out)],
        out_shape=[shape(*out), shape(*out)],
        compiler_params=params(),
        cost_estimate=cost(5, 20),
        name="weights",
    )(a2, dpre, gr, dy, ar, do)


def key_back_kernel(cells, slots, nsums, paired, rows, wide, bounds, x, a1, pk, vr, sk, dq, dx, vec, gvec, vup, bank, w, gq, *refs):
    sums, refs = refs[:nsums], refs[nsums:]
    outs, refs = refs[: 3 if paired else 2], refs[3 if paired else 2 :]
    gt_o = outs[0]
    full, g_s, v_s, rhs, dk_s, dv_s, vec_s, gk_s, gv_s = refs
    blk = pl.program_id(0)
    d = x.shape[1]

    @pl.when(blk == 0)
    def _():
        vec_s[...] = gvec[...]
        gk_s[...] = jnp.zeros_like(gk_s)
        gv_s[...] = jnp.zeros_like(gv_s)
        back_parts(bank, rhs)
        load_sums(bounds, sums, full, slots, cells, True)

    lo, hi, first = cell_range(bounds, blk, cells)
    low = lane_low(BLK)

    def one(c, carry):
        mask = cell_mask(bounds, c, first, FEATS)
        narrow = cell_mask(bounds, c, first, 128)
        for p in range(PAIRS):
            lanes = slice(128 * p, 128 * p + 128)
            v = vr[:, lanes].astype(F32)
            outs = []
            for odd in (0, 1):
                h = 2 * p + odd
                cols = slice(FEATS * h, FEATS * (h + 1))
                aug = (jnp.where(low, 1.0, v) if odd else jnp.where(low, v, 1.0)).astype(BF)
                g = dot(aug, full[c, h])
                g_s[:, cols] = jnp.where(mask, g, g_s[:, cols])
                outs.append(dot_nt(pk[:, cols], full[c, h]))
            v_s[:, lanes] = jnp.where(narrow, jnp.where(low, outs[0], outs[1]), v_s[:, lanes])
        return carry

    lax.fori_loop(lo, hi + 1, one, 0)
    for p in range(PAIRS):
        lanes = slice(128 * p, 128 * p + 128)
        feats = []
        for odd in (0, 1):
            cols = slice(FEATS * (2 * p + odd), FEATS * (2 * p + odd + 1))
            feats.append(g_s[:, cols] * pk[:, cols].astype(F32))
        dk_s[:, lanes] = phi_back(sk[:, lanes].astype(F32), feats, rhs, low).astype(BF)
    dv_s[...] = v_s[...].astype(BF)
    dk, dv = dk_s[...], dv_s[...]
    gk_s[...] += dot_tn(a1[...], dk)
    gv_s[...] += dot_tn(a1[...], dv)
    da1 = dot_nt(dq[...], w[:, :d]) + dot_nt(dk, w[:, d : 2 * d]) + dot_nt(dv, w[:, 2 * d : 3 * d])
    z, r = norm_stats(x[...].astype(F32))
    dz = da1 * vec[0:1]
    m1 = jnp.sum(dz, -1, keepdims=True) * (1.0 / d)
    m2 = jnp.sum(dz * z, -1, keepdims=True) * (1.0 / d)
    gt_o[...] = dx[...] + r * (dz - m1 - z * m2)
    vec_s[0:1, :] += jnp.sum(da1 * z, 0, keepdims=True)
    vec_s[1:2, :] += jnp.sum(da1, 0, keepdims=True)

    @pl.when(blk == pl.num_programs(0) - 1)
    def _():
        vt = pad_rows([vec_s[i : i + 1] for i in range(5)] + by_owner(vup[...], rows, wide), 128).T
        for lo, value in ((0, gq[...].astype(F32)), (d, gk_s[...]), (2 * d, gv_s[...]), (3 * d, vt)):
            cols = slice(lo, lo + value.shape[1])
            if paired:
                kept, sent = both_cores(value.reshape(outs[1].shape[0], 2, rows, value.shape[1]))
                outs[1][:, :, cols] = kept.astype(BF)
                outs[2][:, :, cols] = sent.astype(BF)
            else:
                outs[1][:, cols] = value.astype(BF)


def run_key_back(bounds, x, a1, pk, vr, sk, dq, dx, vec, gvec, vup, bank, w, gq, sums, rows, wide, paired, cells):
    n, d = x.shape
    total = w.shape[1]
    gout = [(d // (2 * rows), rows, total)] * 2 if paired else [(d, total)]
    square = pltpu.VMEM((d, d), F32)
    return pl.pallas_call(
        functools.partial(key_back_kernel, cells, n, len(sums), paired, rows, wide),
        grid=(n // BLK,),
        in_specs=[
            SMEM, rows_spec(d), rows_spec(d), rows_spec(HEADS * FEATS), rows_spec(d), rows_spec(d), rows_spec(d), rows_spec(d),
        ]
        + whole_specs((vec, gvec, vup, bank, w, gq))
        + whole_specs(sums),
        out_specs=[rows_spec(d)] + [whole_spec(g) for g in gout],
        out_shape=[shape(n, d, kind=F32)] + [shape(*g) for g in gout],
        scratch_shapes=[
            pltpu.VMEM((cells, HEADS, 128, FEATS), BF),
            pltpu.VMEM((BLK, HEADS * FEATS), F32),
            pltpu.VMEM((BLK, d), F32),
            pltpu.VMEM((2, 128, FEATS), BF),
            pltpu.VMEM((BLK, d), BF),
            pltpu.VMEM((BLK, d), BF),
            pltpu.VMEM((16, d), F32),
            square,
            square,
        ],
        compiler_params=params(),
        cost_estimate=cost(6, 14),
        name="key_back",
    )(bounds, x, a1, pk, vr, sk, dq, dx, vec, gvec, vup, bank, w, gq, *sums)


AXES = ("dp", "fsdp")
Z_ALL = (0, 1, 2, 3)
LEAD_MASKS = (Z_ALL, (4, 5, 6, 7), (8, 9, 10, 11), (12, 13, 14, 15))


def flip(x, axis, size, mask):
    return lax.ppermute(x, axis, [(i, i ^ mask) for i in range(size)])


def to_core(x, fsdp):
    return flip(x, "fsdp", fsdp, 1)


def to_z(x, fsdp, mask):
    return flip(x, "fsdp", fsdp, 2 * mask)


def tie(*values):
    return lax.optimization_barrier(values)


def same_core_groups(dp, fsdp):
    return [[d * fsdp + 2 * z + c for d in range(dp) for z in range(fsdp // 2)] for c in range(2)]


def chip_groups(fsdp):
    return [[2 * z + c for z in range(fsdp // 2)] for c in range(2)]


def pack_kernel(wide, w_qkv, g1, s1, w_out, g2, s2, w_up, b_up, w_down, b_down, lead, body):
    rows = w_qkv.shape[0]
    d = w_out.shape[1]
    total = w_qkv.shape[1]
    place = lax.broadcasted_iota(jnp.int32, (128, rows), 0)
    up = b_up[...].astype(F32).reshape(1, -1)
    lines = [v[...].astype(F32).reshape(1, -1) for v in (g1, s1, g2, s2, b_down)]
    lines += [up[:, j * rows : (j + 1) * rows] for j in range(wide)]
    table = jnp.zeros((128, rows), F32)
    for i, line in enumerate(lines):
        table = jnp.where(place == i, line, table)
    across = lax.broadcasted_iota(jnp.int32, (rows, rows), 0) == lax.broadcasted_iota(jnp.int32, (rows, rows), 1)
    lead[:, :total] = w_qkv[...]
    lead[:, total:] = dot_nt(jnp.where(across, 1.0, 0.0).astype(BF), table.astype(BF)).astype(BF)
    body[:rows] = w_out[...]
    for j in range(wide):
        body[rows * (1 + j) : rows * (2 + j)] = w_up[:, j * d : (j + 1) * d]
    body[rows * (1 + wide) :] = w_down[...]


def lead_sum_kernel(wide, part, wqkv, *lines):
    total = part[0].astype(F32)
    for k in range(1, part.shape[0]):
        total += part[k].astype(F32)
    cols = wqkv.shape[1]
    wqkv[...] = total[:, :cols]
    table = total[:, cols:].T
    for i in range(5):
        lines[i][...] = table[i]
    lines[5][...] = jnp.concatenate([table[5 + j : 6 + j] for j in range(wide)], 1)[0]


def run_lead_sum(part, cols, wide):
    rows = part.shape[1]
    return pl.pallas_call(
        functools.partial(lead_sum_kernel, wide),
        in_specs=[VM],
        out_specs=[VM] * 7,
        out_shape=[shape(rows, cols, kind=F32)] + [shape(rows, kind=F32)] * 5 + [shape(rows * wide, kind=F32)],
        name="lead_sum",
    )(part)


def body_sum_kernel(rows, wide, *refs):
    parts, (wout, wup, wdown) = refs[:-3], refs[-3:]
    d = wout.shape[1]
    total = parts[0][...].astype(F32)
    for part in parts[1:]:
        total += part[...].astype(F32)
    wout[...] = total[:rows]
    for j in range(wide):
        wup[:, j * d : (j + 1) * d] = total[rows * (1 + j) : rows * (2 + j)]
    wdown[...] = total[rows * (1 + wide) :]


def run_body_sum(parts, rows, wide):
    d = parts[0].shape[1]
    return pl.pallas_call(
        functools.partial(body_sum_kernel, rows, wide),
        in_specs=[VM] * len(parts),
        out_specs=[VM] * 3,
        out_shape=[shape(rows, d, kind=F32), shape(rows, wide * d, kind=F32), shape(rows * wide, d, kind=F32)],
        name="body_sum",
    )(*parts)


def local(dp, fsdp, tokens, bounds, padding, bank, ln1_gain, ln1_bias, w_qkv, w_out, ln2_gain, ln2_bias,
          w_up, b_up, w_down, b_down, cotangent):
    ndev = dp * fsdp
    x = tokens[0]
    dy = cotangent[0]
    n, d = x.shape
    ff = w_up.shape[1]
    cells = bounds.shape[1] - 1
    chips = fsdp // 2
    rows = d // ndev
    wide = ff // d
    frow = ff // ndev
    paired = dp == 4 and fsdp == 8

    shards = (w_qkv, ln1_gain, ln1_bias, w_out, ln2_gain, ln2_bias, w_up, b_up, w_down, b_down)
    if paired:
        lead, body = pl.pallas_call(
            functools.partial(pack_kernel, wide),
            in_specs=[VM] * len(shards),
            out_specs=[VM, VM],
            out_shape=[shape(rows, 3 * d + 128), shape(rows * (1 + wide) + frow, d)],
            name="pack",
        )(*shards)
    else:
        vecs = jnp.concatenate([ln1_gain, ln1_bias, ln2_gain, ln2_bias, b_down, b_up]).reshape(5 + wide, rows)
        lead = jnp.concatenate([w_qkv, jnp.pad(vecs, ((0, 128 - 5 - wide), (0, 0))).T], 1)
        body = jnp.concatenate([w_out] + [w_up[:, j * d : (j + 1) * d] for j in range(wide)] + [w_down], 0)
    keep = padding[0].astype(F32)[:, None]
    cut = rows * (1 + wide)

    if paired:
        lead, body, keep = tie(lead, body, keep)
        first = jnp.stack([lead] + [to_z(lead, fsdp, k) for k in (1, 2, 3)])
        lead_own = [first] + [flip(first, "dp", dp, k) for k in (1, 2, 3)]
        pair = jnp.stack([body, to_z(body, fsdp, 1)])
        pair, *lead_own = tie(pair, *lead_own)
        lead_pieces = lead_own + [to_core(v, fsdp) for v in lead_own]
        four = jnp.concatenate([pair, to_z(pair, fsdp, 2)])
        lead_places = tuple((m, 0, rows) for m in LEAD_MASKS)
    else:
        lead_pieces = [lax.all_gather(lead, AXES, axis=0, tiled=True)]
        parts = lax.all_gather(body, AXES, axis=0)
        take = lambda lo, size: parts[:, lo : lo + size].reshape(ndev * size, d)
        body_pieces = [
            take(0, rows), jnp.concatenate([take((1 + j) * rows, rows) for j in range(wide)], 1), take(cut, frow),
        ]
        lead_places = body_places = None

    def far_sums(out):
        return lax.all_to_all(out, "fsdp", 0, 0, axis_index_groups=chip_groups(fsdp), tiled=True)

    a1, sk, pk, vr, sums, vec, *w = run_keys(bounds, x, keep, bank, lead_pieces, lead_places, cells)
    w = w[0].reshape(d, -1) if paired else lead_pieces[0]
    if paired:
        sums, four = tie(sums, four)
        sums = [sums, to_core(sums, fsdp)]
        out = run_spread(bounds, *sums, chips, n, cells)
        a1_q, four, out = tie(a1, four, out)
        far = far_sums(out)
        up, down = four[:, :cut], four[:, cut:]
        up_x, down_y = flip(up, "dp", dp, 1), flip(down, "dp", dp, 2)
        up_y = flip(jnp.concatenate([up, up_x]), "dp", dp, 2)
        down_x = flip(jnp.concatenate([down, down_y]), "dp", dp, 1)
        sq, pq, up_line = run_queries(a1_q, w, bank, vec, rows, wide)
        up_y, down_x, pq, up_line = tie(up_y, down_x, pq, up_line)
        body_own = [four, up_x, down_y, up_y, down_x]
        body_pieces = body_own + [to_core(v, fsdp) for v in body_own]
        body_places = (
            (Z_ALL, 0, cut + frow), ((4, 5, 6, 7), 0, cut), ((8, 9, 10, 11), cut, cut + frow),
            ((8, 9, 10, 11, 12, 13, 14, 15), 0, cut), ((4, 5, 6, 7, 12, 13, 14, 15), cut, cut + frow),
        )
        sums = sums + [far, to_core(far, fsdp)]
    else:
        sums = [lax.psum(sums, "fsdp")]
        sq, pq, up_line = run_queries(a1, w, bank, vec, rows, wide)
    mixed, gr, dpre, a2, ar, do, dx2, grads, gvec, vup, sums, full = run_middle(
        bounds, x, dy, keep, pq, vec, up_line, sums, body_pieces, body_places, ff, cells
    )
    back = lambda dq, gq, sums: run_key_back(
        bounds, x, a1, pk, vr, sk, dq, dx2, vec, gvec, vup, bank, w, gq, sums, rows, wide, paired, cells
    )
    if paired:
        kept, sent = run_weights(a2, dpre, gr, dy, ar, do, rows)
        got, kept, sent = tie(to_core(sums, fsdp), kept, sent)
        sums = [sums, got]
        out = run_spread(bounds, *sums, chips, n, cells)
        grads, out = tie(grads, out)
        far = far_sums(out)
        dq, gq = run_query_back(bounds, grads, pq, sq, full, bank, a1, cells)
        plus = lambda *parts: functools.reduce(lambda a, b: a + b, [v.astype(F32) for v in parts]).astype(BF)
        half = plus(kept, to_core(sent, fsdp)).reshape((2, 2, chips) + kept.shape[1:])
        ypos, xpos = lax.axis_index("dp") // 2, lax.axis_index("dp") % 2
        pick = lambda value, at, dim: lax.dynamic_index_in_dim(value, at, dim, keepdims=False)
        up, down = half[:, :, :, :cut], half[:, :, :, cut:]
        far, dq, gq, up, down = tie(far, dq, gq, up, down)
        up_got = flip(pick(up, 1 - xpos, 1), "dp", dp, 1)
        down_got = flip(pick(down, 1 - ypos, 0), "dp", dp, 2)
        gt, kept, sent = back(dq, gq, sums + [far, to_core(far, fsdp)])
        kept, sent, up_got, down_got = tie(kept, sent, up_got, down_got)
        up = plus(pick(up, xpos, 1), up_got)
        down = plus(pick(down, ypos, 0), down_got)
        up = plus(pick(up, ypos, 0), flip(pick(up, 1 - ypos, 0), "dp", dp, 2))
        down = plus(pick(down, xpos, 0), flip(pick(down, 1 - xpos, 0), "dp", dp, 1))
        whole = jnp.concatenate([up, down], 1)
        zpos = lax.axis_index("fsdp") // 2
        parts = [pick(whole, zpos, 0)] + [to_z(pick(whole, zpos ^ k, 0), fsdp, k) for k in (1, 2, 3)]
        half = plus(kept, to_core(sent, fsdp))
        part = lax.all_to_all(half, AXES, 0, 0, axis_index_groups=same_core_groups(dp, fsdp), tiled=True)
        wqkv, *vecs = run_lead_sum(part, 3 * d, wide)
        wout, wup, wdown = run_body_sum(parts, rows, wide)
    else:
        dq, gq = run_query_back(bounds, grads, pq, sq, full, bank, a1, cells)
        gt, glead = back(dq, gq, [lax.psum(sums, "fsdp")])
        gup = dot_tn(a2, dpre)
        blocks = lambda g, size: g.reshape(ndev, size, d)
        gbody = jnp.concatenate(
            [blocks(dot_tn(ar, do), rows)]
            + [blocks(gup[:, j * d : (j + 1) * d], rows) for j in range(wide)]
            + [blocks(dot_tn(gr, dy), frow)], 1
        )
        gbody = lax.psum_scatter(gbody, AXES, scatter_dimension=0, tiled=True)[0]
        glead = lax.psum_scatter(glead.astype(F32), AXES, scatter_dimension=0, tiled=True)
        gvec = glead[:, 3 * d :].T
        vecs = [gvec[i] for i in range(5)] + [gvec[5 : 5 + wide].reshape(-1)]
        wqkv, wout, wdown = glead[:, : 3 * d], gbody[:rows], gbody[cut:]
        wup = jnp.concatenate([gbody[(1 + j) * rows : (2 + j) * rows] for j in range(wide)], 1)
    return (
        mixed[None], gt[None], vecs[0], vecs[1], wqkv, wout, vecs[2], vecs[3], wup, vecs[5], wdown, vecs[4],
    )


def solution(mesh):
    both = P(("dp", "fsdp"))
    mat = P(("dp", "fsdp"), None)
    act = P("dp", "fsdp", None)
    return jax.shard_map(
        functools.partial(local, mesh.shape["dp"], mesh.shape["fsdp"]),
        mesh=mesh,
        in_specs=(act, P("dp", None), P("dp", "fsdp"), P(), both, both, mat, mat, both, both, mat, both, mat, both, act),
        out_specs=(act, act, both, both, mat, mat, both, both, mat, both, mat, both),
        check_vma=False,
    )
```

time: 307 us -> 223 us (0.73)
  local copies, waits for them, and re-layouts: 47.4 us -> 8.91 us
  waiting for transfers between devices: 94.9 us -> 57.7 us
  Pallas kernels: 74.7 us -> 104 us
  blocking collectives: 21.5 us -> 0 us
  matrix products: 14.1 us -> 0 us
  starting transfers between devices: 25 us -> 39 us
  between operations: 14.6 us -> 1.08 us
    all_to_all x5 -> x3, waiting for transfers between devices: 85 us -> 2.68 us  [the longest x2 2.68 us: far_sums(): lax.all_to_all(out, 'fsdp', 0, 0, axis_index_groups=chip_groups(fsdp), ti...]
    ppermute x7 -> x34, waiting for transfers between devices: 9.91 us -> 55 us  [flip(): return lax.ppermute(x, axis, [(i, i ^ mask) for i in range(size)])]
    ppermute x7 -> x34, starting transfers between devices: 1.19 us -> 27.5 us  [flip(): return lax.ppermute(x, axis, [(i, i ^ mask) for i in range(size)])]
    pallas_call x8 -> x10, Pallas kernels: 67.1 us -> 93.4 us  [the longest x1 32.6 us: run_middle(): pl.pallas_call(functools.partial(middle_kernel, cells, n, len(sums), plac...]
    all_to_all x1 -> x0, blocking collectives: 21.5 us -> none  [exchange(): lax.all_to_all(out, 'fsdp', 0, 0, axis_index_groups=chip_groups(fsdp), ti...]
    dot_general x6 -> x0, matrix products: 14.1 us -> none  [dot_tn(): lax.dot_general(a, b, (((0,), (0,)), ((), ())), preferred_element_type=F32)]
    all_to_all x5 -> x3, starting transfers between devices: 23.8 us -> 11.6 us  [the longest x2 7.35 us: far_sums(): lax.all_to_all(out, 'fsdp', 0, 0, axis_index_groups=chip_groups(fsdp), ti...]
    slice x12 -> x4, local copies, waits for them, and re-layouts: 12.1 us -> 0.22 us  [the longest x2 0.18 us: local(): up, down = (half[:, :, :, :cut], half[:, :, :, cut:])]
  transfers between devices with their start and end apart: 13 -> 37, of which waited for: 9 -> 19; matrix products, arithmetic and copies ran while one was open for 14% -> 5% of each run, Pallas kernels for 13% -> 29%
where the time goes in v2:
time: 223 us; the launch traced here: 222 us
  Pallas kernels  104 us (47%)
  waiting for transfers between devices  57.7 us (26%)
  starting transfers between devices  39 us (17%)
  other arithmetic  11.7 us (5%)
  local copies, waits for them, and re-layouts  8.91 us (4%)
    ppermute x34, waiting for transfers between devices, flip(): return lax.ppermute(x, axis, [(i, i ^ mask) for i in range(size)])  55 us
    pallas_call x1, Pallas kernels, run_middle(): pl.pallas_call(functools.partial(middle_kernel, cells, n, len(sums), plac...  32.6 us
    ppermute x34, starting transfers between devices, flip(): return lax.ppermute(x, axis, [(i, i ^ mask) for i in range(size)])  27.5 us
    pallas_call x1, Pallas kernels, run_key_back(): pl.pallas_call(functools.partial(key_back_kernel, cells, n, len(sums), pa...  18.4 us
    pallas_call x1, Pallas kernels, run_keys(): pl.pallas_call(functools.partial(key_kernel, cells, places), grid=(n // B...  13.3 us
    pallas_call x1, Pallas kernels, run_weights(): pl.pallas_call(functools.partial(weight_kernel, rows), grid=(wide,), in_s...  11.2 us
    pallas_call x1, Pallas kernels, run_query_back(): pl.pallas_call(functools.partial(query_back_kernel, cells), grid=(n // BL...  10.5 us
    convert_element_type x6, other arithmetic, local(): functools.reduce(lambda a, b: a + b, [v.astype(F32) for v in parts])  8.31 us
  transfers between devices with their start and end apart: 37, of which 19 were waited for; matrix products, arithmetic and copies ran while one was open for 5% of the time, Pallas kernels for 29%

profile of v2, /device:TPU:0, one launch (start us, length us, event | category | flops | bytes accessed | tf_op | source)
XLA Modules:
  0.0 222.2 jit_solution(16286871381166546391)
XLA Ops:
  1.3 2.1 pack.1
  3.4 3.0 %collective-permute-start.1 = (bf16[16,1664]{1,0:T(8,128)(2,1)}, bf16[16,1664]{1,0:T(8,128)(2,1)S(1)}, u32[]{:S(2)}, u32[]{:S(2)}) collective-permute-start(bf16[16,1664]{1,0:T(8,128)(2,1)} %get-tuple-element.88), channel_id=1, source_target_pairs={{0,2},{1,3},{2,0},{3,1},{4,6},{5,7},{6,4},{7,5},{8,10},{9,11},{10,... | collective-permute-start | bytes 159752 | tf_op jit(solution)/shard_map/ppermute | solution.py:737
  6.4 2.6 %collective-permute-start.2 = (bf16[16,1664]{1,0:T(8,128)(2,1)}, bf16[16,1664]{1,0:T(8,128)(2,1)S(1)}, u32[]{:S(2)}, u32[]{:S(2)}) collective-permute-start(bf16[16,1664]{1,0:T(8,128)(2,1)} %get-tuple-element.88), channel_id=1, source_target_pairs={{0,4},{1,5},{2,6},{3,7},{4,0},{5,1},{6,2},{7,3},{8,12},{9,13},{10,... | collective-permute-start | bytes 159752 | tf_op jit(solution)/shard_map/ppermute | solution.py:737
  9.9 2.9 %collective-permute-done.2 = bf16[16,1664]{1,0:T(8,128)(2,1)S(1)} collective-permute-done((bf16[16,1664]{1,0:T(8,128)(2,1)}, bf16[16,1664]{1,0:T(8,128)(2,1)S(1)}, u32[]{:S(2)}, u32[]{:S(2)}) %collective-permute-start.2) | collective-permute-done | bytes 53280 | tf_op jit(solution)/shard_map/ppermute | solution.py:737
  12.8 2.9 %collective-permute-done.3 = bf16[16,1664]{1,0:T(8,128)(2,1)S(1)} collective-permute-done((bf16[16,1664]{1,0:T(8,128)(2,1)}, bf16[16,1664]{1,0:T(8,128)(2,1)S(1)}, u32[]{:S(2)}, u32[]{:S(2)}) %collective-permute-start.3) | collective-permute-done | bytes 53280 | tf_op jit(solution)/shard_map/ppermute | solution.py:737
  21.1 2.8 %collective-permute-done.4.refs_1_ = bf16[4,16,1664]{2,1,0:T(8,128)(2,1)S(1)} collective-permute-done((bf16[4,16,1664]{2,1,0:T(8,128)(2,1)S(1)}, bf16[4,16,1664]{2,1,0:T(8,128)(2,1)S(1)}, u32[]{:S(2)}, u32[]{:S(2)}) %collective-permute-start.4) | collective-permute-done | bytes 213024 | tf_op jit(solution)/shard_map/ppermute | solution.py:737
  23.9 3.5 %collective-permute-done.5.refs_2_ = bf16[4,16,1664]{2,1,0:T(8,128)(2,1)S(1)} collective-permute-done((bf16[4,16,1664]{2,1,0:T(8,128)(2,1)S(1)}, bf16[4,16,1664]{2,1,0:T(8,128)(2,1)S(1)}, u32[]{:S(2)}, u32[]{:S(2)}) %collective-permute-start.5) | collective-permute-done | bytes 213024 | tf_op jit(solution)/shard_map/ppermute | solution.py:737
  30.6 13.3 %keys.1 = (bf16[1024,512]{1,0:T(8,128)(2,1)}, bf16[1024,512]{1,0:T(8,128)(2,1)}, bf16[1024,2048]{1,0:T(8,128)(2,1)}, bf16[1024,512]{1,0:T(8,128)(2,1)}, bf16[2,4...) custom-call(s32[1,5]{1,0:T(1,128)} %bounds.11, bf16[1024,512]{1,0:T(8,128)(2,1)} %bitcast.44, ...), custom_call_target="tpu_custom_call" | custom-call | flops 8000 | bytes 10000 | tf_op jit(solution)/shard_map/keys/pallas_call | solution.py:280
  44.1 3.0 %collective-permute-done.12.got.refs_1_ = bf16[2,4,272,256]{3,2,1,0:T(8,128)(2,1)S(1)} collective-permute-done((bf16[2,4,272,256]{3,2,1,0:T(8,128)(2,1)}, bf16[2,4,272,256]{3,2,1,0:T(8,128)(2,1)S(1)}, u32[]{:S(2)}, u32[]{:S(2)}) %collective-permute-start.12) | collective-permute-done | bytes 1114144 | tf_op jit(solution)/shard_map/ppermute | solution.py:737
  48.1 2.5 %spread.2 = bf16[4,272,256]{2,1,0:T(8,128)(2,1)} custom-call(s32[1,5]{1,0:T(1,128)} %bounds.11, bf16[2,4,272,256]{3,2,1,0:T(8,128)(2,1)} %get-tuple-element.97.own.refs_0_, bf16[2,4,272,256]{3,2,1,0:T(8,128)(2,1)} %copy-done.2), custom_call_target="tpu_custom_call" | custom-call | flops 1 | bytes 2000 | tf_op jit(solution)/shard_map/spread/pallas_call | solution.py:363
  52.2 3.7 %all-to-all-start = ((bf16[4,272,256]{2,1,0:T(8,128)(2,1)}), bf16[4,272,256]{2,1,0:T(8,128)(2,1)S(1)}, u32[]{:S(2)}, u32[]{:S(2)}) async-start(bf16[4,272,256]{2,1,0:T(8,128)(2,1)} %spread.2), calls=%async_computation | async-start | bytes 1114112 | tf_op jit(solution)/shard_map/all_to_all | solution.py:875
  55.9 4.6 %collective-permute-done.13.refs_5_ = bf16[4,80,512]{2,1,0:T(8,128)(2,1)S(1)} collective-permute-done((bf16[4,80,512]{2,1,0:T(8,128)(2,1)S(1)}, bf16[4,80,512]{2,1,0:T(8,128)(2,1)S(1)}, u32[]{:S(2)}, u32[]{:S(2)}) %collective-permute-start.13) | collective-permute-done | bytes 327712 | tf_op jit(solution)/shard_map/ppermute | solution.py:737
  62.4 6.8 %queries.1 = (bf16[1024,512]{1,0:T(8,128)(2,1)}, bf16[1024,2048]{1,0:T(8,128)(2,1)}, f32[8,512]{1,0:T(8,128)}) custom-call(bf16[1024,512]{1,0:T(8,128)(2,1)} %get-tuple-element.99.a1, bf16[512,1664]{1,0:T(8,128)(2,1)} %bitcast.47, f32[64,256]{1,0:T(8,128)} %bank.7, f32[16,512]{1,0:T(8,128)} %get-tuple-element.101.vec), custom_call_target="tpu_custom_call" | custom-call | flops 5000 | bytes 7000 | tf_op jit(solution)/shard_map/queries/pallas_call | solution.py:341
  69.2 5.7 %collective-permute-done.16.refs_8_ = bf16[8,64,512]{2,1,0:T(8,128)(2,1)S(1)} collective-permute-done((bf16[8,64,512]{2,1,0:T(8,128)(2,1)S(1)}, bf16[8,64,512]{2,1,0:T(8,128)(2,1)S(1)}, u32[]{:S(2)}, u32[]{:S(2)}) %collective-permute-start.16) | collective-permute-done | bytes 524320 | tf_op jit(solution)/shard_map/ppermute | solution.py:737
  83.0 32.6 %middle.1 = (bf16[1024,512]{1,0:T(8,128)(2,1)}, bf16[1024,2048]{1,0:T(8,128)(2,1)}, bf16[1024,2048]{1,0:T(8,128)(2,1)}, bf16[1024,512]{1,0:T(8,128)(2,1)}, bf16[...) custom-call(s32[1,5]{1,0:T(1,128)} %bounds.11, ...), custom_call_target="tpu_custom_call" | custom-call | flops 14000 | bytes 30000 | tf_op jit(solution)/shard_map/middle/pallas_call | solution.py:505
  115.6 11.2 %weights.1 = (bf16[16,144,512]{2,1,0:T(8,128)(2,1)}, bf16[16,144,512]{2,1,0:T(8,128)(2,1)}) custom-call(bf16[1024,512]{1,0:T(8,128)(2,1)} %get-tuple-element.115.a2, bf16[1024,2048]{1,0:T(8,128)(2,1)} %get-tuple-element.116.dpre, bf16[1024,2048]{1,0:T(8,128)(2,1)} %get-tuple-element.117.gr, bf16[1024,512]{1,0:T(8,128)(2,1)} %bitcast.50, ...), custom_call_target="tpu_custom_call" | custom-call | flops 5000 | bytes 20000 | tf_op jit(solution)/shard_map/weights/pallas_call | solution.py:617
  127.9 2.5 %spread.3 = bf16[4,272,256]{2,1,0:T(8,128)(2,1)} custom-call(s32[1,5]{1,0:T(1,128)} %bounds.11, bf16[2,4,272,256]{3,2,1,0:T(8,128)(2,1)} %get-tuple-element.114.own.refs_0_, bf16[2,4,272,256]{3,2,1,0:T(8,128)(2,1)} %copy-done.1), custom_call_target="tpu_custom_call" | custom-call | flops 1 | bytes 2000 | tf_op jit(solution)/shard_map/spread/pallas_call | solution.py:363
  130.5 3.7 %all-to-all-start.1 = ((bf16[4,272,256]{2,1,0:T(8,128)(2,1)}), bf16[4,272,256]{2,1,0:T(8,128)(2,1)S(1)}, u32[]{:S(2)}, u32[]{:S(2)}) async-start(bf16[4,272,256]{2,1,0:T(8,128)(2,1)} %spread.3), calls=%async_computation.1 | async-start | bytes 1114112 | tf_op jit(solution)/shard_map/all_to_all | solution.py:875
  134.2 10.5 %query_back.1 = (bf16[1024,512]{1,0:T(8,128)(2,1)}, bf16[512,512]{1,0:T(8,128)(2,1)}) custom-call(s32[1,5]{1,0:T(1,128)} %bounds.11, bf16[1024,1024]{1,0:T(8,128)(2,1)} %get-tuple-element.124.grads, bf16[1024,2048]{1,0:T(8,128)(2,1)} %get-tuple-element.104.pq, bf16[1024,512]{1,0:T(8,128)(2,1)} %get-tuple-element.125.sq, ...), custom_call_target="tpu_custom_call" | custom-call | flops 3000 | bytes 8000 | tf_op jit(solution)/shard_map/query_back/pallas_call | solution.py:573
  144.7 2.4 %add_convert_fusion = bf16[16,144,512]{2,1,0:T(8,128)(2,1)S(1)} fusion(bf16[16,144,512]{2,1,0:T(8,128)(2,1)} %collective-permute-done.24, bf16[16,144,512]{2,1,0:T(8,128)(2,1)S(1)} %copy-done.4), kind=kLoop, calls=%fused_computation | loop fusion | flops 4718592 | bytes 7077888 | tf_op jit(solution)/shard_map/convert_element_type | solution.py:915
  147.3 2.7 %all-to-all-done.1.refs_2_ = bf16[4,272,256]{2,1,0:T(8,128)(2,1)S(1)} async-done(((bf16[4,272,256]{2,1,0:T(8,128)(2,1)}), bf16[4,272,256]{2,1,0:T(8,128)(2,1)S(1)}, u32[]{:S(2)}, u32[]{:S(2)}) %all-to-all-start.1) | async-done | bytes 557088 | tf_op jit(solution)/shard_map/all_to_all | solution.py:875
  153.7 18.4 %key_back.1 = (f32[1024,512]{1,0:T(8,128)}, bf16[16,16,1664]{2,1,0:T(8,128)(2,1)}, bf16[16,16,1664]{2,1,0:T(8,128)(2,1)}) custom-call(s32[1,5]{1,0:T(1,128)} %bounds.11, bf16[1024,512]{1,0:T(8,128)(2,1)} %bitcast.46, bf16[1024,512]{1,0:T(8,128)(2,1)} %get-tuple-element.99.a1, bf16[1024,2048]{1,0:T(8,128)(2,1)} %get-tuple-element.110.pk, ...), custom_call_target="tpu_custom_call" | custom-call | flops 6000 | bytes 14000 | tf_op jit(solution)/shard_map/key_back/pallas_call | solution.py:704
  172.3 2.6 %collective-permute-done.28 = bf16[16,16,1664]{2,1,0:T(8,128)(2,1)S(1)} collective-permute-done((bf16[16,16,1664]{2,1,0:T(8,128)(2,1)}, bf16[16,16,1664]{2,1,0:T(8,128)(2,1)S(1)}, u32[]{:S(2)}, u32[]{:S(2)}) %collective-permute-start.28) | collective-permute-done | bytes 852000 | tf_op jit(solution)/shard_map/ppermute | solution.py:737
  174.9 2.3 %add_convert_fusion.1 = bf16[16,16,1664]{2,1,0:T(8,128)(2,1)} fusion(bf16[16,16,1664]{2,1,0:T(8,128)(2,1)S(1)} %collective-permute-done.28, bf16[16,16,1664]{2,1,0:T(8,128)(2,1)} %get-tuple-element.142), kind=kLoop, calls=%fused_computation.1 | loop fusion | flops 1703936 | bytes 2555904 | tf_op jit(solution)/shard_map/convert_element_type | solution.py:915
  177.2 4.2 %all-to-all-start.2 = ((bf16[16,16,1664]{2,1,0:T(8,128)(2,1)}), bf16[16,16,1664]{2,1,0:T(8,128)(2,1)S(1)}, u32[]{:S(2)}, u32[]{:S(2)}) async-start(bf16[16,16,1664]{2,1,0:T(8,128)(2,1)} %add_convert_fusion.1), calls=%async_computation.2 | async-start | bytes 1703936 | tf_op jit(solution)/shard_map/all_to_all | solution.py:933
  183.5 1.9 collective-permute-start.30
  188.3 9.6 %collective-permute-done.30 = bf16[4,64,512]{2,1,0:T(8,128)(2,1)} collective-permute-done((bf16[4,64,512]{2,1,0:T(8,128)(2,1)}, bf16[4,64,512]{2,1,0:T(8,128)(2,1)}, u32[]{:S(2)}, u32[]{:S(2)}) %collective-permute-start.30) | collective-permute-done | bytes 262176 | tf_op jit(solution)/shard_map/ppermute | solution.py:737
  200.3 3.7 %collective-permute-start.31 = (bf16[144,512]{1,0:T(8,128)(2,1)S(1)}, bf16[144,512]{1,0:T(8,128)(2,1)S(1)}, u32[]{:S(2)}, u32[]{:S(2)}) collective-permute-start(bf16[144,512]{1,0:T(8,128)(2,1)S(1)} %get-tuple-element.158), channel_id=1, source_target_pairs={{0,2},{1,3},{2,0},{3,1},{4,6},{5,7},{6,4},{7,5},{8,10},{9,11},{10,... | collective-permute-start | bytes 442376 | tf_op jit(solution)/shard_map/ppermute | solution.py:737
  206.3 2.4 %collective-permute-done.31.refs_1_ = bf16[144,512]{1,0:T(8,128)(2,1)S(1)} collective-permute-done((bf16[144,512]{1,0:T(8,128)(2,1)S(1)}, bf16[144,512]{1,0:T(8,128)(2,1)S(1)}, u32[]{:S(2)}, u32[]{:S(2)}) %collective-permute-start.31) | collective-permute-done | bytes 147488 | tf_op jit(solution)/shard_map/ppermute | solution.py:737
  208.7 8.0 %collective-permute-done.32.refs_2_ = bf16[144,512]{1,0:T(8,128)(2,1)S(1)} collective-permute-done((bf16[144,512]{1,0:T(8,128)(2,1)S(1)}, bf16[144,512]{1,0:T(8,128)(2,1)S(1)}, u32[]{:S(2)}, u32[]{:S(2)}) %collective-permute-start.32) | collective-permute-done | bytes 147488 | tf_op jit(solution)/shard_map/ppermute | solution.py:737
  217.4 1.9 body_sum.1
  220.2 2.0 lead_sum.1
  (135 shorter events, 39.2 us)
Async XLA Ops:
  3.4 6.5 %collective-permute-start.1 = (bf16[16,1664]{1,0:T(8,128)(2,1)}, bf16[16,1664]{1,0:T(8,128)(2,1)S(1)}, u32[]{:S(2)}, u32[]{:S(2)}) collective-permute-start(bf16[16,1664]{1,0:T(8,128)(2,1)} %get-tuple-element.88), channel_id=1, source_target_pairs={{0,2},{1,3},{2,0},{3,1},{4,6},{5,7},{6,4},{7,5},{8,10},{9,11},{10,... | collective-permute-start | bytes 159752 | tf_op jit(solution)/shard_map/ppermute | solution.py:737
  6.4 6.4 %collective-permute-start.2 = (bf16[16,1664]{1,0:T(8,128)(2,1)}, bf16[16,1664]{1,0:T(8,128)(2,1)S(1)}, u32[]{:S(2)}, u32[]{:S(2)}) collective-permute-start(bf16[16,1664]{1,0:T(8,128)(2,1)} %get-tuple-element.88), channel_id=1, source_target_pairs={{0,4},{1,5},{2,6},{3,7},{4,0},{5,1},{6,2},{7,3},{8,12},{9,13},{10,... | collective-permute-start | bytes 159752 | tf_op jit(solution)/shard_map/ppermute | solution.py:737
  9.0 6.7 %collective-permute-start.3 = (bf16[16,1664]{1,0:T(8,128)(2,1)}, bf16[16,1664]{1,0:T(8,128)(2,1)S(1)}, u32[]{:S(2)}, u32[]{:S(2)}) collective-permute-start(bf16[16,1664]{1,0:T(8,128)(2,1)} %get-tuple-element.88), channel_id=1, source_target_pairs={{0,6},{1,7},{2,4},{3,5},{4,2},{5,3},{6,0},{7,1},{8,14},{9,15},{10,... | collective-permute-start | bytes 159752 | tf_op jit(solution)/shard_map/ppermute | solution.py:737
  9.0 11.1 %collective-permute-start = (bf16[144,512]{1,0:T(8,128)(2,1)}, bf16[144,512]{1,0:T(8,128)(2,1)S(1)}, u32[]{:S(2)}, u32[]{:S(2)}) collective-permute-start(bf16[144,512]{1,0:T(8,128)(2,1)} %get-tuple-element.87), channel_id=1, source_target_pairs={{0,2},{1,3},{2,0},{3,1},{4,6},{5,7},{6,4},{7,5},{8,10},{9,11},{10,... | collective-permute-start | bytes 442376 | tf_op jit(solution)/shard_map/ppermute | solution.py:737
  16.6 7.3 %collective-permute-start.4 = (bf16[4,16,1664]{2,1,0:T(8,128)(2,1)S(1)}, bf16[4,16,1664]{2,1,0:T(8,128)(2,1)S(1)}, u32[]{:S(2)}, u32[]{:S(2)}) collective-permute-start(bf16[4,16,1664]{2,1,0:T(8,128)(2,1)S(1)} %pad_maximum_fusion.4.refs_0_), channel_id=1, source_target_pairs={{0,8},{8,0},{16,24},{24,16},{1,9},{9,1},{17,25},{25,17},{2,10},{10... | collective-permute-start | bytes 638984 | tf_op jit(solution)/shard_map/ppermute | solution.py:737
  18.1 9.3 %collective-permute-start.5 = (bf16[4,16,1664]{2,1,0:T(8,128)(2,1)S(1)}, bf16[4,16,1664]{2,1,0:T(8,128)(2,1)S(1)}, u32[]{:S(2)}, u32[]{:S(2)}) collective-permute-start(bf16[4,16,1664]{2,1,0:T(8,128)(2,1)S(1)} %pad_maximum_fusion.4.refs_0_), channel_id=1, source_target_pairs={{0,16},{8,24},{16,0},{24,8},{1,17},{9,25},{17,1},{25,9},{2,18},{10... | collective-permute-start | bytes 638984 | tf_op jit(solution)/shard_map/ppermute | solution.py:737
  19.6 7.8 %collective-permute-start.6 = (bf16[4,16,1664]{2,1,0:T(8,128)(2,1)S(1)}, bf16[4,16,1664]{2,1,0:T(8,128)(2,1)S(1)}, u32[]{:S(2)}, u32[]{:S(2)}) collective-permute-start(bf16[4,16,1664]{2,1,0:T(8,128)(2,1)S(1)} %pad_maximum_fusion.4.refs_0_), channel_id=1, source_target_pairs={{0,24},{8,16},{16,8},{24,0},{1,25},{9,17},{17,9},{25,1},{2,26},{10... | collective-permute-start | bytes 638984 | tf_op jit(solution)/shard_map/ppermute | solution.py:737
  27.4 16.5 %collective-permute-start.11 = (bf16[2,144,512]{2,1,0:T(8,128)(2,1)S(1)}, bf16[2,144,512]{2,1,0:T(8,128)(2,1)S(1)}, u32[]{:S(2)}, u32[]{:S(2)}) collective-permute-start(bf16[2,144,512]{2,1,0:T(8,128)(2,1)S(1)} %pad_maximum_fusion.3), channel_id=1, source_target_pairs={{0,4},{1,5},{2,6},{3,7},{4,0},{5,1},{6,2},{7,3},{8,12},{9,13},{10,... | collective-permute-start | bytes 884744 | tf_op jit(solution)/shard_map/ppermute | solution.py:737
  44.0 3.0 %collective-permute-start.12 = (bf16[2,4,272,256]{3,2,1,0:T(8,128)(2,1)}, bf16[2,4,272,256]{3,2,1,0:T(8,128)(2,1)S(1)}, u32[]{:S(2)}, u32[]{:S(2)}) collective-permute-start(bf16[2,4,272,256]{3,2,1,0:T(8,128)(2,1)} %get-tuple-element.97.own.refs_0_), channel_id=1, source_target_pairs={{0,1},{1,0},{2,3},{3,2},{4,5},{5,4},{6,7},{7,6},{8,9},{9,8},{10,11... | collective-permute-start | bytes 3342344 | tf_op jit(solution)/shard_map/ppermute | solution.py:737
  50.7 9.8 %collective-permute-start.13 = (bf16[4,80,512]{2,1,0:T(8,128)(2,1)S(1)}, bf16[4,80,512]{2,1,0:T(8,128)(2,1)S(1)}, u32[]{:S(2)}, u32[]{:S(2)}) collective-permute-start(bf16[4,80,512]{2,1,0:T(8,128)(2,1)S(1)} %slice.12), channel_id=1, source_target_pairs={{0,8},{8,0},{16,24},{24,16},{1,9},{9,1},{17,25},{25,17},{2,10},{10... | collective-permute-start | bytes 983048 | tf_op jit(solution)/shard_map/ppermute | solution.py:737
  50.9 11.1 %collective-permute-start.15 = (bf16[4,64,512]{2,1,0:T(8,128)(2,1)S(1)}, bf16[4,64,512]{2,1,0:T(8,128)(2,1)S(1)}, u32[]{:S(2)}, u32[]{:S(2)}) collective-permute-start(bf16[4,64,512]{2,1,0:T(8,128)(2,1)S(1)} %slice.13), channel_id=1, source_target_pairs={{0,16},{8,24},{16,0},{24,8},{1,17},{9,25},{17,1},{25,9},{2,18},{10... | collective-permute-start | bytes 786440 | tf_op jit(solution)/shard_map/ppermute | solution.py:737
  52.2 24.9 %all-to-all-start = ((bf16[4,272,256]{2,1,0:T(8,128)(2,1)}), bf16[4,272,256]{2,1,0:T(8,128)(2,1)S(1)}, u32[]{:S(2)}, u32[]{:S(2)}) async-start(bf16[4,272,256]{2,1,0:T(8,128)(2,1)} %spread.2), calls=%async_computation | async-start | bytes 1114112 | tf_op jit(solution)/shard_map/all_to_all | solution.py:875
  60.5 16.0 %collective-permute-start.14 = (bf16[8,80,512]{2,1,0:T(8,128)(2,1)S(1)}, bf16[8,80,512]{2,1,0:T(8,128)(2,1)S(1)}, u32[]{:S(2)}, u32[]{:S(2)}) collective-permute-start(bf16[8,80,512]{2,1,0:T(8,128)(2,1)S(1)} %pad_maximum_fusion), channel_id=1, source_target_pairs={{0,16},{8,24},{16,0},{24,8},{1,17},{9,25},{17,1},{25,9},{2,18},{10... | collective-permute-start | bytes 1966088 | tf_op jit(solution)/shard_map/ppermute | solution.py:737
  62.1 12.9 %collective-permute-start.16 = (bf16[8,64,512]{2,1,0:T(8,128)(2,1)S(1)}, bf16[8,64,512]{2,1,0:T(8,128)(2,1)S(1)}, u32[]{:S(2)}, u32[]{:S(2)}) collective-permute-start(bf16[8,64,512]{2,1,0:T(8,128)(2,1)S(1)} %pad_maximum_fusion.2), channel_id=1, source_target_pairs={{0,8},{8,0},{16,24},{24,16},{1,9},{9,1},{17,25},{25,17},{2,10},{10... | collective-permute-start | bytes 1572872 | tf_op jit(solution)/shard_map/ppermute | solution.py:737
  76.6 5.4 %collective-permute-start.21 = (bf16[8,80,512]{2,1,0:T(8,128)(2,1)S(1)}, bf16[8,80,512]{2,1,0:T(8,128)(2,1)}, u32[]{:S(2)}, u32[]{:S(2)}) collective-permute-start(bf16[8,80,512]{2,1,0:T(8,128)(2,1)S(1)} %collective-permute-done.14.refs_7_), channel_id=1, source_target_pairs={{0,1},{1,0},{2,3},{3,2},{4,5},{5,4},{6,7},{7,6},{8,9},{9,8},{10,11... | collective-permute-start | bytes 1966088 | tf_op jit(solution)/shard_map/ppermute | solution.py:737
  76.6 3.9 %collective-permute-start.18 = (bf16[4,144,512]{2,1,0:T(8,128)(2,1)S(1)}, bf16[4,144,512]{2,1,0:T(8,128)(2,1)}, u32[]{:S(2)}, u32[]{:S(2)}) collective-permute-start(bf16[4,144,512]{2,1,0:T(8,128)(2,1)S(1)} %pad_maximum_fusion.1.refs_4_), channel_id=1, source_target_pairs={{0,1},{1,0},{2,3},{3,2},{4,5},{5,4},{6,7},{7,6},{8,9},{9,8},{10,11... | collective-permute-start | bytes 1769480 | tf_op jit(solution)/shard_map/ppermute | solution.py:737
  77.1 2.3 %collective-permute-start.20 = (bf16[4,64,512]{2,1,0:T(8,128)(2,1)S(1)}, bf16[4,64,512]{2,1,0:T(8,128)(2,1)S(1)}, u32[]{:S(2)}, u32[]{:S(2)}) collective-permute-start(bf16[4,64,512]{2,1,0:T(8,128)(2,1)S(1)} %collective-permute-done.15.refs_6_), channel_id=1, source_target_pairs={{0,1},{1,0},{2,3},{3,2},{4,5},{5,4},{6,7},{7,6},{8,9},{9,8},{10,11... | collective-permute-start | bytes 786440 | tf_op jit(solution)/shard_map/ppermute | solution.py:737
  77.1 4.7 %collective-permute-start.17 = (bf16[4,272,256]{2,1,0:T(8,128)(2,1)S(1)}, bf16[4,272,256]{2,1,0:T(8,128)(2,1)S(1)}, u32[]{:S(2)}, u32[]{:S(2)}) collective-permute-start(bf16[4,272,256]{2,1,0:T(8,128)(2,1)S(1)} %all-to-all-done.refs_2_), channel_id=1, source_target_pairs={{0,1},{1,0},{2,3},{3,2},{4,5},{5,4},{6,7},{7,6},{8,9},{9,8},{10,11... | collective-permute-start | bytes 1671176 | tf_op jit(solution)/shard_map/ppermute | solution.py:737
  77.6 4.3 %collective-permute-start.22 = (bf16[8,64,512]{2,1,0:T(8,128)(2,1)S(1)}, bf16[8,64,512]{2,1,0:T(8,128)(2,1)S(1)}, u32[]{:S(2)}, u32[]{:S(2)}) collective-permute-start(bf16[8,64,512]{2,1,0:T(8,128)(2,1)S(1)} %collective-permute-done.16.refs_8_), channel_id=1, source_target_pairs={{0,1},{1,0},{2,3},{3,2},{4,5},{5,4},{6,7},{7,6},{8,9},{9,8},{10,11... | collective-permute-start | bytes 1572872 | tf_op jit(solution)/shard_map/ppermute | solution.py:737
  79.4 2.5 %collective-permute-start.19 = (bf16[4,80,512]{2,1,0:T(8,128)(2,1)S(1)}, bf16[4,80,512]{2,1,0:T(8,128)(2,1)S(1)}, u32[]{:S(2)}, u32[]{:S(2)}) collective-permute-start(bf16[4,80,512]{2,1,0:T(8,128)(2,1)S(1)} %collective-permute-done.13.refs_5_), channel_id=1, source_target_pairs={{0,1},{1,0},{2,3},{3,2},{4,5},{5,4},{6,7},{7,6},{8,9},{9,8},{10,11... | collective-permute-start | bytes 983048 | tf_op jit(solution)/shard_map/ppermute | solution.py:737
  115.6 11.3 %collective-permute-start.23 = (bf16[2,4,272,256]{3,2,1,0:T(8,128)(2,1)}, bf16[2,4,272,256]{3,2,1,0:T(8,128)(2,1)S(1)}, u32[]{:S(2)}, u32[]{:S(2)}) collective-permute-start(bf16[2,4,272,256]{3,2,1,0:T(8,128)(2,1)} %get-tuple-element.114.own.refs_0_), channel_id=1, source_target_pairs={{0,1},{1,0},{2,3},{3,2},{4,5},{5,4},{6,7},{7,6},{8,9},{9,8},{10,11... | collective-permute-start | bytes 3342344 | tf_op jit(solution)/shard_map/ppermute | solution.py:737
  126.9 17.8 %collective-permute-start.24 = (bf16[16,144,512]{2,1,0:T(8,128)(2,1)}, bf16[16,144,512]{2,1,0:T(8,128)(2,1)}, u32[]{:S(2)}, u32[]{:S(2)}) collective-permute-start(bf16[16,144,512]{2,1,0:T(8,128)(2,1)} %get-tuple-element.130), channel_id=1, source_target_pairs={{0,1},{1,0},{2,3},{3,2},{4,5},{5,4},{6,7},{7,6},{8,9},{9,8},{10,11... | collective-permute-start | bytes 7077896 | tf_op jit(solution)/shard_map/ppermute | solution.py:737
  130.5 19.6 %all-to-all-start.1 = ((bf16[4,272,256]{2,1,0:T(8,128)(2,1)}), bf16[4,272,256]{2,1,0:T(8,128)(2,1)S(1)}, u32[]{:S(2)}, u32[]{:S(2)}) async-start(bf16[4,272,256]{2,1,0:T(8,128)(2,1)} %spread.3), calls=%async_computation.1 | async-start | bytes 1114112 | tf_op jit(solution)/shard_map/all_to_all | solution.py:875
  151.0 21.2 %collective-permute-start.26 = (bf16[2,4,80,512]{3,2,1,0:T(8,128)(2,1)}, bf16[2,4,80,512]{3,2,1,0:T(8,128)(2,1)}, u32[]{:S(2)}, u32[]{:S(2)}) collective-permute-start(bf16[2,4,80,512]{3,2,1,0:T(8,128)(2,1)} %dynamic-slice_bitcast_fusion), channel_id=1, source_target_pairs={{0,8},{8,0},{16,24},{24,16},{1,9},{9,1},{17,25},{25,17},{2,10},{10... | collective-permute-start | bytes 1966088 | tf_op jit(solution)/shard_map/ppermute | solution.py:737
  151.0 21.1 %collective-permute-start.27 = (bf16[2,4,64,512]{3,2,1,0:T(8,128)(2,1)S(1)}, bf16[2,4,64,512]{3,2,1,0:T(8,128)(2,1)S(1)}, u32[]{:S(2)}, u32[]{:S(2)}) collective-permute-start(bf16[2,4,64,512]{3,2,1,0:T(8,128)(2,1)S(1)} %dynamic-slice_bitcast_fusion.1), channel_id=1, source_target_pairs={{0,16},{8,24},{16,0},{24,8},{1,17},{9,25},{17,1},{25,9},{2,18},{10... | collective-permute-start | bytes 1572872 | tf_op jit(solution)/shard_map/ppermute | solution.py:737
  172.2 2.7 %collective-permute-start.28 = (bf16[16,16,1664]{2,1,0:T(8,128)(2,1)}, bf16[16,16,1664]{2,1,0:T(8,128)(2,1)S(1)}, u32[]{:S(2)}, u32[]{:S(2)}) collective-permute-start(bf16[16,16,1664]{2,1,0:T(8,128)(2,1)} %get-tuple-element.143), channel_id=1, source_target_pairs={{0,1},{1,0},{2,3},{3,2},{4,5},{5,4},{6,7},{7,6},{8,9},{9,8},{10,11... | collective-permute-start | bytes 2555912 | tf_op jit(solution)/shard_map/ppermute | solution.py:737
  177.2 42.1 %all-to-all-start.2 = ((bf16[16,16,1664]{2,1,0:T(8,128)(2,1)}), bf16[16,16,1664]{2,1,0:T(8,128)(2,1)S(1)}, u32[]{:S(2)}, u32[]{:S(2)}) async-start(bf16[16,16,1664]{2,1,0:T(8,128)(2,1)} %add_convert_fusion.1), calls=%async_computation.2 | async-start | bytes 1703936 | tf_op jit(solution)/shard_map/all_to_all | solution.py:933
  183.5 14.4 %collective-permute-start.30 = (bf16[4,64,512]{2,1,0:T(8,128)(2,1)}, bf16[4,64,512]{2,1,0:T(8,128)(2,1)}, u32[]{:S(2)}, u32[]{:S(2)}) collective-permute-start(bf16[4,64,512]{2,1,0:T(8,128)(2,1)} %dynamic-slice_bitcast_fusion.3), channel_id=1, source_target_pairs={{0,8},{8,0},{16,24},{24,16},{1,9},{9,1},{17,25},{25,17},{2,10},{10... | collective-permute-start | bytes 786440 | tf_op jit(solution)/shard_map/ppermute | solution.py:737
  186.8 12.7 %collective-permute-start.29 = (bf16[4,80,512]{2,1,0:T(8,128)(2,1)S(1)}, bf16[4,80,512]{2,1,0:T(8,128)(2,1)S(1)}, u32[]{:S(2)}, u32[]{:S(2)}) collective-permute-start(bf16[4,80,512]{2,1,0:T(8,128)(2,1)S(1)} %dynamic-slice_bitcast_fusion.2), channel_id=1, source_target_pairs={{0,16},{8,24},{16,0},{24,8},{1,17},{9,25},{17,1},{25,9},{2,18},{10... | collective-permute-start | bytes 983048 | tf_op jit(solution)/shard_map/ppermute | solution.py:737
  200.3 8.4 %collective-permute-start.31 = (bf16[144,512]{1,0:T(8,128)(2,1)S(1)}, bf16[144,512]{1,0:T(8,128)(2,1)S(1)}, u32[]{:S(2)}, u32[]{:S(2)}) collective-permute-start(bf16[144,512]{1,0:T(8,128)(2,1)S(1)} %get-tuple-element.158), channel_id=1, source_target_pairs={{0,2},{1,3},{2,0},{3,1},{4,6},{5,7},{6,4},{7,5},{8,10},{9,11},{10,... | collective-permute-start | bytes 442376 | tf_op jit(solution)/shard_map/ppermute | solution.py:737
  204.0 12.7 %collective-permute-start.32 = (bf16[144,512]{1,0:T(8,128)(2,1)S(1)}, bf16[144,512]{1,0:T(8,128)(2,1)S(1)}, u32[]{:S(2)}, u32[]{:S(2)}) collective-permute-start(bf16[144,512]{1,0:T(8,128)(2,1)S(1)} %get-tuple-element.159), channel_id=1, source_target_pairs={{0,4},{1,5},{2,6},{3,7},{4,0},{5,1},{6,2},{7,3},{8,12},{9,13},{10,... | collective-permute-start | bytes 442376 | tf_op jit(solution)/shard_map/ppermute | solution.py:737
  205.3 11.4 %collective-permute-start.33 = (bf16[144,512]{1,0:T(8,128)(2,1)S(1)}, bf16[144,512]{1,0:T(8,128)(2,1)S(1)}, u32[]{:S(2)}, u32[]{:S(2)}) collective-permute-start(bf16[144,512]{1,0:T(8,128)(2,1)S(1)} %get-tuple-element.156), channel_id=1, source_target_pairs={{0,6},{1,7},{2,4},{3,5},{4,2},{5,3},{6,0},{7,1},{8,14},{9,15},{10,... | collective-permute-start | bytes 442376 | tf_op jit(solution)/shard_map/ppermute | solution.py:737
  (35 other events, 173.5 us)

commit v3 on v2

--- a/solution.py
+++ b/solution.py
@@ -15,6 +15,8 @@
 SCALE = HEAD ** (-0.25)
 LOGF = 0.5 * math.log(FEATS)
 BLK = 256
+WIDE_BLK = 512
+SUB = 256
 KVROWS = 272
 BF = jnp.bfloat16
 F32 = jnp.float32
@@ -59,9 +61,16 @@
     return s, feats
 
 
-def cell_range(bounds, blk, cells):
-    first = lax.axis_index("fsdp") * (pl.num_programs(0) * BLK) + blk * BLK
-    return cell_at(bounds, first, cells), cell_at(bounds, first + BLK - 1, cells), first
+def over_cells(bounds, blk, cells, block, body):
+    for sub in range(block // SUB):
+        first = lax.axis_index("fsdp") * (pl.num_programs(0) * block) + blk * block + sub * SUB
+        rows = slice(sub * SUB, (sub + 1) * SUB)
+
+        def one(c, carry):
+            body(c, rows, first)
+            return carry
+
+        lax.fori_loop(cell_at(bounds, first, cells), cell_at(bounds, first + SUB - 1, cells) + 1, one, 0)
 
 
 def cell_at(bounds, slot, cells):
@@ -72,7 +81,7 @@
 
 
 def cell_mask(bounds, c, first, cols):
-    place = lax.broadcasted_iota(jnp.int32, (BLK, cols), 0) + first
+    place = lax.broadcasted_iota(jnp.int32, (SUB, cols), 0) + first
     return (place >= bounds[0, c]) & (place < bounds[0, c + 1])
 
 
@@ -127,6 +136,10 @@
                 full[c, h, HEAD:, :] = body if i % 2 else line
 
 
+def keep_lanes(pad):
+    return jnp.broadcast_to(pad[...].astype(F32), (128, pad.shape[1])).T
+
+
 def feature_parts(bank, main, rest):
     w = bank[...]
     hi = w.astype(BF)
@@ -173,7 +186,7 @@
     return value.reshape(-1, value.shape[-1])
 
 
-def key_kernel(cells, places, bounds, x, keep, bank, *refs):
+def key_kernel(cells, places, bounds, x, pad, bank, *refs):
     count = 2 * len(places) if places else 1
     pieces, (a1_o, sk_o, pk_o, vr_o, sums_o, vec_o), refs = refs[:count], refs[count : count + 6], refs[count + 6 :]
     if places:
@@ -197,6 +210,8 @@
                 copy.wait()
         vec_o[...] = columns(w, 3 * d, 3 * d + 128).astype(F32).T[:16]
 
+    keep = keep_lanes(pad)
+    keep = jnp.concatenate([keep, keep], 1)
     z, _ = norm_stats(x[...].astype(F32))
     a1 = (z * vec_o[0:1] + vec_o[1:2]).astype(BF)
     a1_o[...] = a1
@@ -207,32 +222,37 @@
         sk_o[:, 128 * p : 128 * p + 128] = s.astype(BF)
         for odd in (0, 1):
             h = 2 * p + odd
-            pk_o[:, FEATS * h : FEATS * (h + 1)] = (keep[...] * feats[odd]).astype(BF)
-    lo, hi, first = cell_range(bounds, blk, cells)
-    low = lane_low(BLK)
-
-    def one(c, carry):
+            pk_o[:, FEATS * h : FEATS * (h + 1)] = (keep * feats[odd]).astype(BF)
+    low = lane_low(SUB)
+
+    def one(c, rows, first):
         mask = cell_mask(bounds, c, first, 128)
         for p in range(PAIRS):
-            v = vr_o[:, 128 * p : 128 * p + 128].astype(F32)
+            v = vr_o[rows, 128 * p : 128 * p + 128].astype(F32)
             for odd in (0, 1):
                 h = 2 * p + odd
                 aug = jnp.where(low, 1.0, v) if odd else jnp.where(low, v, 1.0)
                 aug = jnp.where(mask, aug, 0.0).astype(BF)
-                acc[c, h] += dot_tn(aug, pk_o[:, FEATS * h : FEATS * (h + 1)])
-        return carry
-
-    lax.fori_loop(lo, hi + 1, one, 0)
+                acc[c, h] += dot_tn(aug, pk_o[rows, FEATS * h : FEATS * (h + 1)])
+
+    over_cells(bounds, blk, cells, BLK, one)
 
     @pl.when(blk == pl.num_programs(0) - 1)
     def _():
         store_sums(acc, sums_o, cells, False)
 
 
+PAD = pl.BlockSpec((1, BLK), lambda i: (0, i))
+
+
 def rows_spec(cols):
     return pl.BlockSpec((BLK, cols), lambda i: (i, 0))
 
 
+def wide_spec(cols):
+    return pl.BlockSpec((WIDE_BLK, cols), lambda i: (i, 0))
+
+
 def whole_spec(shape):
     return pl.BlockSpec(shape, lambda i: (0,) * len(shape))
 
@@ -243,6 +263,7 @@
 
 SMEM = pl.BlockSpec(memory_space=pltpu.SMEM)
 ANY = pl.BlockSpec(memory_space=pl.ANY)
+HBM = pl.BlockSpec(memory_space=pltpu.HBM)
 VM = pl.BlockSpec(memory_space=pltpu.VMEM)
 
 
@@ -262,7 +283,7 @@
     return jax.ShapeDtypeStruct(dims, kind)
 
 
-def run_keys(bounds, x, keep, bank, pieces, places, cells):
+def run_keys(bounds, x, padding, bank, pieces, places, cells):
     n, d = x.shape
     out_specs = [
         rows_spec(d), rows_spec(d), rows_spec(HEADS * FEATS), rows_spec(d), whole_spec(sums_shape(cells)), whole_spec((16, d)),
@@ -280,7 +301,7 @@
     return pl.pallas_call(
         functools.partial(key_kernel, cells, places),
         grid=(n // BLK,),
-        in_specs=[SMEM, rows_spec(d), rows_spec(1), whole_spec(bank.shape)]
+        in_specs=[SMEM, rows_spec(d), PAD, whole_spec(bank.shape)]
         + ([ANY] * len(pieces) if places else whole_specs(pieces)),
         out_specs=out_specs,
         out_shape=out_shape,
@@ -288,7 +309,7 @@
         compiler_params=params(),
         cost_estimate=cost(8, 10),
         name="keys",
-    )(bounds, x, keep, bank, *pieces)
+    )(bounds, x, padding, bank, *pieces)
 
 
 def shuffle(j, rows, wide, d):
@@ -351,27 +372,37 @@
     )(a1, w, bank, vec)
 
 
-def spread_kernel(cells, slots, bounds, own, got, out):
+def spread_kernel(cells, slots, bounds, own, got, out, mine, theirs, sems):
     spot = lax.axis_index("fsdp")
     core = spot % 2
+    made = []
     for z in range(out.shape[0]):
         c = cell_at(bounds, z * (2 * slots) + jnp.where(z > spot // 2, 0, 2 * slots - 1), cells)
-        out[z] = (own[core, c].astype(F32) + got[core, c].astype(F32)).astype(BF)
+        made.append(pltpu.make_async_copy(own.at[core, c], mine.at[z], sems.at[0, z]))
+        made.append(pltpu.make_async_copy(got.at[core, c], theirs.at[z], sems.at[1, z]))
+    for copy in made:
+        copy.start()
+    for z in range(out.shape[0]):
+        made[2 * z].wait()
+        made[2 * z + 1].wait()
+        out[z] = (mine[z].astype(F32) + theirs[z].astype(F32)).astype(BF)
 
 
 def run_spread(bounds, own, got, chips, slots, cells):
+    part = pltpu.VMEM((chips, KVROWS, FEATS), BF)
     return pl.pallas_call(
         functools.partial(spread_kernel, cells, slots),
-        in_specs=[SMEM, VM, VM],
+        in_specs=[SMEM, ANY, ANY],
         out_specs=VM,
         out_shape=shape(chips, KVROWS, FEATS),
-        compiler_params=pltpu.CompilerParams(vmem_limit_bytes=VMEM_LIMIT),
+        scratch_shapes=[part, part, pltpu.SemaphoreType.DMA((2, chips))],
+        compiler_params=pltpu.CompilerParams(vmem_limit_bytes=4 * 1024 * 1024),
         cost_estimate=cost(0.001, 2),
         name="spread",
     )(bounds, own, got)
 
 
-def middle_kernel(cells, slots, nsums, places, bounds, x, dy_r, keep_r, pq, vec, b_up, *refs):
+def middle_kernel(cells, slots, nsums, places, bounds, x, dy_r, pad, pq, vec, b_up, *refs):
     sums, refs = refs[:nsums], refs[nsums:]
     count = 2 * len(places) if places else 3
     pieces, refs = refs[:count], refs[count:]
@@ -402,30 +433,29 @@
         vup_o[...] = jnp.zeros_like(vup_o)
         load_sums(bounds, sums, full, slots, cells, False)
 
-    lo, hi, first = cell_range(bounds, blk, cells)
-    low = lane_low(BLK)
-
-    def attend(c, carry):
+    low = lane_low(SUB)
+
+    def attend(c, rows, first):
         mask = cell_mask(bounds, c, first, 128)
         for p in range(PAIRS):
             h = 2 * p
             lanes = slice(128 * p, 128 * p + 128)
-            r0 = dot_nt(pq[:, FEATS * h : FEATS * (h + 1)], full[c, h])
-            r1 = dot_nt(pq[:, FEATS * (h + 1) : FEATS * (h + 2)], full[c, h + 1])
+            r0 = dot_nt(pq[rows, FEATS * h : FEATS * (h + 1)], full[c, h])
+            r1 = dot_nt(pq[rows, FEATS * (h + 1) : FEATS * (h + 2)], full[c, h + 1])
             num = jnp.where(low, r0, r1)
             den = pltpu.roll(jnp.where(low, r1, r0), HEAD, 1)
-            num_s[:, lanes] = jnp.where(mask, num, num_s[:, lanes])
-            den_s[:, lanes] = jnp.where(mask, den, den_s[:, lanes])
-        return carry
-
-    lax.fori_loop(lo, hi + 1, attend, 0)
+            num_s[rows, lanes] = jnp.where(mask, num, num_s[rows, lanes])
+            den_s[rows, lanes] = jnp.where(mask, den, den_s[rows, lanes])
+
+    over_cells(bounds, blk, cells, x.shape[0], attend)
     if places:
         @pl.when(blk == 0)
         def _():
             for copy in copies(pieces, places, w, sems):
                 copy.wait()
 
-    keep = keep_r[...]
+    keep = keep_lanes(pad)
+    keep = jnp.concatenate([keep] * (width // 128), 1)
     inv = 1.0 / den_s[...]
     ar = (keep * num_s[...] * inv).astype(BF)
     ar_o[...] = ar
@@ -469,6 +499,7 @@
     dattn = keep * dot_nt(do, w_out()).astype(BF).astype(F32)
     dnum = dattn * inv
     dden = -dnum * num_s[...] * inv
+    low = lane_low(x.shape[0])
     for p in range(PAIRS):
         lanes = slice(128 * p, 128 * p + 128)
         mine = dnum[:, lanes]
@@ -477,26 +508,25 @@
         grads_o[:, 128 * h : 128 * h + 128] = jnp.where(low, mine, swap).astype(BF)
         grads_o[:, 128 * h + 128 : 128 * h + 256] = jnp.where(low, swap, mine).astype(BF)
 
-    def gather(c, carry):
+    def gather(c, rows, first):
         mask = cell_mask(bounds, c, first, 128)
         for h in range(HEADS):
-            part = grads_o[:, 128 * h : 128 * h + 128]
+            part = grads_o[rows, 128 * h : 128 * h + 128]
             part = jnp.where(mask, part.astype(F32), 0.0).astype(BF)
-            acc[c, h] += dot_tn(part, pq[:, FEATS * h : FEATS * (h + 1)])
-        return carry
-
-    lax.fori_loop(lo, hi + 1, gather, 0)
+            acc[c, h] += dot_tn(part, pq[rows, FEATS * h : FEATS * (h + 1)])
+
+    over_cells(bounds, blk, cells, x.shape[0], gather)
 
     @pl.when(blk == pl.num_programs(0) - 1)
     def _():
         store_sums(acc, sums_o, cells, True)
 
 
-def run_middle(bounds, x, dy, keep, pq, vec, b_up, sums, pieces, places, ff, cells):
+def run_middle(bounds, x, dy, padding, pq, vec, b_up, sums, pieces, places, ff, cells):
     n, d = x.shape
     wide = HEADS * 128
     full = (cells, HEADS, 128, FEATS)
-    scratch = [pltpu.VMEM(full, F32), pltpu.VMEM((BLK, d), F32), pltpu.VMEM((BLK, d), F32)]
+    scratch = [pltpu.VMEM(full, F32), pltpu.VMEM((WIDE_BLK, d), F32), pltpu.VMEM((WIDE_BLK, d), F32)]
     if places:
         rows = max(hi for _, _, hi in places)
         chips = 1 + max(m for masks, _, _ in places for m in masks)
@@ -504,15 +534,15 @@
         scratch += [pltpu.VMEM((chips, 2, rows, d), BF), pltpu.SemaphoreType.DMA((number,))]
     return pl.pallas_call(
         functools.partial(middle_kernel, cells, n, len(sums), places),
-        grid=(n // BLK,),
+        grid=(n // WIDE_BLK,),
         in_specs=[
-            SMEM, rows_spec(d), rows_spec(d), rows_spec(1), rows_spec(HEADS * FEATS), whole_spec(vec.shape), whole_spec(b_up.shape),
+            SMEM, wide_spec(d), wide_spec(d), pl.BlockSpec((1, WIDE_BLK), lambda i: (0, i)), wide_spec(HEADS * FEATS), whole_spec(vec.shape), whole_spec(b_up.shape),
         ]
         + whole_specs(sums)
         + ([ANY] * len(pieces) if places else whole_specs(pieces)),
         out_specs=[
-            rows_spec(d), rows_spec(ff), rows_spec(ff), rows_spec(d), rows_spec(d), rows_spec(d),
-            rows_spec(d), rows_spec(wide), whole_spec((16, d)), whole_spec((8, d)),
+            wide_spec(d), wide_spec(ff), wide_spec(ff), wide_spec(d), wide_spec(d), wide_spec(d),
+            wide_spec(d), wide_spec(wide), whole_spec((16, d)), whole_spec((8, d)),
             whole_spec(sums_shape(cells)), whole_spec(full),
         ],
         out_shape=[
@@ -524,7 +554,7 @@
         compiler_params=params(),
         cost_estimate=cost(14, 30),
         name="middle",
-    )(bounds, x, dy, keep, pq, vec, b_up, *sums, *pieces)
+    )(bounds, x, dy, padding, pq, vec, b_up, *sums, *pieces)
 
 
 def phi_back(s, feats, rhs, low):
@@ -534,26 +564,25 @@
     return (jnp.where(low, r0, r1) - s * total) * SCALE
 
 
-def query_back_kernel(cells, bounds, grads, pq, sq, full, bank, a1, dq_o, gq_o, g_s, acc, rhs):
+def query_back_kernel(cells, bounds, grads, pq, sq, full, bank, a1, dq_o, gq_o, sum_o, g_s, rhs):
     blk = pl.program_id(0)
 
     @pl.when(blk == 0)
     def _():
         back_parts(bank, rhs)
-        acc[...] = jnp.zeros_like(acc)
-
-    lo, hi, first = cell_range(bounds, blk, cells)
+        gq_o[...] = jnp.zeros_like(gq_o)
+        sum_o[...] = jnp.zeros_like(sum_o)
+
     low = lane_low(BLK)
 
-    def one(c, carry):
+    def one(c, rows, first):
         mask = cell_mask(bounds, c, first, FEATS)
         for h in range(HEADS):
             cols = slice(FEATS * h, FEATS * (h + 1))
-            g = dot(grads[:, 128 * h : 128 * h + 128], full[c, h])
-            g_s[:, cols] = jnp.where(mask, g, g_s[:, cols])
-        return carry
-
-    lax.fori_loop(lo, hi + 1, one, 0)
+            g = dot(grads[rows, 128 * h : 128 * h + 128], full[c, h])
+            g_s[rows, cols] = jnp.where(mask, g, g_s[rows, cols])
+
+    over_cells(bounds, blk, cells, BLK, one)
     for p in range(PAIRS):
         lanes = slice(128 * p, 128 * p + 128)
         feats = []
@@ -561,11 +590,9 @@
             cols = slice(FEATS * (2 * p + odd), FEATS * (2 * p + odd + 1))
             feats.append(g_s[:, cols] * pq[:, cols].astype(F32))
         dq_o[:, lanes] = phi_back(sq[:, lanes].astype(F32), feats, rhs, low).astype(BF)
-    acc[...] += dot_tn(a1[...], dq_o[...])
-
-    @pl.when(blk == pl.num_programs(0) - 1)
-    def _():
-        gq_o[...] = acc[...].astype(BF)
+    dq = dq_o[...]
+    gq_o[...] += dot_tn(a1[...], dq)
+    sum_o[0:1] += jnp.sum(dq.astype(F32), 0, keepdims=True)
 
 
 def run_query_back(bounds, grads, pq, sq, full, bank, a1, cells):
@@ -577,155 +604,195 @@
             SMEM, rows_spec(HEADS * 128), rows_spec(HEADS * FEATS), rows_spec(d),
             whole_spec(full.shape), whole_spec(bank.shape), rows_spec(d),
         ],
-        out_specs=[rows_spec(d), whole_spec((d, d))],
-        out_shape=[shape(n, d), shape(d, d)],
-        scratch_shapes=[
-            pltpu.VMEM((BLK, HEADS * FEATS), F32), pltpu.VMEM((d, d), F32), pltpu.VMEM((2, 128, FEATS), BF),
-        ],
+        out_specs=[rows_spec(d), whole_spec((d, d)), whole_spec((8, d))],
+        out_shape=[shape(n, d), shape(d, d, kind=F32), shape(8, d, kind=F32)],
+        scratch_shapes=[pltpu.VMEM((BLK, HEADS * FEATS), F32), pltpu.VMEM((2, 128, FEATS), BF)],
         compiler_params=params(),
         cost_estimate=cost(3, 8),
         name="query_back",
     )(bounds, grads, pq, sq, full, bank, a1)
 
 
-def weight_kernel(rows, a2, dpre, gr, dy, ar, do, keep_o, send_o):
+def weight_kernel(rows, a2, dpre, gr, dy, ar, do, top_k, top_s, low_k, low_s, ar_s, do_s, sems):
     j = pl.program_id(0)
+    last = pl.num_programs(0) - 1
     d = a2.shape[1]
-
-    def put(value, block, lo, size):
-        count = d // (2 * size)
-        kept, sent = both_cores(value.reshape(count, 2, size, d))
-        at = (pl.ds(block * count, count), pl.ds(lo, size))
-        keep_o[at] = kept.astype(BF)
-        send_o[at] = sent.astype(BF)
+    made = [pltpu.make_async_copy(src, dst, sems.at[i]) for i, (src, dst) in enumerate(((ar, ar_s), (do, do_s)))]
+
+    def put(value, kept, sent):
+        count, size = kept.shape[:2]
+        mine, theirs = both_cores(value.reshape(count, 2, size, d))
+        kept[...] = mine.astype(BF)
+        sent[...] = theirs.astype(BF)
 
     @pl.when(j == 0)
     def _():
-        put(dot_tn(ar[...], do[...]), 0, 0, rows)
-
-    put(dot_tn(a2[...], dpre[...]), 0, pl.multiple_of(rows * (1 + j), rows), rows)
-    wide = (keep_o.shape[1] // rows - 1) // 2
-    put(dot_tn(gr[...], dy[...]), j, rows * (1 + wide), rows * wide)
+        for copy in made:
+            copy.start()
+
+    @pl.when(j < last)
+    def _():
+        put(dot_tn(a2[...], dpre[...]), top_k, top_s)
+        put(dot_tn(gr[...], dy[...]), low_k, low_s)
+
+    @pl.when(j == last)
+    def _():
+        for copy in made:
+            copy.wait()
+        put(dot_tn(ar_s[...], do_s[...]), top_k, top_s)
 
 
 def run_weights(a2, dpre, gr, dy, ar, do, rows):
     n, d = a2.shape
     wide = dpre.shape[1] // d
-    out = (d // (2 * rows), rows * (1 + 2 * wide), d)
-    cols = pl.BlockSpec((n, d), lambda j: (0, j))
+    chips = d // (2 * rows)
+    cols = pl.BlockSpec((n, d), lambda j: (0, jnp.minimum(j, wide - 1)))
     whole = whole_spec((n, d))
+    top = pl.BlockSpec((chips, rows, d), lambda j: (0, j, 0))
+    low = pl.BlockSpec((chips // wide, rows * wide, d), lambda j: (jnp.minimum(j, wide - 1), 0, 0))
+    tops, lows = shape(chips, rows * (wide + 1), d), shape(chips, rows * wide, d)
     return pl.pallas_call(
         functools.partial(weight_kernel, rows),
-        grid=(wide,),
-        in_specs=[whole, cols, cols, whole, whole, whole],
-        out_specs=[whole_spec(out), whole_spec(out)],
-        out_shape=[shape(*out), shape(*out)],
+        grid=(wide + 1,),
+        in_specs=[whole, cols, cols, whole, HBM, HBM],
+        out_specs=[top, top, low, low],
+        out_shape=[tops, tops, lows, lows],
+        scratch_shapes=[pltpu.VMEM((n, d), BF), pltpu.VMEM((n, d), BF), pltpu.SemaphoreType.DMA((2,))],
         compiler_params=params(),
         cost_estimate=cost(5, 20),
         name="weights",
     )(a2, dpre, gr, dy, ar, do)
 
 
-def key_back_kernel(cells, slots, nsums, paired, rows, wide, bounds, x, a1, pk, vr, sk, dq, dx, vec, gvec, vup, bank, w, gq, *refs):
+def key_back_kernel(cells, slots, nsums, paired, rows, wide, bounds, a1, pk, vr, sk, gvec, vup, bank, w, gq, qsum, *refs):
     sums, refs = refs[:nsums], refs[nsums:]
-    outs, refs = refs[: 3 if paired else 2], refs[3 if paired else 2 :]
-    gt_o = outs[0]
-    full, g_s, v_s, rhs, dk_s, dv_s, vec_s, gk_s, gv_s = refs
+    dk_o, dv_o, outs = refs[0], refs[1], refs[2 : 4 if paired else 3]
+    full, g_s, v_s, rhs, gk_s, gv_s, sum_s = refs[4 if paired else 3 :]
     blk = pl.program_id(0)
-    d = x.shape[1]
+    d = a1.shape[1]
 
     @pl.when(blk == 0)
     def _():
-        vec_s[...] = gvec[...]
         gk_s[...] = jnp.zeros_like(gk_s)
         gv_s[...] = jnp.zeros_like(gv_s)
+        sum_s[...] = qsum[...]
         back_parts(bank, rhs)
         load_sums(bounds, sums, full, slots, cells, True)
 
-    lo, hi, first = cell_range(bounds, blk, cells)
     low = lane_low(BLK)
 
-    def one(c, carry):
+    def one(c, rows, first):
         mask = cell_mask(bounds, c, first, FEATS)
         narrow = cell_mask(bounds, c, first, 128)
+        low = lane_low(SUB)
         for p in range(PAIRS):
             lanes = slice(128 * p, 128 * p + 128)
-            v = vr[:, lanes].astype(F32)
+            v = vr[rows, lanes].astype(F32)
             outs = []
             for odd in (0, 1):
                 h = 2 * p + odd
                 cols = slice(FEATS * h, FEATS * (h + 1))
                 aug = (jnp.where(low, 1.0, v) if odd else jnp.where(low, v, 1.0)).astype(BF)
                 g = dot(aug, full[c, h])
-                g_s[:, cols] = jnp.where(mask, g, g_s[:, cols])
-                outs.append(dot_nt(pk[:, cols], full[c, h]))
-            v_s[:, lanes] = jnp.where(narrow, jnp.where(low, outs[0], outs[1]), v_s[:, lanes])
-        return carry
-
-    lax.fori_loop(lo, hi + 1, one, 0)
+                g_s[rows, cols] = jnp.where(mask, g, g_s[rows, cols])
+                outs.append(dot_nt(pk[rows, cols], full[c, h]))
+            v_s[rows, lanes] = jnp.where(narrow, jnp.where(low, outs[0], outs[1]), v_s[rows, lanes])
+
+    over_cells(bounds, blk, cells, BLK, one)
     for p in range(PAIRS):
         lanes = slice(128 * p, 128 * p + 128)
         feats = []
         for odd in (0, 1):
             cols = slice(FEATS * (2 * p + odd), FEATS * (2 * p + odd + 1))
             feats.append(g_s[:, cols] * pk[:, cols].astype(F32))
-        dk_s[:, lanes] = phi_back(sk[:, lanes].astype(F32), feats, rhs, low).astype(BF)
-    dv_s[...] = v_s[...].astype(BF)
-    dk, dv = dk_s[...], dv_s[...]
+        dk_o[:, lanes] = phi_back(sk[:, lanes].astype(F32), feats, rhs, low).astype(BF)
+    dk = dk_o[...]
+    dv = v_s[...].astype(BF)
+    dv_o[...] = dv
     gk_s[...] += dot_tn(a1[...], dk)
     gv_s[...] += dot_tn(a1[...], dv)
-    da1 = dot_nt(dq[...], w[:, :d]) + dot_nt(dk, w[:, d : 2 * d]) + dot_nt(dv, w[:, 2 * d : 3 * d])
-    z, r = norm_stats(x[...].astype(F32))
-    dz = da1 * vec[0:1]
-    m1 = jnp.sum(dz, -1, keepdims=True) * (1.0 / d)
-    m2 = jnp.sum(dz * z, -1, keepdims=True) * (1.0 / d)
-    gt_o[...] = dx[...] + r * (dz - m1 - z * m2)
-    vec_s[0:1, :] += jnp.sum(da1 * z, 0, keepdims=True)
-    vec_s[1:2, :] += jnp.sum(da1, 0, keepdims=True)
+    sum_s[1:2] += jnp.sum(dk.astype(F32), 0, keepdims=True)
+    sum_s[2:3] += jnp.sum(dv.astype(F32), 0, keepdims=True)
 
     @pl.when(blk == pl.num_programs(0) - 1)
     def _():
-        vt = pad_rows([vec_s[i : i + 1] for i in range(5)] + by_owner(vup[...], rows, wide), 128).T
-        for lo, value in ((0, gq[...].astype(F32)), (d, gk_s[...]), (2 * d, gv_s[...]), (3 * d, vt)):
+        gain = w[:, 3 * d : 3 * d + 1].astype(F32)
+        shift = w[:, 3 * d + 1 : 3 * d + 2].astype(F32)
+        total = jnp.zeros((d, 1), F32)
+        plain = jnp.zeros((d, 1), F32)
+
+        def put(lo, value):
             cols = slice(lo, lo + value.shape[1])
             if paired:
-                kept, sent = both_cores(value.reshape(outs[1].shape[0], 2, rows, value.shape[1]))
-                outs[1][:, :, cols] = kept.astype(BF)
-                outs[2][:, :, cols] = sent.astype(BF)
+                kept, sent = both_cores(value.reshape(outs[0].shape[0], 2, rows, value.shape[1]))
+                outs[0][:, :, cols] = kept.astype(BF)
+                outs[1][:, :, cols] = sent.astype(BF)
             else:
-                outs[1][:, cols] = value.astype(BF)
-
-
-def run_key_back(bounds, x, a1, pk, vr, sk, dq, dx, vec, gvec, vup, bank, w, gq, sums, rows, wide, paired, cells):
-    n, d = x.shape
+                outs[0][:, cols] = value.astype(BF)
+
+        for i, grad in enumerate((gq, gk_s, gv_s)):
+            weight = w[:, i * d : (i + 1) * d].astype(F32)
+            line = sum_s[i : i + 1]
+            total += jnp.sum(weight * grad[...], -1, keepdims=True)
+            plain += jnp.sum(weight * line, -1, keepdims=True)
+            put(i * d, grad[...])
+        lines = [gvec[i : i + 1] for i in range(5)] + by_owner(vup[...], rows, wide)
+        vt = pad_rows(lines, 128).T
+        lane = lax.broadcasted_iota(jnp.int32, vt.shape, 1)
+        vt = jnp.where(lane == 0, (total - shift * plain) / gain, jnp.where(lane == 1, plain, vt))
+        put(3 * d, vt)
+
+
+def run_key_back(bounds, a1, pk, vr, sk, gvec, vup, bank, w, gq, qsum, sums, rows, wide, paired, cells):
+    n, d = a1.shape
     total = w.shape[1]
     gout = [(d // (2 * rows), rows, total)] * 2 if paired else [(d, total)]
     square = pltpu.VMEM((d, d), F32)
     return pl.pallas_call(
         functools.partial(key_back_kernel, cells, n, len(sums), paired, rows, wide),
         grid=(n // BLK,),
-        in_specs=[
-            SMEM, rows_spec(d), rows_spec(d), rows_spec(HEADS * FEATS), rows_spec(d), rows_spec(d), rows_spec(d), rows_spec(d),
-        ]
-        + whole_specs((vec, gvec, vup, bank, w, gq))
+        in_specs=[SMEM, rows_spec(d), rows_spec(HEADS * FEATS), rows_spec(d), rows_spec(d)]
+        + whole_specs((gvec, vup, bank, w, gq, qsum))
         + whole_specs(sums),
-        out_specs=[rows_spec(d)] + [whole_spec(g) for g in gout],
-        out_shape=[shape(n, d, kind=F32)] + [shape(*g) for g in gout],
+        out_specs=[rows_spec(d), rows_spec(d)] + [whole_spec(g) for g in gout],
+        out_shape=[shape(n, d), shape(n, d)] + [shape(*g) for g in gout],
         scratch_shapes=[
             pltpu.VMEM((cells, HEADS, 128, FEATS), BF),
             pltpu.VMEM((BLK, HEADS * FEATS), F32),
             pltpu.VMEM((BLK, d), F32),
             pltpu.VMEM((2, 128, FEATS), BF),
-            pltpu.VMEM((BLK, d), BF),
-            pltpu.VMEM((BLK, d), BF),
-            pltpu.VMEM((16, d), F32),
             square,
             square,
+            pltpu.VMEM((8, d), F32),
         ],
         compiler_params=params(),
         cost_estimate=cost(6, 14),
         name="key_back",
-    )(bounds, x, a1, pk, vr, sk, dq, dx, vec, gvec, vup, bank, w, gq, *sums)
+    )(bounds, a1, pk, vr, sk, gvec, vup, bank, w, gq, qsum, *sums)
+
+
+def token_back_kernel(x, dq, dk, dv, dx, vec, w, gt_o):
+    d = x.shape[1]
+    da1 = dot_nt(dq[...], w[:, :d]) + dot_nt(dk[...], w[:, d : 2 * d]) + dot_nt(dv[...], w[:, 2 * d : 3 * d])
+    z, r = norm_stats(x[...].astype(F32))
+    dz = da1 * vec[0:1]
+    m1 = jnp.sum(dz, -1, keepdims=True) * (1.0 / d)
+    m2 = jnp.sum(dz * z, -1, keepdims=True) * (1.0 / d)
+    gt_o[...] = dx[...] + r * (dz - m1 - z * m2)
+
+
+def run_token_back(x, dq, dk, dv, dx, vec, w):
+    n, d = x.shape
+    return pl.pallas_call(
+        token_back_kernel,
+        grid=(n // BLK,),
+        in_specs=[rows_spec(d)] * 5 + whole_specs((vec, w)),
+        out_specs=rows_spec(d),
+        out_shape=shape(n, d, kind=F32),
+        compiler_params=params(),
+        cost_estimate=cost(2, 8),
+        name="token_back",
+    )(x, dq, dk, dv, dx, vec, w)
 
 
 AXES = ("dp", "fsdp")
@@ -777,10 +844,11 @@
     body[rows * (1 + wide) :] = w_down[...]
 
 
-def lead_sum_kernel(wide, part, wqkv, *lines):
-    total = part[0].astype(F32)
-    for k in range(1, part.shape[0]):
-        total += part[k].astype(F32)
+def lead_sum_kernel(wide, *refs):
+    parts, wqkv, lines = refs[:-7], refs[-7], refs[-6:]
+    total = parts[0][...].astype(F32)
+    for part in parts[1:]:
+        total += part[...].astype(F32)
     cols = wqkv.shape[1]
     wqkv[...] = total[:, :cols]
     table = total[:, cols:].T
@@ -789,15 +857,15 @@
     lines[5][...] = jnp.concatenate([table[5 + j : 6 + j] for j in range(wide)], 1)[0]
 
 
-def run_lead_sum(part, cols, wide):
-    rows = part.shape[1]
+def run_lead_sum(parts, cols, wide):
+    rows = parts[0].shape[0]
     return pl.pallas_call(
         functools.partial(lead_sum_kernel, wide),
-        in_specs=[VM],
+        in_specs=[VM] * len(parts),
         out_specs=[VM] * 7,
         out_shape=[shape(rows, cols, kind=F32)] + [shape(rows, kind=F32)] * 5 + [shape(rows * wide, kind=F32)],
         name="lead_sum",
-    )(part)
+    )(*parts)
 
 
 def body_sum_kernel(rows, wide, *refs):
@@ -806,9 +874,9 @@
     total = parts[0][...].astype(F32)
     for part in parts[1:]:
         total += part[...].astype(F32)
-    wout[...] = total[:rows]
     for j in range(wide):
-        wup[:, j * d : (j + 1) * d] = total[rows * (1 + j) : rows * (2 + j)]
+        wup[:, j * d : (j + 1) * d] = total[rows * j : rows * (j + 1)]
+    wout[...] = total[rows * wide : rows * (1 + wide)]
     wdown[...] = total[rows * (1 + wide) :]
 
 
@@ -850,11 +918,9 @@
         vecs = jnp.concatenate([ln1_gain, ln1_bias, ln2_gain, ln2_bias, b_down, b_up]).reshape(5 + wide, rows)
         lead = jnp.concatenate([w_qkv, jnp.pad(vecs, ((0, 128 - 5 - wide), (0, 0))).T], 1)
         body = jnp.concatenate([w_out] + [w_up[:, j * d : (j + 1) * d] for j in range(wide)] + [w_down], 0)
-    keep = padding[0].astype(F32)[:, None]
     cut = rows * (1 + wide)
 
     if paired:
-        lead, body, keep = tie(lead, body, keep)
         first = jnp.stack([lead] + [to_z(lead, fsdp, k) for k in (1, 2, 3)])
         lead_own = [first] + [flip(first, "dp", dp, k) for k in (1, 2, 3)]
         pair = jnp.stack([body, to_z(body, fsdp, 1)])
@@ -874,13 +940,13 @@
     def far_sums(out):
         return lax.all_to_all(out, "fsdp", 0, 0, axis_index_groups=chip_groups(fsdp), tiled=True)
 
-    a1, sk, pk, vr, sums, vec, *w = run_keys(bounds, x, keep, bank, lead_pieces, lead_places, cells)
+    a1, sk, pk, vr, sums, vec, *w = run_keys(bounds, x, padding, bank, lead_pieces, lead_places, cells)
     w = w[0].reshape(d, -1) if paired else lead_pieces[0]
     if paired:
         sums, four = tie(sums, four)
         sums = [sums, to_core(sums, fsdp)]
         out = run_spread(bounds, *sums, chips, n, cells)
-        a1_q, four, out = tie(a1, four, out)
+        a1_q, out = tie(a1, out)
         far = far_sums(out)
         up, down = four[:, :cut], four[:, cut:]
         up_x, down_y = flip(up, "dp", dp, 1), flip(down, "dp", dp, 2)
@@ -899,43 +965,50 @@
         sums = [lax.psum(sums, "fsdp")]
         sq, pq, up_line = run_queries(a1, w, bank, vec, rows, wide)
     mixed, gr, dpre, a2, ar, do, dx2, grads, gvec, vup, sums, full = run_middle(
-        bounds, x, dy, keep, pq, vec, up_line, sums, body_pieces, body_places, ff, cells
+        bounds, x, dy, padding, pq, vec, up_line, sums, body_pieces, body_places, ff, cells
     )
-    back = lambda dq, gq, sums: run_key_back(
-        bounds, x, a1, pk, vr, sk, dq, dx2, vec, gvec, vup, bank, w, gq, sums, rows, wide, paired, cells
+    back = lambda gq, qsum, sums: run_key_back(
+        bounds, a1, pk, vr, sk, gvec, vup, bank, w, gq, qsum, sums, rows, wide, paired, cells
     )
     if paired:
-        kept, sent = run_weights(a2, dpre, gr, dy, ar, do, rows)
-        got, kept, sent = tie(to_core(sums, fsdp), kept, sent)
+        top, top_sent, low, low_sent = run_weights(a2, dpre, gr, dy, ar, do, rows)
+        got, top_sent, low_sent = tie(to_core(sums, fsdp), top_sent, low_sent)
         sums = [sums, got]
         out = run_spread(bounds, *sums, chips, n, cells)
-        grads, out = tie(grads, out)
         far = far_sums(out)
-        dq, gq = run_query_back(bounds, grads, pq, sq, full, bank, a1, cells)
         plus = lambda *parts: functools.reduce(lambda a, b: a + b, [v.astype(F32) for v in parts]).astype(BF)
-        half = plus(kept, to_core(sent, fsdp)).reshape((2, 2, chips) + kept.shape[1:])
         ypos, xpos = lax.axis_index("dp") // 2, lax.axis_index("dp") % 2
         pick = lambda value, at, dim: lax.dynamic_index_in_dim(value, at, dim, keepdims=False)
-        up, down = half[:, :, :, :cut], half[:, :, :, cut:]
-        far, dq, gq, up, down = tie(far, dq, gq, up, down)
-        up_got = flip(pick(up, 1 - xpos, 1), "dp", dp, 1)
-        down_got = flip(pick(down, 1 - ypos, 0), "dp", dp, 2)
-        gt, kept, sent = back(dq, gq, sums + [far, to_core(far, fsdp)])
-        kept, sent, up_got, down_got = tie(kept, sent, up_got, down_got)
-        up = plus(pick(up, xpos, 1), up_got)
-        down = plus(pick(down, ypos, 0), down_got)
-        up = plus(pick(up, ypos, 0), flip(pick(up, 1 - ypos, 0), "dp", dp, 2))
-        down = plus(pick(down, xpos, 0), flip(pick(down, 1 - xpos, 0), "dp", dp, 1))
-        whole = jnp.concatenate([up, down], 1)
+        by_chip = lambda v: v.reshape((2, 2, chips) + v.shape[1:])
+        tops = [by_chip(v) for v in (top, to_core(top_sent, fsdp))]
+        lows = [by_chip(v) for v in (low, to_core(low_sent, fsdp))]
+        top_sent = plus(*[pick(v, 1 - xpos, 1) for v in tops])
+        low_sent = plus(*[pick(v, 1 - ypos, 0) for v in lows])
+        grads, top_sent, low_sent = tie(grads, top_sent, low_sent)
+        top_got, low_got = flip(top_sent, "dp", dp, 1), flip(low_sent, "dp", dp, 2)
+        dq, gq, qsum = run_query_back(bounds, grads, pq, sq, full, bank, a1, cells)
+        far, gq, qsum, top_got, low_got = tie(far, gq, qsum, top_got, low_got)
+        far_got = to_core(far, fsdp)
+        tops = [pick(v, xpos, 1) for v in tops] + [top_got]
+        lows = [pick(v, ypos, 0) for v in lows] + [low_got]
+        both = lambda y, x: ([pick(v, y, 0) for v in tops], [pick(v, x, 0) for v in lows])
+        top_sent, low_sent = [plus(*v) for v in both(1 - ypos, 1 - xpos)]
+        top_more, low_more = flip(top_sent, "dp", dp, 2), flip(low_sent, "dp", dp, 1)
+        dk, dv, kept, sent = back(gq, qsum, sums + [far, far_got])
+        kept, sent, top_more, low_more = tie(kept, sent, top_more, low_more)
+        tops, lows = both(ypos, xpos)
+        whole = jnp.concatenate([plus(*tops, top_more), plus(*lows, low_more)], 1)
         zpos = lax.axis_index("fsdp") // 2
         parts = [pick(whole, zpos, 0)] + [to_z(pick(whole, zpos ^ k, 0), fsdp, k) for k in (1, 2, 3)]
-        half = plus(kept, to_core(sent, fsdp))
-        part = lax.all_to_all(half, AXES, 0, 0, axis_index_groups=same_core_groups(dp, fsdp), tiled=True)
-        wqkv, *vecs = run_lead_sum(part, 3 * d, wide)
+        half = plus(kept, to_core(sent, fsdp)).reshape((dp, chips) + kept.shape[1:])
+        dpos = lax.axis_index("dp")
+        half = plus(pick(half, dpos, 0), *[flip(pick(half, dpos ^ k, 0), "dp", dp, k) for k in (1, 2, 3)])
+        lead_parts = [pick(half, zpos, 0)] + [to_z(pick(half, zpos ^ k, 0), fsdp, k) for k in (1, 2, 3)]
+        wqkv, *vecs = run_lead_sum(lead_parts, 3 * d, wide)
         wout, wup, wdown = run_body_sum(parts, rows, wide)
     else:
-        dq, gq = run_query_back(bounds, grads, pq, sq, full, bank, a1, cells)
-        gt, glead = back(dq, gq, [lax.psum(sums, "fsdp")])
+        dq, gq, qsum = run_query_back(bounds, grads, pq, sq, full, bank, a1, cells)
+        dk, dv, glead = back(gq, qsum, [lax.psum(sums, "fsdp")])
         gup = dot_tn(a2, dpre)
         blocks = lambda g, size: g.reshape(ndev, size, d)
         gbody = jnp.concatenate(
@@ -949,6 +1022,7 @@
         vecs = [gvec[i] for i in range(5)] + [gvec[5 : 5 + wide].reshape(-1)]
         wqkv, wout, wdown = glead[:, : 3 * d], gbody[:rows], gbody[cut:]
         wup = jnp.concatenate([gbody[(1 + j) * rows : (2 + j) * rows] for j in range(wide)], 1)
+    gt = run_token_back(x, dq, dk, dv, dx2, vec, w)
     return (
         mixed[None], gt[None], vecs[0], vecs[1], wqkv, wout, vecs[2], vecs[3], wup, vecs[5], wdown, vecs[4],
     )

time: 223 us -> 204 us (0.915)
  waiting for transfers between devices: 57.7 us -> 32.9 us
  starting transfers between devices: 39 us -> 49.1 us
  Pallas kernels: 104 us -> 99.4 us
  local copies, waits for them, and re-layouts: 8.91 us -> 5.58 us
    ppermute x34 -> x41, waiting for transfers between devices: 55 us -> 31.8 us  [flip(): return lax.ppermute(x, axis, [(i, i ^ mask) for i in range(size)])]
    ppermute x34 -> x41, starting transfers between devices: 27.5 us -> 37.7 us  [flip(): return lax.ppermute(x, axis, [(i, i ^ mask) for i in range(size)])]
    pallas_call x2 -> x3, Pallas kernels: 13.2 us -> 18.6 us  [the longest x1 10.1 us: run_weights(): pl.pallas_call(functools.partial(weight_kernel, rows), grid=(wide + 1,),...]
    all_to_all x1 -> x0, starting transfers between devices: 4.22 us -> none  [local(): lax.all_to_all(half, AXES, 0, 0, axis_index_groups=same_core_groups(dp, f...]
    pallas_call x1, Pallas kernels: 18.4 us -> 14.3 us  [run_key_back(): pl.pallas_call(functools.partial(key_back_kernel, cells, n, len(sums), pa...]
    all_to_all x2, starting transfers between devices: 7.35 us -> 11.5 us  [far_sums(): lax.all_to_all(out, 'fsdp', 0, 0, axis_index_groups=chip_groups(fsdp), ti...]
    pallas_call x1, Pallas kernels: 32.6 us -> 28.6 us  [run_middle(): pl.pallas_call(functools.partial(middle_kernel, cells, n, len(sums), plac...]
    convert_element_type x6 -> x8, other arithmetic: 8.31 us -> 10.3 us  [local(): functools.reduce(lambda a, b: a + b, [v.astype(F32) for v in parts])]
  transfers between devices with their start and end apart: 37 -> 43, of which waited for: 19 -> 20; matrix products, arithmetic and copies ran while one was open for 5% -> 7% of each run, Pallas kernels for 29% -> 33%
where the time goes in v3:
time: 204 us; the launch traced here: 202 us
  Pallas kernels  99.4 us (49%)
  starting transfers between devices  49.1 us (24%)
  waiting for transfers between devices  32.9 us (16%)
  other arithmetic  13.9 us (7%)
  local copies, waits for them, and re-layouts  5.58 us (3%)
    ppermute x41, starting transfers between devices, flip(): return lax.ppermute(x, axis, [(i, i ^ mask) for i in range(size)])  37.7 us
    ppermute x41, waiting for transfers between devices, flip(): return lax.ppermute(x, axis, [(i, i ^ mask) for i in range(size)])  31.8 us
    pallas_call x1, Pallas kernels, run_middle(): pl.pallas_call(functools.partial(middle_kernel, cells, n, len(sums), plac...  28.6 us
    pallas_call x1, Pallas kernels, run_key_back(): pl.pallas_call(functools.partial(key_back_kernel, cells, n, len(sums), pa...  14.3 us
    pallas_call x1, Pallas kernels, run_keys(): pl.pallas_call(functools.partial(key_kernel, cells, places), grid=(n // B...  12.1 us
    all_to_all x2, starting transfers between devices, far_sums(): lax.all_to_all(out, 'fsdp', 0, 0, axis_index_groups=chip_groups(fsdp), ti...  11.5 us
    convert_element_type x8, other arithmetic, local(): functools.reduce(lambda a, b: a + b, [v.astype(F32) for v in parts])  10.3 us
    pallas_call x1, Pallas kernels, run_weights(): pl.pallas_call(functools.partial(weight_kernel, rows), grid=(wide + 1,),...  10.1 us
  transfers between devices with their start and end apart: 43, of which 20 were waited for; matrix products, arithmetic and copies ran while one was open for 7% of the time, Pallas kernels for 33%

profile of v3, /device:TPU:0, one launch (start us, length us, event | category | flops | bytes accessed | tf_op | source)
XLA Modules:
  0.0 202.0 jit_solution(16395852583393272414)
XLA Ops:
  0.6 2.1 %pack.1 = (bf16[16,1664]{1,0:T(8,128)(2,1)}, bf16[144,512]{1,0:T(8,128)(2,1)}) custom-call(bf16[16,1536]{1,0:T(8,128)(2,1)} %w_qkv.1, bf16[16]{0:T(256)(128)(2,1)} %g1.1, bf16[16]{0:T(256)(128)(2,1)} %s1_.1, bf16[16,512]{1,0:T(8,128)(2,1)} %w_out.1, bf16[16]{0:T(256)(128)(2,1)} %g2.1, bf16[16]{0:T(256)(128)(2,1)} %s2_.1, bf16[16,2048]{1,0:T(8,128)(2,1)} %w_up.1, ...), custom_call_target="tpu_custom_call" | custom-call | tf_op jit(solution)/shard_map/pack/pallas_call | solution.py:910
  2.7 3.0 %collective-permute-start.1 = (bf16[16,1664]{1,0:T(8,128)(2,1)}, bf16[16,1664]{1,0:T(8,128)(2,1)S(1)}, u32[]{:S(2)}, u32[]{:S(2)}) collective-permute-start(bf16[16,1664]{1,0:T(8,128)(2,1)} %get-tuple-element.86), channel_id=1, source_target_pairs={{0,2},{1,3},{2,0},{3,1},{4,6},{5,7},{6,4},{7,5},{8,10},{9,11},{10,... | collective-permute-start | bytes 159752 | tf_op jit(solution)/shard_map/ppermute | solution.py:804
  5.7 2.6 %collective-permute-start.2 = (bf16[16,1664]{1,0:T(8,128)(2,1)}, bf16[16,1664]{1,0:T(8,128)(2,1)S(1)}, u32[]{:S(2)}, u32[]{:S(2)}) collective-permute-start(bf16[16,1664]{1,0:T(8,128)(2,1)} %get-tuple-element.86), channel_id=1, source_target_pairs={{0,4},{1,5},{2,6},{3,7},{4,0},{5,1},{6,2},{7,3},{8,12},{9,13},{10,... | collective-permute-start | bytes 159752 | tf_op jit(solution)/shard_map/ppermute | solution.py:804
  9.2 2.9 %collective-permute-done.2 = bf16[16,1664]{1,0:T(8,128)(2,1)S(1)} collective-permute-done((bf16[16,1664]{1,0:T(8,128)(2,1)}, bf16[16,1664]{1,0:T(8,128)(2,1)S(1)}, u32[]{:S(2)}, u32[]{:S(2)}) %collective-permute-start.2) | collective-permute-done | bytes 53280 | tf_op jit(solution)/shard_map/ppermute | solution.py:804
  12.1 2.9 %collective-permute-done.3 = bf16[16,1664]{1,0:T(8,128)(2,1)S(1)} collective-permute-done((bf16[16,1664]{1,0:T(8,128)(2,1)}, bf16[16,1664]{1,0:T(8,128)(2,1)S(1)}, u32[]{:S(2)}, u32[]{:S(2)}) %collective-permute-start.3) | collective-permute-done | bytes 53280 | tf_op jit(solution)/shard_map/ppermute | solution.py:804
  20.4 2.8 %collective-permute-done.4.refs_1_ = bf16[4,16,1664]{2,1,0:T(8,128)(2,1)S(1)} collective-permute-done((bf16[4,16,1664]{2,1,0:T(8,128)(2,1)S(1)}, bf16[4,16,1664]{2,1,0:T(8,128)(2,1)S(1)}, u32[]{:S(2)}, u32[]{:S(2)}) %collective-permute-start.4) | collective-permute-done | bytes 213024 | tf_op jit(solution)/shard_map/ppermute | solution.py:804
  23.2 3.5 %collective-permute-done.5.refs_2_ = bf16[4,16,1664]{2,1,0:T(8,128)(2,1)S(1)} collective-permute-done((bf16[4,16,1664]{2,1,0:T(8,128)(2,1)S(1)}, bf16[4,16,1664]{2,1,0:T(8,128)(2,1)S(1)}, u32[]{:S(2)}, u32[]{:S(2)}) %collective-permute-start.5) | collective-permute-done | bytes 213024 | tf_op jit(solution)/shard_map/ppermute | solution.py:804
  29.9 12.1 %keys.1 = (bf16[1024,512]{1,0:T(8,128)(2,1)}, bf16[1024,512]{1,0:T(8,128)(2,1)}, bf16[1024,2048]{1,0:T(8,128)(2,1)}, bf16[1024,512]{1,0:T(8,128)(2,1)}, bf16[2,4...) custom-call(s32[1,5]{1,0:T(1,128)} %bounds.11, bf16[1024,512]{1,0:T(8,128)(2,1)} %bitcast.68, ...), custom_call_target="tpu_custom_call" | custom-call | flops 8000 | bytes 10000 | tf_op jit(solution)/shard_map/keys/pallas_call | solution.py:301
  43.5 1.6 collective-permute-start.14
  45.2 3.0 %spread.2 = bf16[4,272,256]{2,1,0:T(8,128)(2,1)} custom-call(s32[1,5]{1,0:T(1,128)S(1)} %copy-done.4, bf16[2,4,272,256]{3,2,1,0:T(8,128)(2,1)S(1)} %copy-done.2, bf16[2,4,272,256]{3,2,1,0:T(8,128)(2,1)S(1)} %collective-permute-done.16.got.refs_1_), custom_call_target="tpu_custom_call" | custom-call | flops 1 | bytes 2000 | tf_op jit(solution)/shard_map/spread/pallas_call | solution.py:393
  48.2 4.1 %all-to-all-start = ((bf16[4,272,256]{2,1,0:T(8,128)(2,1)}), bf16[4,272,256]{2,1,0:T(8,128)(2,1)S(1)}, u32[]{:S(2)}, u32[]{:S(2)}) async-start(bf16[4,272,256]{2,1,0:T(8,128)(2,1)} %spread.2), calls=%async_computation | async-start | bytes 1114112 | tf_op jit(solution)/shard_map/all_to_all | solution.py:941
  52.5 2.2 %collective-permute-start.13 = (bf16[8,80,512]{2,1,0:T(8,128)(2,1)S(1)}, bf16[8,80,512]{2,1,0:T(8,128)(2,1)S(1)}, u32[]{:S(2)}, u32[]{:S(2)}) collective-permute-start(bf16[8,80,512]{2,1,0:T(8,128)(2,1)S(1)} %pad_maximum_fusion), channel_id=1, source_target_pairs={{0,16},{8,24},{16,0},{24,8},{1,17},{9,25},{17,1},{25,9},{2,18},{10... | collective-permute-start | bytes 1966088 | tf_op jit(solution)/shard_map/ppermute | solution.py:804
  56.3 6.7 %queries.1 = (bf16[1024,512]{1,0:T(8,128)(2,1)}, bf16[1024,2048]{1,0:T(8,128)(2,1)}, f32[8,512]{1,0:T(8,128)}) custom-call(bf16[1024,512]{1,0:T(8,128)(2,1)} %get-tuple-element.96.a1, bf16[512,1664]{1,0:T(8,128)(2,1)} %bitcast.65, f32[64,256]{1,0:T(8,128)} %bank.7, f32[16,512]{1,0:T(8,128)} %get-tuple-element.98.vec), custom_call_target="tpu_custom_call" | custom-call | flops 5000 | bytes 7000 | tf_op jit(solution)/shard_map/queries/pallas_call | solution.py:362
  63.0 6.0 %collective-permute-done.15.refs_8_ = bf16[8,64,512]{2,1,0:T(8,128)(2,1)S(1)} collective-permute-done((bf16[8,64,512]{2,1,0:T(8,128)(2,1)S(1)}, bf16[8,64,512]{2,1,0:T(8,128)(2,1)S(1)}, u32[]{:S(2)}, u32[]{:S(2)}) %collective-permute-start.15) | collective-permute-done | bytes 524320 | tf_op jit(solution)/shard_map/ppermute | solution.py:804
  70.4 2.1 %collective-permute-done.20.refs_11_ = bf16[4,64,512]{2,1,0:T(8,128)(2,1)} collective-permute-done((bf16[4,64,512]{2,1,0:T(8,128)(2,1)}, bf16[4,64,512]{2,1,0:T(8,128)(2,1)}, u32[]{:S(2)}, u32[]{:S(2)}) %collective-permute-start.20) | collective-permute-done | bytes 262176 | tf_op jit(solution)/shard_map/ppermute | solution.py:804
  76.0 28.6 %middle.1 = (bf16[1024,512]{1,0:T(8,128)(2,1)}, bf16[1024,2048]{1,0:T(8,128)(2,1)}, bf16[1024,2048]{1,0:T(8,128)(2,1)}, bf16[1024,512]{1,0:T(8,128)(2,1)}, bf16[...) custom-call(s32[1,5]{1,0:T(1,128)} %bounds.11, ...), custom_call_target="tpu_custom_call" | custom-call | flops 14000 | bytes 30000 | tf_op jit(solution)/shard_map/middle/pallas_call | solution.py:535
  104.8 10.1 %weights.1 = (bf16[16,80,512]{2,1,0:T(8,128)(2,1)}, bf16[16,80,512]{2,1,0:T(8,128)(2,1)}, bf16[16,64,512]{2,1,0:T(8,128)(2,1)}, bf16[16,64,512]{2,1,0:T(8,128)(2,1)}) custom-call(bf16[1024,512]{1,0:T(8,128)(2,1)} %get-tuple-element.108.a2, bf16[1024,2048]{1,0:T(8,128)(2,1)} %get-tuple-element.109.dpre, bf16[1024,2048]{1,0:T(8,128)(2,1)} %get-tuple-element.110.gr, ...), custom_call_target="tpu_custom_call" | custom-call | flops 5000 | bytes 20000 | tf_op jit(solution)/shard_map/weights/pallas_call | solution.py:654
  115.6 3.1 %spread.3 = bf16[4,272,256]{2,1,0:T(8,128)(2,1)} custom-call(s32[1,5]{1,0:T(1,128)S(1)} %copy-done.5, bf16[2,4,272,256]{3,2,1,0:T(8,128)(2,1)S(1)} %copy-done, bf16[2,4,272,256]{3,2,1,0:T(8,128)(2,1)S(1)} %collective-permute-done.23.got.refs_1_), custom_call_target="tpu_custom_call" | custom-call | flops 1 | bytes 2000 | tf_op jit(solution)/shard_map/spread/pallas_call | solution.py:393
  118.6 7.4 %all-to-all-start.1 = ((bf16[4,272,256]{2,1,0:T(8,128)(2,1)}), bf16[4,272,256]{2,1,0:T(8,128)(2,1)S(1)}, u32[]{:S(2)}, u32[]{:S(2)}) async-start(bf16[4,272,256]{2,1,0:T(8,128)(2,1)} %spread.3), calls=%async_computation.1 | async-start | bytes 1114112 | tf_op jit(solution)/shard_map/all_to_all | solution.py:941
  126.0 2.0 fusion.4
  128.0 2.1 %fusion = bf16[2,4,80,512]{3,2,1,0:T(8,128)(2,1)} fusion(bf16[2,2,4,80,512]{4,3,2,1,0:T(8,128)(2,1)} %bitcast.11, s32[]{:T(128)S(6)} %select_n.86, bf16[2,2,4,80,512]{4,3,2,1,0:T(8,128)(2,1)S(1)} %bitcast.76), kind=kLoop, calls=%fused_computation.11 | loop fusion | flops 1310720 | bytes 1966084 | tf_op jit(solution)/shard_map/convert_element_type | solution.py:979
  131.2 9.1 %query_back.1 = (bf16[1024,512]{1,0:T(8,128)(2,1)}, f32[512,512]{1,0:T(8,128)}, f32[8,512]{1,0:T(8,128)}) custom-call(s32[1,5]{1,0:T(1,128)} %bounds.11, bf16[1024,1024]{1,0:T(8,128)(2,1)} %get-tuple-element.120.grads, bf16[1024,2048]{1,0:T(8,128)(2,1)} %get-tuple-element.101.pq, bf16[1024,512]{1,0:T(8,128)(2,1)} %get-tuple-element.121.sq, ...), custom_call_target="tpu_custom_call" | custom-call | flops 3000 | bytes 8000 | tf_op jit(solution)/shard_map/query_back/pallas_call | solution.py:600
  141.5 3.3 %collective-permute-done.27 = bf16[2,4,64,512]{3,2,1,0:T(8,128)(2,1)S(1)} collective-permute-done((bf16[2,4,64,512]{3,2,1,0:T(8,128)(2,1)}, bf16[2,4,64,512]{3,2,1,0:T(8,128)(2,1)S(1)}, u32[]{:S(2)}, u32[]{:S(2)}) %collective-permute-start.27) | collective-permute-done | bytes 524320 | tf_op jit(solution)/shard_map/ppermute | solution.py:804
  144.8 2.1 %collective-permute-done.26 = bf16[2,4,80,512]{3,2,1,0:T(8,128)(2,1)} collective-permute-done((bf16[2,4,80,512]{3,2,1,0:T(8,128)(2,1)}, bf16[2,4,80,512]{3,2,1,0:T(8,128)(2,1)}, u32[]{:S(2)}, u32[]{:S(2)}) %collective-permute-start.26) | collective-permute-done | bytes 655392 | tf_op jit(solution)/shard_map/ppermute | solution.py:804
  151.3 14.3 %key_back.1 = (bf16[1024,512]{1,0:T(8,128)(2,1)}, bf16[1024,512]{1,0:T(8,128)(2,1)}, bf16[16,16,1664]{2,1,0:T(8,128)(2,1)}, bf16[16,16,1664]{2,1,0:T(8,128)(2,1)}) custom-call(s32[1,5]{1,0:T(1,128)} %bounds.11, bf16[1024,512]{1,0:T(8,128)(2,1)} %get-tuple-element.96.a1, bf16[1024,2048]{1,0:T(8,128)(2,1)} %get-tuple-element.124.pk, ...), custom_call_target="tpu_custom_call" | custom-call | flops 6000 | bytes 14000 | tf_op jit(solution)/shard_map/key_back/pallas_call | solution.py:751
  171.7 3.1 %collective-permute-start.33 = (bf16[4,16,1664]{2,1,0:T(8,128)(2,1)S(1)}, bf16[4,16,1664]{2,1,0:T(8,128)(2,1)S(1)}, u32[]{:S(2)}, u32[]{:S(2)}) collective-permute-start(bf16[4,16,1664]{2,1,0:T(8,128)(2,1)S(1)} %get-tuple-element.160), channel_id=1, source_target_pairs={{0,16},{8,24},{16,0},{24,8},{1,17},{9,25},{17,1},{25,9},{2,18},{10... | collective-permute-start | bytes 638984 | tf_op jit(solution)/shard_map/ppermute | solution.py:804
  177.5 4.3 %collective-permute-start.39 = (bf16[144,512]{1,0:T(8,128)(2,1)S(1)}, bf16[144,512]{1,0:T(8,128)(2,1)S(1)}, u32[]{:S(2)}, u32[]{:S(2)}) collective-permute-start(bf16[144,512]{1,0:T(8,128)(2,1)S(1)} %get-tuple-element.164), channel_id=1, source_target_pairs={{0,4},{1,5},{2,6},{3,7},{4,0},{5,1},{6,2},{7,3},{8,12},{9,13},{10,... | collective-permute-start | bytes 442376 | tf_op jit(solution)/shard_map/ppermute | solution.py:804
  181.9 2.2 %collective-permute-start.40 = (bf16[144,512]{1,0:T(8,128)(2,1)S(1)}, bf16[144,512]{1,0:T(8,128)(2,1)S(1)}, u32[]{:S(2)}, u32[]{:S(2)}) collective-permute-start(bf16[144,512]{1,0:T(8,128)(2,1)S(1)} %get-tuple-element.161), channel_id=1, source_target_pairs={{0,6},{1,7},{2,4},{3,5},{4,2},{5,3},{6,0},{7,1},{8,14},{9,15},{10,... | collective-permute-start | bytes 442376 | tf_op jit(solution)/shard_map/ppermute | solution.py:804
  186.3 3.8 %collective-permute-start.36 = (bf16[16,1664]{1,0:T(8,128)(2,1)S(1)}, bf16[16,1664]{1,0:T(8,128)(2,1)S(1)}, u32[]{:S(2)}, u32[]{:S(2)}) collective-permute-start(bf16[16,1664]{1,0:T(8,128)(2,1)S(1)} %get-tuple-element.166), channel_id=1, source_target_pairs={{0,4},{1,5},{2,6},{3,7},{4,0},{5,1},{6,2},{7,3},{8,12},{9,13},{10,... | collective-permute-start | bytes 159752 | tf_op jit(solution)/shard_map/ppermute | solution.py:804
  190.4 6.8 %token_back.1 = f32[1024,512]{1,0:T(8,128)} custom-call(bf16[1024,512]{1,0:T(8,128)(2,1)} %bitcast.70, bf16[1024,512]{1,0:T(8,128)(2,1)} %get-tuple-element.123.dq, bf16[1024,512]{1,0:T(8,128)(2,1)} %get-tuple-element.137.dk, bf16[1024,512]{1,0:T(8,128)(2,1)} %get-tuple-element.138.dv, f32[1024,512]{1,0:T(8,128)} %get-tuple-element.139.dx, ...), custom_call_target="tpu_custom_call" | custom-call | flops 2000 | bytes 8000 | tf_op jit(solution)/shard_map/token_back/pallas_call | solution.py:786
  197.9 1.9 body_sum.1
  200.4 1.6 lead_sum.1
  (164 shorter events, 37.5 us)
Async XLA Ops:
  2.7 6.5 %collective-permute-start.1 = (bf16[16,1664]{1,0:T(8,128)(2,1)}, bf16[16,1664]{1,0:T(8,128)(2,1)S(1)}, u32[]{:S(2)}, u32[]{:S(2)}) collective-permute-start(bf16[16,1664]{1,0:T(8,128)(2,1)} %get-tuple-element.86), channel_id=1, source_target_pairs={{0,2},{1,3},{2,0},{3,1},{4,6},{5,7},{6,4},{7,5},{8,10},{9,11},{10,... | collective-permute-start | bytes 159752 | tf_op jit(solution)/shard_map/ppermute | solution.py:804
  5.7 6.4 %collective-permute-start.2 = (bf16[16,1664]{1,0:T(8,128)(2,1)}, bf16[16,1664]{1,0:T(8,128)(2,1)S(1)}, u32[]{:S(2)}, u32[]{:S(2)}) collective-permute-start(bf16[16,1664]{1,0:T(8,128)(2,1)} %get-tuple-element.86), channel_id=1, source_target_pairs={{0,4},{1,5},{2,6},{3,7},{4,0},{5,1},{6,2},{7,3},{8,12},{9,13},{10,... | collective-permute-start | bytes 159752 | tf_op jit(solution)/shard_map/ppermute | solution.py:804
  8.3 6.7 %collective-permute-start.3 = (bf16[16,1664]{1,0:T(8,128)(2,1)}, bf16[16,1664]{1,0:T(8,128)(2,1)S(1)}, u32[]{:S(2)}, u32[]{:S(2)}) collective-permute-start(bf16[16,1664]{1,0:T(8,128)(2,1)} %get-tuple-element.86), channel_id=1, source_target_pairs={{0,6},{1,7},{2,4},{3,5},{4,2},{5,3},{6,0},{7,1},{8,14},{9,15},{10,... | collective-permute-start | bytes 159752 | tf_op jit(solution)/shard_map/ppermute | solution.py:804
  8.3 11.1 %collective-permute-start = (bf16[144,512]{1,0:T(8,128)(2,1)}, bf16[144,512]{1,0:T(8,128)(2,1)S(1)}, u32[]{:S(2)}, u32[]{:S(2)}) collective-permute-start(bf16[144,512]{1,0:T(8,128)(2,1)} %get-tuple-element.85), channel_id=1, source_target_pairs={{0,2},{1,3},{2,0},{3,1},{4,6},{5,7},{6,4},{7,5},{8,10},{9,11},{10,... | collective-permute-start | bytes 442376 | tf_op jit(solution)/shard_map/ppermute | solution.py:804
  15.9 7.3 %collective-permute-start.4 = (bf16[4,16,1664]{2,1,0:T(8,128)(2,1)S(1)}, bf16[4,16,1664]{2,1,0:T(8,128)(2,1)S(1)}, u32[]{:S(2)}, u32[]{:S(2)}) collective-permute-start(bf16[4,16,1664]{2,1,0:T(8,128)(2,1)S(1)} %pad_maximum_fusion.4.refs_0_), channel_id=1, source_target_pairs={{0,8},{8,0},{16,24},{24,16},{1,9},{9,1},{17,25},{25,17},{2,10},{10... | collective-permute-start | bytes 638984 | tf_op jit(solution)/shard_map/ppermute | solution.py:804
  17.4 9.3 %collective-permute-start.5 = (bf16[4,16,1664]{2,1,0:T(8,128)(2,1)S(1)}, bf16[4,16,1664]{2,1,0:T(8,128)(2,1)S(1)}, u32[]{:S(2)}, u32[]{:S(2)}) collective-permute-start(bf16[4,16,1664]{2,1,0:T(8,128)(2,1)S(1)} %pad_maximum_fusion.4.refs_0_), channel_id=1, source_target_pairs={{0,16},{8,24},{16,0},{24,8},{1,17},{9,25},{17,1},{25,9},{2,18},{10... | collective-permute-start | bytes 638984 | tf_op jit(solution)/shard_map/ppermute | solution.py:804
  19.0 7.8 %collective-permute-start.6 = (bf16[4,16,1664]{2,1,0:T(8,128)(2,1)S(1)}, bf16[4,16,1664]{2,1,0:T(8,128)(2,1)S(1)}, u32[]{:S(2)}, u32[]{:S(2)}) collective-permute-start(bf16[4,16,1664]{2,1,0:T(8,128)(2,1)S(1)} %pad_maximum_fusion.4.refs_0_), channel_id=1, source_target_pairs={{0,24},{8,16},{16,8},{24,0},{1,25},{9,17},{17,9},{25,1},{2,26},{10... | collective-permute-start | bytes 638984 | tf_op jit(solution)/shard_map/ppermute | solution.py:804
  26.7 15.3 %collective-permute-start.11 = (bf16[2,144,512]{2,1,0:T(8,128)(2,1)S(1)}, bf16[2,144,512]{2,1,0:T(8,128)(2,1)S(1)}, u32[]{:S(2)}, u32[]{:S(2)}) collective-permute-start(bf16[2,144,512]{2,1,0:T(8,128)(2,1)S(1)} %pad_maximum_fusion.3), channel_id=1, source_target_pairs={{0,4},{1,5},{2,6},{3,7},{4,0},{5,1},{6,2},{7,3},{8,12},{9,13},{10,... | collective-permute-start | bytes 884744 | tf_op jit(solution)/shard_map/ppermute | solution.py:804
  42.4 10.0 %collective-permute-start.12 = (bf16[4,80,512]{2,1,0:T(8,128)(2,1)S(1)}, bf16[4,80,512]{2,1,0:T(8,128)(2,1)S(1)}, u32[]{:S(2)}, u32[]{:S(2)}) collective-permute-start(bf16[4,80,512]{2,1,0:T(8,128)(2,1)S(1)} %slice.6), channel_id=1, source_target_pairs={{0,8},{8,0},{16,24},{24,16},{1,9},{9,1},{17,25},{25,17},{2,10},{10... | collective-permute-start | bytes 983048 | tf_op jit(solution)/shard_map/ppermute | solution.py:804
  43.5 11.2 %collective-permute-start.14 = (bf16[4,64,512]{2,1,0:T(8,128)(2,1)S(1)}, bf16[4,64,512]{2,1,0:T(8,128)(2,1)}, u32[]{:S(2)}, u32[]{:S(2)}) collective-permute-start(bf16[4,64,512]{2,1,0:T(8,128)(2,1)S(1)} %slice.7), channel_id=1, source_target_pairs={{0,16},{8,24},{16,0},{24,8},{1,17},{9,25},{17,1},{25,9},{2,18},{10... | collective-permute-start | bytes 786440 | tf_op jit(solution)/shard_map/ppermute | solution.py:804
  48.2 21.7 %all-to-all-start = ((bf16[4,272,256]{2,1,0:T(8,128)(2,1)}), bf16[4,272,256]{2,1,0:T(8,128)(2,1)S(1)}, u32[]{:S(2)}, u32[]{:S(2)}) async-start(bf16[4,272,256]{2,1,0:T(8,128)(2,1)} %spread.2), calls=%async_computation | async-start | bytes 1114112 | tf_op jit(solution)/shard_map/all_to_all | solution.py:941
  52.5 16.8 %collective-permute-start.13 = (bf16[8,80,512]{2,1,0:T(8,128)(2,1)S(1)}, bf16[8,80,512]{2,1,0:T(8,128)(2,1)S(1)}, u32[]{:S(2)}, u32[]{:S(2)}) collective-permute-start(bf16[8,80,512]{2,1,0:T(8,128)(2,1)S(1)} %pad_maximum_fusion), channel_id=1, source_target_pairs={{0,16},{8,24},{16,0},{24,8},{1,17},{9,25},{17,1},{25,9},{2,18},{10... | collective-permute-start | bytes 1966088 | tf_op jit(solution)/shard_map/ppermute | solution.py:804
  55.7 13.3 %collective-permute-start.15 = (bf16[8,64,512]{2,1,0:T(8,128)(2,1)S(1)}, bf16[8,64,512]{2,1,0:T(8,128)(2,1)S(1)}, u32[]{:S(2)}, u32[]{:S(2)}) collective-permute-start(bf16[8,64,512]{2,1,0:T(8,128)(2,1)S(1)} %pad_maximum_fusion.2), channel_id=1, source_target_pairs={{0,8},{8,0},{16,24},{24,16},{1,9},{9,1},{17,25},{25,17},{2,10},{10... | collective-permute-start | bytes 1572872 | tf_op jit(solution)/shard_map/ppermute | solution.py:804
  69.3 5.3 %collective-permute-start.21 = (bf16[8,80,512]{2,1,0:T(8,128)(2,1)S(1)}, bf16[8,80,512]{2,1,0:T(8,128)(2,1)S(1)}, u32[]{:S(2)}, u32[]{:S(2)}) collective-permute-start(bf16[8,80,512]{2,1,0:T(8,128)(2,1)S(1)} %collective-permute-done.13.refs_7_), channel_id=1, source_target_pairs={{0,1},{1,0},{2,3},{3,2},{4,5},{5,4},{6,7},{7,6},{8,9},{9,8},{10,11... | collective-permute-start | bytes 1966088 | tf_op jit(solution)/shard_map/ppermute | solution.py:804
  69.9 4.8 %collective-permute-start.17 = (bf16[4,272,256]{2,1,0:T(8,128)(2,1)S(1)}, bf16[4,272,256]{2,1,0:T(8,128)(2,1)S(1)}, u32[]{:S(2)}, u32[]{:S(2)}) collective-permute-start(bf16[4,272,256]{2,1,0:T(8,128)(2,1)S(1)} %all-to-all-done.refs_2_), channel_id=1, source_target_pairs={{0,1},{1,0},{2,3},{3,2},{4,5},{5,4},{6,7},{7,6},{8,9},{9,8},{10,11... | collective-permute-start | bytes 1671176 | tf_op jit(solution)/shard_map/ppermute | solution.py:804
  104.6 10.4 %collective-permute-start.23 = (bf16[2,4,272,256]{3,2,1,0:T(8,128)(2,1)}, bf16[2,4,272,256]{3,2,1,0:T(8,128)(2,1)S(1)}, u32[]{:S(2)}, u32[]{:S(2)}) collective-permute-start(bf16[2,4,272,256]{3,2,1,0:T(8,128)(2,1)} %get-tuple-element.114.own.refs_0_), channel_id=1, source_target_pairs={{0,1},{1,0},{2,3},{3,2},{4,5},{5,4},{6,7},{7,6},{8,9},{9,8},{10,11... | collective-permute-start | bytes 3342344 | tf_op jit(solution)/shard_map/ppermute | solution.py:804
  115.0 13.0 %collective-permute-start.24 = (bf16[16,80,512]{2,1,0:T(8,128)(2,1)}, bf16[16,80,512]{2,1,0:T(8,128)(2,1)}, u32[]{:S(2)}, u32[]{:S(2)}) collective-permute-start(bf16[16,80,512]{2,1,0:T(8,128)(2,1)} %get-tuple-element.117), channel_id=1, source_target_pairs={{0,1},{1,0},{2,3},{3,2},{4,5},{5,4},{6,7},{7,6},{8,9},{9,8},{10,11... | collective-permute-start | bytes 3932168 | tf_op jit(solution)/shard_map/ppermute | solution.py:804
  115.4 10.6 %collective-permute-start.25 = (bf16[16,64,512]{2,1,0:T(8,128)(2,1)}, bf16[16,64,512]{2,1,0:T(8,128)(2,1)}, u32[]{:S(2)}, u32[]{:S(2)}) collective-permute-start(bf16[16,64,512]{2,1,0:T(8,128)(2,1)} %get-tuple-element.119), channel_id=1, source_target_pairs={{0,1},{1,0},{2,3},{3,2},{4,5},{5,4},{6,7},{7,6},{8,9},{9,8},{10,11... | collective-permute-start | bytes 3145736 | tf_op jit(solution)/shard_map/ppermute | solution.py:804
  118.6 22.8 %all-to-all-start.1 = ((bf16[4,272,256]{2,1,0:T(8,128)(2,1)}), bf16[4,272,256]{2,1,0:T(8,128)(2,1)S(1)}, u32[]{:S(2)}, u32[]{:S(2)}) async-start(bf16[4,272,256]{2,1,0:T(8,128)(2,1)} %spread.3), calls=%async_computation.1 | async-start | bytes 1114112 | tf_op jit(solution)/shard_map/all_to_all | solution.py:941
  130.1 16.8 %collective-permute-start.26 = (bf16[2,4,80,512]{3,2,1,0:T(8,128)(2,1)}, bf16[2,4,80,512]{3,2,1,0:T(8,128)(2,1)}, u32[]{:S(2)}, u32[]{:S(2)}) collective-permute-start(bf16[2,4,80,512]{3,2,1,0:T(8,128)(2,1)} %fusion), channel_id=1, source_target_pairs={{0,8},{8,0},{16,24},{24,16},{1,9},{9,1},{17,25},{25,17},{2,10},{10... | collective-permute-start | bytes 1966088 | tf_op jit(solution)/shard_map/ppermute | solution.py:804
  131.2 13.6 %collective-permute-start.27 = (bf16[2,4,64,512]{3,2,1,0:T(8,128)(2,1)}, bf16[2,4,64,512]{3,2,1,0:T(8,128)(2,1)S(1)}, u32[]{:S(2)}, u32[]{:S(2)}) collective-permute-start(bf16[2,4,64,512]{3,2,1,0:T(8,128)(2,1)} %fusion.4), channel_id=1, source_target_pairs={{0,16},{8,24},{16,0},{24,8},{1,17},{9,25},{17,1},{25,9},{2,18},{10... | collective-permute-start | bytes 1572872 | tf_op jit(solution)/shard_map/ppermute | solution.py:804
  148.1 17.5 %collective-permute-start.29 = (bf16[4,80,512]{2,1,0:T(8,128)(2,1)S(1)}, bf16[4,80,512]{2,1,0:T(8,128)(2,1)}, u32[]{:S(2)}, u32[]{:S(2)}) collective-permute-start(bf16[4,80,512]{2,1,0:T(8,128)(2,1)S(1)} %fusion.3), channel_id=1, source_target_pairs={{0,16},{8,24},{16,0},{24,8},{1,17},{9,25},{17,1},{25,9},{2,18},{10... | collective-permute-start | bytes 983048 | tf_op jit(solution)/shard_map/ppermute | solution.py:804
  149.6 16.0 %collective-permute-start.30 = (bf16[4,64,512]{2,1,0:T(8,128)(2,1)S(1)}, bf16[4,64,512]{2,1,0:T(8,128)(2,1)S(1)}, u32[]{:S(2)}, u32[]{:S(2)}) collective-permute-start(bf16[4,64,512]{2,1,0:T(8,128)(2,1)S(1)} %fusion.7), channel_id=1, source_target_pairs={{0,8},{8,0},{16,24},{24,16},{1,9},{9,1},{17,25},{25,17},{2,10},{10... | collective-permute-start | bytes 786440 | tf_op jit(solution)/shard_map/ppermute | solution.py:804
  170.4 11.4 %collective-permute-start.32 = (bf16[4,16,1664]{2,1,0:T(8,128)(2,1)S(1)}, bf16[4,16,1664]{2,1,0:T(8,128)(2,1)S(1)}, u32[]{:S(2)}, u32[]{:S(2)}) collective-permute-start(bf16[4,16,1664]{2,1,0:T(8,128)(2,1)S(1)} %get-tuple-element.158), channel_id=1, source_target_pairs={{0,8},{8,0},{16,24},{24,16},{1,9},{9,1},{17,25},{25,17},{2,10},{10... | collective-permute-start | bytes 638984 | tf_op jit(solution)/shard_map/ppermute | solution.py:804
  171.7 12.3 %collective-permute-start.33 = (bf16[4,16,1664]{2,1,0:T(8,128)(2,1)S(1)}, bf16[4,16,1664]{2,1,0:T(8,128)(2,1)S(1)}, u32[]{:S(2)}, u32[]{:S(2)}) collective-permute-start(bf16[4,16,1664]{2,1,0:T(8,128)(2,1)S(1)} %get-tuple-element.160), channel_id=1, source_target_pairs={{0,16},{8,24},{16,0},{24,8},{1,17},{9,25},{17,1},{25,9},{2,18},{10... | collective-permute-start | bytes 638984 | tf_op jit(solution)/shard_map/ppermute | solution.py:804
  174.8 10.4 %collective-permute-start.34 = (bf16[4,16,1664]{2,1,0:T(8,128)(2,1)S(1)}, bf16[4,16,1664]{2,1,0:T(8,128)(2,1)S(1)}, u32[]{:S(2)}, u32[]{:S(2)}) collective-permute-start(bf16[4,16,1664]{2,1,0:T(8,128)(2,1)S(1)} %get-tuple-element.159), channel_id=1, source_target_pairs={{0,24},{8,16},{16,8},{24,0},{1,25},{9,17},{17,9},{25,1},{2,26},{10... | collective-permute-start | bytes 638984 | tf_op jit(solution)/shard_map/ppermute | solution.py:804
  177.2 12.9 %collective-permute-start.38 = (bf16[144,512]{1,0:T(8,128)(2,1)S(1)}, bf16[144,512]{1,0:T(8,128)(2,1)S(1)}, u32[]{:S(2)}, u32[]{:S(2)}) collective-permute-start(bf16[144,512]{1,0:T(8,128)(2,1)S(1)} %get-tuple-element.163), channel_id=1, source_target_pairs={{0,2},{1,3},{2,0},{3,1},{4,6},{5,7},{6,4},{7,5},{8,10},{9,11},{10,... | collective-permute-start | bytes 442376 | tf_op jit(solution)/shard_map/ppermute | solution.py:804
  177.5 19.6 %collective-permute-start.39 = (bf16[144,512]{1,0:T(8,128)(2,1)S(1)}, bf16[144,512]{1,0:T(8,128)(2,1)S(1)}, u32[]{:S(2)}, u32[]{:S(2)}) collective-permute-start(bf16[144,512]{1,0:T(8,128)(2,1)S(1)} %get-tuple-element.164), channel_id=1, source_target_pairs={{0,4},{1,5},{2,6},{3,7},{4,0},{5,1},{6,2},{7,3},{8,12},{9,13},{10,... | collective-permute-start | bytes 442376 | tf_op jit(solution)/shard_map/ppermute | solution.py:804
  181.9 15.3 %collective-permute-start.40 = (bf16[144,512]{1,0:T(8,128)(2,1)S(1)}, bf16[144,512]{1,0:T(8,128)(2,1)S(1)}, u32[]{:S(2)}, u32[]{:S(2)}) collective-permute-start(bf16[144,512]{1,0:T(8,128)(2,1)S(1)} %get-tuple-element.161), channel_id=1, source_target_pairs={{0,6},{1,7},{2,4},{3,5},{4,2},{5,3},{6,0},{7,1},{8,14},{9,15},{10,... | collective-permute-start | bytes 442376 | tf_op jit(solution)/shard_map/ppermute | solution.py:804
  186.0 13.8 %collective-permute-start.35 = (bf16[16,1664]{1,0:T(8,128)(2,1)S(1)}, bf16[16,1664]{1,0:T(8,128)(2,1)S(1)}, u32[]{:S(2)}, u32[]{:S(2)}) collective-permute-start(bf16[16,1664]{1,0:T(8,128)(2,1)S(1)} %get-tuple-element.167), channel_id=1, source_target_pairs={{0,2},{1,3},{2,0},{3,1},{4,6},{5,7},{6,4},{7,5},{8,10},{9,11},{10,... | collective-permute-start | bytes 159752 | tf_op jit(solution)/shard_map/ppermute | solution.py:804
  186.3 13.4 %collective-permute-start.36 = (bf16[16,1664]{1,0:T(8,128)(2,1)S(1)}, bf16[16,1664]{1,0:T(8,128)(2,1)S(1)}, u32[]{:S(2)}, u32[]{:S(2)}) collective-permute-start(bf16[16,1664]{1,0:T(8,128)(2,1)S(1)} %get-tuple-element.166), channel_id=1, source_target_pairs={{0,4},{1,5},{2,6},{3,7},{4,0},{5,1},{6,2},{7,3},{8,12},{9,13},{10,... | collective-permute-start | bytes 159752 | tf_op jit(solution)/shard_map/ppermute | solution.py:804
  190.1 9.7 %collective-permute-start.37 = (bf16[16,1664]{1,0:T(8,128)(2,1)S(1)}, bf16[16,1664]{1,0:T(8,128)(2,1)S(1)}, u32[]{:S(2)}, u32[]{:S(2)}) collective-permute-start(bf16[16,1664]{1,0:T(8,128)(2,1)S(1)} %get-tuple-element.165), channel_id=1, source_target_pairs={{0,6},{1,7},{2,4},{3,5},{4,2},{5,3},{6,0},{7,1},{8,14},{9,15},{10,... | collective-permute-start | bytes 159752 | tf_op jit(solution)/shard_map/ppermute | solution.py:804
  (51 other events, 217.7 us)

commit v4 on v3

--- a/solution.py
+++ b/solution.py
@@ -664,15 +664,53 @@
     )(a2, dpre, gr, dy, ar, do)
 
 
+def fold_kernel(parts, *refs):
+    ins, outs, bufs, sems = refs[:4], refs[4 : 4 + parts], refs[4 + parts : 8 + parts], refs[8 + parts]
+    me = lax.axis_index("dp")
+    size = ins[0].shape[0] // parts
+    made = []
+    for k in range(parts):
+        rows = pl.ds((me ^ k) * size, size)
+        for i in range(4):
+            made.append(pltpu.make_async_copy(ins[i].at[rows], bufs[i].at[k], sems.at[k, i]))
+    for copy in made:
+        copy.start()
+    cut = ins[0].shape[1]
+    for k in range(parts):
+        for copy in made[4 * k : 4 * k + 4]:
+            copy.wait()
+        outs[k][:, :cut] = (bufs[0][k].astype(F32) + bufs[1][k].astype(F32)).astype(BF)
+        outs[k][:, cut:] = (bufs[2][k].astype(F32) + bufs[3][k].astype(F32)).astype(BF)
+
+
+def run_fold(top, top_got, low, low_got, parts):
+    size, d = top.shape[0] // parts, top.shape[2]
+    out = shape(size, top.shape[1] + low.shape[1], d)
+    bufs = [pltpu.VMEM((parts, size) + v.shape[1:], BF) for v in (top, top_got, low, low_got)]
+    return pl.pallas_call(
+        functools.partial(fold_kernel, parts),
+        in_specs=[ANY] * 4,
+        out_specs=[VM] * parts,
+        out_shape=[out] * parts,
+        scratch_shapes=bufs + [pltpu.SemaphoreType.DMA((parts, 4))],
+        compiler_params=pltpu.CompilerParams(vmem_limit_bytes=16 * 1024 * 1024),
+        cost_estimate=cost(0.001, 7),
+        name="fold",
+    )(top, top_got, low, low_got)
+
+
 def key_back_kernel(cells, slots, nsums, paired, rows, wide, bounds, a1, pk, vr, sk, gvec, vup, bank, w, gq, qsum, *refs):
     sums, refs = refs[:nsums], refs[nsums:]
     dk_o, dv_o, outs = refs[0], refs[1], refs[2 : 4 if paired else 3]
-    full, g_s, v_s, rhs, gk_s, gv_s, sum_s = refs[4 if paired else 3 :]
+    full, g_s, v_s, rhs, gk_s, gv_s, sum_s, w_s, gq_s, sems = refs[4 if paired else 3 :]
+    made = [pltpu.make_async_copy(a, b, sems.at[i]) for i, (a, b) in enumerate(((w, w_s), (gq, gq_s)))]
     blk = pl.program_id(0)
     d = a1.shape[1]
 
     @pl.when(blk == 0)
     def _():
+        for copy in made:
+            copy.start()
         gk_s[...] = jnp.zeros_like(gk_s)
         gv_s[...] = jnp.zeros_like(gv_s)
         sum_s[...] = qsum[...]
@@ -716,8 +754,10 @@
 
     @pl.when(blk == pl.num_programs(0) - 1)
     def _():
-        gain = w[:, 3 * d : 3 * d + 1].astype(F32)
-        shift = w[:, 3 * d + 1 : 3 * d + 2].astype(F32)
+        for copy in made:
+            copy.wait()
+        gain = w_s[:, 3 * d : 3 * d + 1].astype(F32)
+        shift = w_s[:, 3 * d + 1 : 3 * d + 2].astype(F32)
         total = jnp.zeros((d, 1), F32)
         plain = jnp.zeros((d, 1), F32)
 
@@ -730,8 +770,8 @@
             else:
                 outs[0][:, cols] = value.astype(BF)
 
-        for i, grad in enumerate((gq, gk_s, gv_s)):
-            weight = w[:, i * d : (i + 1) * d].astype(F32)
+        for i, grad in enumerate((gq_s, gk_s, gv_s)):
+            weight = w_s[:, i * d : (i + 1) * d].astype(F32)
             line = sum_s[i : i + 1]
             total += jnp.sum(weight * grad[...], -1, keepdims=True)
             plain += jnp.sum(weight * line, -1, keepdims=True)
@@ -752,7 +792,7 @@
         functools.partial(key_back_kernel, cells, n, len(sums), paired, rows, wide),
         grid=(n // BLK,),
         in_specs=[SMEM, rows_spec(d), rows_spec(HEADS * FEATS), rows_spec(d), rows_spec(d)]
-        + whole_specs((gvec, vup, bank, w, gq, qsum))
+        + whole_specs((gvec, vup, bank)) + [HBM, HBM] + whole_specs((qsum,))
         + whole_specs(sums),
         out_specs=[rows_spec(d), rows_spec(d)] + [whole_spec(g) for g in gout],
         out_shape=[shape(n, d), shape(n, d)] + [shape(*g) for g in gout],
@@ -764,6 +804,9 @@
             square,
             square,
             pltpu.VMEM((8, d), F32),
+            pltpu.VMEM(w.shape, BF),
+            square,
+            pltpu.SemaphoreType.DMA((2,)),
         ],
         compiler_params=params(),
         cost_estimate=cost(6, 14),
@@ -844,11 +887,17 @@
     body[rows * (1 + wide) :] = w_down[...]
 
 
-def lead_sum_kernel(wide, *refs):
-    parts, wqkv, lines = refs[:-7], refs[-7], refs[-6:]
-    total = parts[0][...].astype(F32)
-    for part in parts[1:]:
-        total += part[...].astype(F32)
+def final_kernel(rows, wide, count, *refs):
+    parts, outs = refs[:count], refs[2 * count :]
+    wout, wup, wdown, wqkv, *lines = outs
+    d = wout.shape[1]
+    add = lambda refs: functools.reduce(lambda a, b: a + b, [v[...].astype(F32) for v in refs])
+    total = add(refs[count : 2 * count])
+    for j in range(wide):
+        wup[:, j * d : (j + 1) * d] = total[rows * j : rows * (j + 1)]
+    wout[...] = total[rows * wide : rows * (1 + wide)]
+    wdown[...] = total[rows * (1 + wide) :]
+    total = add(parts)
     cols = wqkv.shape[1]
     wqkv[...] = total[:, :cols]
     table = total[:, cols:].T
@@ -857,38 +906,20 @@
     lines[5][...] = jnp.concatenate([table[5 + j : 6 + j] for j in range(wide)], 1)[0]
 
 
-def run_lead_sum(parts, cols, wide):
-    rows = parts[0].shape[0]
+def run_final(lead_parts, body_parts, rows, wide):
+    d = body_parts[0].shape[1]
     return pl.pallas_call(
-        functools.partial(lead_sum_kernel, wide),
-        in_specs=[VM] * len(parts),
-        out_specs=[VM] * 7,
-        out_shape=[shape(rows, cols, kind=F32)] + [shape(rows, kind=F32)] * 5 + [shape(rows * wide, kind=F32)],
-        name="lead_sum",
-    )(*parts)
-
-
-def body_sum_kernel(rows, wide, *refs):
-    parts, (wout, wup, wdown) = refs[:-3], refs[-3:]
-    d = wout.shape[1]
-    total = parts[0][...].astype(F32)
-    for part in parts[1:]:
-        total += part[...].astype(F32)
-    for j in range(wide):
-        wup[:, j * d : (j + 1) * d] = total[rows * j : rows * (j + 1)]
-    wout[...] = total[rows * wide : rows * (1 + wide)]
-    wdown[...] = total[rows * (1 + wide) :]
-
-
-def run_body_sum(parts, rows, wide):
-    d = parts[0].shape[1]
-    return pl.pallas_call(
-        functools.partial(body_sum_kernel, rows, wide),
-        in_specs=[VM] * len(parts),
-        out_specs=[VM] * 3,
-        out_shape=[shape(rows, d, kind=F32), shape(rows, wide * d, kind=F32), shape(rows * wide, d, kind=F32)],
-        name="body_sum",
-    )(*parts)
+        functools.partial(final_kernel, rows, wide, len(lead_parts)),
+        in_specs=[VM] * (2 * len(lead_parts)),
+        out_specs=[VM] * 10,
+        out_shape=[
+            shape(rows, d, kind=F32), shape(rows, wide * d, kind=F32), shape(rows * wide, d, kind=F32),
+            shape(rows, 3 * d, kind=F32),
+        ]
+        + [shape(rows, kind=F32)] * 5
+        + [shape(rows * wide, kind=F32)],
+        name="final",
+    )(*lead_parts, *body_parts)
 
 
 def local(dp, fsdp, tokens, bounds, padding, bank, ln1_gain, ln1_bias, w_qkv, w_out, ln2_gain, ln2_bias,
@@ -953,9 +984,9 @@
         up_y = flip(jnp.concatenate([up, up_x]), "dp", dp, 2)
         down_x = flip(jnp.concatenate([down, down_y]), "dp", dp, 1)
         sq, pq, up_line = run_queries(a1_q, w, bank, vec, rows, wide)
-        up_y, down_x, pq, up_line = tie(up_y, down_x, pq, up_line)
-        body_own = [four, up_x, down_y, up_y, down_x]
-        body_pieces = body_own + [to_core(v, fsdp) for v in body_own]
+        early = [to_core(v, fsdp) for v in (four, up_x, down_y)]
+        up_y, down_x, pq, up_line, *early = tie(up_y, down_x, pq, up_line, *early)
+        body_pieces = [four, up_x, down_y, up_y, down_x] + early + [to_core(v, fsdp) for v in (up_y, down_x)]
         body_places = (
             (Z_ALL, 0, cut + frow), ((4, 5, 6, 7), 0, cut), ((8, 9, 10, 11), cut, cut + frow),
             ((8, 9, 10, 11, 12, 13, 14, 15), 0, cut), ((4, 5, 6, 7, 12, 13, 14, 15), cut, cut + frow),
@@ -977,35 +1008,22 @@
         out = run_spread(bounds, *sums, chips, n, cells)
         far = far_sums(out)
         plus = lambda *parts: functools.reduce(lambda a, b: a + b, [v.astype(F32) for v in parts]).astype(BF)
-        ypos, xpos = lax.axis_index("dp") // 2, lax.axis_index("dp") % 2
         pick = lambda value, at, dim: lax.dynamic_index_in_dim(value, at, dim, keepdims=False)
-        by_chip = lambda v: v.reshape((2, 2, chips) + v.shape[1:])
-        tops = [by_chip(v) for v in (top, to_core(top_sent, fsdp))]
-        lows = [by_chip(v) for v in (low, to_core(low_sent, fsdp))]
-        top_sent = plus(*[pick(v, 1 - xpos, 1) for v in tops])
-        low_sent = plus(*[pick(v, 1 - ypos, 0) for v in lows])
-        grads, top_sent, low_sent = tie(grads, top_sent, low_sent)
-        top_got, low_got = flip(top_sent, "dp", dp, 1), flip(low_sent, "dp", dp, 2)
+        folded = run_fold(top, to_core(top_sent, fsdp), low, to_core(low_sent, fsdp), dp)
+        grads, *folded = tie(grads, *folded)
+        spread = [flip(v, "dp", dp, k) for k, v in enumerate(folded) if k]
         dq, gq, qsum = run_query_back(bounds, grads, pq, sq, full, bank, a1, cells)
-        far, gq, qsum, top_got, low_got = tie(far, gq, qsum, top_got, low_got)
-        far_got = to_core(far, fsdp)
-        tops = [pick(v, xpos, 1) for v in tops] + [top_got]
-        lows = [pick(v, ypos, 0) for v in lows] + [low_got]
-        both = lambda y, x: ([pick(v, y, 0) for v in tops], [pick(v, x, 0) for v in lows])
-        top_sent, low_sent = [plus(*v) for v in both(1 - ypos, 1 - xpos)]
-        top_more, low_more = flip(top_sent, "dp", dp, 2), flip(low_sent, "dp", dp, 1)
-        dk, dv, kept, sent = back(gq, qsum, sums + [far, far_got])
-        kept, sent, top_more, low_more = tie(kept, sent, top_more, low_more)
-        tops, lows = both(ypos, xpos)
-        whole = jnp.concatenate([plus(*tops, top_more), plus(*lows, low_more)], 1)
+        far, gq, qsum = tie(far, gq, qsum)
+        dk, dv, kept, sent = back(gq, qsum, sums + [far, to_core(far, fsdp)])
+        kept, sent, *spread = tie(kept, sent, *spread)
+        whole = plus(folded[0], *spread)
         zpos = lax.axis_index("fsdp") // 2
         parts = [pick(whole, zpos, 0)] + [to_z(pick(whole, zpos ^ k, 0), fsdp, k) for k in (1, 2, 3)]
         half = plus(kept, to_core(sent, fsdp)).reshape((dp, chips) + kept.shape[1:])
         dpos = lax.axis_index("dp")
         half = plus(pick(half, dpos, 0), *[flip(pick(half, dpos ^ k, 0), "dp", dp, k) for k in (1, 2, 3)])
         lead_parts = [pick(half, zpos, 0)] + [to_z(pick(half, zpos ^ k, 0), fsdp, k) for k in (1, 2, 3)]
-        wqkv, *vecs = run_lead_sum(lead_parts, 3 * d, wide)
-        wout, wup, wdown = run_body_sum(parts, rows, wide)
+        wout, wup, wdown, wqkv, *vecs = run_final(lead_parts, parts, rows, wide)
     else:
         dq, gq, qsum = run_query_back(bounds, grads, pq, sq, full, bank, a1, cells)
         dk, dv, glead = back(gq, qsum, [lax.psum(sums, "fsdp")])

time: 204 us -> 194 us (0.951)
  other arithmetic: 13.9 us -> 4.76 us
  waiting for transfers between devices: 32.9 us -> 30.4 us
    convert_element_type x8 -> x3, other arithmetic: 10.3 us -> 1.78 us  [local(): functools.reduce(lambda a, b: a + b, [v.astype(F32) for v in parts])]
    ppermute x41 -> x40, starting transfers between devices: 37.7 us -> 39.5 us  [flip(): return lax.ppermute(x, axis, [(i, i ^ mask) for i in range(size)])]
    ppermute x41 -> x40, waiting for transfers between devices: 31.8 us -> 30.4 us  [flip(): return lax.ppermute(x, axis, [(i, i ^ mask) for i in range(size)])]
    unnamed x80 -> x66, local copies, waits for them, and re-layouts: 4.83 us -> 4.53 us
  transfers between devices with their start and end apart: 43 -> 42, of which waited for: 20 -> 15; matrix products, arithmetic and copies ran while one was open for 7% -> 3% of each run, Pallas kernels for 33% -> 35%
where the time goes in v4:
time: 194 us; the launch traced here: 193 us
  Pallas kernels  99.8 us (51%)
  starting transfers between devices  50.2 us (26%)
  waiting for transfers between devices  30.4 us (16%)
  local copies, waits for them, and re-layouts  6.68 us (3%)
  other arithmetic  4.76 us (2%)
    ppermute x40, starting transfers between devices, flip(): return lax.ppermute(x, axis, [(i, i ^ mask) for i in range(size)])  39.5 us
    ppermute x40, waiting for transfers between devices, flip(): return lax.ppermute(x, axis, [(i, i ^ mask) for i in range(size)])  30.4 us
    pallas_call x1, Pallas kernels, run_middle(): pl.pallas_call(functools.partial(middle_kernel, cells, n, len(sums), plac...  28.6 us
    pallas_call x1, Pallas kernels, run_key_back(): pl.pallas_call(functools.partial(key_back_kernel, cells, n, len(sums), pa...  13.4 us
    pallas_call x1, Pallas kernels, run_keys(): pl.pallas_call(functools.partial(key_kernel, cells, places), grid=(n // B...  12 us
    all_to_all x2, starting transfers between devices, far_sums(): lax.all_to_all(out, 'fsdp', 0, 0, axis_index_groups=chip_groups(fsdp), ti...  10.7 us
    pallas_call x1, Pallas kernels, run_weights(): pl.pallas_call(functools.partial(weight_kernel, rows), grid=(wide + 1,),...  10.1 us
    pallas_call x1, Pallas kernels, run_query_back(): pl.pallas_call(functools.partial(query_back_kernel, cells), grid=(n // BL...  9.16 us
  transfers between devices with their start and end apart: 42, of which 15 were waited for; matrix products, arithmetic and copies ran while one was open for 3% of the time, Pallas kernels for 35%

profile of v4, /device:TPU:0, one launch (start us, length us, event | category | flops | bytes accessed | tf_op | source)
XLA Modules:
  0.0 193.1 jit_solution(1534190040649005791)
XLA Ops:
  0.6 2.1 %pack.1 = (bf16[16,1664]{1,0:T(8,128)(2,1)}, bf16[144,512]{1,0:T(8,128)(2,1)}) custom-call(bf16[16,1536]{1,0:T(8,128)(2,1)} %w_qkv.1, bf16[16]{0:T(256)(128)(2,1)} %g1.1, bf16[16]{0:T(256)(128)(2,1)} %s1_.1, bf16[16,512]{1,0:T(8,128)(2,1)} %w_out.1, bf16[16]{0:T(256)(128)(2,1)} %g2.1, bf16[16]{0:T(256)(128)(2,1)} %s2_.1, bf16[16,2048]{1,0:T(8,128)(2,1)} %w_up.1, ...), custom_call_target="tpu_custom_call" | custom-call | tf_op jit(solution)/shard_map/pack/pallas_call | solution.py:941
  2.7 3.0 %collective-permute-start.1 = (bf16[16,1664]{1,0:T(8,128)(2,1)}, bf16[16,1664]{1,0:T(8,128)(2,1)S(1)}, u32[]{:S(2)}, u32[]{:S(2)}) collective-permute-start(bf16[16,1664]{1,0:T(8,128)(2,1)} %get-tuple-element.94), channel_id=1, source_target_pairs={{0,2},{1,3},{2,0},{3,1},{4,6},{5,7},{6,4},{7,5},{8,10},{9,11},{10,... | collective-permute-start | bytes 159752 | tf_op jit(solution)/shard_map/ppermute | solution.py:847
  5.7 2.6 %collective-permute-start.2 = (bf16[16,1664]{1,0:T(8,128)(2,1)}, bf16[16,1664]{1,0:T(8,128)(2,1)S(1)}, u32[]{:S(2)}, u32[]{:S(2)}) collective-permute-start(bf16[16,1664]{1,0:T(8,128)(2,1)} %get-tuple-element.94), channel_id=1, source_target_pairs={{0,4},{1,5},{2,6},{3,7},{4,0},{5,1},{6,2},{7,3},{8,12},{9,13},{10,... | collective-permute-start | bytes 159752 | tf_op jit(solution)/shard_map/ppermute | solution.py:847
  9.2 2.9 %collective-permute-done.2 = bf16[16,1664]{1,0:T(8,128)(2,1)S(1)} collective-permute-done((bf16[16,1664]{1,0:T(8,128)(2,1)}, bf16[16,1664]{1,0:T(8,128)(2,1)S(1)}, u32[]{:S(2)}, u32[]{:S(2)}) %collective-permute-start.2) | collective-permute-done | bytes 53280 | tf_op jit(solution)/shard_map/ppermute | solution.py:847
  12.1 2.9 %collective-permute-done.3 = bf16[16,1664]{1,0:T(8,128)(2,1)S(1)} collective-permute-done((bf16[16,1664]{1,0:T(8,128)(2,1)}, bf16[16,1664]{1,0:T(8,128)(2,1)S(1)}, u32[]{:S(2)}, u32[]{:S(2)}) %collective-permute-start.3) | collective-permute-done | bytes 53280 | tf_op jit(solution)/shard_map/ppermute | solution.py:847
  15.9 1.6 collective-permute-start.4
  20.4 2.8 %collective-permute-done.4.refs_1_ = bf16[4,16,1664]{2,1,0:T(8,128)(2,1)S(1)} collective-permute-done((bf16[4,16,1664]{2,1,0:T(8,128)(2,1)S(1)}, bf16[4,16,1664]{2,1,0:T(8,128)(2,1)S(1)}, u32[]{:S(2)}, u32[]{:S(2)}) %collective-permute-start.4) | collective-permute-done | bytes 213024 | tf_op jit(solution)/shard_map/ppermute | solution.py:847
  23.2 3.5 %collective-permute-done.5.refs_2_ = bf16[4,16,1664]{2,1,0:T(8,128)(2,1)S(1)} collective-permute-done((bf16[4,16,1664]{2,1,0:T(8,128)(2,1)S(1)}, bf16[4,16,1664]{2,1,0:T(8,128)(2,1)S(1)}, u32[]{:S(2)}, u32[]{:S(2)}) %collective-permute-start.5) | collective-permute-done | bytes 213024 | tf_op jit(solution)/shard_map/ppermute | solution.py:847
  29.9 12.0 %keys.1 = (bf16[1024,512]{1,0:T(8,128)(2,1)}, bf16[1024,512]{1,0:T(8,128)(2,1)}, bf16[1024,2048]{1,0:T(8,128)(2,1)}, bf16[1024,512]{1,0:T(8,128)(2,1)}, bf16[2,4...) custom-call(s32[1,5]{1,0:T(1,128)} %bounds.11, bf16[1024,512]{1,0:T(8,128)(2,1)} %bitcast.40, ...), custom_call_target="tpu_custom_call" | custom-call | flops 8000 | bytes 10000 | tf_op jit(solution)/shard_map/keys/pallas_call | solution.py:301
  42.3 2.0 %collective-permute-start.12 = (bf16[4,80,512]{2,1,0:T(8,128)(2,1)S(1)}, bf16[4,80,512]{2,1,0:T(8,128)(2,1)S(1)}, u32[]{:S(2)}, u32[]{:S(2)}) collective-permute-start(bf16[4,80,512]{2,1,0:T(8,128)(2,1)S(1)} %slice.6), channel_id=1, source_target_pairs={{0,8},{8,0},{16,24},{24,16},{1,9},{9,1},{17,25},{25,17},{2,10},{10... | collective-permute-start | bytes 983048 | tf_op jit(solution)/shard_map/ppermute | solution.py:847
  45.5 3.0 %spread.2 = bf16[4,272,256]{2,1,0:T(8,128)(2,1)} custom-call(s32[1,5]{1,0:T(1,128)S(1)} %copy-done.6, bf16[2,4,272,256]{3,2,1,0:T(8,128)(2,1)S(1)} %copy-done, bf16[2,4,272,256]{3,2,1,0:T(8,128)(2,1)S(1)} %collective-permute-done.16.got.refs_1_), custom_call_target="tpu_custom_call" | custom-call | flops 1 | bytes 2000 | tf_op jit(solution)/shard_map/spread/pallas_call | solution.py:393
  48.6 3.7 %all-to-all-start = ((bf16[4,272,256]{2,1,0:T(8,128)(2,1)}), bf16[4,272,256]{2,1,0:T(8,128)(2,1)S(1)}, u32[]{:S(2)}, u32[]{:S(2)}) async-start(bf16[4,272,256]{2,1,0:T(8,128)(2,1)} %spread.2), calls=%async_computation | async-start | bytes 1114112 | tf_op jit(solution)/shard_map/all_to_all | solution.py:972
  52.8 2.2 %collective-permute-start.13 = (bf16[8,80,512]{2,1,0:T(8,128)(2,1)S(1)}, bf16[8,80,512]{2,1,0:T(8,128)(2,1)S(1)}, u32[]{:S(2)}, u32[]{:S(2)}) collective-permute-start(bf16[8,80,512]{2,1,0:T(8,128)(2,1)S(1)} %pad_maximum_fusion), channel_id=1, source_target_pairs={{0,16},{8,24},{16,0},{24,8},{1,17},{9,25},{17,1},{25,9},{2,18},{10... | collective-permute-start | bytes 1966088 | tf_op jit(solution)/shard_map/ppermute | solution.py:847
  57.0 6.8 %queries.1 = (bf16[1024,512]{1,0:T(8,128)(2,1)}, bf16[1024,2048]{1,0:T(8,128)(2,1)}, f32[8,512]{1,0:T(8,128)}) custom-call(bf16[1024,512]{1,0:T(8,128)(2,1)} %get-tuple-element.104.a1, bf16[512,1664]{1,0:T(8,128)(2,1)} %bitcast.37, f32[64,256]{1,0:T(8,128)} %bank.7, f32[16,512]{1,0:T(8,128)} %get-tuple-element.106.vec), custom_call_target="tpu_custom_call" | custom-call | flops 5000 | bytes 7000 | tf_op jit(solution)/shard_map/queries/pallas_call | solution.py:362
  63.8 6.8 %collective-permute-done.15.refs_8_ = bf16[8,64,512]{2,1,0:T(8,128)(2,1)} collective-permute-done((bf16[8,64,512]{2,1,0:T(8,128)(2,1)S(1)}, bf16[8,64,512]{2,1,0:T(8,128)(2,1)}, u32[]{:S(2)}, u32[]{:S(2)}) %collective-permute-start.15) | collective-permute-done | bytes 524320 | tf_op jit(solution)/shard_map/ppermute | solution.py:847
  71.3 3.2 %collective-permute-done.22.refs_13_ = bf16[8,64,512]{2,1,0:T(8,128)(2,1)S(1)} collective-permute-done((bf16[8,64,512]{2,1,0:T(8,128)(2,1)}, bf16[8,64,512]{2,1,0:T(8,128)(2,1)S(1)}, u32[]{:S(2)}, u32[]{:S(2)}) %collective-permute-start.22) | collective-permute-done | bytes 524320 | tf_op jit(solution)/shard_map/ppermute | solution.py:847
  75.7 28.6 %middle.1 = (bf16[1024,512]{1,0:T(8,128)(2,1)}, bf16[1024,2048]{1,0:T(8,128)(2,1)}, bf16[1024,2048]{1,0:T(8,128)(2,1)}, bf16[1024,512]{1,0:T(8,128)(2,1)}, bf16[...) custom-call(s32[1,5]{1,0:T(1,128)} %bounds.11, ...), custom_call_target="tpu_custom_call" | custom-call | flops 14000 | bytes 30000 | tf_op jit(solution)/shard_map/middle/pallas_call | solution.py:535
  104.4 10.1 %weights.1 = (bf16[16,80,512]{2,1,0:T(8,128)(2,1)}, bf16[16,80,512]{2,1,0:T(8,128)(2,1)}, bf16[16,64,512]{2,1,0:T(8,128)(2,1)}, bf16[16,64,512]{2,1,0:T(8,128)(2,1)}) custom-call(bf16[1024,512]{1,0:T(8,128)(2,1)} %get-tuple-element.119.a2, bf16[1024,2048]{1,0:T(8,128)(2,1)} %get-tuple-element.120.dpre, bf16[1024,2048]{1,0:T(8,128)(2,1)} %get-tuple-element.121.gr, ...), custom_call_target="tpu_custom_call" | custom-call | flops 5000 | bytes 20000 | tf_op jit(solution)/shard_map/weights/pallas_call | solution.py:654
  115.2 3.1 %spread.3 = bf16[4,272,256]{2,1,0:T(8,128)(2,1)} custom-call(s32[1,5]{1,0:T(1,128)S(1)} %copy-done.7, bf16[2,4,272,256]{3,2,1,0:T(8,128)(2,1)S(1)} %copy-done.1, bf16[2,4,272,256]{3,2,1,0:T(8,128)(2,1)S(1)} %collective-permute-done.23.got.refs_1_), custom_call_target="tpu_custom_call" | custom-call | flops 1 | bytes 2000 | tf_op jit(solution)/shard_map/spread/pallas_call | solution.py:393
  118.3 7.0 %all-to-all-start.1 = ((bf16[4,272,256]{2,1,0:T(8,128)(2,1)}), bf16[4,272,256]{2,1,0:T(8,128)(2,1)}, u32[]{:S(2)}, u32[]{:S(2)}) async-start(bf16[4,272,256]{2,1,0:T(8,128)(2,1)} %spread.3), calls=%async_computation.1 | async-start | bytes 1114112 | tf_op jit(solution)/shard_map/all_to_all | solution.py:972
  126.5 2.7 %fold.1 = (bf16[4,144,512]{2,1,0:T(8,128)(2,1)S(1)}, bf16[4,144,512]{2,1,0:T(8,128)(2,1)}, bf16[4,144,512]{2,1,0:T(8,128)(2,1)S(1)}, bf16[4,144,512]{2,1,0:T(8,128)(2,1)S(1)}) custom-call(bf16[16,80,512]{2,1,0:T(8,128)(2,1)S(1)} %copy-done.4, bf16[16,80,512]{2,1,0:T(8,128)(2,1)} %collective-permute-done.24.refs_1_, bf16[16,64,512]{2,1,0:T(8,128)(2,1)S(1)} %copy-done.5, ...), custom_call_target="tpu_custom_call" | custom-call | flops 1 | bytes 7000 | tf_op jit(solution)/shard_map/fold/pallas_call | solution.py:690
  130.4 2.4 %collective-permute-start.29 = (bf16[4,144,512]{2,1,0:T(8,128)(2,1)S(1)}, bf16[4,144,512]{2,1,0:T(8,128)(2,1)S(1)}, u32[]{:S(2)}, u32[]{:S(2)}) collective-permute-start(bf16[4,144,512]{2,1,0:T(8,128)(2,1)S(1)} %get-tuple-element.157), channel_id=1, source_target_pairs={{0,24},{8,16},{16,8},{24,0},{1,25},{9,17},{17,9},{25,1},{2,26},{10... | collective-permute-start | bytes 1769480 | tf_op jit(solution)/shard_map/ppermute | solution.py:847
  132.8 9.2 %query_back.1 = (bf16[1024,512]{1,0:T(8,128)(2,1)}, f32[512,512]{1,0:T(8,128)}, f32[8,512]{1,0:T(8,128)}) custom-call(s32[1,5]{1,0:T(1,128)} %bounds.11, bf16[1024,1024]{1,0:T(8,128)(2,1)} %get-tuple-element.135.grads, bf16[1024,2048]{1,0:T(8,128)(2,1)} %get-tuple-element.109.pq, bf16[1024,512]{1,0:T(8,128)(2,1)} %get-tuple-element.136.sq, ...), custom_call_target="tpu_custom_call" | custom-call | flops 3000 | bytes 8000 | tf_op jit(solution)/shard_map/query_back/pallas_call | solution.py:600
  142.0 2.2 %collective-permute-done.26.refs_3_ = bf16[4,272,256]{2,1,0:T(8,128)(2,1)S(1)} collective-permute-done((bf16[4,272,256]{2,1,0:T(8,128)(2,1)}, bf16[4,272,256]{2,1,0:T(8,128)(2,1)S(1)}, u32[]{:S(2)}, u32[]{:S(2)}) %collective-permute-start.26) | collective-permute-done | bytes 557088 | tf_op jit(solution)/shard_map/ppermute | solution.py:847
  145.0 13.4 %key_back.1 = (bf16[1024,512]{1,0:T(8,128)(2,1)}, bf16[1024,512]{1,0:T(8,128)(2,1)}, bf16[16,16,1664]{2,1,0:T(8,128)(2,1)}, bf16[16,16,1664]{2,1,0:T(8,128)(2,1)}) custom-call(s32[1,5]{1,0:T(1,128)} %bounds.11, bf16[1024,512]{1,0:T(8,128)(2,1)} %get-tuple-element.104.a1, bf16[1024,2048]{1,0:T(8,128)(2,1)} %get-tuple-element.139.pk, ...), custom_call_target="tpu_custom_call" | custom-call | flops 6000 | bytes 14000 | tf_op jit(solution)/shard_map/key_back/pallas_call | solution.py:791
  158.7 2.5 %collective-permute-done.30 = bf16[16,16,1664]{2,1,0:T(8,128)(2,1)S(1)} collective-permute-done((bf16[16,16,1664]{2,1,0:T(8,128)(2,1)}, bf16[16,16,1664]{2,1,0:T(8,128)(2,1)S(1)}, u32[]{:S(2)}, u32[]{:S(2)}) %collective-permute-start.30) | collective-permute-done | bytes 852000 | tf_op jit(solution)/shard_map/ppermute | solution.py:847
  162.6 3.3 %collective-permute-start.31 = (bf16[4,16,1664]{2,1,0:T(8,128)(2,1)S(1)}, bf16[4,16,1664]{2,1,0:T(8,128)(2,1)S(1)}, u32[]{:S(2)}, u32[]{:S(2)}) collective-permute-start(bf16[4,16,1664]{2,1,0:T(8,128)(2,1)S(1)} %get-tuple-element.174), channel_id=1, source_target_pairs={{0,8},{8,0},{16,24},{24,16},{1,9},{9,1},{17,25},{25,17},{2,10},{10... | collective-permute-start | bytes 638984 | tf_op jit(solution)/shard_map/ppermute | solution.py:847
  169.1 4.2 %collective-permute-start.38 = (bf16[144,512]{1,0:T(8,128)(2,1)S(1)}, bf16[144,512]{1,0:T(8,128)(2,1)S(1)}, u32[]{:S(2)}, u32[]{:S(2)}) collective-permute-start(bf16[144,512]{1,0:T(8,128)(2,1)S(1)} %get-tuple-element.178), channel_id=1, source_target_pairs={{0,4},{1,5},{2,6},{3,7},{4,0},{5,1},{6,2},{7,3},{8,12},{9,13},{10,... | collective-permute-start | bytes 442376 | tf_op jit(solution)/shard_map/ppermute | solution.py:847
  173.4 3.0 %collective-permute-start.39 = (bf16[144,512]{1,0:T(8,128)(2,1)S(1)}, bf16[144,512]{1,0:T(8,128)(2,1)S(1)}, u32[]{:S(2)}, u32[]{:S(2)}) collective-permute-start(bf16[144,512]{1,0:T(8,128)(2,1)S(1)} %get-tuple-element.177), channel_id=1, source_target_pairs={{0,6},{1,7},{2,4},{3,5},{4,2},{5,3},{6,0},{7,1},{8,14},{9,15},{10,... | collective-permute-start | bytes 442376 | tf_op jit(solution)/shard_map/ppermute | solution.py:847
  178.4 3.4 %collective-permute-start.35 = (bf16[16,1664]{1,0:T(8,128)(2,1)S(1)}, bf16[16,1664]{1,0:T(8,128)(2,1)S(1)}, u32[]{:S(2)}, u32[]{:S(2)}) collective-permute-start(bf16[16,1664]{1,0:T(8,128)(2,1)S(1)} %get-tuple-element.182), channel_id=1, source_target_pairs={{0,4},{1,5},{2,6},{3,7},{4,0},{5,1},{6,2},{7,3},{8,12},{9,13},{10,... | collective-permute-start | bytes 159752 | tf_op jit(solution)/shard_map/ppermute | solution.py:847
  182.8 6.8 %token_back.1 = f32[1024,512]{1,0:T(8,128)} custom-call(bf16[1024,512]{1,0:T(8,128)(2,1)} %bitcast.42, bf16[1024,512]{1,0:T(8,128)(2,1)} %get-tuple-element.138.dq, bf16[1024,512]{1,0:T(8,128)(2,1)} %get-tuple-element.150.dk, bf16[1024,512]{1,0:T(8,128)(2,1)} %get-tuple-element.151.dv, f32[1024,512]{1,0:T(8,128)} %get-tuple-element.152.dx, ...), custom_call_target="tpu_custom_call" | custom-call | flops 2000 | bytes 8000 | tf_op jit(solution)/shard_map/token_back/pallas_call | solution.py:829
  190.8 2.1 %final.1 = (f32[16,512]{1,0:T(8,128)}, f32[16,2048]{1,0:T(8,128)}, f32[64,512]{1,0:T(8,128)}, f32[16,1536]{1,0:T(8,128)}, f32[16]{0:T(128)}, /*index=5*/f32[16]{...) custom-call(bf16[16,1664]{1,0:T(8,128)(2,1)} %get-tuple-element.184.refs_0_, bf16[16,1664]{1,0:T(8,128)(2,1)} %copy-done.30, ...), custom_call_target="tpu_custom_call" | custom-call | tf_op jit(solution)/shard_map/final/pallas_call | solution.py:911
  (143 shorter events, 26.7 us)
Async XLA Ops:
  2.7 6.5 %collective-permute-start.1 = (bf16[16,1664]{1,0:T(8,128)(2,1)}, bf16[16,1664]{1,0:T(8,128)(2,1)S(1)}, u32[]{:S(2)}, u32[]{:S(2)}) collective-permute-start(bf16[16,1664]{1,0:T(8,128)(2,1)} %get-tuple-element.94), channel_id=1, source_target_pairs={{0,2},{1,3},{2,0},{3,1},{4,6},{5,7},{6,4},{7,5},{8,10},{9,11},{10,... | collective-permute-start | bytes 159752 | tf_op jit(solution)/shard_map/ppermute | solution.py:847
  5.7 6.4 %collective-permute-start.2 = (bf16[16,1664]{1,0:T(8,128)(2,1)}, bf16[16,1664]{1,0:T(8,128)(2,1)S(1)}, u32[]{:S(2)}, u32[]{:S(2)}) collective-permute-start(bf16[16,1664]{1,0:T(8,128)(2,1)} %get-tuple-element.94), channel_id=1, source_target_pairs={{0,4},{1,5},{2,6},{3,7},{4,0},{5,1},{6,2},{7,3},{8,12},{9,13},{10,... | collective-permute-start | bytes 159752 | tf_op jit(solution)/shard_map/ppermute | solution.py:847
  8.3 6.7 %collective-permute-start.3 = (bf16[16,1664]{1,0:T(8,128)(2,1)}, bf16[16,1664]{1,0:T(8,128)(2,1)S(1)}, u32[]{:S(2)}, u32[]{:S(2)}) collective-permute-start(bf16[16,1664]{1,0:T(8,128)(2,1)} %get-tuple-element.94), channel_id=1, source_target_pairs={{0,6},{1,7},{2,4},{3,5},{4,2},{5,3},{6,0},{7,1},{8,14},{9,15},{10,... | collective-permute-start | bytes 159752 | tf_op jit(solution)/shard_map/ppermute | solution.py:847
  8.3 11.1 %collective-permute-start = (bf16[144,512]{1,0:T(8,128)(2,1)}, bf16[144,512]{1,0:T(8,128)(2,1)S(1)}, u32[]{:S(2)}, u32[]{:S(2)}) collective-permute-start(bf16[144,512]{1,0:T(8,128)(2,1)} %get-tuple-element.93), channel_id=1, source_target_pairs={{0,2},{1,3},{2,0},{3,1},{4,6},{5,7},{6,4},{7,5},{8,10},{9,11},{10,... | collective-permute-start | bytes 442376 | tf_op jit(solution)/shard_map/ppermute | solution.py:847
  15.9 7.3 %collective-permute-start.4 = (bf16[4,16,1664]{2,1,0:T(8,128)(2,1)S(1)}, bf16[4,16,1664]{2,1,0:T(8,128)(2,1)S(1)}, u32[]{:S(2)}, u32[]{:S(2)}) collective-permute-start(bf16[4,16,1664]{2,1,0:T(8,128)(2,1)S(1)} %pad_maximum_fusion.4.refs_0_), channel_id=1, source_target_pairs={{0,8},{8,0},{16,24},{24,16},{1,9},{9,1},{17,25},{25,17},{2,10},{10... | collective-permute-start | bytes 638984 | tf_op jit(solution)/shard_map/ppermute | solution.py:847
  17.4 9.3 %collective-permute-start.5 = (bf16[4,16,1664]{2,1,0:T(8,128)(2,1)S(1)}, bf16[4,16,1664]{2,1,0:T(8,128)(2,1)S(1)}, u32[]{:S(2)}, u32[]{:S(2)}) collective-permute-start(bf16[4,16,1664]{2,1,0:T(8,128)(2,1)S(1)} %pad_maximum_fusion.4.refs_0_), channel_id=1, source_target_pairs={{0,16},{8,24},{16,0},{24,8},{1,17},{9,25},{17,1},{25,9},{2,18},{10... | collective-permute-start | bytes 638984 | tf_op jit(solution)/shard_map/ppermute | solution.py:847
  19.0 7.8 %collective-permute-start.6 = (bf16[4,16,1664]{2,1,0:T(8,128)(2,1)S(1)}, bf16[4,16,1664]{2,1,0:T(8,128)(2,1)S(1)}, u32[]{:S(2)}, u32[]{:S(2)}) collective-permute-start(bf16[4,16,1664]{2,1,0:T(8,128)(2,1)S(1)} %pad_maximum_fusion.4.refs_0_), channel_id=1, source_target_pairs={{0,24},{8,16},{16,8},{24,0},{1,25},{9,17},{17,9},{25,1},{2,26},{10... | collective-permute-start | bytes 638984 | tf_op jit(solution)/shard_map/ppermute | solution.py:847
  26.7 15.2 %collective-permute-start.11 = (bf16[2,144,512]{2,1,0:T(8,128)(2,1)S(1)}, bf16[2,144,512]{2,1,0:T(8,128)(2,1)S(1)}, u32[]{:S(2)}, u32[]{:S(2)}) collective-permute-start(bf16[2,144,512]{2,1,0:T(8,128)(2,1)S(1)} %pad_maximum_fusion.3), channel_id=1, source_target_pairs={{0,4},{1,5},{2,6},{3,7},{4,0},{5,1},{6,2},{7,3},{8,12},{9,13},{10,... | collective-permute-start | bytes 884744 | tf_op jit(solution)/shard_map/ppermute | solution.py:847
  42.3 10.4 %collective-permute-start.12 = (bf16[4,80,512]{2,1,0:T(8,128)(2,1)S(1)}, bf16[4,80,512]{2,1,0:T(8,128)(2,1)S(1)}, u32[]{:S(2)}, u32[]{:S(2)}) collective-permute-start(bf16[4,80,512]{2,1,0:T(8,128)(2,1)S(1)} %slice.6), channel_id=1, source_target_pairs={{0,8},{8,0},{16,24},{24,16},{1,9},{9,1},{17,25},{25,17},{2,10},{10... | collective-permute-start | bytes 983048 | tf_op jit(solution)/shard_map/ppermute | solution.py:847
  45.1 9.9 %collective-permute-start.14 = (bf16[4,64,512]{2,1,0:T(8,128)(2,1)}, bf16[4,64,512]{2,1,0:T(8,128)(2,1)}, u32[]{:S(2)}, u32[]{:S(2)}) collective-permute-start(bf16[4,64,512]{2,1,0:T(8,128)(2,1)} %slice.7), channel_id=1, source_target_pairs={{0,16},{8,24},{16,0},{24,8},{1,17},{9,25},{17,1},{25,9},{2,18},{10... | collective-permute-start | bytes 786440 | tf_op jit(solution)/shard_map/ppermute | solution.py:847
  48.6 22.1 %all-to-all-start = ((bf16[4,272,256]{2,1,0:T(8,128)(2,1)}), bf16[4,272,256]{2,1,0:T(8,128)(2,1)S(1)}, u32[]{:S(2)}, u32[]{:S(2)}) async-start(bf16[4,272,256]{2,1,0:T(8,128)(2,1)} %spread.2), calls=%async_computation | async-start | bytes 1114112 | tf_op jit(solution)/shard_map/all_to_all | solution.py:972
  52.8 17.8 %collective-permute-start.13 = (bf16[8,80,512]{2,1,0:T(8,128)(2,1)S(1)}, bf16[8,80,512]{2,1,0:T(8,128)(2,1)S(1)}, u32[]{:S(2)}, u32[]{:S(2)}) collective-permute-start(bf16[8,80,512]{2,1,0:T(8,128)(2,1)S(1)} %pad_maximum_fusion), channel_id=1, source_target_pairs={{0,16},{8,24},{16,0},{24,8},{1,17},{9,25},{17,1},{25,9},{2,18},{10... | collective-permute-start | bytes 1966088 | tf_op jit(solution)/shard_map/ppermute | solution.py:847
  55.0 8.7 %collective-permute-start.17 = (bf16[4,144,512]{2,1,0:T(8,128)(2,1)S(1)}, bf16[4,144,512]{2,1,0:T(8,128)(2,1)S(1)}, u32[]{:S(2)}, u32[]{:S(2)}) collective-permute-start(bf16[4,144,512]{2,1,0:T(8,128)(2,1)S(1)} %pad_maximum_fusion.1.refs_4_), channel_id=1, source_target_pairs={{0,1},{1,0},{2,3},{3,2},{4,5},{5,4},{6,7},{7,6},{8,9},{9,8},{10,11... | collective-permute-start | bytes 1769480 | tf_op jit(solution)/shard_map/ppermute | solution.py:847
  56.1 14.5 %collective-permute-start.15 = (bf16[8,64,512]{2,1,0:T(8,128)(2,1)S(1)}, bf16[8,64,512]{2,1,0:T(8,128)(2,1)}, u32[]{:S(2)}, u32[]{:S(2)}) collective-permute-start(bf16[8,64,512]{2,1,0:T(8,128)(2,1)S(1)} %pad_maximum_fusion.2), channel_id=1, source_target_pairs={{0,8},{8,0},{16,24},{24,16},{1,9},{9,1},{17,25},{25,17},{2,10},{10... | collective-permute-start | bytes 1572872 | tf_op jit(solution)/shard_map/ppermute | solution.py:847
  56.4 7.3 %collective-permute-start.18 = (bf16[4,80,512]{2,1,0:T(8,128)(2,1)S(1)}, bf16[4,80,512]{2,1,0:T(8,128)(2,1)S(1)}, u32[]{:S(2)}, u32[]{:S(2)}) collective-permute-start(bf16[4,80,512]{2,1,0:T(8,128)(2,1)S(1)} %collective-permute-done.12.refs_5_), channel_id=1, source_target_pairs={{0,1},{1,0},{2,3},{3,2},{4,5},{5,4},{6,7},{7,6},{8,9},{9,8},{10,11... | collective-permute-start | bytes 983048 | tf_op jit(solution)/shard_map/ppermute | solution.py:847
  56.7 7.0 %collective-permute-start.19 = (bf16[4,64,512]{2,1,0:T(8,128)(2,1)}, bf16[4,64,512]{2,1,0:T(8,128)(2,1)S(1)}, u32[]{:S(2)}, u32[]{:S(2)}) collective-permute-start(bf16[4,64,512]{2,1,0:T(8,128)(2,1)} %collective-permute-done.14.refs_6_), channel_id=1, source_target_pairs={{0,1},{1,0},{2,3},{3,2},{4,5},{5,4},{6,7},{7,6},{8,9},{9,8},{10,11... | collective-permute-start | bytes 786440 | tf_op jit(solution)/shard_map/ppermute | solution.py:847
  104.2 10.3 %collective-permute-start.23 = (bf16[2,4,272,256]{3,2,1,0:T(8,128)(2,1)}, bf16[2,4,272,256]{3,2,1,0:T(8,128)(2,1)S(1)}, u32[]{:S(2)}, u32[]{:S(2)}) collective-permute-start(bf16[2,4,272,256]{3,2,1,0:T(8,128)(2,1)} %get-tuple-element.125.own.refs_0_), channel_id=1, source_target_pairs={{0,1},{1,0},{2,3},{3,2},{4,5},{5,4},{6,7},{7,6},{8,9},{9,8},{10,11... | collective-permute-start | bytes 3342344 | tf_op jit(solution)/shard_map/ppermute | solution.py:847
  114.6 10.7 %collective-permute-start.24 = (bf16[16,80,512]{2,1,0:T(8,128)(2,1)}, bf16[16,80,512]{2,1,0:T(8,128)(2,1)}, u32[]{:S(2)}, u32[]{:S(2)}) collective-permute-start(bf16[16,80,512]{2,1,0:T(8,128)(2,1)} %get-tuple-element.128), channel_id=1, source_target_pairs={{0,1},{1,0},{2,3},{3,2},{4,5},{5,4},{6,7},{7,6},{8,9},{9,8},{10,11... | collective-permute-start | bytes 3932168 | tf_op jit(solution)/shard_map/ppermute | solution.py:847
  115.0 10.2 %collective-permute-start.25 = (bf16[16,64,512]{2,1,0:T(8,128)(2,1)}, bf16[16,64,512]{2,1,0:T(8,128)(2,1)}, u32[]{:S(2)}, u32[]{:S(2)}) collective-permute-start(bf16[16,64,512]{2,1,0:T(8,128)(2,1)} %get-tuple-element.130), channel_id=1, source_target_pairs={{0,1},{1,0},{2,3},{3,2},{4,5},{5,4},{6,7},{7,6},{8,9},{9,8},{10,11... | collective-permute-start | bytes 3145736 | tf_op jit(solution)/shard_map/ppermute | solution.py:847
  118.3 23.7 %all-to-all-start.1 = ((bf16[4,272,256]{2,1,0:T(8,128)(2,1)}), bf16[4,272,256]{2,1,0:T(8,128)(2,1)}, u32[]{:S(2)}, u32[]{:S(2)}) async-start(bf16[4,272,256]{2,1,0:T(8,128)(2,1)} %spread.3), calls=%async_computation.1 | async-start | bytes 1114112 | tf_op jit(solution)/shard_map/all_to_all | solution.py:972
  129.2 29.2 %collective-permute-start.27 = (bf16[4,144,512]{2,1,0:T(8,128)(2,1)}, bf16[4,144,512]{2,1,0:T(8,128)(2,1)S(1)}, u32[]{:S(2)}, u32[]{:S(2)}) collective-permute-start(bf16[4,144,512]{2,1,0:T(8,128)(2,1)} %get-tuple-element.155), channel_id=1, source_target_pairs={{0,8},{8,0},{16,24},{24,16},{1,9},{9,1},{17,25},{25,17},{2,10},{10... | collective-permute-start | bytes 1769480 | tf_op jit(solution)/shard_map/ppermute | solution.py:847
  129.4 29.1 %collective-permute-start.28 = (bf16[4,144,512]{2,1,0:T(8,128)(2,1)S(1)}, bf16[4,144,512]{2,1,0:T(8,128)(2,1)S(1)}, u32[]{:S(2)}, u32[]{:S(2)}) collective-permute-start(bf16[4,144,512]{2,1,0:T(8,128)(2,1)S(1)} %get-tuple-element.156), channel_id=1, source_target_pairs={{0,16},{8,24},{16,0},{24,8},{1,17},{9,25},{17,1},{25,9},{2,18},{10... | collective-permute-start | bytes 1769480 | tf_op jit(solution)/shard_map/ppermute | solution.py:847
  130.4 28.1 %collective-permute-start.29 = (bf16[4,144,512]{2,1,0:T(8,128)(2,1)S(1)}, bf16[4,144,512]{2,1,0:T(8,128)(2,1)S(1)}, u32[]{:S(2)}, u32[]{:S(2)}) collective-permute-start(bf16[4,144,512]{2,1,0:T(8,128)(2,1)S(1)} %get-tuple-element.157), channel_id=1, source_target_pairs={{0,24},{8,16},{16,8},{24,0},{1,25},{9,17},{17,9},{25,1},{2,26},{10... | collective-permute-start | bytes 1769480 | tf_op jit(solution)/shard_map/ppermute | solution.py:847
  162.6 10.8 %collective-permute-start.31 = (bf16[4,16,1664]{2,1,0:T(8,128)(2,1)S(1)}, bf16[4,16,1664]{2,1,0:T(8,128)(2,1)S(1)}, u32[]{:S(2)}, u32[]{:S(2)}) collective-permute-start(bf16[4,16,1664]{2,1,0:T(8,128)(2,1)S(1)} %get-tuple-element.174), channel_id=1, source_target_pairs={{0,8},{8,0},{16,24},{24,16},{1,9},{9,1},{17,25},{25,17},{2,10},{10... | collective-permute-start | bytes 638984 | tf_op jit(solution)/shard_map/ppermute | solution.py:847
  165.9 10.5 %collective-permute-start.32 = (bf16[4,16,1664]{2,1,0:T(8,128)(2,1)S(1)}, bf16[4,16,1664]{2,1,0:T(8,128)(2,1)S(1)}, u32[]{:S(2)}, u32[]{:S(2)}) collective-permute-start(bf16[4,16,1664]{2,1,0:T(8,128)(2,1)S(1)} %get-tuple-element.176), channel_id=1, source_target_pairs={{0,16},{8,24},{16,0},{24,8},{1,17},{9,25},{17,1},{25,9},{2,18},{10... | collective-permute-start | bytes 638984 | tf_op jit(solution)/shard_map/ppermute | solution.py:847
  166.4 11.2 %collective-permute-start.33 = (bf16[4,16,1664]{2,1,0:T(8,128)(2,1)S(1)}, bf16[4,16,1664]{2,1,0:T(8,128)(2,1)S(1)}, u32[]{:S(2)}, u32[]{:S(2)}) collective-permute-start(bf16[4,16,1664]{2,1,0:T(8,128)(2,1)S(1)} %get-tuple-element.175), channel_id=1, source_target_pairs={{0,24},{8,16},{16,8},{24,0},{1,25},{9,17},{17,9},{25,1},{2,26},{10... | collective-permute-start | bytes 638984 | tf_op jit(solution)/shard_map/ppermute | solution.py:847
  168.8 13.0 %collective-permute-start.37 = (bf16[144,512]{1,0:T(8,128)(2,1)S(1)}, bf16[144,512]{1,0:T(8,128)(2,1)S(1)}, u32[]{:S(2)}, u32[]{:S(2)}) collective-permute-start(bf16[144,512]{1,0:T(8,128)(2,1)S(1)} %get-tuple-element.179), channel_id=1, source_target_pairs={{0,2},{1,3},{2,0},{3,1},{4,6},{5,7},{6,4},{7,5},{8,10},{9,11},{10,... | collective-permute-start | bytes 442376 | tf_op jit(solution)/shard_map/ppermute | solution.py:847
  169.1 20.4 %collective-permute-start.38 = (bf16[144,512]{1,0:T(8,128)(2,1)S(1)}, bf16[144,512]{1,0:T(8,128)(2,1)S(1)}, u32[]{:S(2)}, u32[]{:S(2)}) collective-permute-start(bf16[144,512]{1,0:T(8,128)(2,1)S(1)} %get-tuple-element.178), channel_id=1, source_target_pairs={{0,4},{1,5},{2,6},{3,7},{4,0},{5,1},{6,2},{7,3},{8,12},{9,13},{10,... | collective-permute-start | bytes 442376 | tf_op jit(solution)/shard_map/ppermute | solution.py:847
  173.4 16.2 %collective-permute-start.39 = (bf16[144,512]{1,0:T(8,128)(2,1)S(1)}, bf16[144,512]{1,0:T(8,128)(2,1)S(1)}, u32[]{:S(2)}, u32[]{:S(2)}) collective-permute-start(bf16[144,512]{1,0:T(8,128)(2,1)S(1)} %get-tuple-element.177), channel_id=1, source_target_pairs={{0,6},{1,7},{2,4},{3,5},{4,2},{5,3},{6,0},{7,1},{8,14},{9,15},{10,... | collective-permute-start | bytes 442376 | tf_op jit(solution)/shard_map/ppermute | solution.py:847
  178.4 11.2 %collective-permute-start.34 = (bf16[16,1664]{1,0:T(8,128)(2,1)S(1)}, bf16[16,1664]{1,0:T(8,128)(2,1)S(1)}, u32[]{:S(2)}, u32[]{:S(2)}) collective-permute-start(bf16[16,1664]{1,0:T(8,128)(2,1)S(1)} %get-tuple-element.183), channel_id=1, source_target_pairs={{0,2},{1,3},{2,0},{3,1},{4,6},{5,7},{6,4},{7,5},{8,10},{9,11},{10,... | collective-permute-start | bytes 159752 | tf_op jit(solution)/shard_map/ppermute | solution.py:847
  178.4 11.8 %collective-permute-start.35 = (bf16[16,1664]{1,0:T(8,128)(2,1)S(1)}, bf16[16,1664]{1,0:T(8,128)(2,1)S(1)}, u32[]{:S(2)}, u32[]{:S(2)}) collective-permute-start(bf16[16,1664]{1,0:T(8,128)(2,1)S(1)} %get-tuple-element.182), channel_id=1, source_target_pairs={{0,4},{1,5},{2,6},{3,7},{4,0},{5,1},{6,2},{7,3},{8,12},{9,13},{10,... | collective-permute-start | bytes 159752 | tf_op jit(solution)/shard_map/ppermute | solution.py:847
  181.8 8.4 %collective-permute-start.36 = (bf16[16,1664]{1,0:T(8,128)(2,1)S(1)}, bf16[16,1664]{1,0:T(8,128)(2,1)S(1)}, u32[]{:S(2)}, u32[]{:S(2)}) collective-permute-start(bf16[16,1664]{1,0:T(8,128)(2,1)S(1)} %get-tuple-element.181), channel_id=1, source_target_pairs={{0,6},{1,7},{2,4},{3,5},{4,2},{5,3},{6,0},{7,1},{8,14},{9,15},{10,... | collective-permute-start | bytes 159752 | tf_op jit(solution)/shard_map/ppermute | solution.py:847
  (43 other events, 175.8 us)

commit v5 on v4

--- a/solution.py
+++ b/solution.py
@@ -190,7 +190,8 @@
     count = 2 * len(places) if places else 1
     pieces, (a1_o, sk_o, pk_o, vr_o, sums_o, vec_o), refs = refs[:count], refs[count : count + 6], refs[count + 6 :]
     if places:
-        w, acc, rm, rr, sems = refs
+        w_o, acc, rm, rr, w, sems, out_sem = refs
+        leave = pltpu.make_async_copy(w, w_o, out_sem)
     else:
         w = pieces[0]
         acc, rm, rr = refs
@@ -208,6 +209,7 @@
         if places:
             for copy in made:
                 copy.wait()
+            leave.start()
         vec_o[...] = columns(w, 3 * d, 3 * d + 128).astype(F32).T[:16]
 
     keep = keep_lanes(pad)
@@ -240,6 +242,8 @@
     @pl.when(blk == pl.num_programs(0) - 1)
     def _():
         store_sums(acc, sums_o, cells, False)
+        if places:
+            leave.wait()
 
 
 PAD = pl.BlockSpec((1, BLK), lambda i: (0, i))
@@ -295,9 +299,9 @@
     if places:
         piece = pieces[0].shape
         w = (d // (2 * piece[1]), 2) + piece[1:]
-        out_specs.append(whole_spec(w))
+        out_specs.append(HBM)
         out_shape.append(shape(*w))
-        scratch.append(pltpu.SemaphoreType.DMA((d // piece[1],)))
+        scratch += [pltpu.VMEM(w, BF), pltpu.SemaphoreType.DMA((d // piece[1],)), pltpu.SemaphoreType.DMA]
     return pl.pallas_call(
         functools.partial(key_kernel, cells, places),
         grid=(n // BLK,),
@@ -392,7 +396,7 @@
     part = pltpu.VMEM((chips, KVROWS, FEATS), BF)
     return pl.pallas_call(
         functools.partial(spread_kernel, cells, slots),
-        in_specs=[SMEM, ANY, ANY],
+        in_specs=[SMEM, HBM, ANY],
         out_specs=VM,
         out_shape=shape(chips, KVROWS, FEATS),
         scratch_shapes=[part, part, pltpu.SemaphoreType.DMA((2, chips))],
@@ -406,13 +410,13 @@
     sums, refs = refs[:nsums], refs[nsums:]
     count = 2 * len(places) if places else 3
     pieces, refs = refs[:count], refs[count:]
-    mixed_o, gr_o, dpre_o, a2_o, ar_o, do_o, dx_o, grads_o, vec_o, vup_o, sums_o, full = refs[:12]
-    acc, num_s, den_s = refs[12:15]
+    mixed_o, gr_o, dpre_o, a2_o, ar_o, do_o, dx_o, grads_o, vec_o, vup_o, sums_o, full_o = refs[:12]
+    acc, num_s, den_s, full, gr_s, dpre_s, out_sems = refs[12:19]
     blk = pl.program_id(0)
     width = x.shape[1]
     wide = gr_o.shape[1] // width
     if places:
-        w, sems = refs[15:]
+        w, sems = refs[19:]
         rows = width // (2 * w.shape[0])
         base = rows * (1 + wide)
         w_out = lambda: w[:, :, 0:rows, :].reshape(width, width)
@@ -423,6 +427,15 @@
         w_up = lambda j: pieces[1][:, j * width : (j + 1) * width]
         w_down = lambda j: pieces[2][j * width : (j + 1) * width, :]
 
+    full_out = pltpu.make_async_copy(full, full_o, out_sems.at[2, 0])
+    size = x.shape[0]
+
+    def leave(i, j, at):
+        src, dst = ((gr_s, gr_o), (dpre_s, dpre_o))[i]
+        cols = slice(j * width, (j + 1) * width)
+        rows = pl.ds(pl.multiple_of(at * size, size), size)
+        return pltpu.make_async_copy(src.at[:, cols], dst.at[rows, cols], out_sems.at[i, j])
+
     @pl.when(blk == 0)
     def _():
         if places:
@@ -432,6 +445,13 @@
         vec_o[...] = jnp.zeros_like(vec_o)
         vup_o[...] = jnp.zeros_like(vup_o)
         load_sums(bounds, sums, full, slots, cells, False)
+        full_out.start()
+
+    @pl.when(blk > 0)
+    def _():
+        for j in range(wide):
+            leave(0, j, blk - 1).wait()
+            leave(1, j, blk - 1).wait()
 
     low = lane_low(SUB)
 
@@ -478,10 +498,12 @@
         act = pre * half
         slope = half + act * (1.0 - t) * (k0 + (3.0 * k1) * sq)
         gr = act.astype(BF)
-        gr_o[:, cols] = gr
+        gr_s[:, cols] = gr
+        leave(0, j, blk).start()
         mixed += dot(gr, w_down(j))
         dpre = (dot_nt(dy, w_down(j)) * slope).astype(BF)
-        dpre_o[:, cols] = dpre
+        dpre_s[:, cols] = dpre
+        leave(1, j, blk).start()
         da2 += dot_nt(dpre, w_up(j))
         vup_o[j : j + 1] += jnp.sum(dpre.astype(F32), 0, keepdims=True)
     mixed_o[...] = mixed.astype(BF)
@@ -520,13 +542,20 @@
     @pl.when(blk == pl.num_programs(0) - 1)
     def _():
         store_sums(acc, sums_o, cells, True)
+        full_out.wait()
+        for j in range(wide):
+            leave(0, j, blk).wait()
+            leave(1, j, blk).wait()
 
 
 def run_middle(bounds, x, dy, padding, pq, vec, b_up, sums, pieces, places, ff, cells):
     n, d = x.shape
     wide = HEADS * 128
     full = (cells, HEADS, 128, FEATS)
-    scratch = [pltpu.VMEM(full, F32), pltpu.VMEM((WIDE_BLK, d), F32), pltpu.VMEM((WIDE_BLK, d), F32)]
+    scratch = [
+        pltpu.VMEM(full, F32), pltpu.VMEM((WIDE_BLK, d), F32), pltpu.VMEM((WIDE_BLK, d), F32), pltpu.VMEM(full, BF),
+        pltpu.VMEM((WIDE_BLK, ff), BF), pltpu.VMEM((WIDE_BLK, ff), BF), pltpu.SemaphoreType.DMA((3, ff // d)),
+    ]
     if places:
         rows = max(hi for _, _, hi in places)
         chips = 1 + max(m for masks, _, _ in places for m in masks)
@@ -541,9 +570,9 @@
         + whole_specs(sums)
         + ([ANY] * len(pieces) if places else whole_specs(pieces)),
         out_specs=[
-            wide_spec(d), wide_spec(ff), wide_spec(ff), wide_spec(d), wide_spec(d), wide_spec(d),
+            wide_spec(d), HBM, HBM, wide_spec(d), wide_spec(d), wide_spec(d),
             wide_spec(d), wide_spec(wide), whole_spec((16, d)), whole_spec((8, d)),
-            whole_spec(sums_shape(cells)), whole_spec(full),
+            whole_spec(sums_shape(cells)), HBM,
         ],
         out_shape=[
             shape(n, d), shape(n, ff), shape(n, ff), shape(n, d), shape(n, d), shape(n, d),
@@ -689,7 +718,7 @@
     bufs = [pltpu.VMEM((parts, size) + v.shape[1:], BF) for v in (top, top_got, low, low_got)]
     return pl.pallas_call(
         functools.partial(fold_kernel, parts),
-        in_specs=[ANY] * 4,
+        in_specs=[HBM, ANY, HBM, ANY],
         out_specs=[VM] * parts,
         out_shape=[out] * parts,
         scratch_shapes=bufs + [pltpu.SemaphoreType.DMA((parts, 4))],
@@ -828,9 +857,9 @@
     n, d = x.shape
     return pl.pallas_call(
         token_back_kernel,
-        grid=(n // BLK,),
-        in_specs=[rows_spec(d)] * 5 + whole_specs((vec, w)),
-        out_specs=rows_spec(d),
+        grid=(n // WIDE_BLK,),
+        in_specs=[wide_spec(d)] * 5 + whole_specs((vec, w)),
+        out_specs=wide_spec(d),
         out_shape=shape(n, d, kind=F32),
         compiler_params=params(),
         cost_estimate=cost(2, 8),

time: 194 us -> 190 us (0.979)
  starting transfers between devices: 50.2 us -> 48.1 us
  transfers between devices with their start and end apart: 42 -> 42, of which waited for: 15 -> 15; matrix products, arithmetic and copies ran while one was open for 3% -> 3% of each run, Pallas kernels for 35% -> 36%
where the time goes in v5:
time: 190 us; the launch traced here: 189 us
  Pallas kernels  99.3 us (52%)
  starting transfers between devices  48.1 us (25%)
  waiting for transfers between devices  28.8 us (15%)
  local copies, waits for them, and re-layouts  6.66 us (4%)
  other arithmetic  4.75 us (2%)
    ppermute x40, starting transfers between devices, flip(): return lax.ppermute(x, axis, [(i, i ^ mask) for i in range(size)])  38.1 us
    ppermute x40, waiting for transfers between devices, flip(): return lax.ppermute(x, axis, [(i, i ^ mask) for i in range(size)])  28.8 us
    pallas_call x1, Pallas kernels, run_middle(): pl.pallas_call(functools.partial(middle_kernel, cells, n, len(sums), plac...  27.6 us
    pallas_call x1, Pallas kernels, run_key_back(): pl.pallas_call(functools.partial(key_back_kernel, cells, n, len(sums), pa...  14.1 us
    pallas_call x1, Pallas kernels, run_keys(): pl.pallas_call(functools.partial(key_kernel, cells, places), grid=(n // B...  11.8 us
    pallas_call x1, Pallas kernels, run_weights(): pl.pallas_call(functools.partial(weight_kernel, rows), grid=(wide + 1,),...  10.1 us
    all_to_all x2, starting transfers between devices, far_sums(): lax.all_to_all(out, 'fsdp', 0, 0, axis_index_groups=chip_groups(fsdp), ti...  10 us
    pallas_call x1, Pallas kernels, run_query_back(): pl.pallas_call(functools.partial(query_back_kernel, cells), grid=(n // BL...  9.58 us
  transfers between devices with their start and end apart: 42, of which 15 were waited for; matrix products, arithmetic and copies ran while one was open for 3% of the time, Pallas kernels for 36%

profile of v5, /device:TPU:0, one launch (start us, length us, event | category | flops | bytes accessed | tf_op | source)
XLA Modules:
  0.0 189.2 jit_solution(16397393238622105157)
XLA Ops:
  0.6 2.1 %pack.1 = (bf16[16,1664]{1,0:T(8,128)(2,1)}, bf16[144,512]{1,0:T(8,128)(2,1)}) custom-call(bf16[16,1536]{1,0:T(8,128)(2,1)} %w_qkv.1, bf16[16]{0:T(256)(128)(2,1)} %g1.1, bf16[16]{0:T(256)(128)(2,1)} %s1_.1, bf16[16,512]{1,0:T(8,128)(2,1)} %w_out.1, bf16[16]{0:T(256)(128)(2,1)} %g2.1, bf16[16]{0:T(256)(128)(2,1)} %s2_.1, bf16[16,2048]{1,0:T(8,128)(2,1)} %w_up.1, ...), custom_call_target="tpu_custom_call" | custom-call | tf_op jit(solution)/shard_map/pack/pallas_call | solution.py:970
  2.7 3.0 %collective-permute-start.1 = (bf16[16,1664]{1,0:T(8,128)(2,1)}, bf16[16,1664]{1,0:T(8,128)(2,1)S(1)}, u32[]{:S(2)}, u32[]{:S(2)}) collective-permute-start(bf16[16,1664]{1,0:T(8,128)(2,1)} %get-tuple-element.94), channel_id=1, source_target_pairs={{0,2},{1,3},{2,0},{3,1},{4,6},{5,7},{6,4},{7,5},{8,10},{9,11},{10,... | collective-permute-start | bytes 159752 | tf_op jit(solution)/shard_map/ppermute | solution.py:876
  5.7 2.6 %collective-permute-start.2 = (bf16[16,1664]{1,0:T(8,128)(2,1)}, bf16[16,1664]{1,0:T(8,128)(2,1)S(1)}, u32[]{:S(2)}, u32[]{:S(2)}) collective-permute-start(bf16[16,1664]{1,0:T(8,128)(2,1)} %get-tuple-element.94), channel_id=1, source_target_pairs={{0,4},{1,5},{2,6},{3,7},{4,0},{5,1},{6,2},{7,3},{8,12},{9,13},{10,... | collective-permute-start | bytes 159752 | tf_op jit(solution)/shard_map/ppermute | solution.py:876
  9.2 2.9 %collective-permute-done.2 = bf16[16,1664]{1,0:T(8,128)(2,1)S(1)} collective-permute-done((bf16[16,1664]{1,0:T(8,128)(2,1)}, bf16[16,1664]{1,0:T(8,128)(2,1)S(1)}, u32[]{:S(2)}, u32[]{:S(2)}) %collective-permute-start.2) | collective-permute-done | bytes 53280 | tf_op jit(solution)/shard_map/ppermute | solution.py:876
  12.1 2.9 %collective-permute-done.3 = bf16[16,1664]{1,0:T(8,128)(2,1)S(1)} collective-permute-done((bf16[16,1664]{1,0:T(8,128)(2,1)}, bf16[16,1664]{1,0:T(8,128)(2,1)S(1)}, u32[]{:S(2)}, u32[]{:S(2)}) %collective-permute-start.3) | collective-permute-done | bytes 53280 | tf_op jit(solution)/shard_map/ppermute | solution.py:876
  15.9 1.6 collective-permute-start.4
  17.4 1.5 collective-permute-start.5
  20.4 2.8 %collective-permute-done.4.refs_1_ = bf16[4,16,1664]{2,1,0:T(8,128)(2,1)S(1)} collective-permute-done((bf16[4,16,1664]{2,1,0:T(8,128)(2,1)S(1)}, bf16[4,16,1664]{2,1,0:T(8,128)(2,1)S(1)}, u32[]{:S(2)}, u32[]{:S(2)}) %collective-permute-start.4) | collective-permute-done | bytes 213024 | tf_op jit(solution)/shard_map/ppermute | solution.py:876
  23.2 3.5 %collective-permute-done.5.refs_2_ = bf16[4,16,1664]{2,1,0:T(8,128)(2,1)S(1)} collective-permute-done((bf16[4,16,1664]{2,1,0:T(8,128)(2,1)S(1)}, bf16[4,16,1664]{2,1,0:T(8,128)(2,1)S(1)}, u32[]{:S(2)}, u32[]{:S(2)}) %collective-permute-start.5) | collective-permute-done | bytes 213024 | tf_op jit(solution)/shard_map/ppermute | solution.py:876
  29.9 11.8 %keys.1 = (bf16[1024,512]{1,0:T(8,128)(2,1)}, bf16[1024,512]{1,0:T(8,128)(2,1)}, bf16[1024,2048]{1,0:T(8,128)(2,1)}, bf16[1024,512]{1,0:T(8,128)(2,1)}, bf16[2,4...) custom-call(s32[1,5]{1,0:T(1,128)} %bounds.11, bf16[1024,512]{1,0:T(8,128)(2,1)} %bitcast.40, ...), custom_call_target="tpu_custom_call" | custom-call | flops 8000 | bytes 10000 | tf_op jit(solution)/shard_map/keys/pallas_call | solution.py:305
  45.1 3.0 %spread.2 = bf16[4,272,256]{2,1,0:T(8,128)(2,1)} custom-call(s32[1,5]{1,0:T(1,128)S(1)} %copy-done.6, bf16[2,4,272,256]{3,2,1,0:T(8,128)(2,1)S(1)} %copy-done, bf16[2,4,272,256]{3,2,1,0:T(8,128)(2,1)S(1)} %collective-permute-done.16.got.refs_1_), custom_call_target="tpu_custom_call" | custom-call | flops 1 | bytes 2000 | tf_op jit(solution)/shard_map/spread/pallas_call | solution.py:397
  48.1 3.6 %all-to-all-start = ((bf16[4,272,256]{2,1,0:T(8,128)(2,1)}), bf16[4,272,256]{2,1,0:T(8,128)(2,1)S(1)}, u32[]{:S(2)}, u32[]{:S(2)}) async-start(bf16[4,272,256]{2,1,0:T(8,128)(2,1)} %spread.2), calls=%async_computation | async-start | bytes 1114112 | tf_op jit(solution)/shard_map/all_to_all | solution.py:1001
  54.4 1.4 collective-permute-start.15
  56.2 6.7 %queries.1 = (bf16[1024,512]{1,0:T(8,128)(2,1)}, bf16[1024,2048]{1,0:T(8,128)(2,1)}, f32[8,512]{1,0:T(8,128)}) custom-call(bf16[1024,512]{1,0:T(8,128)(2,1)} %get-tuple-element.104.a1, bf16[512,1664]{1,0:T(8,128)(2,1)} %bitcast.37, f32[64,256]{1,0:T(8,128)} %bank.7, f32[16,512]{1,0:T(8,128)} %get-tuple-element.106.vec), custom_call_target="tpu_custom_call" | custom-call | flops 5000 | bytes 7000 | tf_op jit(solution)/shard_map/queries/pallas_call | solution.py:366
  63.0 5.8 %collective-permute-done.15.refs_8_ = bf16[8,64,512]{2,1,0:T(8,128)(2,1)} collective-permute-done((bf16[8,64,512]{2,1,0:T(8,128)(2,1)S(1)}, bf16[8,64,512]{2,1,0:T(8,128)(2,1)}, u32[]{:S(2)}, u32[]{:S(2)}) %collective-permute-start.15) | collective-permute-done | bytes 524320 | tf_op jit(solution)/shard_map/ppermute | solution.py:876
  69.6 3.2 %collective-permute-done.22.refs_13_ = bf16[8,64,512]{2,1,0:T(8,128)(2,1)S(1)} collective-permute-done((bf16[8,64,512]{2,1,0:T(8,128)(2,1)}, bf16[8,64,512]{2,1,0:T(8,128)(2,1)S(1)}, u32[]{:S(2)}, u32[]{:S(2)}) %collective-permute-start.22) | collective-permute-done | bytes 524320 | tf_op jit(solution)/shard_map/ppermute | solution.py:876
  73.9 27.6 %middle.1 = (bf16[1024,512]{1,0:T(8,128)(2,1)}, bf16[1024,2048]{1,0:T(8,128)(2,1)}, bf16[1024,2048]{1,0:T(8,128)(2,1)}, bf16[1024,512]{1,0:T(8,128)(2,1)}, bf16[...) custom-call(s32[1,5]{1,0:T(1,128)} %bounds.11, ...), custom_call_target="tpu_custom_call" | custom-call | flops 14000 | bytes 30000 | tf_op jit(solution)/shard_map/middle/pallas_call | solution.py:564
  101.7 10.1 %weights.1 = (bf16[16,80,512]{2,1,0:T(8,128)(2,1)}, bf16[16,80,512]{2,1,0:T(8,128)(2,1)}, bf16[16,64,512]{2,1,0:T(8,128)(2,1)}, bf16[16,64,512]{2,1,0:T(8,128)(2,1)}) custom-call(bf16[1024,512]{1,0:T(8,128)(2,1)} %get-tuple-element.119.a2, bf16[1024,2048]{1,0:T(8,128)(2,1)} %get-tuple-element.120.dpre, bf16[1024,2048]{1,0:T(8,128)(2,1)} %get-tuple-element.121.gr, ...), custom_call_target="tpu_custom_call" | custom-call | flops 5000 | bytes 20000 | tf_op jit(solution)/shard_map/weights/pallas_call | solution.py:683
  112.5 3.1 %spread.3 = bf16[4,272,256]{2,1,0:T(8,128)(2,1)} custom-call(s32[1,5]{1,0:T(1,128)S(1)} %copy-done.7, bf16[2,4,272,256]{3,2,1,0:T(8,128)(2,1)S(1)} %copy-done.1, bf16[2,4,272,256]{3,2,1,0:T(8,128)(2,1)S(1)} %collective-permute-done.23.got.refs_1_), custom_call_target="tpu_custom_call" | custom-call | flops 1 | bytes 2000 | tf_op jit(solution)/shard_map/spread/pallas_call | solution.py:397
  115.6 6.4 %all-to-all-start.1 = ((bf16[4,272,256]{2,1,0:T(8,128)(2,1)}), bf16[4,272,256]{2,1,0:T(8,128)(2,1)}, u32[]{:S(2)}, u32[]{:S(2)}) async-start(bf16[4,272,256]{2,1,0:T(8,128)(2,1)} %spread.3), calls=%async_computation.1 | async-start | bytes 1114112 | tf_op jit(solution)/shard_map/all_to_all | solution.py:1001
  123.2 2.7 %fold.1 = (bf16[4,144,512]{2,1,0:T(8,128)(2,1)S(1)}, bf16[4,144,512]{2,1,0:T(8,128)(2,1)}, bf16[4,144,512]{2,1,0:T(8,128)(2,1)S(1)}, bf16[4,144,512]{2,1,0:T(8,128)(2,1)S(1)}) custom-call(bf16[16,80,512]{2,1,0:T(8,128)(2,1)S(1)} %copy-done.4, bf16[16,80,512]{2,1,0:T(8,128)(2,1)} %collective-permute-done.24.refs_1_, bf16[16,64,512]{2,1,0:T(8,128)(2,1)S(1)} %copy-done.5, ...), custom_call_target="tpu_custom_call" | custom-call | flops 1 | bytes 7000 | tf_op jit(solution)/shard_map/fold/pallas_call | solution.py:719
  127.2 2.2 %collective-permute-start.29 = (bf16[4,144,512]{2,1,0:T(8,128)(2,1)S(1)}, bf16[4,144,512]{2,1,0:T(8,128)(2,1)S(1)}, u32[]{:S(2)}, u32[]{:S(2)}) collective-permute-start(bf16[4,144,512]{2,1,0:T(8,128)(2,1)S(1)} %get-tuple-element.157), channel_id=1, source_target_pairs={{0,24},{8,16},{16,8},{24,0},{1,25},{9,17},{17,9},{25,1},{2,26},{10... | collective-permute-start | bytes 1769480 | tf_op jit(solution)/shard_map/ppermute | solution.py:876
  129.5 9.6 %query_back.1 = (bf16[1024,512]{1,0:T(8,128)(2,1)}, f32[512,512]{1,0:T(8,128)}, f32[8,512]{1,0:T(8,128)}) custom-call(s32[1,5]{1,0:T(1,128)} %bounds.11, bf16[1024,1024]{1,0:T(8,128)(2,1)} %get-tuple-element.135.grads, bf16[1024,2048]{1,0:T(8,128)(2,1)} %get-tuple-element.109.pq, bf16[1024,512]{1,0:T(8,128)(2,1)} %get-tuple-element.136.sq, ...), custom_call_target="tpu_custom_call" | custom-call | flops 3000 | bytes 8000 | tf_op jit(solution)/shard_map/query_back/pallas_call | solution.py:629
  139.1 2.2 %collective-permute-done.26.refs_3_ = bf16[4,272,256]{2,1,0:T(8,128)(2,1)S(1)} collective-permute-done((bf16[4,272,256]{2,1,0:T(8,128)(2,1)}, bf16[4,272,256]{2,1,0:T(8,128)(2,1)S(1)}, u32[]{:S(2)}, u32[]{:S(2)}) %collective-permute-start.26) | collective-permute-done | bytes 557088 | tf_op jit(solution)/shard_map/ppermute | solution.py:876
  142.1 14.1 %key_back.1 = (bf16[1024,512]{1,0:T(8,128)(2,1)}, bf16[1024,512]{1,0:T(8,128)(2,1)}, bf16[16,16,1664]{2,1,0:T(8,128)(2,1)}, bf16[16,16,1664]{2,1,0:T(8,128)(2,1)}) custom-call(s32[1,5]{1,0:T(1,128)} %bounds.11, bf16[1024,512]{1,0:T(8,128)(2,1)} %get-tuple-element.104.a1, bf16[1024,2048]{1,0:T(8,128)(2,1)} %get-tuple-element.139.pk, ...), custom_call_target="tpu_custom_call" | custom-call | flops 6000 | bytes 14000 | tf_op jit(solution)/shard_map/key_back/pallas_call | solution.py:820
  156.4 2.5 %collective-permute-done.30 = bf16[16,16,1664]{2,1,0:T(8,128)(2,1)S(1)} collective-permute-done((bf16[16,16,1664]{2,1,0:T(8,128)(2,1)}, bf16[16,16,1664]{2,1,0:T(8,128)(2,1)S(1)}, u32[]{:S(2)}, u32[]{:S(2)}) %collective-permute-start.30) | collective-permute-done | bytes 852000 | tf_op jit(solution)/shard_map/ppermute | solution.py:876
  161.2 1.6 collective-permute-start.32
  165.8 3.5 %collective-permute-start.38 = (bf16[144,512]{1,0:T(8,128)(2,1)S(1)}, bf16[144,512]{1,0:T(8,128)(2,1)S(1)}, u32[]{:S(2)}, u32[]{:S(2)}) collective-permute-start(bf16[144,512]{1,0:T(8,128)(2,1)S(1)} %get-tuple-element.178), channel_id=1, source_target_pairs={{0,4},{1,5},{2,6},{3,7},{4,0},{5,1},{6,2},{7,3},{8,12},{9,13},{10,... | collective-permute-start | bytes 442376 | tf_op jit(solution)/shard_map/ppermute | solution.py:876
  169.4 3.0 %collective-permute-start.39 = (bf16[144,512]{1,0:T(8,128)(2,1)S(1)}, bf16[144,512]{1,0:T(8,128)(2,1)S(1)}, u32[]{:S(2)}, u32[]{:S(2)}) collective-permute-start(bf16[144,512]{1,0:T(8,128)(2,1)S(1)} %get-tuple-element.177), channel_id=1, source_target_pairs={{0,6},{1,7},{2,4},{3,5},{4,2},{5,3},{6,0},{7,1},{8,14},{9,15},{10,... | collective-permute-start | bytes 442376 | tf_op jit(solution)/shard_map/ppermute | solution.py:876
  174.6 4.4 %collective-permute-start.35 = (bf16[16,1664]{1,0:T(8,128)(2,1)S(1)}, bf16[16,1664]{1,0:T(8,128)(2,1)S(1)}, u32[]{:S(2)}, u32[]{:S(2)}) collective-permute-start(bf16[16,1664]{1,0:T(8,128)(2,1)S(1)} %get-tuple-element.182), channel_id=1, source_target_pairs={{0,4},{1,5},{2,6},{3,7},{4,0},{5,1},{6,2},{7,3},{8,12},{9,13},{10,... | collective-permute-start | bytes 159752 | tf_op jit(solution)/shard_map/ppermute | solution.py:876
  179.0 6.4 %token_back.1 = f32[1024,512]{1,0:T(8,128)} custom-call(bf16[1024,512]{1,0:T(8,128)(2,1)} %bitcast.42, bf16[1024,512]{1,0:T(8,128)(2,1)} %get-tuple-element.138.dq, bf16[1024,512]{1,0:T(8,128)(2,1)} %get-tuple-element.150.dk, bf16[1024,512]{1,0:T(8,128)(2,1)} %get-tuple-element.151.dv, f32[1024,512]{1,0:T(8,128)} %get-tuple-element.152.dx, ...), custom_call_target="tpu_custom_call" | custom-call | flops 2000 | bytes 8000 | tf_op jit(solution)/shard_map/token_back/pallas_call | solution.py:858
  186.9 2.1 %final.1 = (f32[16,512]{1,0:T(8,128)}, f32[16,2048]{1,0:T(8,128)}, f32[64,512]{1,0:T(8,128)}, f32[16,1536]{1,0:T(8,128)}, f32[16]{0:T(128)}, /*index=5*/f32[16]{...) custom-call(bf16[16,1664]{1,0:T(8,128)(2,1)} %get-tuple-element.184.refs_0_, bf16[16,1664]{1,0:T(8,128)(2,1)} %copy-done.30, ...), custom_call_target="tpu_custom_call" | custom-call | tf_op jit(solution)/shard_map/final/pallas_call | solution.py:940
  (143 shorter events, 27.7 us)
Async XLA Ops:
  2.7 6.5 %collective-permute-start.1 = (bf16[16,1664]{1,0:T(8,128)(2,1)}, bf16[16,1664]{1,0:T(8,128)(2,1)S(1)}, u32[]{:S(2)}, u32[]{:S(2)}) collective-permute-start(bf16[16,1664]{1,0:T(8,128)(2,1)} %get-tuple-element.94), channel_id=1, source_target_pairs={{0,2},{1,3},{2,0},{3,1},{4,6},{5,7},{6,4},{7,5},{8,10},{9,11},{10,... | collective-permute-start | bytes 159752 | tf_op jit(solution)/shard_map/ppermute | solution.py:876
  5.7 6.4 %collective-permute-start.2 = (bf16[16,1664]{1,0:T(8,128)(2,1)}, bf16[16,1664]{1,0:T(8,128)(2,1)S(1)}, u32[]{:S(2)}, u32[]{:S(2)}) collective-permute-start(bf16[16,1664]{1,0:T(8,128)(2,1)} %get-tuple-element.94), channel_id=1, source_target_pairs={{0,4},{1,5},{2,6},{3,7},{4,0},{5,1},{6,2},{7,3},{8,12},{9,13},{10,... | collective-permute-start | bytes 159752 | tf_op jit(solution)/shard_map/ppermute | solution.py:876
  8.3 6.7 %collective-permute-start.3 = (bf16[16,1664]{1,0:T(8,128)(2,1)}, bf16[16,1664]{1,0:T(8,128)(2,1)S(1)}, u32[]{:S(2)}, u32[]{:S(2)}) collective-permute-start(bf16[16,1664]{1,0:T(8,128)(2,1)} %get-tuple-element.94), channel_id=1, source_target_pairs={{0,6},{1,7},{2,4},{3,5},{4,2},{5,3},{6,0},{7,1},{8,14},{9,15},{10,... | collective-permute-start | bytes 159752 | tf_op jit(solution)/shard_map/ppermute | solution.py:876
  8.3 11.1 %collective-permute-start = (bf16[144,512]{1,0:T(8,128)(2,1)}, bf16[144,512]{1,0:T(8,128)(2,1)S(1)}, u32[]{:S(2)}, u32[]{:S(2)}) collective-permute-start(bf16[144,512]{1,0:T(8,128)(2,1)} %get-tuple-element.93), channel_id=1, source_target_pairs={{0,2},{1,3},{2,0},{3,1},{4,6},{5,7},{6,4},{7,5},{8,10},{9,11},{10,... | collective-permute-start | bytes 442376 | tf_op jit(solution)/shard_map/ppermute | solution.py:876
  15.9 7.3 %collective-permute-start.4 = (bf16[4,16,1664]{2,1,0:T(8,128)(2,1)S(1)}, bf16[4,16,1664]{2,1,0:T(8,128)(2,1)S(1)}, u32[]{:S(2)}, u32[]{:S(2)}) collective-permute-start(bf16[4,16,1664]{2,1,0:T(8,128)(2,1)S(1)} %pad_maximum_fusion.4.refs_0_), channel_id=1, source_target_pairs={{0,8},{8,0},{16,24},{24,16},{1,9},{9,1},{17,25},{25,17},{2,10},{10... | collective-permute-start | bytes 638984 | tf_op jit(solution)/shard_map/ppermute | solution.py:876
  17.4 9.3 %collective-permute-start.5 = (bf16[4,16,1664]{2,1,0:T(8,128)(2,1)S(1)}, bf16[4,16,1664]{2,1,0:T(8,128)(2,1)S(1)}, u32[]{:S(2)}, u32[]{:S(2)}) collective-permute-start(bf16[4,16,1664]{2,1,0:T(8,128)(2,1)S(1)} %pad_maximum_fusion.4.refs_0_), channel_id=1, source_target_pairs={{0,16},{8,24},{16,0},{24,8},{1,17},{9,25},{17,1},{25,9},{2,18},{10... | collective-permute-start | bytes 638984 | tf_op jit(solution)/shard_map/ppermute | solution.py:876
  19.0 7.8 %collective-permute-start.6 = (bf16[4,16,1664]{2,1,0:T(8,128)(2,1)S(1)}, bf16[4,16,1664]{2,1,0:T(8,128)(2,1)S(1)}, u32[]{:S(2)}, u32[]{:S(2)}) collective-permute-start(bf16[4,16,1664]{2,1,0:T(8,128)(2,1)S(1)} %pad_maximum_fusion.4.refs_0_), channel_id=1, source_target_pairs={{0,24},{8,16},{16,8},{24,0},{1,25},{9,17},{17,9},{25,1},{2,26},{10... | collective-permute-start | bytes 638984 | tf_op jit(solution)/shard_map/ppermute | solution.py:876
  26.7 15.0 %collective-permute-start.11 = (bf16[2,144,512]{2,1,0:T(8,128)(2,1)S(1)}, bf16[2,144,512]{2,1,0:T(8,128)(2,1)S(1)}, u32[]{:S(2)}, u32[]{:S(2)}) collective-permute-start(bf16[2,144,512]{2,1,0:T(8,128)(2,1)S(1)} %pad_maximum_fusion.3), channel_id=1, source_target_pairs={{0,4},{1,5},{2,6},{3,7},{4,0},{5,1},{6,2},{7,3},{8,12},{9,13},{10,... | collective-permute-start | bytes 884744 | tf_op jit(solution)/shard_map/ppermute | solution.py:876
  42.0 10.2 %collective-permute-start.12 = (bf16[4,80,512]{2,1,0:T(8,128)(2,1)S(1)}, bf16[4,80,512]{2,1,0:T(8,128)(2,1)S(1)}, u32[]{:S(2)}, u32[]{:S(2)}) collective-permute-start(bf16[4,80,512]{2,1,0:T(8,128)(2,1)S(1)} %slice.6), channel_id=1, source_target_pairs={{0,8},{8,0},{16,24},{24,16},{1,9},{9,1},{17,25},{25,17},{2,10},{10... | collective-permute-start | bytes 983048 | tf_op jit(solution)/shard_map/ppermute | solution.py:876
  43.7 9.6 %collective-permute-start.14 = (bf16[4,64,512]{2,1,0:T(8,128)(2,1)}, bf16[4,64,512]{2,1,0:T(8,128)(2,1)}, u32[]{:S(2)}, u32[]{:S(2)}) collective-permute-start(bf16[4,64,512]{2,1,0:T(8,128)(2,1)} %slice.7), channel_id=1, source_target_pairs={{0,16},{8,24},{16,0},{24,8},{1,17},{9,25},{17,1},{25,9},{2,18},{10... | collective-permute-start | bytes 786440 | tf_op jit(solution)/shard_map/ppermute | solution.py:876
  48.1 20.8 %all-to-all-start = ((bf16[4,272,256]{2,1,0:T(8,128)(2,1)}), bf16[4,272,256]{2,1,0:T(8,128)(2,1)S(1)}, u32[]{:S(2)}, u32[]{:S(2)}) async-start(bf16[4,272,256]{2,1,0:T(8,128)(2,1)} %spread.2), calls=%async_computation | async-start | bytes 1114112 | tf_op jit(solution)/shard_map/all_to_all | solution.py:1001
  52.2 16.7 %collective-permute-start.13 = (bf16[8,80,512]{2,1,0:T(8,128)(2,1)S(1)}, bf16[8,80,512]{2,1,0:T(8,128)(2,1)S(1)}, u32[]{:S(2)}, u32[]{:S(2)}) collective-permute-start(bf16[8,80,512]{2,1,0:T(8,128)(2,1)S(1)} %pad_maximum_fusion), channel_id=1, source_target_pairs={{0,16},{8,24},{16,0},{24,8},{1,17},{9,25},{17,1},{25,9},{2,18},{10... | collective-permute-start | bytes 1966088 | tf_op jit(solution)/shard_map/ppermute | solution.py:876
  53.3 9.7 %collective-permute-start.17 = (bf16[4,144,512]{2,1,0:T(8,128)(2,1)S(1)}, bf16[4,144,512]{2,1,0:T(8,128)(2,1)S(1)}, u32[]{:S(2)}, u32[]{:S(2)}) collective-permute-start(bf16[4,144,512]{2,1,0:T(8,128)(2,1)S(1)} %pad_maximum_fusion.1.refs_4_), channel_id=1, source_target_pairs={{0,1},{1,0},{2,3},{3,2},{4,5},{5,4},{6,7},{7,6},{8,9},{9,8},{10,11... | collective-permute-start | bytes 1769480 | tf_op jit(solution)/shard_map/ppermute | solution.py:876
  54.4 14.5 %collective-permute-start.15 = (bf16[8,64,512]{2,1,0:T(8,128)(2,1)S(1)}, bf16[8,64,512]{2,1,0:T(8,128)(2,1)}, u32[]{:S(2)}, u32[]{:S(2)}) collective-permute-start(bf16[8,64,512]{2,1,0:T(8,128)(2,1)S(1)} %pad_maximum_fusion.2), channel_id=1, source_target_pairs={{0,8},{8,0},{16,24},{24,16},{1,9},{9,1},{17,25},{25,17},{2,10},{10... | collective-permute-start | bytes 1572872 | tf_op jit(solution)/shard_map/ppermute | solution.py:876
  55.7 7.3 %collective-permute-start.18 = (bf16[4,80,512]{2,1,0:T(8,128)(2,1)S(1)}, bf16[4,80,512]{2,1,0:T(8,128)(2,1)S(1)}, u32[]{:S(2)}, u32[]{:S(2)}) collective-permute-start(bf16[4,80,512]{2,1,0:T(8,128)(2,1)S(1)} %collective-permute-done.12.refs_5_), channel_id=1, source_target_pairs={{0,1},{1,0},{2,3},{3,2},{4,5},{5,4},{6,7},{7,6},{8,9},{9,8},{10,11... | collective-permute-start | bytes 983048 | tf_op jit(solution)/shard_map/ppermute | solution.py:876
  56.0 7.0 %collective-permute-start.19 = (bf16[4,64,512]{2,1,0:T(8,128)(2,1)}, bf16[4,64,512]{2,1,0:T(8,128)(2,1)S(1)}, u32[]{:S(2)}, u32[]{:S(2)}) collective-permute-start(bf16[4,64,512]{2,1,0:T(8,128)(2,1)} %collective-permute-done.14.refs_6_), channel_id=1, source_target_pairs={{0,1},{1,0},{2,3},{3,2},{4,5},{5,4},{6,7},{7,6},{8,9},{9,8},{10,11... | collective-permute-start | bytes 786440 | tf_op jit(solution)/shard_map/ppermute | solution.py:876
  101.6 10.2 %collective-permute-start.23 = (bf16[2,4,272,256]{3,2,1,0:T(8,128)(2,1)}, bf16[2,4,272,256]{3,2,1,0:T(8,128)(2,1)S(1)}, u32[]{:S(2)}, u32[]{:S(2)}) collective-permute-start(bf16[2,4,272,256]{3,2,1,0:T(8,128)(2,1)} %get-tuple-element.125.own.refs_0_), channel_id=1, source_target_pairs={{0,1},{1,0},{2,3},{3,2},{4,5},{5,4},{6,7},{7,6},{8,9},{9,8},{10,11... | collective-permute-start | bytes 3342344 | tf_op jit(solution)/shard_map/ppermute | solution.py:876
  111.8 10.1 %collective-permute-start.24 = (bf16[16,80,512]{2,1,0:T(8,128)(2,1)}, bf16[16,80,512]{2,1,0:T(8,128)(2,1)}, u32[]{:S(2)}, u32[]{:S(2)}) collective-permute-start(bf16[16,80,512]{2,1,0:T(8,128)(2,1)} %get-tuple-element.128), channel_id=1, source_target_pairs={{0,1},{1,0},{2,3},{3,2},{4,5},{5,4},{6,7},{7,6},{8,9},{9,8},{10,11... | collective-permute-start | bytes 3932168 | tf_op jit(solution)/shard_map/ppermute | solution.py:876
  112.4 9.6 %collective-permute-start.25 = (bf16[16,64,512]{2,1,0:T(8,128)(2,1)}, bf16[16,64,512]{2,1,0:T(8,128)(2,1)}, u32[]{:S(2)}, u32[]{:S(2)}) collective-permute-start(bf16[16,64,512]{2,1,0:T(8,128)(2,1)} %get-tuple-element.130), channel_id=1, source_target_pairs={{0,1},{1,0},{2,3},{3,2},{4,5},{5,4},{6,7},{7,6},{8,9},{9,8},{10,11... | collective-permute-start | bytes 3145736 | tf_op jit(solution)/shard_map/ppermute | solution.py:876
  115.6 23.5 %all-to-all-start.1 = ((bf16[4,272,256]{2,1,0:T(8,128)(2,1)}), bf16[4,272,256]{2,1,0:T(8,128)(2,1)}, u32[]{:S(2)}, u32[]{:S(2)}) async-start(bf16[4,272,256]{2,1,0:T(8,128)(2,1)} %spread.3), calls=%async_computation.1 | async-start | bytes 1114112 | tf_op jit(solution)/shard_map/all_to_all | solution.py:1001
  125.9 30.4 %collective-permute-start.27 = (bf16[4,144,512]{2,1,0:T(8,128)(2,1)}, bf16[4,144,512]{2,1,0:T(8,128)(2,1)S(1)}, u32[]{:S(2)}, u32[]{:S(2)}) collective-permute-start(bf16[4,144,512]{2,1,0:T(8,128)(2,1)} %get-tuple-element.155), channel_id=1, source_target_pairs={{0,8},{8,0},{16,24},{24,16},{1,9},{9,1},{17,25},{25,17},{2,10},{10... | collective-permute-start | bytes 1769480 | tf_op jit(solution)/shard_map/ppermute | solution.py:876
  126.7 29.6 %collective-permute-start.28 = (bf16[4,144,512]{2,1,0:T(8,128)(2,1)S(1)}, bf16[4,144,512]{2,1,0:T(8,128)(2,1)S(1)}, u32[]{:S(2)}, u32[]{:S(2)}) collective-permute-start(bf16[4,144,512]{2,1,0:T(8,128)(2,1)S(1)} %get-tuple-element.156), channel_id=1, source_target_pairs={{0,16},{8,24},{16,0},{24,8},{1,17},{9,25},{17,1},{25,9},{2,18},{10... | collective-permute-start | bytes 1769480 | tf_op jit(solution)/shard_map/ppermute | solution.py:876
  127.2 29.1 %collective-permute-start.29 = (bf16[4,144,512]{2,1,0:T(8,128)(2,1)S(1)}, bf16[4,144,512]{2,1,0:T(8,128)(2,1)S(1)}, u32[]{:S(2)}, u32[]{:S(2)}) collective-permute-start(bf16[4,144,512]{2,1,0:T(8,128)(2,1)S(1)} %get-tuple-element.157), channel_id=1, source_target_pairs={{0,24},{8,16},{16,8},{24,0},{1,25},{9,17},{17,9},{25,1},{2,26},{10... | collective-permute-start | bytes 1769480 | tf_op jit(solution)/shard_map/ppermute | solution.py:876
  160.4 9.0 %collective-permute-start.31 = (bf16[4,16,1664]{2,1,0:T(8,128)(2,1)S(1)}, bf16[4,16,1664]{2,1,0:T(8,128)(2,1)S(1)}, u32[]{:S(2)}, u32[]{:S(2)}) collective-permute-start(bf16[4,16,1664]{2,1,0:T(8,128)(2,1)S(1)} %get-tuple-element.174), channel_id=1, source_target_pairs={{0,8},{8,0},{16,24},{24,16},{1,9},{9,1},{17,25},{25,17},{2,10},{10... | collective-permute-start | bytes 638984 | tf_op jit(solution)/shard_map/ppermute | solution.py:876
  161.2 11.6 %collective-permute-start.32 = (bf16[4,16,1664]{2,1,0:T(8,128)(2,1)S(1)}, bf16[4,16,1664]{2,1,0:T(8,128)(2,1)S(1)}, u32[]{:S(2)}, u32[]{:S(2)}) collective-permute-start(bf16[4,16,1664]{2,1,0:T(8,128)(2,1)S(1)} %get-tuple-element.176), channel_id=1, source_target_pairs={{0,16},{8,24},{16,0},{24,8},{1,17},{9,25},{17,1},{25,9},{2,18},{10... | collective-permute-start | bytes 638984 | tf_op jit(solution)/shard_map/ppermute | solution.py:876
  162.8 10.0 %collective-permute-start.33 = (bf16[4,16,1664]{2,1,0:T(8,128)(2,1)S(1)}, bf16[4,16,1664]{2,1,0:T(8,128)(2,1)S(1)}, u32[]{:S(2)}, u32[]{:S(2)}) collective-permute-start(bf16[4,16,1664]{2,1,0:T(8,128)(2,1)S(1)} %get-tuple-element.175), channel_id=1, source_target_pairs={{0,24},{8,16},{16,8},{24,0},{1,25},{9,17},{17,9},{25,1},{2,26},{10... | collective-permute-start | bytes 638984 | tf_op jit(solution)/shard_map/ppermute | solution.py:876
  164.9 14.1 %collective-permute-start.37 = (bf16[144,512]{1,0:T(8,128)(2,1)S(1)}, bf16[144,512]{1,0:T(8,128)(2,1)S(1)}, u32[]{:S(2)}, u32[]{:S(2)}) collective-permute-start(bf16[144,512]{1,0:T(8,128)(2,1)S(1)} %get-tuple-element.179), channel_id=1, source_target_pairs={{0,2},{1,3},{2,0},{3,1},{4,6},{5,7},{6,4},{7,5},{8,10},{9,11},{10,... | collective-permute-start | bytes 442376 | tf_op jit(solution)/shard_map/ppermute | solution.py:876
  165.8 19.6 %collective-permute-start.38 = (bf16[144,512]{1,0:T(8,128)(2,1)S(1)}, bf16[144,512]{1,0:T(8,128)(2,1)S(1)}, u32[]{:S(2)}, u32[]{:S(2)}) collective-permute-start(bf16[144,512]{1,0:T(8,128)(2,1)S(1)} %get-tuple-element.178), channel_id=1, source_target_pairs={{0,4},{1,5},{2,6},{3,7},{4,0},{5,1},{6,2},{7,3},{8,12},{9,13},{10,... | collective-permute-start | bytes 442376 | tf_op jit(solution)/shard_map/ppermute | solution.py:876
  169.4 16.0 %collective-permute-start.39 = (bf16[144,512]{1,0:T(8,128)(2,1)S(1)}, bf16[144,512]{1,0:T(8,128)(2,1)S(1)}, u32[]{:S(2)}, u32[]{:S(2)}) collective-permute-start(bf16[144,512]{1,0:T(8,128)(2,1)S(1)} %get-tuple-element.177), channel_id=1, source_target_pairs={{0,6},{1,7},{2,4},{3,5},{4,2},{5,3},{6,0},{7,1},{8,14},{9,15},{10,... | collective-permute-start | bytes 442376 | tf_op jit(solution)/shard_map/ppermute | solution.py:876
  173.5 11.9 %collective-permute-start.34 = (bf16[16,1664]{1,0:T(8,128)(2,1)S(1)}, bf16[16,1664]{1,0:T(8,128)(2,1)S(1)}, u32[]{:S(2)}, u32[]{:S(2)}) collective-permute-start(bf16[16,1664]{1,0:T(8,128)(2,1)S(1)} %get-tuple-element.183), channel_id=1, source_target_pairs={{0,2},{1,3},{2,0},{3,1},{4,6},{5,7},{6,4},{7,5},{8,10},{9,11},{10,... | collective-permute-start | bytes 159752 | tf_op jit(solution)/shard_map/ppermute | solution.py:876
  174.6 11.7 %collective-permute-start.35 = (bf16[16,1664]{1,0:T(8,128)(2,1)S(1)}, bf16[16,1664]{1,0:T(8,128)(2,1)S(1)}, u32[]{:S(2)}, u32[]{:S(2)}) collective-permute-start(bf16[16,1664]{1,0:T(8,128)(2,1)S(1)} %get-tuple-element.182), channel_id=1, source_target_pairs={{0,4},{1,5},{2,6},{3,7},{4,0},{5,1},{6,2},{7,3},{8,12},{9,13},{10,... | collective-permute-start | bytes 159752 | tf_op jit(solution)/shard_map/ppermute | solution.py:876
  179.0 7.3 %collective-permute-start.36 = (bf16[16,1664]{1,0:T(8,128)(2,1)S(1)}, bf16[16,1664]{1,0:T(8,128)(2,1)S(1)}, u32[]{:S(2)}, u32[]{:S(2)}) collective-permute-start(bf16[16,1664]{1,0:T(8,128)(2,1)S(1)} %get-tuple-element.181), channel_id=1, source_target_pairs={{0,6},{1,7},{2,4},{3,5},{4,2},{5,3},{6,0},{7,1},{8,14},{9,15},{10,... | collective-permute-start | bytes 159752 | tf_op jit(solution)/shard_map/ppermute | solution.py:876
  (43 other events, 169.1 us)

commit v6 on v5

--- a/solution.py
+++ b/solution.py
@@ -271,8 +271,8 @@
 VM = pl.BlockSpec(memory_space=pltpu.VMEM)
 
 
-def params():
-    return pltpu.CompilerParams(vmem_limit_bytes=VMEM_LIMIT, dimension_semantics=("arbitrary",))
+def params(limit=VMEM_LIMIT):
+    return pltpu.CompilerParams(vmem_limit_bytes=limit, dimension_semantics=("arbitrary",))
 
 
 def cost(gflop, mb):
@@ -861,7 +861,7 @@
         in_specs=[wide_spec(d)] * 5 + whole_specs((vec, w)),
         out_specs=wide_spec(d),
         out_shape=shape(n, d, kind=F32),
-        compiler_params=params(),
+        compiler_params=params(40 * 1024 * 1024),
         cost_estimate=cost(2, 8),
         name="token_back",
     )(x, dq, dk, dv, dx, vec, w)

time: 190 us -> 191 us (level)
  Pallas kernels: 99.3 us -> 94.5 us
  starting transfers between devices: 48.1 us -> 51.1 us
  waiting for transfers between devices: 28.8 us -> 31.8 us
    ppermute x40, waiting for transfers between devices: 28.8 us -> 31.8 us  [flip(): return lax.ppermute(x, axis, [(i, i ^ mask) for i in range(size)])]
    pallas_call x1, Pallas kernels: 6.36 us -> 3.56 us  [run_token_back(): pl.pallas_call(token_back_kernel, grid=(n // WIDE_BLK,), in_specs=[wide_s...]
    ppermute x40, starting transfers between devices: 38.1 us -> 40.1 us  [flip(): return lax.ppermute(x, axis, [(i, i ^ mask) for i in range(size)])]
    unnamed x66 -> x80, local copies, waits for them, and re-layouts: 4.51 us -> 4.57 us
  transfers between devices with their start and end apart: 42 -> 42, of which waited for: 15 -> 13; matrix products, arithmetic and copies ran while one was open for 3% -> 3% of each run, Pallas kernels for 36% -> 33%
where the time goes in v6:
time: 191 us; the launch traced here: 190 us
  Pallas kernels  94.5 us (49%)
  starting transfers between devices  51.1 us (27%)
  waiting for transfers between devices  31.8 us (17%)
  local copies, waits for them, and re-layouts  6.72 us (4%)
  other arithmetic  4.9 us (3%)
    ppermute x40, starting transfers between devices, flip(): return lax.ppermute(x, axis, [(i, i ^ mask) for i in range(size)])  40.1 us
    ppermute x40, waiting for transfers between devices, flip(): return lax.ppermute(x, axis, [(i, i ^ mask) for i in range(size)])  31.8 us
    pallas_call x1, Pallas kernels, run_middle(): pl.pallas_call(functools.partial(middle_kernel, cells, n, len(sums), plac...  27.1 us
    pallas_call x1, Pallas kernels, run_key_back(): pl.pallas_call(functools.partial(key_back_kernel, cells, n, len(sums), pa...  13.4 us
    pallas_call x1, Pallas kernels, run_keys(): pl.pallas_call(functools.partial(key_kernel, cells, places), grid=(n // B...  11.4 us
    all_to_all x2, starting transfers between devices, far_sums(): lax.all_to_all(out, 'fsdp', 0, 0, axis_index_groups=chip_groups(fsdp), ti...  11 us
    pallas_call x1, Pallas kernels, run_weights(): pl.pallas_call(functools.partial(weight_kernel, rows), grid=(wide + 1,),...  10.1 us
    pallas_call x1, Pallas kernels, run_query_back(): pl.pallas_call(functools.partial(query_back_kernel, cells), grid=(n // BL...  9.19 us
  transfers between devices with their start and end apart: 42, of which 13 were waited for; matrix products, arithmetic and copies ran while one was open for 3% of the time, Pallas kernels for 33%

profile of v6, /device:TPU:0, one launch (start us, length us, event | category | flops | bytes accessed | tf_op | source)
XLA Modules:
  0.0 190.4 jit_solution(14340827653001722607)
XLA Ops:
  0.6 2.1 %pack.1 = (bf16[16,1664]{1,0:T(8,128)(2,1)}, bf16[144,512]{1,0:T(8,128)(2,1)}) custom-call(bf16[16,1536]{1,0:T(8,128)(2,1)} %w_qkv.1, bf16[16]{0:T(256)(128)(2,1)} %g1.1, bf16[16]{0:T(256)(128)(2,1)} %s1_.1, bf16[16,512]{1,0:T(8,128)(2,1)} %w_out.1, bf16[16]{0:T(256)(128)(2,1)} %g2.1, bf16[16]{0:T(256)(128)(2,1)} %s2_.1, bf16[16,2048]{1,0:T(8,128)(2,1)} %w_up.1, ...), custom_call_target="tpu_custom_call" | custom-call | tf_op jit(solution)/shard_map/pack/pallas_call | solution.py:970
  2.7 3.0 %collective-permute-start.1 = (bf16[16,1664]{1,0:T(8,128)(2,1)}, bf16[16,1664]{1,0:T(8,128)(2,1)S(1)}, u32[]{:S(2)}, u32[]{:S(2)}) collective-permute-start(bf16[16,1664]{1,0:T(8,128)(2,1)} %get-tuple-element.94), channel_id=1, source_target_pairs={{0,2},{1,3},{2,0},{3,1},{4,6},{5,7},{6,4},{7,5},{8,10},{9,11},{10,... | collective-permute-start | bytes 159752 | tf_op jit(solution)/shard_map/ppermute | solution.py:876
  5.7 2.6 %collective-permute-start.2 = (bf16[16,1664]{1,0:T(8,128)(2,1)}, bf16[16,1664]{1,0:T(8,128)(2,1)S(1)}, u32[]{:S(2)}, u32[]{:S(2)}) collective-permute-start(bf16[16,1664]{1,0:T(8,128)(2,1)} %get-tuple-element.94), channel_id=1, source_target_pairs={{0,4},{1,5},{2,6},{3,7},{4,0},{5,1},{6,2},{7,3},{8,12},{9,13},{10,... | collective-permute-start | bytes 159752 | tf_op jit(solution)/shard_map/ppermute | solution.py:876
  9.2 2.9 %collective-permute-done.2 = bf16[16,1664]{1,0:T(8,128)(2,1)S(1)} collective-permute-done((bf16[16,1664]{1,0:T(8,128)(2,1)}, bf16[16,1664]{1,0:T(8,128)(2,1)S(1)}, u32[]{:S(2)}, u32[]{:S(2)}) %collective-permute-start.2) | collective-permute-done | bytes 53280 | tf_op jit(solution)/shard_map/ppermute | solution.py:876
  12.1 2.9 %collective-permute-done.3 = bf16[16,1664]{1,0:T(8,128)(2,1)S(1)} collective-permute-done((bf16[16,1664]{1,0:T(8,128)(2,1)}, bf16[16,1664]{1,0:T(8,128)(2,1)S(1)}, u32[]{:S(2)}, u32[]{:S(2)}) %collective-permute-start.3) | collective-permute-done | bytes 53280 | tf_op jit(solution)/shard_map/ppermute | solution.py:876
  15.9 1.6 collective-permute-start.4
  20.4 2.8 %collective-permute-done.4.refs_1_ = bf16[4,16,1664]{2,1,0:T(8,128)(2,1)S(1)} collective-permute-done((bf16[4,16,1664]{2,1,0:T(8,128)(2,1)S(1)}, bf16[4,16,1664]{2,1,0:T(8,128)(2,1)S(1)}, u32[]{:S(2)}, u32[]{:S(2)}) %collective-permute-start.4) | collective-permute-done | bytes 213024 | tf_op jit(solution)/shard_map/ppermute | solution.py:876
  23.2 3.5 %collective-permute-done.5.refs_2_ = bf16[4,16,1664]{2,1,0:T(8,128)(2,1)S(1)} collective-permute-done((bf16[4,16,1664]{2,1,0:T(8,128)(2,1)S(1)}, bf16[4,16,1664]{2,1,0:T(8,128)(2,1)S(1)}, u32[]{:S(2)}, u32[]{:S(2)}) %collective-permute-start.5) | collective-permute-done | bytes 213024 | tf_op jit(solution)/shard_map/ppermute | solution.py:876
  30.0 11.4 %keys.1 = (bf16[1024,512]{1,0:T(8,128)(2,1)}, bf16[1024,512]{1,0:T(8,128)(2,1)}, bf16[1024,2048]{1,0:T(8,128)(2,1)}, bf16[1024,512]{1,0:T(8,128)(2,1)}, bf16[2,4...) custom-call(s32[1,5]{1,0:T(1,128)} %bounds.11, bf16[1024,512]{1,0:T(8,128)(2,1)} %bitcast.40, ...), custom_call_target="tpu_custom_call" | custom-call | flops 8000 | bytes 10000 | tf_op jit(solution)/shard_map/keys/pallas_call | solution.py:305
  44.7 3.0 %spread.2 = bf16[4,272,256]{2,1,0:T(8,128)(2,1)} custom-call(s32[1,5]{1,0:T(1,128)S(1)} %copy-done.13, bf16[2,4,272,256]{3,2,1,0:T(8,128)(2,1)S(1)} %copy-done.2, bf16[2,4,272,256]{3,2,1,0:T(8,128)(2,1)S(1)} %collective-permute-done.16.got.refs_1_), custom_call_target="tpu_custom_call" | custom-call | flops 1 | bytes 2000 | tf_op jit(solution)/shard_map/spread/pallas_call | solution.py:397
  47.7 4.0 %all-to-all-start = ((bf16[4,272,256]{2,1,0:T(8,128)(2,1)}), bf16[4,272,256]{2,1,0:T(8,128)(2,1)S(1)}, u32[]{:S(2)}, u32[]{:S(2)}) async-start(bf16[4,272,256]{2,1,0:T(8,128)(2,1)} %spread.2), calls=%async_computation | async-start | bytes 1114112 | tf_op jit(solution)/shard_map/all_to_all | solution.py:1001
  51.8 1.8 collective-permute-start.13
  55.9 6.7 %queries.1 = (bf16[1024,512]{1,0:T(8,128)(2,1)}, bf16[1024,2048]{1,0:T(8,128)(2,1)}, f32[8,512]{1,0:T(8,128)}) custom-call(bf16[1024,512]{1,0:T(8,128)(2,1)} %get-tuple-element.104.a1, bf16[512,1664]{1,0:T(8,128)(2,1)} %bitcast.37, f32[64,256]{1,0:T(8,128)} %bank.7, f32[16,512]{1,0:T(8,128)} %get-tuple-element.106.vec), custom_call_target="tpu_custom_call" | custom-call | flops 5000 | bytes 7000 | tf_op jit(solution)/shard_map/queries/pallas_call | solution.py:366
  62.7 6.6 %collective-permute-done.15.refs_8_ = bf16[8,64,512]{2,1,0:T(8,128)(2,1)} collective-permute-done((bf16[8,64,512]{2,1,0:T(8,128)(2,1)S(1)}, bf16[8,64,512]{2,1,0:T(8,128)(2,1)}, u32[]{:S(2)}, u32[]{:S(2)}) %collective-permute-start.15) | collective-permute-done | bytes 524320 | tf_op jit(solution)/shard_map/ppermute | solution.py:876
  70.0 3.2 %collective-permute-done.22.refs_13_ = bf16[8,64,512]{2,1,0:T(8,128)(2,1)S(1)} collective-permute-done((bf16[8,64,512]{2,1,0:T(8,128)(2,1)}, bf16[8,64,512]{2,1,0:T(8,128)(2,1)S(1)}, u32[]{:S(2)}, u32[]{:S(2)}) %collective-permute-start.22) | collective-permute-done | bytes 524320 | tf_op jit(solution)/shard_map/ppermute | solution.py:876
  74.3 27.1 %middle.1 = (bf16[1024,512]{1,0:T(8,128)(2,1)}, bf16[1024,2048]{1,0:T(8,128)(2,1)}, bf16[1024,2048]{1,0:T(8,128)(2,1)}, bf16[1024,512]{1,0:T(8,128)(2,1)}, bf16[...) custom-call(s32[1,5]{1,0:T(1,128)} %bounds.11, ...), custom_call_target="tpu_custom_call" | custom-call | flops 14000 | bytes 30000 | tf_op jit(solution)/shard_map/middle/pallas_call | solution.py:564
  101.6 10.1 %weights.1 = (bf16[16,80,512]{2,1,0:T(8,128)(2,1)}, bf16[16,80,512]{2,1,0:T(8,128)(2,1)}, bf16[16,64,512]{2,1,0:T(8,128)(2,1)}, bf16[16,64,512]{2,1,0:T(8,128)(2,1)}) custom-call(bf16[1024,512]{1,0:T(8,128)(2,1)} %get-tuple-element.119.a2, bf16[1024,2048]{1,0:T(8,128)(2,1)} %get-tuple-element.120.dpre, bf16[1024,2048]{1,0:T(8,128)(2,1)} %get-tuple-element.121.gr, ...), custom_call_target="tpu_custom_call" | custom-call | flops 5000 | bytes 20000 | tf_op jit(solution)/shard_map/weights/pallas_call | solution.py:683
  112.4 3.1 %spread.3 = bf16[4,272,256]{2,1,0:T(8,128)(2,1)} custom-call(s32[1,5]{1,0:T(1,128)S(1)} %copy-done.14, bf16[2,4,272,256]{3,2,1,0:T(8,128)(2,1)S(1)} %copy-done.3, bf16[2,4,272,256]{3,2,1,0:T(8,128)(2,1)S(1)} %collective-permute-done.23.got.refs_1_), custom_call_target="tpu_custom_call" | custom-call | flops 1 | bytes 2000 | tf_op jit(solution)/shard_map/spread/pallas_call | solution.py:397
  115.5 6.9 %all-to-all-start.1 = ((bf16[4,272,256]{2,1,0:T(8,128)(2,1)}), bf16[4,272,256]{2,1,0:T(8,128)(2,1)}, u32[]{:S(2)}, u32[]{:S(2)}) async-start(bf16[4,272,256]{2,1,0:T(8,128)(2,1)} %spread.3), calls=%async_computation.1 | async-start | bytes 1114112 | tf_op jit(solution)/shard_map/all_to_all | solution.py:1001
  123.7 2.7 %fold.1 = (bf16[4,144,512]{2,1,0:T(8,128)(2,1)S(1)}, bf16[4,144,512]{2,1,0:T(8,128)(2,1)}, bf16[4,144,512]{2,1,0:T(8,128)(2,1)S(1)}, bf16[4,144,512]{2,1,0:T(8,128)(2,1)S(1)}) custom-call(bf16[16,80,512]{2,1,0:T(8,128)(2,1)S(1)} %copy-done.7, bf16[16,80,512]{2,1,0:T(8,128)(2,1)} %collective-permute-done.24.refs_1_, bf16[16,64,512]{2,1,0:T(8,128)(2,1)S(1)} %copy-done.11, ...), custom_call_target="tpu_custom_call" | custom-call | flops 1 | bytes 7000 | tf_op jit(solution)/shard_map/fold/pallas_call | solution.py:719
  128.1 1.9 collective-permute-start.29
  130.0 9.2 %query_back.1 = (bf16[1024,512]{1,0:T(8,128)(2,1)}, f32[512,512]{1,0:T(8,128)}, f32[8,512]{1,0:T(8,128)}) custom-call(s32[1,5]{1,0:T(1,128)} %bounds.11, bf16[1024,1024]{1,0:T(8,128)(2,1)} %get-tuple-element.135.grads, bf16[1024,2048]{1,0:T(8,128)(2,1)} %get-tuple-element.109.pq, bf16[1024,512]{1,0:T(8,128)(2,1)} %get-tuple-element.136.sq, ...), custom_call_target="tpu_custom_call" | custom-call | flops 3000 | bytes 8000 | tf_op jit(solution)/shard_map/query_back/pallas_call | solution.py:629
  139.2 2.2 %collective-permute-done.26.refs_3_ = bf16[4,272,256]{2,1,0:T(8,128)(2,1)S(1)} collective-permute-done((bf16[4,272,256]{2,1,0:T(8,128)(2,1)}, bf16[4,272,256]{2,1,0:T(8,128)(2,1)S(1)}, u32[]{:S(2)}, u32[]{:S(2)}) %collective-permute-start.26) | collective-permute-done | bytes 557088 | tf_op jit(solution)/shard_map/ppermute | solution.py:876
  142.2 13.4 %key_back.1 = (bf16[1024,512]{1,0:T(8,128)(2,1)}, bf16[1024,512]{1,0:T(8,128)(2,1)}, bf16[16,16,1664]{2,1,0:T(8,128)(2,1)}, bf16[16,16,1664]{2,1,0:T(8,128)(2,1)}) custom-call(s32[1,5]{1,0:T(1,128)} %bounds.11, bf16[1024,512]{1,0:T(8,128)(2,1)} %get-tuple-element.104.a1, bf16[1024,2048]{1,0:T(8,128)(2,1)} %get-tuple-element.139.pk, ...), custom_call_target="tpu_custom_call" | custom-call | flops 6000 | bytes 14000 | tf_op jit(solution)/shard_map/key_back/pallas_call | solution.py:820
  155.9 2.4 %collective-permute-done.30 = bf16[16,16,1664]{2,1,0:T(8,128)(2,1)S(1)} collective-permute-done((bf16[16,16,1664]{2,1,0:T(8,128)(2,1)}, bf16[16,16,1664]{2,1,0:T(8,128)(2,1)S(1)}, u32[]{:S(2)}, u32[]{:S(2)}) %collective-permute-start.30) | collective-permute-done | bytes 852000 | tf_op jit(solution)/shard_map/ppermute | solution.py:876
  164.5 2.0 %collective-permute-start.37 = (bf16[144,512]{1,0:T(8,128)(2,1)S(1)}, bf16[144,512]{1,0:T(8,128)(2,1)S(1)}, u32[]{:S(2)}, u32[]{:S(2)}) collective-permute-start(bf16[144,512]{1,0:T(8,128)(2,1)S(1)} %get-tuple-element.179), channel_id=1, source_target_pairs={{0,2},{1,3},{2,0},{3,1},{4,6},{5,7},{6,4},{7,5},{8,10},{9,11},{10,... | collective-permute-start | bytes 442376 | tf_op jit(solution)/shard_map/ppermute | solution.py:876
  166.5 4.2 %collective-permute-start.38 = (bf16[144,512]{1,0:T(8,128)(2,1)S(1)}, bf16[144,512]{1,0:T(8,128)(2,1)S(1)}, u32[]{:S(2)}, u32[]{:S(2)}) collective-permute-start(bf16[144,512]{1,0:T(8,128)(2,1)S(1)} %get-tuple-element.178), channel_id=1, source_target_pairs={{0,4},{1,5},{2,6},{3,7},{4,0},{5,1},{6,2},{7,3},{8,12},{9,13},{10,... | collective-permute-start | bytes 442376 | tf_op jit(solution)/shard_map/ppermute | solution.py:876
  170.7 3.0 %collective-permute-start.39 = (bf16[144,512]{1,0:T(8,128)(2,1)S(1)}, bf16[144,512]{1,0:T(8,128)(2,1)S(1)}, u32[]{:S(2)}, u32[]{:S(2)}) collective-permute-start(bf16[144,512]{1,0:T(8,128)(2,1)S(1)} %get-tuple-element.177), channel_id=1, source_target_pairs={{0,6},{1,7},{2,4},{3,5},{4,2},{5,3},{6,0},{7,1},{8,14},{9,15},{10,... | collective-permute-start | bytes 442376 | tf_op jit(solution)/shard_map/ppermute | solution.py:876
  175.5 4.4 %collective-permute-start.35 = (bf16[16,1664]{1,0:T(8,128)(2,1)S(1)}, bf16[16,1664]{1,0:T(8,128)(2,1)S(1)}, u32[]{:S(2)}, u32[]{:S(2)}) collective-permute-start(bf16[16,1664]{1,0:T(8,128)(2,1)S(1)} %get-tuple-element.182), channel_id=1, source_target_pairs={{0,4},{1,5},{2,6},{3,7},{4,0},{5,1},{6,2},{7,3},{8,12},{9,13},{10,... | collective-permute-start | bytes 159752 | tf_op jit(solution)/shard_map/ppermute | solution.py:876
  180.1 3.6 %token_back.1 = f32[1024,512]{1,0:T(8,128)} custom-call(bf16[1024,512]{1,0:T(8,128)(2,1)S(1)} %bitcast.42, bf16[1024,512]{1,0:T(8,128)(2,1)S(1)} %copy-done.8, bf16[1024,512]{1,0:T(8,128)(2,1)S(1)} %copy-done.9, bf16[1024,512]{1,0:T(8,128)(2,1)S(1)} %copy-done.10, f32[1024,512]{1,0:T(8,128)S(1)} %copy-done.6, f32[16,512]{1,0:T(8,128)S(1)} %copy-done.12, ...), custom_call_target="tpu_custom_call" | custom-call | flops 2000 | bytes 8000 | tf_op jit(solution)/shard_map/token_back/pallas_call | solution.py:858
  183.7 3.8 %collective-permute-done.35.refs_2_ = bf16[16,1664]{1,0:T(8,128)(2,1)S(1)} collective-permute-done((bf16[16,1664]{1,0:T(8,128)(2,1)S(1)}, bf16[16,1664]{1,0:T(8,128)(2,1)S(1)}, u32[]{:S(2)}, u32[]{:S(2)}) %collective-permute-start.35) | collective-permute-done | bytes 53280 | tf_op jit(solution)/shard_map/ppermute | solution.py:876
  188.2 2.1 %final.1 = (f32[16,512]{1,0:T(8,128)}, f32[16,2048]{1,0:T(8,128)}, f32[64,512]{1,0:T(8,128)}, f32[16,1536]{1,0:T(8,128)}, f32[16]{0:T(128)}, /*index=5*/f32[16]{...) custom-call(bf16[16,1664]{1,0:T(8,128)(2,1)} %get-tuple-element.184.refs_0_, bf16[16,1664]{1,0:T(8,128)(2,1)} %copy-done.37, ...), custom_call_target="tpu_custom_call" | custom-call | tf_op jit(solution)/shard_map/final/pallas_call | solution.py:940
  (157 shorter events, 28.6 us)
Async XLA Ops:
  2.7 6.5 %collective-permute-start.1 = (bf16[16,1664]{1,0:T(8,128)(2,1)}, bf16[16,1664]{1,0:T(8,128)(2,1)S(1)}, u32[]{:S(2)}, u32[]{:S(2)}) collective-permute-start(bf16[16,1664]{1,0:T(8,128)(2,1)} %get-tuple-element.94), channel_id=1, source_target_pairs={{0,2},{1,3},{2,0},{3,1},{4,6},{5,7},{6,4},{7,5},{8,10},{9,11},{10,... | collective-permute-start | bytes 159752 | tf_op jit(solution)/shard_map/ppermute | solution.py:876
  5.7 6.4 %collective-permute-start.2 = (bf16[16,1664]{1,0:T(8,128)(2,1)}, bf16[16,1664]{1,0:T(8,128)(2,1)S(1)}, u32[]{:S(2)}, u32[]{:S(2)}) collective-permute-start(bf16[16,1664]{1,0:T(8,128)(2,1)} %get-tuple-element.94), channel_id=1, source_target_pairs={{0,4},{1,5},{2,6},{3,7},{4,0},{5,1},{6,2},{7,3},{8,12},{9,13},{10,... | collective-permute-start | bytes 159752 | tf_op jit(solution)/shard_map/ppermute | solution.py:876
  8.3 6.7 %collective-permute-start.3 = (bf16[16,1664]{1,0:T(8,128)(2,1)}, bf16[16,1664]{1,0:T(8,128)(2,1)S(1)}, u32[]{:S(2)}, u32[]{:S(2)}) collective-permute-start(bf16[16,1664]{1,0:T(8,128)(2,1)} %get-tuple-element.94), channel_id=1, source_target_pairs={{0,6},{1,7},{2,4},{3,5},{4,2},{5,3},{6,0},{7,1},{8,14},{9,15},{10,... | collective-permute-start | bytes 159752 | tf_op jit(solution)/shard_map/ppermute | solution.py:876
  8.3 11.1 %collective-permute-start = (bf16[144,512]{1,0:T(8,128)(2,1)}, bf16[144,512]{1,0:T(8,128)(2,1)S(1)}, u32[]{:S(2)}, u32[]{:S(2)}) collective-permute-start(bf16[144,512]{1,0:T(8,128)(2,1)} %get-tuple-element.93), channel_id=1, source_target_pairs={{0,2},{1,3},{2,0},{3,1},{4,6},{5,7},{6,4},{7,5},{8,10},{9,11},{10,... | collective-permute-start | bytes 442376 | tf_op jit(solution)/shard_map/ppermute | solution.py:876
  15.9 7.3 %collective-permute-start.4 = (bf16[4,16,1664]{2,1,0:T(8,128)(2,1)S(1)}, bf16[4,16,1664]{2,1,0:T(8,128)(2,1)S(1)}, u32[]{:S(2)}, u32[]{:S(2)}) collective-permute-start(bf16[4,16,1664]{2,1,0:T(8,128)(2,1)S(1)} %pad_maximum_fusion.4.refs_0_), channel_id=1, source_target_pairs={{0,8},{8,0},{16,24},{24,16},{1,9},{9,1},{17,25},{25,17},{2,10},{10... | collective-permute-start | bytes 638984 | tf_op jit(solution)/shard_map/ppermute | solution.py:876
  17.4 9.3 %collective-permute-start.5 = (bf16[4,16,1664]{2,1,0:T(8,128)(2,1)S(1)}, bf16[4,16,1664]{2,1,0:T(8,128)(2,1)S(1)}, u32[]{:S(2)}, u32[]{:S(2)}) collective-permute-start(bf16[4,16,1664]{2,1,0:T(8,128)(2,1)S(1)} %pad_maximum_fusion.4.refs_0_), channel_id=1, source_target_pairs={{0,16},{8,24},{16,0},{24,8},{1,17},{9,25},{17,1},{25,9},{2,18},{10... | collective-permute-start | bytes 638984 | tf_op jit(solution)/shard_map/ppermute | solution.py:876
  19.0 7.8 %collective-permute-start.6 = (bf16[4,16,1664]{2,1,0:T(8,128)(2,1)S(1)}, bf16[4,16,1664]{2,1,0:T(8,128)(2,1)S(1)}, u32[]{:S(2)}, u32[]{:S(2)}) collective-permute-start(bf16[4,16,1664]{2,1,0:T(8,128)(2,1)S(1)} %pad_maximum_fusion.4.refs_0_), channel_id=1, source_target_pairs={{0,24},{8,16},{16,8},{24,0},{1,25},{9,17},{17,9},{25,1},{2,26},{10... | collective-permute-start | bytes 638984 | tf_op jit(solution)/shard_map/ppermute | solution.py:876
  26.7 14.7 %collective-permute-start.11 = (bf16[2,144,512]{2,1,0:T(8,128)(2,1)S(1)}, bf16[2,144,512]{2,1,0:T(8,128)(2,1)S(1)}, u32[]{:S(2)}, u32[]{:S(2)}) collective-permute-start(bf16[2,144,512]{2,1,0:T(8,128)(2,1)S(1)} %pad_maximum_fusion.3), channel_id=1, source_target_pairs={{0,4},{1,5},{2,6},{3,7},{4,0},{5,1},{6,2},{7,3},{8,12},{9,13},{10,... | collective-permute-start | bytes 884744 | tf_op jit(solution)/shard_map/ppermute | solution.py:876
  41.8 9.9 %collective-permute-start.12 = (bf16[4,80,512]{2,1,0:T(8,128)(2,1)S(1)}, bf16[4,80,512]{2,1,0:T(8,128)(2,1)S(1)}, u32[]{:S(2)}, u32[]{:S(2)}) collective-permute-start(bf16[4,80,512]{2,1,0:T(8,128)(2,1)S(1)} %slice.6), channel_id=1, source_target_pairs={{0,8},{8,0},{16,24},{24,16},{1,9},{9,1},{17,25},{25,17},{2,10},{10... | collective-permute-start | bytes 983048 | tf_op jit(solution)/shard_map/ppermute | solution.py:876
  43.6 10.1 %collective-permute-start.14 = (bf16[4,64,512]{2,1,0:T(8,128)(2,1)}, bf16[4,64,512]{2,1,0:T(8,128)(2,1)}, u32[]{:S(2)}, u32[]{:S(2)}) collective-permute-start(bf16[4,64,512]{2,1,0:T(8,128)(2,1)} %slice.7), channel_id=1, source_target_pairs={{0,16},{8,24},{16,0},{24,8},{1,17},{9,25},{17,1},{25,9},{2,18},{10... | collective-permute-start | bytes 786440 | tf_op jit(solution)/shard_map/ppermute | solution.py:876
  47.7 21.6 %all-to-all-start = ((bf16[4,272,256]{2,1,0:T(8,128)(2,1)}), bf16[4,272,256]{2,1,0:T(8,128)(2,1)S(1)}, u32[]{:S(2)}, u32[]{:S(2)}) async-start(bf16[4,272,256]{2,1,0:T(8,128)(2,1)} %spread.2), calls=%async_computation | async-start | bytes 1114112 | tf_op jit(solution)/shard_map/all_to_all | solution.py:1001
  51.8 17.4 %collective-permute-start.13 = (bf16[8,80,512]{2,1,0:T(8,128)(2,1)S(1)}, bf16[8,80,512]{2,1,0:T(8,128)(2,1)S(1)}, u32[]{:S(2)}, u32[]{:S(2)}) collective-permute-start(bf16[8,80,512]{2,1,0:T(8,128)(2,1)S(1)} %pad_maximum_fusion), channel_id=1, source_target_pairs={{0,16},{8,24},{16,0},{24,8},{1,17},{9,25},{17,1},{25,9},{2,18},{10... | collective-permute-start | bytes 1966088 | tf_op jit(solution)/shard_map/ppermute | solution.py:876
  53.7 8.9 %collective-permute-start.17 = (bf16[4,144,512]{2,1,0:T(8,128)(2,1)S(1)}, bf16[4,144,512]{2,1,0:T(8,128)(2,1)S(1)}, u32[]{:S(2)}, u32[]{:S(2)}) collective-permute-start(bf16[4,144,512]{2,1,0:T(8,128)(2,1)S(1)} %pad_maximum_fusion.1.refs_4_), channel_id=1, source_target_pairs={{0,1},{1,0},{2,3},{3,2},{4,5},{5,4},{6,7},{7,6},{8,9},{9,8},{10,11... | collective-permute-start | bytes 1769480 | tf_op jit(solution)/shard_map/ppermute | solution.py:876
  54.8 14.5 %collective-permute-start.15 = (bf16[8,64,512]{2,1,0:T(8,128)(2,1)S(1)}, bf16[8,64,512]{2,1,0:T(8,128)(2,1)}, u32[]{:S(2)}, u32[]{:S(2)}) collective-permute-start(bf16[8,64,512]{2,1,0:T(8,128)(2,1)S(1)} %pad_maximum_fusion.2), channel_id=1, source_target_pairs={{0,8},{8,0},{16,24},{24,16},{1,9},{9,1},{17,25},{25,17},{2,10},{10... | collective-permute-start | bytes 1572872 | tf_op jit(solution)/shard_map/ppermute | solution.py:876
  55.3 7.3 %collective-permute-start.18 = (bf16[4,80,512]{2,1,0:T(8,128)(2,1)S(1)}, bf16[4,80,512]{2,1,0:T(8,128)(2,1)S(1)}, u32[]{:S(2)}, u32[]{:S(2)}) collective-permute-start(bf16[4,80,512]{2,1,0:T(8,128)(2,1)S(1)} %collective-permute-done.12.refs_5_), channel_id=1, source_target_pairs={{0,1},{1,0},{2,3},{3,2},{4,5},{5,4},{6,7},{7,6},{8,9},{9,8},{10,11... | collective-permute-start | bytes 983048 | tf_op jit(solution)/shard_map/ppermute | solution.py:876
  55.6 7.0 %collective-permute-start.19 = (bf16[4,64,512]{2,1,0:T(8,128)(2,1)}, bf16[4,64,512]{2,1,0:T(8,128)(2,1)S(1)}, u32[]{:S(2)}, u32[]{:S(2)}) collective-permute-start(bf16[4,64,512]{2,1,0:T(8,128)(2,1)} %collective-permute-done.14.refs_6_), channel_id=1, source_target_pairs={{0,1},{1,0},{2,3},{3,2},{4,5},{5,4},{6,7},{7,6},{8,9},{9,8},{10,11... | collective-permute-start | bytes 786440 | tf_op jit(solution)/shard_map/ppermute | solution.py:876
  101.4 10.3 %collective-permute-start.23 = (bf16[2,4,272,256]{3,2,1,0:T(8,128)(2,1)}, bf16[2,4,272,256]{3,2,1,0:T(8,128)(2,1)S(1)}, u32[]{:S(2)}, u32[]{:S(2)}) collective-permute-start(bf16[2,4,272,256]{3,2,1,0:T(8,128)(2,1)} %get-tuple-element.125.own.refs_0_), channel_id=1, source_target_pairs={{0,1},{1,0},{2,3},{3,2},{4,5},{5,4},{6,7},{7,6},{8,9},{9,8},{10,11... | collective-permute-start | bytes 3342344 | tf_op jit(solution)/shard_map/ppermute | solution.py:876
  111.8 10.6 %collective-permute-start.24 = (bf16[16,80,512]{2,1,0:T(8,128)(2,1)}, bf16[16,80,512]{2,1,0:T(8,128)(2,1)}, u32[]{:S(2)}, u32[]{:S(2)}) collective-permute-start(bf16[16,80,512]{2,1,0:T(8,128)(2,1)} %get-tuple-element.128), channel_id=1, source_target_pairs={{0,1},{1,0},{2,3},{3,2},{4,5},{5,4},{6,7},{7,6},{8,9},{9,8},{10,11... | collective-permute-start | bytes 3932168 | tf_op jit(solution)/shard_map/ppermute | solution.py:876
  112.2 10.2 %collective-permute-start.25 = (bf16[16,64,512]{2,1,0:T(8,128)(2,1)}, bf16[16,64,512]{2,1,0:T(8,128)(2,1)}, u32[]{:S(2)}, u32[]{:S(2)}) collective-permute-start(bf16[16,64,512]{2,1,0:T(8,128)(2,1)} %get-tuple-element.130), channel_id=1, source_target_pairs={{0,1},{1,0},{2,3},{3,2},{4,5},{5,4},{6,7},{7,6},{8,9},{9,8},{10,11... | collective-permute-start | bytes 3145736 | tf_op jit(solution)/shard_map/ppermute | solution.py:876
  115.5 23.7 %all-to-all-start.1 = ((bf16[4,272,256]{2,1,0:T(8,128)(2,1)}), bf16[4,272,256]{2,1,0:T(8,128)(2,1)}, u32[]{:S(2)}, u32[]{:S(2)}) async-start(bf16[4,272,256]{2,1,0:T(8,128)(2,1)} %spread.3), calls=%async_computation.1 | async-start | bytes 1114112 | tf_op jit(solution)/shard_map/all_to_all | solution.py:1001
  126.4 29.2 %collective-permute-start.27 = (bf16[4,144,512]{2,1,0:T(8,128)(2,1)}, bf16[4,144,512]{2,1,0:T(8,128)(2,1)S(1)}, u32[]{:S(2)}, u32[]{:S(2)}) collective-permute-start(bf16[4,144,512]{2,1,0:T(8,128)(2,1)} %get-tuple-element.155), channel_id=1, source_target_pairs={{0,8},{8,0},{16,24},{24,16},{1,9},{9,1},{17,25},{25,17},{2,10},{10... | collective-permute-start | bytes 1769480 | tf_op jit(solution)/shard_map/ppermute | solution.py:876
  127.7 28.0 %collective-permute-start.28 = (bf16[4,144,512]{2,1,0:T(8,128)(2,1)S(1)}, bf16[4,144,512]{2,1,0:T(8,128)(2,1)S(1)}, u32[]{:S(2)}, u32[]{:S(2)}) collective-permute-start(bf16[4,144,512]{2,1,0:T(8,128)(2,1)S(1)} %get-tuple-element.156), channel_id=1, source_target_pairs={{0,16},{8,24},{16,0},{24,8},{1,17},{9,25},{17,1},{25,9},{2,18},{10... | collective-permute-start | bytes 1769480 | tf_op jit(solution)/shard_map/ppermute | solution.py:876
  128.1 27.6 %collective-permute-start.29 = (bf16[4,144,512]{2,1,0:T(8,128)(2,1)S(1)}, bf16[4,144,512]{2,1,0:T(8,128)(2,1)S(1)}, u32[]{:S(2)}, u32[]{:S(2)}) collective-permute-start(bf16[4,144,512]{2,1,0:T(8,128)(2,1)S(1)} %get-tuple-element.157), channel_id=1, source_target_pairs={{0,24},{8,16},{16,8},{24,0},{1,25},{9,17},{17,9},{25,1},{2,26},{10... | collective-permute-start | bytes 1769480 | tf_op jit(solution)/shard_map/ppermute | solution.py:876
  159.9 10.9 %collective-permute-start.31 = (bf16[4,16,1664]{2,1,0:T(8,128)(2,1)S(1)}, bf16[4,16,1664]{2,1,0:T(8,128)(2,1)S(1)}, u32[]{:S(2)}, u32[]{:S(2)}) collective-permute-start(bf16[4,16,1664]{2,1,0:T(8,128)(2,1)S(1)} %get-tuple-element.174), channel_id=1, source_target_pairs={{0,8},{8,0},{16,24},{24,16},{1,9},{9,1},{17,25},{25,17},{2,10},{10... | collective-permute-start | bytes 638984 | tf_op jit(solution)/shard_map/ppermute | solution.py:876
  161.2 12.6 %collective-permute-start.32 = (bf16[4,16,1664]{2,1,0:T(8,128)(2,1)S(1)}, bf16[4,16,1664]{2,1,0:T(8,128)(2,1)S(1)}, u32[]{:S(2)}, u32[]{:S(2)}) collective-permute-start(bf16[4,16,1664]{2,1,0:T(8,128)(2,1)S(1)} %get-tuple-element.176), channel_id=1, source_target_pairs={{0,16},{8,24},{16,0},{24,8},{1,17},{9,25},{17,1},{25,9},{2,18},{10... | collective-permute-start | bytes 638984 | tf_op jit(solution)/shard_map/ppermute | solution.py:876
  162.7 11.1 %collective-permute-start.33 = (bf16[4,16,1664]{2,1,0:T(8,128)(2,1)S(1)}, bf16[4,16,1664]{2,1,0:T(8,128)(2,1)S(1)}, u32[]{:S(2)}, u32[]{:S(2)}) collective-permute-start(bf16[4,16,1664]{2,1,0:T(8,128)(2,1)S(1)} %get-tuple-element.175), channel_id=1, source_target_pairs={{0,24},{8,16},{16,8},{24,0},{1,25},{9,17},{17,9},{25,1},{2,26},{10... | collective-permute-start | bytes 638984 | tf_op jit(solution)/shard_map/ppermute | solution.py:876
  164.5 15.5 %collective-permute-start.37 = (bf16[144,512]{1,0:T(8,128)(2,1)S(1)}, bf16[144,512]{1,0:T(8,128)(2,1)S(1)}, u32[]{:S(2)}, u32[]{:S(2)}) collective-permute-start(bf16[144,512]{1,0:T(8,128)(2,1)S(1)} %get-tuple-element.179), channel_id=1, source_target_pairs={{0,2},{1,3},{2,0},{3,1},{4,6},{5,7},{6,4},{7,5},{8,10},{9,11},{10,... | collective-permute-start | bytes 442376 | tf_op jit(solution)/shard_map/ppermute | solution.py:876
  166.5 17.1 %collective-permute-start.38 = (bf16[144,512]{1,0:T(8,128)(2,1)S(1)}, bf16[144,512]{1,0:T(8,128)(2,1)S(1)}, u32[]{:S(2)}, u32[]{:S(2)}) collective-permute-start(bf16[144,512]{1,0:T(8,128)(2,1)S(1)} %get-tuple-element.178), channel_id=1, source_target_pairs={{0,4},{1,5},{2,6},{3,7},{4,0},{5,1},{6,2},{7,3},{8,12},{9,13},{10,... | collective-permute-start | bytes 442376 | tf_op jit(solution)/shard_map/ppermute | solution.py:876
  170.7 12.9 %collective-permute-start.39 = (bf16[144,512]{1,0:T(8,128)(2,1)S(1)}, bf16[144,512]{1,0:T(8,128)(2,1)S(1)}, u32[]{:S(2)}, u32[]{:S(2)}) collective-permute-start(bf16[144,512]{1,0:T(8,128)(2,1)S(1)} %get-tuple-element.177), channel_id=1, source_target_pairs={{0,6},{1,7},{2,4},{3,5},{4,2},{5,3},{6,0},{7,1},{8,14},{9,15},{10,... | collective-permute-start | bytes 442376 | tf_op jit(solution)/shard_map/ppermute | solution.py:876
  174.5 9.2 %collective-permute-start.34 = (bf16[16,1664]{1,0:T(8,128)(2,1)S(1)}, bf16[16,1664]{1,0:T(8,128)(2,1)S(1)}, u32[]{:S(2)}, u32[]{:S(2)}) collective-permute-start(bf16[16,1664]{1,0:T(8,128)(2,1)S(1)} %get-tuple-element.183), channel_id=1, source_target_pairs={{0,2},{1,3},{2,0},{3,1},{4,6},{5,7},{6,4},{7,5},{8,10},{9,11},{10,... | collective-permute-start | bytes 159752 | tf_op jit(solution)/shard_map/ppermute | solution.py:876
  175.5 12.0 %collective-permute-start.35 = (bf16[16,1664]{1,0:T(8,128)(2,1)S(1)}, bf16[16,1664]{1,0:T(8,128)(2,1)S(1)}, u32[]{:S(2)}, u32[]{:S(2)}) collective-permute-start(bf16[16,1664]{1,0:T(8,128)(2,1)S(1)} %get-tuple-element.182), channel_id=1, source_target_pairs={{0,4},{1,5},{2,6},{3,7},{4,0},{5,1},{6,2},{7,3},{8,12},{9,13},{10,... | collective-permute-start | bytes 159752 | tf_op jit(solution)/shard_map/ppermute | solution.py:876
  180.0 7.5 %collective-permute-start.36 = (bf16[16,1664]{1,0:T(8,128)(2,1)S(1)}, bf16[16,1664]{1,0:T(8,128)(2,1)S(1)}, u32[]{:S(2)}, u32[]{:S(2)}) collective-permute-start(bf16[16,1664]{1,0:T(8,128)(2,1)S(1)} %get-tuple-element.181), channel_id=1, source_target_pairs={{0,6},{1,7},{2,4},{3,5},{4,2},{5,3},{6,0},{7,1},{8,14},{9,15},{10,... | collective-permute-start | bytes 159752 | tf_op jit(solution)/shard_map/ppermute | solution.py:876
  (50 other events, 308.2 us)
